TPU v7x, 32 devices: a whole 2x2x4 slice. The times are simulated.
32 devices in a mesh: groups: 2 (over y), inst: 4 (over z), tp: 4 (over x, core).
Axes of the slice: x: 2, y: 2, z: 4, core: 2. Of those that a mesh axis runs over, the one named last changes fastest.
Arguments:
- queries: bfloat16 [256, 2, 64, 128], P(('groups', 'inst'), None, 'tp'), parts along dimension 0, may hold values from -48 to 48
- new_kv: bfloat16 [256, 2, 2, 8, 128], P(('groups', 'inst'), None, None, 'tp'), parts along dimension 0, may hold values from -4 to 4
- pool_codes: bfloat16 [384, 2, 8, 128, 128], P(('groups', 'inst'), None, 'tp'), parts along dimension 0, may hold values from -6 to 6
- pool_scales: bfloat16 [384, 2, 8], P(('groups', 'inst'), None, 'tp'), parts along dimension 0, may hold values from 0.19921875 to 2.5
- tables: int32 [256, 16], P(('groups', 'inst')), parts along dimension 0, may hold values from 0 to 55, as said below
- ctx_len: int32 [256], P(('groups', 'inst')), parts along dimension 0, may hold values from 1 to 2048
- mig_block: int32 [8, 4], P(('groups', 'inst')), parts along dimension 0, may hold values from 0 to 47, as said below
- mig_dest: int32 [8, 4], P(('groups', 'inst')), parts along dimension 0, may hold values from 0 to 3, as said below
Outputs:
- attn_out: bfloat16 [256, 2, 8192], P(('groups', 'inst'), None, 'tp'), parts along dimension 0
- moved_to: int32 [8, 4], P(('groups', 'inst')), parts along dimension 0
There are 2 independent parts, one for each index of `groups`. A program takes and returns all parts, laid end to end along the dimension named above; each array names one. Nothing has to cross between parts.
Inputs may be any that keep to these rules, and one draw needn't show every extreme that they name: `mig_dest`: at most 2 of one instance's listed blocks go to one destination, and in every draw one destination receives 2 from every instance. `mig_block`: the blocks listed by one instance are distinct. `tables`: entries below 48 name the instance's own blocks; an entry 48 + a names the a-th block arriving there, arrivals ordered by source instance and then by list position; every entry is below 48 plus the number of blocks arriving at that instance. Entries may repeat.
All inputs are finite; a program needn't handle non-finite values.
Results may differ from a plain program's by a relative error of at most 0.0034.
Values may be sent and summed in bfloat16 or wider, within the bound.
No kernel may reach another device: no remote copies, remote signals or barrier semaphores. Data moves between devices by JAX's collectives and lax.ppermute only.
A program may use at most 64 MiB of HBM per device.

v0:
```python
import jax
import jax.numpy as jnp
from jax import lax
from jax.sharding import PartitionSpec as P

CAP = 2


def shards(queries, new_kv, pool_codes, pool_scales, tables, ctx_len, mig_block, mig_dest):
    instances = lax.axis_size("inst")
    pool_size = pool_codes.shape[0]
    requests, steps, q_heads, head_dim = queries.shape
    kv_heads = new_kv.shape[3]
    per_head = q_heads // kv_heads
    spans = tables.shape[1]
    block_len = pool_codes.shape[3]
    factor = head_dim ** (-0.5)
    targets = mig_dest[0]
    sources = mig_block[0]
    listed = targets.shape[0]
    order = jnp.arange(listed)
    same = (targets[:, None] == targets[None, :]) & (order[None, :] < order[:, None])
    rank = jnp.sum(same.astype(jnp.int32), axis=1)
    hits = (targets[None, :] == jnp.arange(instances)[:, None]).astype(jnp.int32)
    sent_count = jnp.sum(hits, axis=1)
    count_rows = lax.all_gather(sent_count[None, :], "inst", axis=0, tiled=True)
    own_index = lax.axis_index("inst")
    below = jnp.arange(instances)[:, None] < own_index
    before = jnp.sum(jnp.where(below, count_rows, 0), axis=0)
    moved_to = (pool_size + jnp.sum(hits * before[:, None], axis=0) + rank)[None, :]
    select = (hits[:, None, :] == 1) & (rank[None, None, :] == jnp.arange(CAP)[None, :, None])
    filled = jnp.any(select, axis=2)
    picked = jnp.sum(jnp.where(select, sources[None, None, :], 0), axis=2)
    slots = instances * CAP

    def fetch(table, row_ids):
        rows = jnp.take(table, row_ids.reshape(-1), axis=0, mode="clip")
        return rows.reshape(row_ids.shape + table.shape[1:])

    group_size = 8
    groups_n = requests // group_size
    query_groups = queries.reshape(groups_n, group_size, steps, kv_heads, per_head, head_dim)
    fresh_groups = new_kv.reshape(groups_n, group_size, steps, 2, kv_heads, head_dim)
    length_groups = ctx_len.reshape(groups_n, group_size)
    causal = jnp.arange(steps)[None, :] <= jnp.arange(steps)[:, None]
    place = jnp.arange(spans)[:, None] * block_len + jnp.arange(block_len)[None, :]

    def multiplicity(row_ids, length, first, count):
        onehot = ((row_ids - first)[:, :, None] == jnp.arange(count)[None, None, :]).astype(
            jnp.float32
        )
        live = (place[None] < length[:, None, None]).astype(jnp.float32)
        return jnp.einsum("reb,rep->rbp", onehot, live, precision=lax.Precision.HIGHEST)

    def cached_scores(query_rows, keys, key_scale, mult):
        scores = jnp.einsum(
            "rtkgd,bkpd->rtkgbp", query_rows, keys, preferred_element_type=jnp.float32
        )
        scores = scores * key_scale.T.astype(jnp.float32)[None, None, :, None, :, None] * factor
        return jnp.where(mult[:, None, None, None] > 0, scores, -jnp.inf)

    def fresh_scores(query_rows, fresh):
        scores = (
            jnp.einsum(
                "rtkgd,rukd->rtkgu", query_rows, fresh[:, :, 0], preferred_element_type=jnp.float32
            )
            * factor
        )
        return jnp.where(causal[None, :, None, None, :], scores, -jnp.inf)

    def weigh(scores, top, value_scale, mult):
        weights = jnp.exp(scores - top[..., None, None])
        many_mult = mult[:, None, None, None]
        part_total = jnp.sum(weights * many_mult, axis=(4, 5))
        scaled = (weights * value_scale.T.astype(jnp.float32)[None, None, :, None, :, None]).astype(
            jnp.bfloat16
        )
        repeated = scaled.astype(jnp.float32) * many_mult
        high = repeated.astype(jnp.bfloat16)
        low = (repeated - high.astype(jnp.float32)).astype(jnp.bfloat16)
        return (part_total, high, low)

    def apply_values(high, low, values):
        mixed = jnp.einsum("rtkgbp,bkpd->rtkgd", high, values, preferred_element_type=jnp.float32)
        return mixed + jnp.einsum(
            "rtkgbp,bkpd->rtkgd", low, values, preferred_element_type=jnp.float32
        )

    def front(items, arr_keys, arr_key_scales, arr_value_scales):
        query_rows, fresh, row_ids, length = items
        own_mult = multiplicity(row_ids, length, 0, pool_size)
        arr_mult = multiplicity(row_ids, length, pool_size, slots)
        own_s = cached_scores(query_rows, pool_codes[:, 0], pool_scales[:, 0], own_mult)
        arr_s = cached_scores(query_rows, arr_keys, arr_key_scales, arr_mult)
        new_s = fresh_scores(query_rows, fresh)
        top = jnp.maximum(
            jnp.maximum(jnp.max(own_s, axis=(4, 5)), jnp.max(arr_s, axis=(4, 5))),
            jnp.max(new_s, axis=4),
        )
        own_total, own_high, own_low = weigh(own_s, top, pool_scales[:, 1], own_mult)
        arr_total, arr_high, arr_low = weigh(arr_s, top, arr_value_scales, arr_mult)
        fresh_w = jnp.exp(new_s - top[..., None])
        total = own_total + arr_total + jnp.sum(fresh_w, axis=4)
        mixed = apply_values(own_high, own_low, pool_codes[:, 1])
        mixed = mixed + jnp.einsum(
            "rtkgu,rukd->rtkgd",
            fresh_w.astype(jnp.bfloat16),
            fresh[:, :, 1],
            preferred_element_type=jnp.float32,
        )
        return (mixed, total, top, arr_high, arr_low)

    def finish(mixed, total):
        return (
            (mixed / total[..., None])
            .astype(jnp.bfloat16)
            .reshape(group_size, steps, q_heads * head_dim)
        )

    block_shape = (kv_heads, block_len, head_dim)
    send_codes = jnp.where(filled[:, :, None, None, None, None], fetch(pool_codes, picked), 0)
    send_scales = jnp.where(filled[:, :, None, None], fetch(pool_scales, picked), 0)
    codes_in, scales_in = (
        lax.all_to_all(send_codes, "inst", split_axis=0, concat_axis=0, tiled=True),
        lax.all_to_all(send_scales, "inst", split_axis=0, concat_axis=0, tiled=True),
    )
    valid = scales_in[:, :, 0, 0].reshape(-1) > 0
    arrival_rank = jnp.cumsum(valid.astype(jnp.int32)) - 1
    offset = tables - pool_size
    match = valid[None, None, :] & (arrival_rank[None, None, :] == offset[:, :, None])
    slot = jnp.sum(jnp.where(match, jnp.arange(slots)[None, None, :], 0), axis=2)
    block_ids = jnp.where(tables < pool_size, tables, pool_size + slot)
    id_groups = block_ids.reshape(groups_n, group_size, spans)
    arr_keys = codes_in[:, :, 0].reshape((slots,) + block_shape)
    arr_values = codes_in[:, :, 1].reshape((slots,) + block_shape)
    arr_key_scales = scales_in[:, :, 0].reshape(slots, kv_heads)
    arr_value_scales = scales_in[:, :, 1].reshape(slots, kv_heads)

    def per_group(items):
        mixed, total, top, arr_high, arr_low = front(
            items, arr_keys, arr_key_scales, arr_value_scales
        )
        mixed = mixed + apply_values(arr_high, arr_low, arr_values)
        return finish(mixed, total)

    outputs = lax.map(per_group, (query_groups, fresh_groups, id_groups, length_groups))
    return (outputs.reshape(requests, steps, q_heads * head_dim), moved_to)


def solution(mesh):
    in_specs = (
        P(("groups", "inst"), None, "tp", None),
        P(("groups", "inst"), None, None, "tp", None),
        P(("groups", "inst"), None, "tp", None, None),
        P(("groups", "inst"), None, "tp"),
        P(("groups", "inst"), None),
        P(("groups", "inst")),
        P(("groups", "inst"), None),
        P(("groups", "inst"), None),
    )
    out_specs = (P(("groups", "inst"), None, "tp"), P(("groups", "inst"), None))
    return jax.shard_map(shards, mesh=mesh, in_specs=in_specs, out_specs=out_specs, check_vma=False)
```

profile of v0, /device:TPU:0, one launch (start us, length us, event | category | flops | bytes accessed | tf_op | source)
XLA Modules:
  0.0 122.0 jit_solution(16718258543931531321)
XLA Ops:
  0.6 0.7 convert_compare_fusion
  1.3 0.8 convert_reduce_fusion
  2.1 1.2 %dynamic-slice = u32[1]{0:T(128)} dynamic-slice(u32[32]{0:T(128)} %constant.84, u32[]{:T(128)S(6)} %add.118), dynamic_slice_sizes={1} | dynamic-slice | bytes 12
  4.0 0.2 dynamic-update-slice
  4.2 9.9 %all-reduce = s32[16]{0:T(128)S(1)} all-reduce(s32[16]{0:T(128)S(1)} %dynamic-update-slice), channel_id=2, replica_groups=mesh['groups'=2,'inst'=4,'tp'=4] {'inst'}, use_global_device_ids=true, to_apply=%add | all-reduce | flops 16 | bytes 128
  14.3 0.9 select_reduce_fusion.1
  15.5 0.8 fusion.70
  16.5 0.8 copy.133
  17.3 0.6 gather_fusion
  18.0 0.6 copy.135
  18.6 3.2 %all-to-all-start = ((bf16[4,2,2,2]{1,3,2,0:T(2,128)(2,1)}), bf16[4,2,2,2]{1,3,2,0:T(2,128)(2,1)S(1)}, u32[]{:S(2)}, u32[]{:S(2)}) async-start(bf16[4,2,2,2]{1,3,2,0:T(2,128)(2,1)} %copy.135), calls=%async_computation | async-start | bytes 8192 | tf_op jit(solution)/shard_map/all_to_all | solution.py:125
  21.9 3.5 %gather_fusion.1 = bf16[8,2,2,128,128]{4,3,2,1,0:T(8,128)(2,1)S(1)} fusion(bf16[48,2,2,128,128]{4,3,2,1,0:T(8,128)(2,1)} %param.12, s32[1024]{0:T(1024)S(1)} %pad_clamp_fusion), kind=kCustom, calls=%fused_computation.1 | custom fusion | bytes 2097184 | tf_op jit(solution)/shard_map/jit(_take)/gather | solution.py:37
  25.4 8.1 %copy.145 = bf16[48,2,2,128,128]{4,3,0,2,1:T(8,128)(2,1)} copy(bf16[48,2,2,128,128]{4,3,2,1,0:T(8,128)(2,1)} %param.12) | data formatting | bytes 12582912
  33.8 1.1 copy.138
  34.8 5.0 %all-to-all-start.1 = ((bf16[4,2,2,2,128,128]{5,4,1,3,2,0:T(8,128)(2,1)}), bf16[4,2,2,2,128,128]{5,4,1,3,2,0:T(8,128)(2,1)S(1)}, u32[]{:S(2)}, u32[]{:S(2)}) async-start(bf16[4,2,2,2,128,128]{5,4,1,3,2,0:T(8,128)(2,1)} %copy.138), calls=%async_computation.1 | async-start | bytes 2097152 | tf_op jit(solution)/shard_map/all_to_all | solution.py:124
  39.9 0.5 add_bitcast_fusion
  41.2 22.1 %all-to-all-done.1 = bf16[4,2,2,2,128,128]{5,4,1,3,2,0:T(8,128)(2,1)S(1)} async-done(((bf16[4,2,2,2,128,128]{5,4,1,3,2,0:T(8,128)(2,1)}), bf16[4,2,2,2,128,128]{5,4,1,3,2,0:T(8,128)(2,1)S(1)}, u32[]{:S(2)}, u32[]{:S(2)}) %all-to-all-start.1) | async-done | bytes 1048608 | tf_op jit(solution)/shard_map/all_to_all | solution.py:124
  63.6 57.6 %while.13 = (s32[]{:T(128)}, bf16[4,8,2,2048]{3,2,1,0:T(2,128)(2,1)S(1)}, s32[4,8,16]{2,1,0:T(8,128)S(1)}, s32[4,8]{1,0:T(4,128)S(1)}, bf16[4,8,2,2,8,128]{5,4,3...) while((s32[]{:T(128)}, ...), condition=%wide.region_12.13_spmd.clone, body=%wide.region_5.12_spmd.clone.sunk | while | flops 1466208128 | bytes 62336220 | solution.py:146
  63.8 0.7 constant_dynamic-slice_fusion.12
  64.7 0.4 fusion.111
  65.2 0.3 broadcast_compare_fusion.5
  65.5 0.4 fusion.110
  65.9 3.3 %bitcast_reduce_fusion.2 = (f32[8,2,2,8]{3,1,0,2:T(2,128)S(1)}, f32[2,8,2,8,48,128]{5,3,4,2,1,0:T(8,128)S(1)}) fusion(f32[2,48]{1,0:T(2,128)S(1)} %get-tuple-element.451, pred[8,48,128]{2,1,0:T(8,128)(4,1)S(1)} %get-tuple-element.453, bf16[48,2,2,128,128]{4,3,0,2,1:T(8,128)(2,1)} %get-tuple-element.495, ...), kind=kOutput, calls=%fused_computation.5.clone.1 | convolution fusion | flops 408944384 | bytes 9553924 | tf_op jit(solution)/shard_map/while/body/eval_jaxpr/rtkgd,bkpd->rtkgbp/dot_general | solution.py:56
  69.3 0.3 multiply_reduce_fusion.5
  69.7 2.5 %multiply_reduce_fusion.4 = f32[8,2,2,8]{3,1,0,2:T(2,128)S(1)} fusion(f32[2,8,2,8,48,128]{5,3,4,2,1,0:T(8,128)S(1)} %get-tuple-element.457, f32[8,48,128]{2,1,0:T(8,128)S(1)} %get-tuple-element.456, f32[8,2,2,8]{3,1,0,2:T(2,128)S(1)} %copy_maximum_fusion.2, f32[2,48]{1,0:T(2,128)S(1)} %get-tuple-element.451, pred[8,48,128]{2,1,0:T(8,128)(4,1)S(1)} %get-tuple-element.453), kind=kLoop, calls=%fused_computation.7.clone.1 | loop fusion | flops 9436928 | bytes 6539648 | tf_op jit(solution)/shard_map/while/body/eval_jaxpr/reduce_sum | solution.py:74
  72.2 2.4 %fusion.113 = f32[2,8,2,8,128]{4,3,2,1,0:T(8,128)S(1)} fusion(bf16[48,2,2,128,128]{4,3,0,2,1:T(8,128)(2,1)S(1)} %bitcast.222, f32[8,48,128]{2,1,0:T(8,128)S(1)} %get-tuple-element.456, f32[2,8,2,8,48,128]{5,3,4,2,1,0:T(8,128)S(1)} %get-tuple-element.457, f32[2,48]{1,0:T(2,128)S(1)} %get-tuple-element.458, ...), kind=kOutput, calls=%fused_computation.30.clone.1 | convolution fusion | flops 421527552 | bytes 9832448 | tf_op jit(solution)/shard_map/while/body/eval_jaxpr/rtkgbp,bkpd->rtkgd/dot_general | solution.py:85
  74.6 2.2 %fusion.114 = f32[8,2,2,8,128]{4,3,1,0,2:T(8,128)S(1)} fusion(f32[2,8,2,8,128]{4,3,2,1,0:T(8,128)S(1)} %fusion.113, bf16[48,2,2,128,128]{4,3,0,2,1:T(8,128)(2,1)S(1)} %bitcast.222, f32[8,48,128]{2,1,0:T(8,128)S(1)} %get-tuple-element.456, f32[2,8,2,8,48,128]{5,3,4,2,1,0:T(8,128)S(1)} %get-tuple-element.457, f32[2,48]{1,0:T(2,128)S(1)} %get-tuple-element.458, ...), kind=kOutput, calls=%fused_computation.37.clone.1 | convolution fusion | flops 416841728 | bytes 9963520 | tf_op jit(solution)/shard_map/while/body/eval_jaxpr/rtkgbp,bkpd->rtkgd/dot_general | solution.py:84
  76.9 0.4 convolution_bitcast_fusion.4
  77.3 0.4 fusion.112
  78.2 0.7 constant_dynamic-slice_fusion.12
  79.1 0.4 fusion.111
  79.6 0.3 broadcast_compare_fusion.5
  79.9 0.4 fusion.110
  80.3 3.3 %bitcast_reduce_fusion.2 = (f32[8,2,2,8]{3,1,0,2:T(2,128)S(1)}, f32[2,8,2,8,48,128]{5,3,4,2,1,0:T(8,128)S(1)}) fusion(f32[2,48]{1,0:T(2,128)S(1)} %get-tuple-element.451, pred[8,48,128]{2,1,0:T(8,128)(4,1)S(1)} %get-tuple-element.453, bf16[48,2,2,128,128]{4,3,0,2,1:T(8,128)(2,1)} %get-tuple-element.495, ...), kind=kOutput, calls=%fused_computation.5.clone.1 | convolution fusion | flops 408944384 | bytes 9553924 | tf_op jit(solution)/shard_map/while/body/eval_jaxpr/rtkgd,bkpd->rtkgbp/dot_general | solution.py:56
  83.7 0.3 multiply_reduce_fusion.5
  84.1 2.5 %multiply_reduce_fusion.4 = f32[8,2,2,8]{3,1,0,2:T(2,128)S(1)} fusion(f32[2,8,2,8,48,128]{5,3,4,2,1,0:T(8,128)S(1)} %get-tuple-element.457, f32[8,48,128]{2,1,0:T(8,128)S(1)} %get-tuple-element.456, f32[8,2,2,8]{3,1,0,2:T(2,128)S(1)} %copy_maximum_fusion.2, f32[2,48]{1,0:T(2,128)S(1)} %get-tuple-element.451, pred[8,48,128]{2,1,0:T(8,128)(4,1)S(1)} %get-tuple-element.453), kind=kLoop, calls=%fused_computation.7.clone.1 | loop fusion | flops 9436928 | bytes 6539648 | tf_op jit(solution)/shard_map/while/body/eval_jaxpr/reduce_sum | solution.py:74
  86.6 2.4 %fusion.113 = f32[2,8,2,8,128]{4,3,2,1,0:T(8,128)S(1)} fusion(bf16[48,2,2,128,128]{4,3,0,2,1:T(8,128)(2,1)S(1)} %bitcast.222, f32[8,48,128]{2,1,0:T(8,128)S(1)} %get-tuple-element.456, f32[2,8,2,8,48,128]{5,3,4,2,1,0:T(8,128)S(1)} %get-tuple-element.457, f32[2,48]{1,0:T(2,128)S(1)} %get-tuple-element.458, ...), kind=kOutput, calls=%fused_computation.30.clone.1 | convolution fusion | flops 421527552 | bytes 9832448 | tf_op jit(solution)/shard_map/while/body/eval_jaxpr/rtkgbp,bkpd->rtkgd/dot_general | solution.py:85
  89.1 2.2 %fusion.114 = f32[8,2,2,8,128]{4,3,1,0,2:T(8,128)S(1)} fusion(f32[2,8,2,8,128]{4,3,2,1,0:T(8,128)S(1)} %fusion.113, bf16[48,2,2,128,128]{4,3,0,2,1:T(8,128)(2,1)S(1)} %bitcast.222, f32[8,48,128]{2,1,0:T(8,128)S(1)} %get-tuple-element.456, f32[2,8,2,8,48,128]{5,3,4,2,1,0:T(8,128)S(1)} %get-tuple-element.457, f32[2,48]{1,0:T(2,128)S(1)} %get-tuple-element.458, ...), kind=kOutput, calls=%fused_computation.37.clone.1 | convolution fusion | flops 416841728 | bytes 9963520 | tf_op jit(solution)/shard_map/while/body/eval_jaxpr/rtkgbp,bkpd->rtkgd/dot_general | solution.py:84
  91.3 0.4 convolution_bitcast_fusion.4
  91.7 0.4 fusion.112
  92.1 0.2 fusion.116
  92.6 0.7 constant_dynamic-slice_fusion.12
  93.6 0.4 fusion.111
  94.0 0.3 broadcast_compare_fusion.5
  94.3 0.4 fusion.110
  94.7 3.3 %bitcast_reduce_fusion.2 = (f32[8,2,2,8]{3,1,0,2:T(2,128)S(1)}, f32[2,8,2,8,48,128]{5,3,4,2,1,0:T(8,128)S(1)}) fusion(f32[2,48]{1,0:T(2,128)S(1)} %get-tuple-element.451, pred[8,48,128]{2,1,0:T(8,128)(4,1)S(1)} %get-tuple-element.453, bf16[48,2,2,128,128]{4,3,0,2,1:T(8,128)(2,1)} %get-tuple-element.495, ...), kind=kOutput, calls=%fused_computation.5.clone.1 | convolution fusion | flops 408944384 | bytes 9553924 | tf_op jit(solution)/shard_map/while/body/eval_jaxpr/rtkgd,bkpd->rtkgbp/dot_general | solution.py:56
  98.2 0.3 multiply_reduce_fusion.5
  98.5 2.5 %multiply_reduce_fusion.4 = f32[8,2,2,8]{3,1,0,2:T(2,128)S(1)} fusion(f32[2,8,2,8,48,128]{5,3,4,2,1,0:T(8,128)S(1)} %get-tuple-element.457, f32[8,48,128]{2,1,0:T(8,128)S(1)} %get-tuple-element.456, f32[8,2,2,8]{3,1,0,2:T(2,128)S(1)} %copy_maximum_fusion.2, f32[2,48]{1,0:T(2,128)S(1)} %get-tuple-element.451, pred[8,48,128]{2,1,0:T(8,128)(4,1)S(1)} %get-tuple-element.453), kind=kLoop, calls=%fused_computation.7.clone.1 | loop fusion | flops 9436928 | bytes 6539648 | tf_op jit(solution)/shard_map/while/body/eval_jaxpr/reduce_sum | solution.py:74
  101.0 2.4 %fusion.113 = f32[2,8,2,8,128]{4,3,2,1,0:T(8,128)S(1)} fusion(bf16[48,2,2,128,128]{4,3,0,2,1:T(8,128)(2,1)S(1)} %bitcast.222, f32[8,48,128]{2,1,0:T(8,128)S(1)} %get-tuple-element.456, f32[2,8,2,8,48,128]{5,3,4,2,1,0:T(8,128)S(1)} %get-tuple-element.457, f32[2,48]{1,0:T(2,128)S(1)} %get-tuple-element.458, ...), kind=kOutput, calls=%fused_computation.30.clone.1 | convolution fusion | flops 421527552 | bytes 9832448 | tf_op jit(solution)/shard_map/while/body/eval_jaxpr/rtkgbp,bkpd->rtkgd/dot_general | solution.py:85
  103.5 2.2 %fusion.114 = f32[8,2,2,8,128]{4,3,1,0,2:T(8,128)S(1)} fusion(f32[2,8,2,8,128]{4,3,2,1,0:T(8,128)S(1)} %fusion.113, bf16[48,2,2,128,128]{4,3,0,2,1:T(8,128)(2,1)S(1)} %bitcast.222, f32[8,48,128]{2,1,0:T(8,128)S(1)} %get-tuple-element.456, f32[2,8,2,8,48,128]{5,3,4,2,1,0:T(8,128)S(1)} %get-tuple-element.457, f32[2,48]{1,0:T(2,128)S(1)} %get-tuple-element.458, ...), kind=kOutput, calls=%fused_computation.37.clone.1 | convolution fusion | flops 416841728 | bytes 9963520 | tf_op jit(solution)/shard_map/while/body/eval_jaxpr/rtkgbp,bkpd->rtkgd/dot_general | solution.py:84
  105.7 0.4 convolution_bitcast_fusion.4
  106.1 0.4 fusion.112
  107.0 0.7 constant_dynamic-slice_fusion.12
  108.0 0.4 fusion.111
  108.4 0.3 broadcast_compare_fusion.5
  108.7 0.4 fusion.110
  109.2 3.3 %bitcast_reduce_fusion.2 = (f32[8,2,2,8]{3,1,0,2:T(2,128)S(1)}, f32[2,8,2,8,48,128]{5,3,4,2,1,0:T(8,128)S(1)}) fusion(f32[2,48]{1,0:T(2,128)S(1)} %get-tuple-element.451, pred[8,48,128]{2,1,0:T(8,128)(4,1)S(1)} %get-tuple-element.453, bf16[48,2,2,128,128]{4,3,0,2,1:T(8,128)(2,1)} %get-tuple-element.495, ...), kind=kOutput, calls=%fused_computation.5.clone.1 | convolution fusion | flops 408944384 | bytes 9553924 | tf_op jit(solution)/shard_map/while/body/eval_jaxpr/rtkgd,bkpd->rtkgbp/dot_general | solution.py:56
  112.6 0.3 multiply_reduce_fusion.5
  112.9 2.5 %multiply_reduce_fusion.4 = f32[8,2,2,8]{3,1,0,2:T(2,128)S(1)} fusion(f32[2,8,2,8,48,128]{5,3,4,2,1,0:T(8,128)S(1)} %get-tuple-element.457, f32[8,48,128]{2,1,0:T(8,128)S(1)} %get-tuple-element.456, f32[8,2,2,8]{3,1,0,2:T(2,128)S(1)} %copy_maximum_fusion.2, f32[2,48]{1,0:T(2,128)S(1)} %get-tuple-element.451, pred[8,48,128]{2,1,0:T(8,128)(4,1)S(1)} %get-tuple-element.453), kind=kLoop, calls=%fused_computation.7.clone.1 | loop fusion | flops 9436928 | bytes 6539648 | tf_op jit(solution)/shard_map/while/body/eval_jaxpr/reduce_sum | solution.py:74
  115.4 2.4 %fusion.113 = f32[2,8,2,8,128]{4,3,2,1,0:T(8,128)S(1)} fusion(bf16[48,2,2,128,128]{4,3,0,2,1:T(8,128)(2,1)S(1)} %bitcast.222, f32[8,48,128]{2,1,0:T(8,128)S(1)} %get-tuple-element.456, f32[2,8,2,8,48,128]{5,3,4,2,1,0:T(8,128)S(1)} %get-tuple-element.457, f32[2,48]{1,0:T(2,128)S(1)} %get-tuple-element.458, ...), kind=kOutput, calls=%fused_computation.30.clone.1 | convolution fusion | flops 421527552 | bytes 9832448 | tf_op jit(solution)/shard_map/while/body/eval_jaxpr/rtkgbp,bkpd->rtkgd/dot_general | solution.py:85
  117.9 2.2 %fusion.114 = f32[8,2,2,8,128]{4,3,1,0,2:T(8,128)S(1)} fusion(f32[2,8,2,8,128]{4,3,2,1,0:T(8,128)S(1)} %fusion.113, bf16[48,2,2,128,128]{4,3,0,2,1:T(8,128)(2,1)S(1)} %bitcast.222, f32[8,48,128]{2,1,0:T(8,128)S(1)} %get-tuple-element.456, f32[2,8,2,8,48,128]{5,3,4,2,1,0:T(8,128)S(1)} %get-tuple-element.457, f32[2,48]{1,0:T(2,128)S(1)} %get-tuple-element.458, ...), kind=kOutput, calls=%fused_computation.37.clone.1 | convolution fusion | flops 416841728 | bytes 9963520 | tf_op jit(solution)/shard_map/while/body/eval_jaxpr/rtkgbp,bkpd->rtkgd/dot_general | solution.py:84
  120.1 0.4 convolution_bitcast_fusion.4
  120.5 0.4 fusion.112
  121.3 0.7 copy-done.4
  (125 shorter events, 4.9 us)
Async XLA Ops:
  18.6 16.2 %all-to-all-start = ((bf16[4,2,2,2]{1,3,2,0:T(2,128)(2,1)}), bf16[4,2,2,2]{1,3,2,0:T(2,128)(2,1)S(1)}, u32[]{:S(2)}, u32[]{:S(2)}) async-start(bf16[4,2,2,2]{1,3,2,0:T(2,128)(2,1)} %copy.135), calls=%async_computation | async-start | bytes 8192 | tf_op jit(solution)/shard_map/all_to_all | solution.py:125
  25.4 8.1 %copy-start.3 = (s32[32]{0:T(128)S(1)}, s32[32]{0:T(128)}, u32[]{:S(2)}) copy-start(s32[32]{0:T(128)} %param.15) | copy-start | bytes 388
  33.5 6.9 %copy-start.2 = (s32[32,16]{0,1:T(8,128)S(1)}, s32[32,16]{0,1:T(8,128)}, u32[]{:S(2)}) copy-start(s32[32,16]{0,1:T(8,128)} %param.14) | copy-start | bytes 6148
  33.6 30.0 %copy-start = (bf16[32,2,16,128]{3,2,1,0:T(8,128)(2,1)S(1)}, bf16[32,2,16,128]{3,2,1,0:T(8,128)(2,1)}, u32[]{:S(2)}) copy-start(bf16[32,2,16,128]{3,2,1,0:T(8,128)(2,1)} %param.10) | copy-start | bytes 786436
  33.6 30.0 %copy-start.1 = (bf16[48,2,2]{0,2,1:T(2,128)(2,1)S(1)}, bf16[48,2,2]{0,2,1:T(2,128)(2,1)}, u32[]{:S(2)}) copy-start(bf16[48,2,2]{0,2,1:T(2,128)(2,1)} %param.13) | copy-start | bytes 1156
  34.8 28.5 %all-to-all-start.1 = ((bf16[4,2,2,2,128,128]{5,4,1,3,2,0:T(8,128)(2,1)}), bf16[4,2,2,2,128,128]{5,4,1,3,2,0:T(8,128)(2,1)S(1)}, u32[]{:S(2)}, u32[]{:S(2)}) async-start(bf16[4,2,2,2,128,128]{5,4,1,3,2,0:T(8,128)(2,1)} %copy.138), calls=%async_computation.1 | async-start | bytes 2097152 | tf_op jit(solution)/shard_map/all_to_all | solution.py:124
  65.9 6.3 %slice-start = ((s8[6291456]{0:T(1024)(128)(4,1)}), s8[4194304]{0:T(1024)(128)(4,1)S(1)}, s32[]{:S(2)}) async-start(s8[6291456]{0:T(1024)(128)(4,1)} %bitcast.221), calls=%async_computation.2 | async-start | bytes 8388608 | tf_op jit(solution)/shard_map/while
  65.9 6.3 %slice-start.1 = ((s8[6291456]{0:T(1024)(128)(4,1)}), s8[2097152]{0:T(1024)(128)(4,1)S(1)}, s32[]{:S(2)}) async-start(s8[6291456]{0:T(1024)(128)(4,1)} %bitcast.221), calls=%async_computation.3 | async-start | bytes 4194304 | tf_op jit(solution)/shard_map/while
  80.3 6.3 %slice-start = ((s8[6291456]{0:T(1024)(128)(4,1)}), s8[4194304]{0:T(1024)(128)(4,1)S(1)}, s32[]{:S(2)}) async-start(s8[6291456]{0:T(1024)(128)(4,1)} %bitcast.221), calls=%async_computation.2 | async-start | bytes 8388608 | tf_op jit(solution)/shard_map/while
  80.3 6.3 %slice-start.1 = ((s8[6291456]{0:T(1024)(128)(4,1)}), s8[2097152]{0:T(1024)(128)(4,1)S(1)}, s32[]{:S(2)}) async-start(s8[6291456]{0:T(1024)(128)(4,1)} %bitcast.221), calls=%async_computation.3 | async-start | bytes 4194304 | tf_op jit(solution)/shard_map/while
  94.7 6.3 %slice-start = ((s8[6291456]{0:T(1024)(128)(4,1)}), s8[4194304]{0:T(1024)(128)(4,1)S(1)}, s32[]{:S(2)}) async-start(s8[6291456]{0:T(1024)(128)(4,1)} %bitcast.221), calls=%async_computation.2 | async-start | bytes 8388608 | tf_op jit(solution)/shard_map/while
  94.7 6.3 %slice-start.1 = ((s8[6291456]{0:T(1024)(128)(4,1)}), s8[2097152]{0:T(1024)(128)(4,1)S(1)}, s32[]{:S(2)}) async-start(s8[6291456]{0:T(1024)(128)(4,1)} %bitcast.221), calls=%async_computation.3 | async-start | bytes 4194304 | tf_op jit(solution)/shard_map/while
  109.1 6.3 %slice-start = ((s8[6291456]{0:T(1024)(128)(4,1)}), s8[4194304]{0:T(1024)(128)(4,1)S(1)}, s32[]{:S(2)}) async-start(s8[6291456]{0:T(1024)(128)(4,1)} %bitcast.221), calls=%async_computation.2 | async-start | bytes 8388608 | tf_op jit(solution)/shard_map/while
  109.1 6.3 %slice-start.1 = ((s8[6291456]{0:T(1024)(128)(4,1)}), s8[2097152]{0:T(1024)(128)(4,1)S(1)}, s32[]{:S(2)}) async-start(s8[6291456]{0:T(1024)(128)(4,1)} %bitcast.221), calls=%async_computation.3 | async-start | bytes 4194304 | tf_op jit(solution)/shard_map/while
  121.3 0.7 copy-start.4
where the time goes:
time: 123 us; the launch traced here: 122 us
  matrix products  41.3 us (34%)
  waiting for transfers between devices  22.1 us (18%)
  local copies, waits for them, and re-layouts  21.6 us (18%)
  other arithmetic  16.6 us (13%)
  blocking collectives  9.89 us (8%)
  starting transfers between devices  8.29 us (7%)
  between operations  1.46 us (1%)
    all_to_all x1, waiting for transfers between devices, shards(): lax.all_to_all(send_codes, 'inst', split_axis=0, concat_axis=0, tiled=True)  22.1 us
    dot_general x8, matrix products, cached_scores(): jnp.einsum('rtkgd,bkpd->rtkgbp', query_rows, keys, preferred_element_type...  14.9 us
    dot_general x8, matrix products, apply_values(): jnp.einsum('rtkgbp,bkpd->rtkgd', low, values, preferred_element_type=jnp....  11.4 us
    reduce_sum x8, other arithmetic, weigh(): part_total = jnp.sum(weights * many_mult, axis=(4, 5))  11.3 us
    unnamed x19, local copies, waits for them, and re-layouts  11.3 us
    dot_general x8, matrix products, apply_values(): jnp.einsum('rtkgbp,bkpd->rtkgd', high, values, preferred_element_type=jnp...  10.5 us
    unnamed x1, blocking collectives  9.89 us
    all_to_all x1, starting transfers between devices, shards(): lax.all_to_all(send_codes, 'inst', split_axis=0, concat_axis=0, tiled=True)  5.05 us
  transfers between devices with their start and end apart: 2, of which 1 were waited for; matrix products, arithmetic and copies ran while one was open for 12% of the time, Pallas kernels for 0%

commit v1 on v0

v1 whole, which is shorter than its diff:
```python
import functools
import math

import jax
import jax.numpy as jnp
from jax import lax
from jax.experimental import pallas as pl
from jax.experimental.pallas import tpu as pltpu
from jax.sharding import PartitionSpec as P

CAP = 2
LOG2E = math.log2(math.e)
MIB = 1 << 20
SMEM_SPEC = pl.BlockSpec(memory_space=pltpu.SMEM)
VMEM_SPEC = pl.BlockSpec(memory_space=pltpu.VMEM)
ANY_SPEC = pl.BlockSpec(memory_space=pl.ANY)
NT = (((1,), (1,)), ((), ()))


def pack_kernel(instances, listed, dest_ref, block_ref, pool_ref, *rest):
    send_refs, (index_ref, sems) = rest[:instances], rest[instances:]
    me = lax.axis_index("inst")

    def clear(slot, carry):
        index_ref[slot] = 0
        return carry

    lax.fori_loop(0, instances * CAP, clear, 0)

    def place(m, carry):
        dest = dest_ref[0, m]

        def earlier(m2, rank):
            return rank + jnp.where(dest_ref[0, m2] == dest, 1, 0)

        rank = jnp.minimum(lax.fori_loop(0, m, earlier, 0), CAP - 1)
        shift = lax.rem(dest - me + instances, instances)
        index_ref[shift * CAP + rank] = block_ref[0, m]
        return carry

    lax.fori_loop(0, listed, place, 0)
    copies = []
    for shift in list(range(1, instances)) + [0]:
        for rank in range(CAP):
            slot = shift * CAP + rank
            copies.append(
                pltpu.make_async_copy(
                    pool_ref.at[index_ref[slot]], send_refs[shift].at[rank], sems.at[slot]
                )
            )
            copies[-1].start()
    for copy in copies:
        copy.wait()


def count_log(tables, length, ids, block_len, spans, store):
    requests, width = tables.shape[0], ids.shape[1]
    whole = length // block_len
    rest = length - whole * block_len
    full = jnp.zeros((requests, width), jnp.float32)
    part = jnp.zeros((requests, width), jnp.float32)
    for e in range(spans):
        hit = tables[:, e : e + 1] == ids
        full = full + jnp.where(hit & (whole > e), 1.0, 0.0)
        part = part + jnp.where(hit & (whole == e), 1.0, 0.0)
    inside = lax.broadcasted_iota(jnp.int32, (requests, block_len), 1) < rest
    for b in range(width):
        count = jnp.broadcast_to(full[:, b : b + 1], (requests, block_len)) + jnp.where(
            inside, jnp.broadcast_to(part[:, b : b + 1], (requests, block_len)), 0.0
        )
        store(b, jnp.where(count > 0, jnp.log(jnp.maximum(count, 1.0)) * LOG2E, -jnp.inf))


def score_tiles(query, keys, log_ref, scale_row, rows, store):
    height, wide = min(256, query.shape[0]), min(256, keys.shape[0])
    for top in range(0, query.shape[0], height):
        for left in range(0, keys.shape[0], wide):
            part = lax.dot_general(
                query[top : top + height],
                keys[left : left + wide],
                NT,
                preferred_element_type=jnp.float32,
            )
            scale = scale_row[:, left : left + wide]
            for r in range(height // rows):
                request = top // rows + r
                store(
                    request * rows,
                    left,
                    part[r * rows : (r + 1) * rows] * scale
                    + log_ref[request : request + 1, left : left + wide],
                )


def lane_fold(value, op):
    parts = [value[:, i : i + 128] for i in range(0, value.shape[1], 128)]
    while len(parts) > 1:
        parts = [
            op(parts[i], parts[i + 1]) if i + 1 < len(parts) else parts[i]
            for i in range(0, len(parts), 2)
        ]
    return parts[0]


def spread(column, width):
    return jnp.concatenate([column] * (width // 128), axis=1)


def own_kernel(
    dims,
    tables_ref, length_ref, scale_ref, q_ref, fresh_ref, codes_ref,
    acc_ref, top_ref, total_ref,
    log_ref, row_ref, t_ref, new_ref, p_ref,
):
    pool, heads, rows, steps, block_len, spans, factor, group = dims
    phase, chunk = pl.program_id(0), pl.program_id(1)
    chunks = pool // group
    height = q_ref.shape[1]
    width = group * block_len

    @pl.when((phase == 0) & (chunk == 0))
    def _():
        ids = lax.broadcasted_iota(jnp.int32, (1, pool), 1)

        def store(b, value):
            lane = (b % group) * block_len
            log_ref[b // group, :, lane : lane + block_len] = value

        count_log(tables_ref[...], length_ref[...], ids, block_len, spans, store)
        for b in range(pool):
            lane = (b % group) * block_len
            for h in range(heads):
                row_ref[b // group, h : h + 1, lane : lane + block_len] = jnp.full(
                    (1, block_len), scale_ref[0, h * pool + b] * (factor * LOG2E)
                )
                row_ref[b // group, heads + h : heads + h + 1, lane : lane + block_len] = jnp.full(
                    (1, block_len), scale_ref[0, (heads + h) * pool + b]
                )
        shape = (height, fresh_ref.shape[2])
        row = lax.broadcasted_iota(jnp.int32, shape, 0)
        col = lax.broadcasted_iota(jnp.int32, shape, 1)
        seen = (col // steps == row // rows) & (col % steps <= row % steps)
        for h in range(heads):
            score = lax.dot_general(
                q_ref[h], fresh_ref[0, h], NT, preferred_element_type=jnp.float32
            )
            score = jnp.where(seen, score * (factor * LOG2E), -jnp.inf)
            new_ref[h] = score
            top_ref[h] = lane_fold(score, jnp.maximum)

    @pl.when(phase == 0)
    def _():
        for h in range(heads):

            def store(row, lane, value, h=h):
                t_ref[h, chunk, row : row + rows, lane : lane + value.shape[1]] = value

            score_tiles(
                q_ref[h],
                codes_ref[:, 0, h].reshape(width, codes_ref.shape[-1]),
                log_ref.at[chunk],
                row_ref[chunk, h : h + 1, :],
                rows,
                store,
            )
            for row in range(0, height, rows):
                at = pl.ds(row, rows)
                top_ref[h, at] = jnp.maximum(
                    top_ref[h, at], lane_fold(t_ref[h, chunk, at], jnp.maximum)
                )

    @pl.when((phase == 1) & (chunk == 0))
    def _():
        for h in range(heads):
            top = jnp.broadcast_to(
                jnp.max(top_ref[h], axis=1, keepdims=True), (height, 128)
            )
            top_ref[h] = top
            weight = jnp.exp2(new_ref[h] - spread(top, new_ref.shape[2]))
            total_ref[h] = lane_fold(weight, jnp.add)
            acc_ref[h] = jnp.dot(
                weight.astype(jnp.bfloat16), fresh_ref[1, h], preferred_element_type=jnp.float32
            )

    @pl.when(phase == 1)
    def _():
        for h in range(heads):
            scale = row_ref[chunk, heads + h : heads + h + 1, :]
            for row in range(0, height, rows):
                at = pl.ds(row, rows)
                weight = jnp.exp2(t_ref[h, chunk, at] - spread(top_ref[h, at], width))
                total_ref[h, at] += lane_fold(weight, jnp.add)
                p_ref[h, at] = (weight * scale).astype(jnp.bfloat16)
            acc_ref[h] += jnp.dot(
                p_ref[h],
                codes_ref[:, 0, h].reshape(width, codes_ref.shape[-1]),
                preferred_element_type=jnp.float32,
            )

    @pl.when((phase == 1) & (chunk == chunks - 1))
    def _():
        for h in range(heads):
            total_ref[h] = jnp.broadcast_to(
                jnp.sum(total_ref[h], axis=1, keepdims=True), (height, 128)
            )


def route_kernel(
    dims, lists_ref, tables_ref, length_ref, moved_ref, log_ref, row_ref, counts_ref
):
    pool, heads, instances, listed, block_len, spans, factor = dims
    me = lax.axis_index("inst")

    def dest(shift, m):
        return lists_ref[shift, m].astype(jnp.int32)

    def count(shift, carry):
        def one(m, total):
            return total + jnp.where(dest(shift, m) == me, 1, 0)

        counts_ref[shift] = lax.fori_loop(0, listed, one, 0)
        return carry

    lax.fori_loop(0, instances, count, 0)

    def move(m, carry):
        target = dest(0, m)

        def same(m2, total):
            return total + jnp.where(dest(0, m2) == target, 1, 0)

        def lower(shift, total):
            def one(m2, inner):
                return inner + jnp.where(dest(shift, m2) == target, 1, 0)

            found = lax.fori_loop(0, listed, one, 0)
            return total + jnp.where(shift <= me, found, 0)

        moved_ref[0, m] = (
            pool + lax.fori_loop(0, m, same, 0) + lax.fori_loop(1, instances, lower, 0)
        )
        return carry

    lax.fori_loop(0, listed, move, 0)
    slots = instances * CAP
    lane = lax.broadcasted_iota(jnp.int32, (1, slots), 1)
    ids = jnp.full((1, slots), -1, jnp.int32)
    for shift in range(instances):
        source = lax.rem(me - shift + instances, instances)

        def before(other, total):
            other_source = lax.rem(me - other + instances, instances)
            return total + jnp.where(other_source < source, counts_ref[other], 0)

        first = lax.fori_loop(0, instances, before, 0)
        for rank in range(CAP):
            name = jnp.where(rank < counts_ref[shift], pool + first + rank, -1)
            ids = jnp.where(lane == shift * CAP + rank, name, ids)

            def find(m, carry):
                seen, block = carry
                hit = dest(shift, m) == me
                block = jnp.where(
                    hit & (seen == rank), lists_ref[shift, listed + m].astype(jnp.int32), block
                )
                return seen + jnp.where(hit, 1, 0), block

            _, block = lax.fori_loop(0, listed, find, (0, 0))
            at = (shift * CAP + rank) * block_len
            for h in range(heads):
                row_ref[h : h + 1, at : at + block_len] = jnp.full(
                    (1, block_len),
                    lists_ref[shift, 2 * listed + h * pool + block] * (factor * LOG2E),
                )
                row_ref[heads + h : heads + h + 1, at : at + block_len] = jnp.full(
                    (1, block_len), lists_ref[shift, 2 * listed + (heads + h) * pool + block]
                )

    def store(b, value):
        log_ref[:, b * block_len : (b + 1) * block_len] = value

    count_log(tables_ref[...], length_ref[...], ids, block_len, spans, store)


def arrival_kernel(
    dims, sources, q_ref, log_ref, row_ref, acc_ref, top_ref, total_ref, *rest
):
    heads, rows, block_len = dims
    code_refs, (out_ref, t_ref, p_ref) = rest[:sources], rest[sources:]
    height = q_ref.shape[1]
    width = CAP * block_len
    for h in range(heads):
        for s, codes_ref in enumerate(code_refs):
            left = s * width

            def store(row, lane, value, h=h, left=left):
                t_ref[h, row : row + rows, left + lane : left + lane + value.shape[1]] = value

            score_tiles(
                q_ref[h],
                codes_ref[:, 0, h].reshape(width, codes_ref.shape[-1]),
                log_ref.at[:, left : left + width],
                row_ref[h : h + 1, left : left + width],
                rows,
                store,
            )
    for h in range(heads):
        scale = row_ref[heads + h : heads + h + 1, :]
        for row in range(0, height, rows):
            at = pl.ds(row, rows)
            score = t_ref[h, at]
            own_top = top_ref[h, at]
            top = jnp.maximum(
                own_top, jnp.max(lane_fold(score, jnp.maximum), axis=1, keepdims=True)
            )
            weight = jnp.exp2(score - spread(top, score.shape[1]))
            keep = jnp.exp2(own_top - top)
            total = total_ref[h, at] * keep + jnp.sum(
                lane_fold(weight, jnp.add), axis=1, keepdims=True
            )
            p_ref[h, at] = (weight * scale).astype(jnp.bfloat16)
            t_ref[h, at, 0:128] = keep
            t_ref[h, at, 128:256] = 1.0 / total
        mixed = acc_ref[h] * t_ref[h, :, 0:128]
        for s, codes_ref in enumerate(code_refs):
            mixed = mixed + jnp.dot(
                p_ref[h, :, s * width : (s + 1) * width],
                codes_ref[:, 1, h].reshape(width, codes_ref.shape[-1]),
                preferred_element_type=jnp.float32,
            )
        result = (mixed * t_ref[h, :, 128:256]).astype(jnp.bfloat16)
        out_ref[:, h] = result.reshape(height // rows, rows, result.shape[-1])


def shards(queries, new_kv, pool_codes, pool_scales, tables, ctx_len, mig_block, mig_dest):
    instances = lax.axis_size("inst")
    pool = pool_codes.shape[0]
    requests, steps, q_heads, head_dim = queries.shape
    heads = new_kv.shape[3]
    per_head = q_heads // heads
    spans = tables.shape[1]
    block_len = pool_codes.shape[3]
    listed = mig_dest.shape[1]
    factor = head_dim ** (-0.5)
    rows = per_head * steps
    height = requests * rows
    slots = instances * CAP
    group = 8
    f32, bf16 = jnp.float32, jnp.bfloat16

    block_shape = pool_codes.shape[1:]
    send = pl.pallas_call(
        functools.partial(pack_kernel, instances, listed),
        out_shape=[jax.ShapeDtypeStruct((CAP,) + block_shape, bf16)] * instances,
        in_specs=[SMEM_SPEC, SMEM_SPEC, ANY_SPEC],
        out_specs=[ANY_SPEC] * instances,
        scratch_shapes=[pltpu.SMEM((slots,), jnp.int32), pltpu.SemaphoreType.DMA((slots,))],
        cost_estimate=pl.CostEstimate(
            flops=0, bytes_accessed=2 * slots * math.prod(block_shape) * 2, transcendentals=0
        ),
        name="pack_blocks",
    )(mig_dest, mig_block, pool_codes)

    def from_shift(value, shift):
        if shift == 0:
            return value
        return lax.ppermute(
            value, "inst", [(j, (j + shift) % instances) for j in range(instances)]
        )

    codes_in = [from_shift(send[shift], shift) for shift in range(instances)]

    flat_scales = jnp.transpose(pool_scales, (1, 2, 0)).reshape(1, -1).astype(f32)
    lists = jnp.concatenate([mig_dest.astype(f32), mig_block.astype(f32), flat_scales], axis=1)
    lists_in = jnp.concatenate(
        [from_shift(lists, shift) for shift in range(instances)], axis=0
    )

    query_rows = (
        queries.reshape(requests, steps, heads, per_head, head_dim)
        .transpose(2, 0, 3, 1, 4)
        .reshape(heads, height, head_dim)
    )
    fresh_len = requests * steps
    fresh = new_kv.transpose(2, 3, 0, 1, 4).reshape(2, heads, fresh_len, head_dim)
    fresh = jnp.pad(fresh, ((0, 0), (0, 0), (0, -fresh_len % 128), (0, 0)))
    length = ctx_len[:, None]
    width = group * block_len
    chunks = pool // group
    tokens = pool * block_len

    def whole(shape):
        return pl.BlockSpec(shape, lambda p, c: (0,) * len(shape))

    stat = (heads, height, head_dim)
    acc, top, total = pl.pallas_call(
        functools.partial(
            own_kernel, (pool, heads, rows, steps, block_len, spans, factor, group)
        ),
        grid=(2, chunks),
        out_shape=[jax.ShapeDtypeStruct(stat, f32)] * 3,
        in_specs=[
            whole(tables.shape),
            whole(length.shape),
            SMEM_SPEC,
            whole(query_rows.shape),
            whole(fresh.shape),
            pl.BlockSpec(
                (group, 1, heads, block_len, head_dim), lambda p, c: (c, p, 0, 0, 0)
            ),
        ],
        out_specs=[whole(stat)] * 3,
        scratch_shapes=[
            pltpu.VMEM((chunks, requests, width), f32),
            pltpu.VMEM((chunks, 2 * heads, width), f32),
            pltpu.VMEM((heads, chunks, height, width), f32),
            pltpu.VMEM((heads, height, fresh.shape[2]), f32),
            pltpu.VMEM((heads, height, width), bf16),
        ],
        compiler_params=pltpu.CompilerParams(vmem_limit_bytes=48 * MIB),
        cost_estimate=pl.CostEstimate(
            flops=4 * heads * height * tokens * head_dim,
            bytes_accessed=pool_codes.size * 2,
            transcendentals=heads * height * tokens,
        ),
        name="own_blocks",
    )(tables, length, flat_scales, query_rows, fresh, pool_codes)

    moved_to, log_in, rows_in = pl.pallas_call(
        functools.partial(
            route_kernel, (pool, heads, instances, listed, block_len, spans, factor)
        ),
        out_shape=[
            jax.ShapeDtypeStruct((1, listed), jnp.int32),
            jax.ShapeDtypeStruct((requests, slots * block_len), f32),
            jax.ShapeDtypeStruct((2 * heads, slots * block_len), f32),
        ],
        in_specs=[SMEM_SPEC, VMEM_SPEC, VMEM_SPEC],
        out_specs=[SMEM_SPEC, VMEM_SPEC, VMEM_SPEC],
        scratch_shapes=[pltpu.SMEM((instances,), jnp.int32)],
        name="route_arrivals",
    )(lists_in, tables, length)

    out = pl.pallas_call(
        functools.partial(arrival_kernel, (heads, rows, block_len), instances),
        out_shape=jax.ShapeDtypeStruct((requests, heads, rows, head_dim), bf16),
        in_specs=[VMEM_SPEC] * (6 + instances),
        out_specs=VMEM_SPEC,
        scratch_shapes=[
            pltpu.VMEM((heads, height, slots * block_len), f32),
            pltpu.VMEM((heads, height, slots * block_len), bf16),
        ],
        compiler_params=pltpu.CompilerParams(vmem_limit_bytes=48 * MIB),
        cost_estimate=pl.CostEstimate(
            flops=4 * heads * height * slots * block_len * head_dim,
            bytes_accessed=slots * math.prod(block_shape) * 2,
            transcendentals=heads * height * slots * block_len,
        ),
        name="arrived_blocks",
    )(query_rows, log_in, rows_in, acc, top, total, *codes_in)
    out = (
        out.reshape(requests, q_heads, steps, head_dim)
        .transpose(0, 2, 1, 3)
        .reshape(requests, steps, q_heads * head_dim)
    )
    return out, moved_to


def solution(mesh):
    in_specs = (
        P(("groups", "inst"), None, "tp", None),
        P(("groups", "inst"), None, None, "tp", None),
        P(("groups", "inst"), None, "tp", None, None),
        P(("groups", "inst"), None, "tp"),
        P(("groups", "inst"), None),
        P(("groups", "inst")),
        P(("groups", "inst"), None),
        P(("groups", "inst"), None),
    )
    out_specs = (P(("groups", "inst"), None, "tp"), P(("groups", "inst"), None))
    return jax.shard_map(shards, mesh=mesh, in_specs=in_specs, out_specs=out_specs, check_vma=False)
```

time: 123 us -> 71.4 us (0.58)
  Pallas kernels: 0 us -> 53.5 us
  matrix products: 41.3 us -> 0 us
  waiting for transfers between devices: 22.1 us -> 0.02 us
  local copies, waits for them, and re-layouts: 21.6 us -> 2.16 us
  other arithmetic: 16.6 us -> 2.79 us
  blocking collectives: 9.89 us -> 0 us
  starting transfers between devices: 8.29 us -> 11.1 us
    pallas_call x0 -> x4, Pallas kernels: none -> 53.5 us  [the longest x1 33.7 us: shards(): pl.pallas_call(functools.partial(pack_kernel, instances, listed), out_sha...]
    dot_general x40 -> x0, matrix products: 41.3 us -> none  [the longest x8 14.9 us: cached_scores(): jnp.einsum('rtkgd,bkpd->rtkgbp', query_rows, keys, preferred_element_type...]
    all_to_all x2 -> x0, waiting for transfers between devices: 22.1 us -> none  [the longest x1 22.1 us: shards(): lax.all_to_all(send_codes, 'inst', split_axis=0, concat_axis=0, tiled=True)]
    reduce_sum x13 -> x0, other arithmetic: 14 us -> none  [the longest x8 11.3 us: weigh(): part_total = jnp.sum(weights * many_mult, axis=(4, 5))]
    ppermute x0 -> x6, starting transfers between devices: none -> 11.1 us  [from_shift(): lax.ppermute(value, 'inst', [(j, (j + shift) % instances) for j in range(...]
    unnamed x1 -> x0, blocking collectives: 9.89 us -> none
    unnamed x19, local copies, waits for them, and re-layouts: 11.3 us -> 1.72 us
    all_to_all x2 -> x0, starting transfers between devices: 8.29 us -> none  [the longest x1 5.05 us: shards(): lax.all_to_all(send_codes, 'inst', split_axis=0, concat_axis=0, tiled=True)]
  transfers between devices with their start and end apart: 2 -> 6, of which waited for: 1 -> 0; matrix products, arithmetic and copies ran while one was open for 12% -> 2% of each run, Pallas kernels for 0% -> 72%
where the time goes in v1:
time: 71.4 us; the launch traced here: 70.4 us
  Pallas kernels  53.5 us (75%)
  starting transfers between devices  11.1 us (16%)
  other arithmetic  2.79 us (4%)
  local copies, waits for them, and re-layouts  2.16 us (3%)
  between operations  0.81 us (1%)
    pallas_call x1, Pallas kernels, shards(): pl.pallas_call(functools.partial(pack_kernel, instances, listed), out_sha...  33.7 us
    pallas_call x1, Pallas kernels, shards(): pl.pallas_call(functools.partial(own_kernel, (pool, heads, rows, steps, b...  13.7 us
    ppermute x6, starting transfers between devices, from_shift(): lax.ppermute(value, 'inst', [(j, (j + shift) % instances) for j in range(...  11.1 us
    pallas_call x1, Pallas kernels, shards(): pl.pallas_call(functools.partial(route_kernel, (pool, heads, instances, l...  3.43 us
    pallas_call x1, Pallas kernels, shards(): pl.pallas_call(functools.partial(arrival_kernel, (heads, rows, block_len)...  2.67 us
    unnamed x19, local copies, waits for them, and re-layouts  1.72 us
  transfers between devices with their start and end apart: 6, of which 0 were waited for; matrix products, arithmetic and copies ran while one was open for 2% of the time, Pallas kernels for 72%

profile of v1, /device:TPU:0, one launch (start us, length us, event | category | flops | bytes accessed | tf_op | source)
XLA Modules:
  0.0 70.4 jit_solution(8672109811411610466)
XLA Ops:
  0.6 0.0 copy-start.7
  0.6 0.0 copy-start.8
  0.7 0.0 copy-start.6
  0.7 0.0 copy-start.5
  0.7 0.7 %convert_element_type.16 = f32[1,4]{1,0:T(1,128)S(1)} convert(s32[1,4]{1,0:T(1,128)} %block_ref.1) | non-fusion elementwise | flops 4 | bytes 32 | tf_op jit(solution)/shard_map/convert_element_type | solution.py:374
  1.4 0.7 convert_element_type.15
  2.0 0.7 convert_bitcast_fusion
  2.7 0.1 reshape.39.scale_ref
  2.8 0.1 pad_maximum_fusion.1
  2.9 5.1 %collective-permute-start.2 = (f32[1,200]{1,0:T(1,128)S(1)}, f32[1,200]{1,0:T(1,128)S(1)}, u32[]{:S(2)}, u32[]{:S(2)}) collective-permute-start(f32[1,200]{1,0:T(1,128)S(1)} %pad_maximum_fusion.1), channel_id=1, source_target_pairs={{0,12},{4,0},{8,4},{12,8},{1,13},{5,1},{9,5},{13,9},{2,14},{6,2},{... | collective-permute-start | bytes 2408 | tf_op jit(solution)/shard_map/ppermute | solution.py:367
  7.9 0.0 collective-permute-start.1
  7.9 1.0 %collective-permute-start = (f32[1,200]{1,0:T(1,128)S(1)}, f32[1,200]{1,0:T(1,128)S(1)}, u32[]{:S(2)}, u32[]{:S(2)}) collective-permute-start(f32[1,200]{1,0:T(1,128)S(1)} %pad_maximum_fusion.1), channel_id=1, source_target_pairs={{0,4},{4,8},{8,12},{12,0},{1,5},{5,9},{9,13},{13,1},{2,6},{6,10},{... | collective-permute-start | bytes 2408 | tf_op jit(solution)/shard_map/ppermute | solution.py:367
  8.9 33.7 %pack_blocks.1 = (bf16[2,2,2,128,128]{4,3,2,1,0:T(8,128)(2,1)}, bf16[2,2,2,128,128]{4,3,2,1,0:T(8,128)(2,1)}, bf16[2,2,2,128,128]{4,3,2,1,0:T(8,128)(2,1)}, bf16[2,2,2,128,128]{4,3,2,1,0:T(8,128)(2,1)}) custom-call(s32[1,4]{1,0:T(1,128)} %dest_ref.1, s32[1,4]{1,0:T(1,128)} %block_ref.1, bf16[48,2,2,128,128]{4,3,2,1,0:T(8,128)(2,1)} %pool_ref.1), custom_call_target="tpu_custom_call" | custom-call | bytes 2097152 | tf_op jit(solution)/shard_map/pack_blocks/pallas_call | solution.py:352
  42.7 2.5 %collective-permute-start.3 = (bf16[2,2,2,128,128]{4,3,2,1,0:T(8,128)(2,1)}, bf16[2,2,2,128,128]{4,3,2,1,0:T(8,128)(2,1)S(1)}, u32[]{:S(2)}, u32[]{:S(2)}) collective-permute-start(bf16[2,2,2,128,128]{4,3,2,1,0:T(8,128)(2,1)} %get-tuple-element.18), channel_id=1, source_target_pairs={{0,4},{4,8},{8,12},{12,0},{1,5},{5,9},{9,13},{13,1},{2,6},{6,10},{... | collective-permute-start | bytes 786440 | tf_op jit(solution)/shard_map/ppermute | solution.py:367
  45.2 0.9 %collective-permute-start.4 = (bf16[2,2,2,128,128]{4,3,2,1,0:T(8,128)(2,1)}, bf16[2,2,2,128,128]{4,3,2,1,0:T(8,128)(2,1)S(1)}, u32[]{:S(2)}, u32[]{:S(2)}) collective-permute-start(bf16[2,2,2,128,128]{4,3,2,1,0:T(8,128)(2,1)} %get-tuple-element.19), channel_id=1, source_target_pairs={{0,8},{4,12},{8,0},{12,4},{1,9},{5,13},{9,1},{13,5},{2,10},{6,14},... | collective-permute-start | bytes 786440 | tf_op jit(solution)/shard_map/ppermute | solution.py:367
  46.1 0.0 copy-done.7
  46.1 0.1 copy.11.tables_ref
  46.2 0.0 copy-start.2
  46.2 0.0 copy-done.8
  46.2 0.1 copy.12.length_ref
  46.3 0.0 copy-start.3
  46.3 0.0 copy-done.6
  46.3 0.1 copy.13
  46.4 0.0 copy-done.5
  46.4 0.0 copy-start
  46.4 0.2 copy.10
  46.6 0.0 collective-permute-done.2
  46.6 1.6 %collective-permute-start.5 = (bf16[2,2,2,128,128]{4,3,2,1,0:T(8,128)(2,1)}, bf16[2,2,2,128,128]{4,3,2,1,0:T(8,128)(2,1)S(1)}, u32[]{:S(2)}, u32[]{:S(2)}) collective-permute-start(bf16[2,2,2,128,128]{4,3,2,1,0:T(8,128)(2,1)} %get-tuple-element.20), channel_id=1, source_target_pairs={{0,12},{4,0},{8,4},{12,8},{1,13},{5,1},{9,5},{13,9},{2,14},{6,2},{... | collective-permute-start | bytes 786440 | tf_op jit(solution)/shard_map/ppermute | solution.py:367
  48.2 13.7 %own_blocks.1 = (f32[2,512,128]{2,1,0:T(8,128)S(1)}, f32[2,512,128]{2,1,0:T(8,128)S(1)}, f32[2,512,128]{2,1,0:T(8,128)S(1)}) custom-call(s32[32,16]{1,0:T(8,128)S(1)} %copy.11.tables_ref, s32[32,1]{1,0:T(8,128)S(1)} %copy.12.length_ref, f32[1,192]{1,0:T(1,128)S(1)} %reshape.39.scale_ref, bf16[2,512,128]{2,1,0:T(8,128)(2,1)S(1)} %bitcast.14, ...), custom_call_target="tpu_custom_call" | custom-call | flops 3221225472 | bytes 6291456 | tf_op jit(solution)/shard_map/own_blocks/pallas_call | solution.py:396
  61.9 0.0 copy-done.2
  61.9 0.0 copy-done.3
  61.9 0.0 collective-permute-done.1
  61.9 0.0 collective-permute-done
  61.9 0.7 pad_maximum_fusion.lists_ref
  62.6 3.4 %route_arrivals.1 = (s32[1,4]{1,0:T(1,128)}, f32[32,1024]{1,0:T(8,128)}, f32[4,1024]{1,0:T(4,128)}) custom-call(f32[4,200]{1,0:T(4,128)} %pad_maximum_fusion.lists_ref, s32[32,16]{1,0:T(8,128)} %copy-done.2, s32[32,1]{1,0:T(8,128)} %copy-done.3), custom_call_target="tpu_custom_call" | custom-call | tf_op jit(solution)/shard_map/route_arrivals/pallas_call | solution.py:429
  66.0 0.0 collective-permute-done.3.rest_1_
  66.1 0.0 collective-permute-done.4.rest_2_
  66.1 0.0 collective-permute-done.5.rest_3_
  66.1 0.0 copy-done
  66.1 0.0 copy-start.1
  66.1 0.9 %copy-done.1 = f32[32,1024]{1,0:T(8,128)S(1)} copy-done((f32[32,1024]{1,0:T(8,128)S(1)}, f32[32,1024]{1,0:T(8,128)}, u32[]{:S(2)}) %copy-start.1) | copy-done | bytes 131096
  67.0 0.0 copy-start.4
  67.0 0.7 %copy-done.4 = f32[4,1024]{1,0:T(4,128)S(1)} copy-done((f32[4,1024]{1,0:T(4,128)S(1)}, f32[4,1024]{1,0:T(4,128)}, u32[]{:S(2)}) %copy-start.4) | copy-done | bytes 16408
  67.7 2.7 %arrived_blocks.1 = bf16[32,2,16,128]{3,2,1,0:T(8,128)(2,1)} custom-call(bf16[2,512,128]{2,1,0:T(8,128)(2,1)S(1)} %bitcast.15, f32[32,1024]{1,0:T(8,128)S(1)} %copy-done.1, f32[4,1024]{1,0:T(4,128)S(1)} %copy-done.4, f32[2,512,128]{2,1,0:T(8,128)S(1)} %get-tuple-element.14.acc_ref, f32[2,512,128]{2,1,0:T(8,128)S(1)} %get-tuple-element.15.top_ref, ...), custom_call_target="tpu_custom_call" | custom-call | flops 536870912 | bytes 1048576 | tf_op jit(solution)/shard_map/arrived_blocks/pallas_call | solution.py:444
  (1 shorter events, 0.0 us)
Async XLA Ops:
  0.6 45.5 %copy-start.7 = (s32[32,16]{0,1:T(8,128)S(1)}, s32[32,16]{0,1:T(8,128)}, u32[]{:S(2)}) copy-start(s32[32,16]{0,1:T(8,128)} %param.12) | copy-start | bytes 6148
  0.6 45.6 %copy-start.8 = (s32[32]{0:T(128)S(1)}, s32[32]{0:T(128)}, u32[]{:S(2)}) copy-start(s32[32]{0:T(128)} %param.13) | copy-start | bytes 388
  0.7 45.7 %copy-start.6 = (bf16[32,2,2,2,128]{4,3,2,1,0:T(2,128)(2,1)S(1)}, bf16[32,2,2,2,128]{4,3,2,1,0:T(2,128)(2,1)}, u32[]{:S(2)}) copy-start(bf16[32,2,2,2,128]{4,3,2,1,0:T(2,128)(2,1)} %param.9) | copy-start | bytes 196612
  0.7 45.7 %copy-start.5 = (bf16[32,2,16,128]{3,2,1,0:T(8,128)(2,1)S(1)}, bf16[32,2,16,128]{3,2,1,0:T(8,128)(2,1)}, u32[]{:S(2)}) copy-start(bf16[32,2,16,128]{3,2,1,0:T(8,128)(2,1)} %param.8) | copy-start | bytes 786436
  2.9 43.7 %collective-permute-start.2 = (f32[1,200]{1,0:T(1,128)S(1)}, f32[1,200]{1,0:T(1,128)S(1)}, u32[]{:S(2)}, u32[]{:S(2)}) collective-permute-start(f32[1,200]{1,0:T(1,128)S(1)} %pad_maximum_fusion.1), channel_id=1, source_target_pairs={{0,12},{4,0},{8,4},{12,8},{1,13},{5,1},{9,5},{13,9},{2,14},{6,2},{... | collective-permute-start | bytes 2408 | tf_op jit(solution)/shard_map/ppermute | solution.py:367
  7.9 54.0 %collective-permute-start.1 = (f32[1,200]{1,0:T(1,128)S(1)}, f32[1,200]{1,0:T(1,128)S(1)}, u32[]{:S(2)}, u32[]{:S(2)}) collective-permute-start(f32[1,200]{1,0:T(1,128)S(1)} %pad_maximum_fusion.1), channel_id=1, source_target_pairs={{0,8},{4,12},{8,0},{12,4},{1,9},{5,13},{9,1},{13,5},{2,10},{6,14},... | collective-permute-start | bytes 2408 | tf_op jit(solution)/shard_map/ppermute | solution.py:367
  7.9 54.0 %collective-permute-start = (f32[1,200]{1,0:T(1,128)S(1)}, f32[1,200]{1,0:T(1,128)S(1)}, u32[]{:S(2)}, u32[]{:S(2)}) collective-permute-start(f32[1,200]{1,0:T(1,128)S(1)} %pad_maximum_fusion.1), channel_id=1, source_target_pairs={{0,4},{4,8},{8,12},{12,0},{1,5},{5,9},{9,13},{13,1},{2,6},{6,10},{... | collective-permute-start | bytes 2408 | tf_op jit(solution)/shard_map/ppermute | solution.py:367
  42.7 23.3 %collective-permute-start.3 = (bf16[2,2,2,128,128]{4,3,2,1,0:T(8,128)(2,1)}, bf16[2,2,2,128,128]{4,3,2,1,0:T(8,128)(2,1)S(1)}, u32[]{:S(2)}, u32[]{:S(2)}) collective-permute-start(bf16[2,2,2,128,128]{4,3,2,1,0:T(8,128)(2,1)} %get-tuple-element.18), channel_id=1, source_target_pairs={{0,4},{4,8},{8,12},{12,0},{1,5},{5,9},{9,13},{13,1},{2,6},{6,10},{... | collective-permute-start | bytes 786440 | tf_op jit(solution)/shard_map/ppermute | solution.py:367
  45.2 20.8 %collective-permute-start.4 = (bf16[2,2,2,128,128]{4,3,2,1,0:T(8,128)(2,1)}, bf16[2,2,2,128,128]{4,3,2,1,0:T(8,128)(2,1)S(1)}, u32[]{:S(2)}, u32[]{:S(2)}) collective-permute-start(bf16[2,2,2,128,128]{4,3,2,1,0:T(8,128)(2,1)} %get-tuple-element.19), channel_id=1, source_target_pairs={{0,8},{4,12},{8,0},{12,4},{1,9},{5,13},{9,1},{13,5},{2,10},{6,14},... | collective-permute-start | bytes 786440 | tf_op jit(solution)/shard_map/ppermute | solution.py:367
  46.2 15.7 %copy-start.2 = (s32[32,16]{1,0:T(8,128)}, s32[32,16]{1,0:T(8,128)S(1)}, u32[]{:S(2)}) copy-start(s32[32,16]{1,0:T(8,128)S(1)} %copy.11.tables_ref) | copy-start | bytes 6148
  46.3 15.6 %copy-start.3 = (s32[32,1]{1,0:T(8,128)}, s32[32,1]{1,0:T(8,128)S(1)}, u32[]{:S(2)}) copy-start(s32[32,1]{1,0:T(8,128)S(1)} %copy.12.length_ref) | copy-start | bytes 388
  46.4 19.7 %copy-start = (bf16[2,2,2,128,128]{4,3,2,1,0:T(8,128)(2,1)S(1)}, bf16[2,2,2,128,128]{4,3,2,1,0:T(8,128)(2,1)}, u32[]{:S(2)}) copy-start(bf16[2,2,2,128,128]{4,3,2,1,0:T(8,128)(2,1)} %get-tuple-element.17.rest_0_) | copy-start | bytes 786436
  46.6 19.4 %collective-permute-start.5 = (bf16[2,2,2,128,128]{4,3,2,1,0:T(8,128)(2,1)}, bf16[2,2,2,128,128]{4,3,2,1,0:T(8,128)(2,1)S(1)}, u32[]{:S(2)}, u32[]{:S(2)}) collective-permute-start(bf16[2,2,2,128,128]{4,3,2,1,0:T(8,128)(2,1)} %get-tuple-element.20), channel_id=1, source_target_pairs={{0,12},{4,0},{8,4},{12,8},{1,13},{5,1},{9,5},{13,9},{2,14},{6,2},{... | collective-permute-start | bytes 786440 | tf_op jit(solution)/shard_map/ppermute | solution.py:367
  66.1 0.9 %copy-start.1 = (f32[32,1024]{1,0:T(8,128)S(1)}, f32[32,1024]{1,0:T(8,128)}, u32[]{:S(2)}) copy-start(f32[32,1024]{1,0:T(8,128)} %get-tuple-element.12.log_ref) | copy-start | bytes 393220
  67.0 0.7 %copy-start.4 = (f32[4,1024]{1,0:T(4,128)S(1)}, f32[4,1024]{1,0:T(4,128)}, u32[]{:S(2)}) copy-start(f32[4,1024]{1,0:T(4,128)} %get-tuple-element.13.row_ref) | copy-start | bytes 49156

commit v2 on v1

--- a/solution.py
+++ b/solution.py
@@ -13,7 +13,7 @@
 MIB = 1 << 20
 SMEM_SPEC = pl.BlockSpec(memory_space=pltpu.SMEM)
 VMEM_SPEC = pl.BlockSpec(memory_space=pltpu.VMEM)
-ANY_SPEC = pl.BlockSpec(memory_space=pl.ANY)
+HBM_SPEC = pl.BlockSpec(memory_space=pltpu.HBM)
 NT = (((1,), (1,)), ((), ()))
 
 
@@ -205,76 +205,78 @@
             )
 
 
-def route_kernel(
-    dims, lists_ref, tables_ref, length_ref, moved_ref, log_ref, row_ref, counts_ref
-):
+def loop(count, body, init):
+    if count <= 8:
+        for i in range(count):
+            init = body(i, init)
+        return init
+    return lax.fori_loop(0, count, body, init)
+
+
+def route_kernel(dims, lists_ref, tables_ref, length_ref, moved_ref, log_ref, row_ref):
     pool, heads, instances, listed, block_len, spans, factor = dims
     me = lax.axis_index("inst")
 
     def dest(shift, m):
         return lists_ref[shift, m].astype(jnp.int32)
 
-    def count(shift, carry):
-        def one(m, total):
-            return total + jnp.where(dest(shift, m) == me, 1, 0)
-
-        counts_ref[shift] = lax.fori_loop(0, listed, one, 0)
-        return carry
-
-    lax.fori_loop(0, instances, count, 0)
+    def source_of(shift):
+        source = me - shift
+        return jnp.where(source < 0, source + instances, source)
+
+    def count(shift, target):
+        return loop(
+            listed, lambda m, n: n + jnp.where(dest(shift, m) == target, 1, 0), jnp.int32(0)
+        )
 
     def move(m, carry):
         target = dest(0, m)
-
-        def same(m2, total):
-            return total + jnp.where(dest(0, m2) == target, 1, 0)
-
-        def lower(shift, total):
-            def one(m2, inner):
-                return inner + jnp.where(dest(shift, m2) == target, 1, 0)
-
-            found = lax.fori_loop(0, listed, one, 0)
-            return total + jnp.where(shift <= me, found, 0)
-
-        moved_ref[0, m] = (
-            pool + lax.fori_loop(0, m, same, 0) + lax.fori_loop(1, instances, lower, 0)
+        rank = loop(
+            listed,
+            lambda m2, n: n + jnp.where((dest(0, m2) == target) & (m2 < m), 1, 0),
+            jnp.int32(0),
+        )
+        moved_ref[0, m] = loop(
+            instances,
+            lambda shift, n: n + jnp.where(source_of(shift) < me, count(shift, target), 0),
+            pool + rank,
         )
         return carry
 
-    lax.fori_loop(0, listed, move, 0)
+    loop(listed, move, 0)
     slots = instances * CAP
     lane = lax.broadcasted_iota(jnp.int32, (1, slots), 1)
-    ids = jnp.full((1, slots), -1, jnp.int32)
-    for shift in range(instances):
-        source = lax.rem(me - shift + instances, instances)
-
-        def before(other, total):
-            other_source = lax.rem(me - other + instances, instances)
-            return total + jnp.where(other_source < source, counts_ref[other], 0)
-
-        first = lax.fori_loop(0, instances, before, 0)
+
+    def place(shift, ids):
+        source = source_of(shift)
+        first = loop(
+            instances,
+            lambda other, n: n + jnp.where(source_of(other) < source, count(other, me), 0),
+            jnp.int32(pool),
+        )
+        seen = jnp.int32(0)
+        blocks = [jnp.int32(0)] * CAP
+
+        def find(m, carry):
+            seen, blocks = carry
+            hit = dest(shift, m) == me
+            block = lists_ref[shift, listed + m].astype(jnp.int32)
+            blocks = [jnp.where(hit & (seen == r), block, blocks[r]) for r in range(CAP)]
+            return seen + jnp.where(hit, 1, 0), blocks
+
+        seen, blocks = loop(listed, find, (seen, blocks))
         for rank in range(CAP):
-            name = jnp.where(rank < counts_ref[shift], pool + first + rank, -1)
-            ids = jnp.where(lane == shift * CAP + rank, name, ids)
-
-            def find(m, carry):
-                seen, block = carry
-                hit = dest(shift, m) == me
-                block = jnp.where(
-                    hit & (seen == rank), lists_ref[shift, listed + m].astype(jnp.int32), block
-                )
-                return seen + jnp.where(hit, 1, 0), block
-
-            _, block = lax.fori_loop(0, listed, find, (0, 0))
-            at = (shift * CAP + rank) * block_len
+            slot = shift * CAP + rank
+            ids = jnp.where(lane == slot, jnp.where(rank < seen, first + rank, -1), ids)
+            at = pl.ds(pl.multiple_of(slot * block_len, block_len), block_len)
             for h in range(heads):
-                row_ref[h : h + 1, at : at + block_len] = jnp.full(
-                    (1, block_len),
-                    lists_ref[shift, 2 * listed + h * pool + block] * (factor * LOG2E),
-                )
-                row_ref[heads + h : heads + h + 1, at : at + block_len] = jnp.full(
-                    (1, block_len), lists_ref[shift, 2 * listed + (heads + h) * pool + block]
-                )
+                key = lists_ref[shift, 2 * listed + h * pool + blocks[rank]]
+                value = lists_ref[shift, 2 * listed + (heads + h) * pool + blocks[rank]]
+                row_ref[h : h + 1, at] = jnp.full((1, block_len), key * (factor * LOG2E))
+                row_ref[heads + h : heads + h + 1, at] = jnp.full((1, block_len), value)
+        return ids
+
+    ids = loop(instances, place, jnp.full((1, slots), -1, jnp.int32))
 
     def store(b, value):
         log_ref[:, b * block_len : (b + 1) * block_len] = value
@@ -352,9 +354,12 @@
     send = pl.pallas_call(
         functools.partial(pack_kernel, instances, listed),
         out_shape=[jax.ShapeDtypeStruct((CAP,) + block_shape, bf16)] * instances,
-        in_specs=[SMEM_SPEC, SMEM_SPEC, ANY_SPEC],
-        out_specs=[ANY_SPEC] * instances,
+        in_specs=[SMEM_SPEC, SMEM_SPEC, HBM_SPEC],
+        out_specs=[VMEM_SPEC] * instances,
         scratch_shapes=[pltpu.SMEM((slots,), jnp.int32), pltpu.SemaphoreType.DMA((slots,))],
+        compiler_params=pltpu.CompilerParams(
+            vmem_limit_bytes=(2 * slots * math.prod(block_shape) * 2) + 4 * MIB
+        ),
         cost_estimate=pl.CostEstimate(
             flops=0, bytes_accessed=2 * slots * math.prod(block_shape) * 2, transcendentals=0
         ),
@@ -368,8 +373,10 @@
             value, "inst", [(j, (j + shift) % instances) for j in range(instances)]
         )
 
+    mig_dest, mig_block, pool_scales, *send = lax.optimization_barrier(
+        (mig_dest, mig_block, pool_scales, *send)
+    )
     codes_in = [from_shift(send[shift], shift) for shift in range(instances)]
-
     flat_scales = jnp.transpose(pool_scales, (1, 2, 0)).reshape(1, -1).astype(f32)
     lists = jnp.concatenate([mig_dest.astype(f32), mig_block.astype(f32), flat_scales], axis=1)
     lists_in = jnp.concatenate(
@@ -437,10 +444,12 @@
         ],
         in_specs=[SMEM_SPEC, VMEM_SPEC, VMEM_SPEC],
         out_specs=[SMEM_SPEC, VMEM_SPEC, VMEM_SPEC],
-        scratch_shapes=[pltpu.SMEM((instances,), jnp.int32)],
+        compiler_params=pltpu.CompilerParams(vmem_limit_bytes=8 * MIB),
         name="route_arrivals",
     )(lists_in, tables, length)
 
+    arrival_bytes = 6 * heads * height * slots * block_len + 8 * math.prod(stat)
+    arrival_bytes += 4 * slots * math.prod(block_shape)
     out = pl.pallas_call(
         functools.partial(arrival_kernel, (heads, rows, block_len), instances),
         out_shape=jax.ShapeDtypeStruct((requests, heads, rows, head_dim), bf16),
@@ -450,7 +459,7 @@
             pltpu.VMEM((heads, height, slots * block_len), f32),
             pltpu.VMEM((heads, height, slots * block_len), bf16),
         ],
-        compiler_params=pltpu.CompilerParams(vmem_limit_bytes=48 * MIB),
+        compiler_params=pltpu.CompilerParams(vmem_limit_bytes=arrival_bytes + 8 * MIB),
         cost_estimate=pl.CostEstimate(
             flops=4 * heads * height * slots * block_len * head_dim,
             bytes_accessed=slots * math.prod(block_shape) * 2,

time: 71.4 us -> 40 us (0.56)
  the two profiles are of different devices: /device:TPU:0 before, /device:TPU:9 now
where the time goes in v2:
time: 40 us; the launch traced here: 39.6 us
  Pallas kernels  20.4 us (51%)
  starting transfers between devices  7.1 us (18%)
  waiting for transfers between devices  6.51 us (16%)
  local copies, waits for them, and re-layouts  4.63 us (12%)
  between operations  0.78 us (2%)
    pallas_call x1, Pallas kernels, shards(): pl.pallas_call(functools.partial(own_kernel, (pool, heads, rows, steps, b...  13.9 us
    ppermute x6, starting transfers between devices, from_shift(): lax.ppermute(value, 'inst', [(j, (j + shift) % instances) for j in range(...  7.1 us
    ppermute x6, waiting for transfers between devices, from_shift(): lax.ppermute(value, 'inst', [(j, (j + shift) % instances) for j in range(...  6.51 us
    unnamed x17, local copies, waits for them, and re-layouts  4.18 us
    pallas_call x1, Pallas kernels, shards(): pl.pallas_call(functools.partial(arrival_kernel, (heads, rows, block_len)...  2.77 us
    pallas_call x1, Pallas kernels, shards(): pl.pallas_call(functools.partial(pack_kernel, instances, listed), out_sha...  2.14 us
    pallas_call x1, Pallas kernels, shards(): pl.pallas_call(functools.partial(route_kernel, (pool, heads, instances, l...  1.61 us
  transfers between devices with their start and end apart: 6, of which 2 were waited for; matrix products, arithmetic and copies ran while one was open for 1% of the time, Pallas kernels for 39%

profile of v2, /device:TPU:9, one launch (start us, length us, event | category | flops | bytes accessed | tf_op | source)
XLA Modules:
  0.0 39.6 jit_solution(17606185433087432250)
XLA Ops:
  0.6 0.0 copy-start
  0.6 2.8 %copy-done = bf16[48,2,2,128,128]{4,3,2,1,0:T(8,128)(2,1)S(1)} copy-done((bf16[48,2,2,128,128]{4,3,2,1,0:T(8,128)(2,1)S(1)}, bf16[48,2,2,128,128]{4,3,2,1,0:T(8,128)(2,1)}, u32[]{:S(2)}) %copy-start) | copy-done | bytes 6291480
  3.4 0.0 copy-start.1
  3.4 0.7 %copy-done.1 = s32[1,4]{1,0:T(1,128)S(1)} copy-done((s32[1,4]{1,0:T(1,128)S(1)}, s32[1,4]{1,0:T(1,128)}, u32[]{:S(2)}) %copy-start.1) | copy-done | bytes 40
  4.1 0.0 copy-start.2
  4.1 0.7 %copy-done.2 = s32[1,4]{1,0:T(1,128)S(1)} copy-done((s32[1,4]{1,0:T(1,128)S(1)}, s32[1,4]{1,0:T(1,128)}, u32[]{:S(2)}) %copy-start.2) | copy-done | bytes 40
  4.7 0.0 copy-start.6
  4.7 0.0 copy-start.5
  4.7 0.0 copy-start.7
  4.7 0.0 copy-start.4
  4.7 0.0 copy-start.3
  4.8 2.1 %pack_blocks.1 = (bf16[2,2,2,128,128]{4,3,2,1,0:T(8,128)(2,1)S(1)}, bf16[2,2,2,128,128]{4,3,2,1,0:T(8,128)(2,1)S(1)}, bf16[2,2,2,128,128]{4,3,2,1,0:T(8,128)(2,1)S(1)}, bf16[2,2,2,128,128]{4,3,2,1,0:T(8,128)(2,1)S(1)}) custom-call(s32[1,4]{1,0:T(1,128)S(1)} %copy-done.1, s32[1,4]{1,0:T(1,128)S(1)} %copy-done.2, bf16[48,2,2,128,128]{4,3,2,1,0:T(8,128)(2,1)S(1)} %copy-done), custom_call_target="tpu_custom_call" | custom-call | bytes 2097152 | tf_op jit(solution)/shard_map/pack_blocks/pallas_call | solution.py:354
  6.9 0.0 copy-done.6
  6.9 0.1 reshape.39.scale_ref
  7.0 0.1 pad_maximum_fusion.1
  7.1 0.0 collective-permute-start.2
  7.1 2.5 %collective-permute-start.1 = (f32[1,200]{1,0:T(1,128)S(1)}, f32[1,200]{1,0:T(1,128)S(1)}, u32[]{:S(2)}, u32[]{:S(2)}) collective-permute-start(f32[1,200]{1,0:T(1,128)S(1)} %pad_maximum_fusion.1), channel_id=1, source_target_pairs={{0,8},{4,12},{8,0},{12,4},{1,9},{5,13},{9,1},{13,5},{2,10},{6,14},... | collective-permute-start | bytes 2408 | tf_op jit(solution)/shard_map/ppermute | solution.py:372
  9.6 2.2 %collective-permute-start = (f32[1,200]{1,0:T(1,128)S(1)}, f32[1,200]{1,0:T(1,128)S(1)}, u32[]{:S(2)}, u32[]{:S(2)}) collective-permute-start(f32[1,200]{1,0:T(1,128)S(1)} %pad_maximum_fusion.1), channel_id=1, source_target_pairs={{0,4},{4,8},{8,12},{12,0},{1,5},{5,9},{9,13},{13,1},{2,6},{6,10},{... | collective-permute-start | bytes 2408 | tf_op jit(solution)/shard_map/ppermute | solution.py:372
  11.8 0.0 collective-permute-start.3
  11.8 1.3 %collective-permute-start.4 = (bf16[2,2,2,128,128]{4,3,2,1,0:T(8,128)(2,1)S(1)}, bf16[2,2,2,128,128]{4,3,2,1,0:T(8,128)(2,1)S(1)}, u32[]{:S(2)}, u32[]{:S(2)}) collective-permute-start(bf16[2,2,2,128,128]{4,3,2,1,0:T(8,128)(2,1)S(1)} %get-tuple-element.33), channel_id=1, source_target_pairs={{0,8},{4,12},{8,0},{12,4},{1,9},{5,13},{9,1},{13,5},{2,10},{6,14},... | collective-permute-start | bytes 786440 | tf_op jit(solution)/shard_map/ppermute | solution.py:372
  13.1 0.0 copy-done.5
  13.1 0.1 copy.11.tables_ref
  13.2 0.0 copy-done.7
  13.2 0.1 copy.12.length_ref
  13.3 0.0 copy-done.4
  13.3 0.1 copy.13
  13.4 0.0 copy-done.3
  13.4 0.2 copy.10
  13.6 0.0 collective-permute-done.2
  13.6 1.1 %collective-permute-start.5 = (bf16[2,2,2,128,128]{4,3,2,1,0:T(8,128)(2,1)S(1)}, bf16[2,2,2,128,128]{4,3,2,1,0:T(8,128)(2,1)S(1)}, u32[]{:S(2)}, u32[]{:S(2)}) collective-permute-start(bf16[2,2,2,128,128]{4,3,2,1,0:T(8,128)(2,1)S(1)} %get-tuple-element.34), channel_id=1, source_target_pairs={{0,12},{4,0},{8,4},{12,8},{1,13},{5,1},{9,5},{13,9},{2,14},{6,2},{... | collective-permute-start | bytes 786440 | tf_op jit(solution)/shard_map/ppermute | solution.py:372
  14.7 13.9 %own_blocks.1 = (f32[2,512,128]{2,1,0:T(8,128)S(1)}, f32[2,512,128]{2,1,0:T(8,128)S(1)}, f32[2,512,128]{2,1,0:T(8,128)S(1)}) custom-call(s32[32,16]{1,0:T(8,128)S(1)} %copy.11.tables_ref, s32[32,1]{1,0:T(8,128)S(1)} %copy.12.length_ref, f32[1,192]{1,0:T(1,128)S(1)} %reshape.39.scale_ref, bf16[2,512,128]{2,1,0:T(8,128)(2,1)S(1)} %bitcast.14, ...), custom_call_target="tpu_custom_call" | custom-call | flops 3221225472 | bytes 6291456 | tf_op jit(solution)/shard_map/own_blocks/pallas_call | solution.py:403
  28.6 0.0 collective-permute-done.1
  28.6 0.0 collective-permute-done
  28.6 0.1 pad_maximum_fusion.lists_ref
  28.7 1.6 %route_arrivals.1 = (s32[1,4]{1,0:T(1,128)}, f32[32,1024]{1,0:T(8,128)S(1)}, f32[4,1024]{1,0:T(4,128)S(1)}) custom-call(f32[4,200]{1,0:T(4,128)S(1)} %pad_maximum_fusion.lists_ref, s32[32,16]{1,0:T(8,128)S(1)} %copy.11.tables_ref, s32[32,1]{1,0:T(8,128)S(1)} %copy.12.length_ref), custom_call_target="tpu_custom_call" | custom-call | tf_op jit(solution)/shard_map/route_arrivals/pallas_call | solution.py:436
  30.3 0.0 collective-permute-done.3.rest_1_
  30.3 2.7 %collective-permute-done.4.rest_2_ = bf16[2,2,2,128,128]{4,3,2,1,0:T(8,128)(2,1)S(1)} collective-permute-done((bf16[2,2,2,128,128]{4,3,2,1,0:T(8,128)(2,1)S(1)}, bf16[2,2,2,128,128]{4,3,2,1,0:T(8,128)(2,1)S(1)}, u32[]{:S(2)}, u32[]{:S(2)}) %collective-permute-start.4) | collective-permute-done | bytes 262176 | tf_op jit(solution)/shard_map/ppermute | solution.py:372
  33.1 3.8 %collective-permute-done.5.rest_3_ = bf16[2,2,2,128,128]{4,3,2,1,0:T(8,128)(2,1)S(1)} collective-permute-done((bf16[2,2,2,128,128]{4,3,2,1,0:T(8,128)(2,1)S(1)}, bf16[2,2,2,128,128]{4,3,2,1,0:T(8,128)(2,1)S(1)}, u32[]{:S(2)}, u32[]{:S(2)}) %collective-permute-start.5) | collective-permute-done | bytes 262176 | tf_op jit(solution)/shard_map/ppermute | solution.py:372
  36.8 2.8 %arrived_blocks.1 = bf16[32,2,16,128]{3,2,1,0:T(8,128)(2,1)} custom-call(bf16[2,512,128]{2,1,0:T(8,128)(2,1)S(1)} %bitcast.15, f32[32,1024]{1,0:T(8,128)S(1)} %get-tuple-element.26.log_ref, f32[4,1024]{1,0:T(4,128)S(1)} %get-tuple-element.27.row_ref, f32[2,512,128]{2,1,0:T(8,128)S(1)} %get-tuple-element.28.acc_ref, ...), custom_call_target="tpu_custom_call" | custom-call | flops 536870912 | bytes 1048576 | tf_op jit(solution)/shard_map/arrived_blocks/pallas_call | solution.py:453
  (4 shorter events, 0.0 us)
Async XLA Ops:
  0.6 2.8 %copy-start = (bf16[48,2,2,128,128]{4,3,2,1,0:T(8,128)(2,1)S(1)}, bf16[48,2,2,128,128]{4,3,2,1,0:T(8,128)(2,1)}, u32[]{:S(2)}) copy-start(bf16[48,2,2,128,128]{4,3,2,1,0:T(8,128)(2,1)} %codes_ref.1) | copy-start | bytes 18874372
  3.4 0.7 %copy-start.1 = (s32[1,4]{1,0:T(1,128)S(1)}, s32[1,4]{1,0:T(1,128)}, u32[]{:S(2)}) copy-start(s32[1,4]{1,0:T(1,128)} %dest_ref.1) | copy-start | bytes 52
  4.1 0.7 %copy-start.2 = (s32[1,4]{1,0:T(1,128)S(1)}, s32[1,4]{1,0:T(1,128)}, u32[]{:S(2)}) copy-start(s32[1,4]{1,0:T(1,128)} %block_ref.1) | copy-start | bytes 52
  4.7 2.2 %copy-start.6 = (bf16[48,2,2]{0,2,1:T(2,128)(2,1)S(1)}, bf16[48,2,2]{0,2,1:T(2,128)(2,1)}, u32[]{:S(2)}) copy-start(bf16[48,2,2]{0,2,1:T(2,128)(2,1)} %param.11) | copy-start | bytes 1156
  4.7 8.4 %copy-start.5 = (s32[32,16]{0,1:T(8,128)S(1)}, s32[32,16]{0,1:T(8,128)}, u32[]{:S(2)}) copy-start(s32[32,16]{0,1:T(8,128)} %param.12) | copy-start | bytes 6148
  4.7 8.5 %copy-start.7 = (s32[32]{0:T(128)S(1)}, s32[32]{0:T(128)}, u32[]{:S(2)}) copy-start(s32[32]{0:T(128)} %param.13) | copy-start | bytes 388
  4.7 8.6 %copy-start.4 = (bf16[32,2,2,2,128]{4,3,2,1,0:T(2,128)(2,1)S(1)}, bf16[32,2,2,2,128]{4,3,2,1,0:T(2,128)(2,1)}, u32[]{:S(2)}) copy-start(bf16[32,2,2,2,128]{4,3,2,1,0:T(2,128)(2,1)} %param.9) | copy-start | bytes 196612
  4.7 8.6 %copy-start.3 = (bf16[32,2,16,128]{3,2,1,0:T(8,128)(2,1)S(1)}, bf16[32,2,16,128]{3,2,1,0:T(8,128)(2,1)}, u32[]{:S(2)}) copy-start(bf16[32,2,16,128]{3,2,1,0:T(8,128)(2,1)} %param.8) | copy-start | bytes 786436
  7.1 6.5 %collective-permute-start.2 = (f32[1,200]{1,0:T(1,128)S(1)}, f32[1,200]{1,0:T(1,128)S(1)}, u32[]{:S(2)}, u32[]{:S(2)}) collective-permute-start(f32[1,200]{1,0:T(1,128)S(1)} %pad_maximum_fusion.1), channel_id=1, source_target_pairs={{0,12},{4,0},{8,4},{12,8},{1,13},{5,1},{9,5},{13,9},{2,14},{6,2},{... | collective-permute-start | bytes 2408 | tf_op jit(solution)/shard_map/ppermute | solution.py:372
  7.1 21.5 %collective-permute-start.1 = (f32[1,200]{1,0:T(1,128)S(1)}, f32[1,200]{1,0:T(1,128)S(1)}, u32[]{:S(2)}, u32[]{:S(2)}) collective-permute-start(f32[1,200]{1,0:T(1,128)S(1)} %pad_maximum_fusion.1), channel_id=1, source_target_pairs={{0,8},{4,12},{8,0},{12,4},{1,9},{5,13},{9,1},{13,5},{2,10},{6,14},... | collective-permute-start | bytes 2408 | tf_op jit(solution)/shard_map/ppermute | solution.py:372
  9.6 19.0 %collective-permute-start = (f32[1,200]{1,0:T(1,128)S(1)}, f32[1,200]{1,0:T(1,128)S(1)}, u32[]{:S(2)}, u32[]{:S(2)}) collective-permute-start(f32[1,200]{1,0:T(1,128)S(1)} %pad_maximum_fusion.1), channel_id=1, source_target_pairs={{0,4},{4,8},{8,12},{12,0},{1,5},{5,9},{9,13},{13,1},{2,6},{6,10},{... | collective-permute-start | bytes 2408 | tf_op jit(solution)/shard_map/ppermute | solution.py:372
  11.8 18.5 %collective-permute-start.3 = (bf16[2,2,2,128,128]{4,3,2,1,0:T(8,128)(2,1)S(1)}, bf16[2,2,2,128,128]{4,3,2,1,0:T(8,128)(2,1)S(1)}, u32[]{:S(2)}, u32[]{:S(2)}) collective-permute-start(bf16[2,2,2,128,128]{4,3,2,1,0:T(8,128)(2,1)S(1)} %get-tuple-element.32), channel_id=1, source_target_pairs={{0,4},{4,8},{8,12},{12,0},{1,5},{5,9},{9,13},{13,1},{2,6},{6,10},{... | collective-permute-start | bytes 786440 | tf_op jit(solution)/shard_map/ppermute | solution.py:372
  11.8 21.3 %collective-permute-start.4 = (bf16[2,2,2,128,128]{4,3,2,1,0:T(8,128)(2,1)S(1)}, bf16[2,2,2,128,128]{4,3,2,1,0:T(8,128)(2,1)S(1)}, u32[]{:S(2)}, u32[]{:S(2)}) collective-permute-start(bf16[2,2,2,128,128]{4,3,2,1,0:T(8,128)(2,1)S(1)} %get-tuple-element.33), channel_id=1, source_target_pairs={{0,8},{4,12},{8,0},{12,4},{1,9},{5,13},{9,1},{13,5},{2,10},{6,14},... | collective-permute-start | bytes 786440 | tf_op jit(solution)/shard_map/ppermute | solution.py:372
  13.6 23.2 %collective-permute-start.5 = (bf16[2,2,2,128,128]{4,3,2,1,0:T(8,128)(2,1)S(1)}, bf16[2,2,2,128,128]{4,3,2,1,0:T(8,128)(2,1)S(1)}, u32[]{:S(2)}, u32[]{:S(2)}) collective-permute-start(bf16[2,2,2,128,128]{4,3,2,1,0:T(8,128)(2,1)S(1)} %get-tuple-element.34), channel_id=1, source_target_pairs={{0,12},{4,0},{8,4},{12,8},{1,13},{5,1},{9,5},{13,9},{2,14},{6,2},{... | collective-permute-start | bytes 786440 | tf_op jit(solution)/shard_map/ppermute | solution.py:372

commit v3 on v2

--- a/solution.py
+++ b/solution.py
@@ -17,40 +17,57 @@
 NT = (((1,), (1,)), ((), ()))
 
 
-def pack_kernel(instances, listed, dest_ref, block_ref, pool_ref, *rest):
-    send_refs, (index_ref, sems) = rest[:instances], rest[instances:]
+def loop(count, body, init):
+    if count <= 8:
+        for i in range(count):
+            init = body(i, init)
+        return init
+    return lax.fori_loop(0, count, body, init)
+
+
+def pack_kernel(instances, listed, rest_only, dest_ref, block_ref, pool_ref, *refs):
+    slots = instances if rest_only else instances + 1
+    send_refs, (index_ref, held_ref, in_sems, out_sems) = refs[:slots], refs[slots:]
     me = lax.axis_index("inst")
-
-    def clear(slot, carry):
+    for slot in range(slots):
         index_ref[slot] = 0
-        return carry
-
-    lax.fori_loop(0, instances * CAP, clear, 0)
 
     def place(m, carry):
         dest = dest_ref[0, m]
-
-        def earlier(m2, rank):
-            return rank + jnp.where(dest_ref[0, m2] == dest, 1, 0)
-
-        rank = jnp.minimum(lax.fori_loop(0, m, earlier, 0), CAP - 1)
-        shift = lax.rem(dest - me + instances, instances)
-        index_ref[shift * CAP + rank] = block_ref[0, m]
+        rank = loop(
+            listed,
+            lambda m2, n: n + jnp.where((dest_ref[0, m2] == dest) & (m2 < m), 1, 0),
+            jnp.int32(0),
+        )
+        shift = jnp.where(dest < me, dest - me + instances, dest - me)
+
+        if rest_only:
+
+            @pl.when(rank > 0)
+            def _():
+                index_ref[shift] = block_ref[0, m]
+
+        else:
+            index_ref[jnp.where(rank > 0, instances, shift)] = block_ref[0, m]
         return carry
 
-    lax.fori_loop(0, listed, place, 0)
-    copies = []
-    for shift in list(range(1, instances)) + [0]:
-        for rank in range(CAP):
-            slot = shift * CAP + rank
-            copies.append(
-                pltpu.make_async_copy(
-                    pool_ref.at[index_ref[slot]], send_refs[shift].at[rank], sems.at[slot]
-                )
-            )
-            copies[-1].start()
-    for copy in copies:
-        copy.wait()
+    loop(listed, place, 0)
+    loads = []
+    order = [slots - 1] + list(range(slots - 1))
+    for slot in order:
+        loads.append(
+            pltpu.make_async_copy(pool_ref.at[index_ref[slot]], held_ref.at[slot], in_sems.at[slot])
+        )
+        loads[-1].start()
+    stores = []
+    for slot, load in zip(order, loads):
+        load.wait()
+        stores.append(
+            pltpu.make_async_copy(held_ref.at[slot], send_refs[slot].at[0], out_sems.at[slot])
+        )
+        stores[-1].start()
+    for store in stores:
+        store.wait()
 
 
 def count_log(tables, length, ids, block_len, spans, store):
@@ -205,73 +222,69 @@
             )
 
 
-def loop(count, body, init):
-    if count <= 8:
-        for i in range(count):
-            init = body(i, init)
-        return init
-    return lax.fori_loop(0, count, body, init)
-
-
-def route_kernel(dims, lists_ref, tables_ref, length_ref, moved_ref, log_ref, row_ref):
-    pool, heads, instances, listed, block_len, spans, factor = dims
+def route_kernel(
+    dims, lists_ref, tables_ref, length_ref, own_ref, moved_ref, more_ref, log_ref, row_ref
+):
+    pool, heads, instances, groups, listed, block_len, spans, factor = dims
     me = lax.axis_index("inst")
-
-    def dest(shift, m):
-        return lists_ref[shift, m].astype(jnp.int32)
-
-    def source_of(shift):
-        source = me - shift
-        return jnp.where(source < 0, source + instances, source)
-
-    def count(shift, target):
+    base = lax.axis_index("groups") * instances
+
+    def dest(row, m):
+        return lists_ref[row, m].astype(jnp.int32)
+
+    def count(row, target):
         return loop(
-            listed, lambda m, n: n + jnp.where(dest(shift, m) == target, 1, 0), jnp.int32(0)
+            listed, lambda m, n: n + jnp.where(dest(row, m) == target, 1, 0), jnp.int32(0)
+        )
+
+    def rank(row, m):
+        target = dest(row, m)
+        return loop(
+            listed,
+            lambda m2, n: n + jnp.where((dest(row, m2) == target) & (m2 < m), 1, 0),
+            jnp.int32(0),
+        )
+
+    def before(source, target):
+        return loop(
+            instances,
+            lambda j, n: n + jnp.where(j < source, count(base + j, target), 0),
+            jnp.int32(pool),
         )
 
     def move(m, carry):
-        target = dest(0, m)
-        rank = loop(
-            listed,
-            lambda m2, n: n + jnp.where((dest(0, m2) == target) & (m2 < m), 1, 0),
-            jnp.int32(0),
-        )
-        moved_ref[0, m] = loop(
-            instances,
-            lambda shift, n: n + jnp.where(source_of(shift) < me, count(shift, target), 0),
-            pool + rank,
-        )
+        moved_ref[0, m] = before(me, dest(base + me, m)) + rank(base + me, m)
         return carry
 
     loop(listed, move, 0)
+
+    def seconds(row, more):
+        found = loop(listed, lambda m, n: n + jnp.minimum(rank(row, m), 1), jnp.int32(0))
+        return jnp.maximum(more, jnp.where(found > 1, 1, 0))
+
+    more_ref[0] = loop(groups * instances, seconds, jnp.int32(0))
     slots = instances * CAP
     lane = lax.broadcasted_iota(jnp.int32, (1, slots), 1)
 
-    def place(shift, ids):
-        source = source_of(shift)
-        first = loop(
-            instances,
-            lambda other, n: n + jnp.where(source_of(other) < source, count(other, me), 0),
-            jnp.int32(pool),
-        )
-        seen = jnp.int32(0)
-        blocks = [jnp.int32(0)] * CAP
+    def place(j, ids):
+        row = base + j
+        first = before(j, me)
 
         def find(m, carry):
             seen, blocks = carry
-            hit = dest(shift, m) == me
-            block = lists_ref[shift, listed + m].astype(jnp.int32)
+            hit = dest(row, m) == me
+            block = lists_ref[row, listed + m].astype(jnp.int32)
             blocks = [jnp.where(hit & (seen == r), block, blocks[r]) for r in range(CAP)]
             return seen + jnp.where(hit, 1, 0), blocks
 
-        seen, blocks = loop(listed, find, (seen, blocks))
-        for rank in range(CAP):
-            slot = shift * CAP + rank
-            ids = jnp.where(lane == slot, jnp.where(rank < seen, first + rank, -1), ids)
+        seen, blocks = loop(listed, find, (jnp.int32(0), [jnp.int32(0)] * CAP))
+        shift = jnp.where(me < j, me - j + instances, me - j)
+        for r, slot in enumerate((shift, instances + j)):
+            ids = jnp.where(lane == slot, jnp.where(r < seen, first + r, -1), ids)
             at = pl.ds(pl.multiple_of(slot * block_len, block_len), block_len)
             for h in range(heads):
-                key = lists_ref[shift, 2 * listed + h * pool + blocks[rank]]
-                value = lists_ref[shift, 2 * listed + (heads + h) * pool + blocks[rank]]
+                key = lists_ref[row, 2 * listed + h * pool + blocks[r]]
+                value = lists_ref[row, 2 * listed + (heads + h) * pool + blocks[r]]
                 row_ref[h : h + 1, at] = jnp.full((1, block_len), key * (factor * LOG2E))
                 row_ref[heads + h : heads + h + 1, at] = jnp.full((1, block_len), value)
         return ids
@@ -285,22 +298,27 @@
 
 
 def arrival_kernel(
-    dims, sources, q_ref, log_ref, row_ref, acc_ref, top_ref, total_ref, *rest
+    dims, q_ref, log_ref, row_ref, acc_ref, top_ref, total_ref, *rest
 ):
-    heads, rows, block_len = dims
-    code_refs, (out_ref, t_ref, p_ref) = rest[:sources], rest[sources:]
+    heads, rows, block_len, instances = dims
+    first_refs, (second_ref, out_ref, t_ref, p_ref) = rest[:instances], rest[instances:]
     height = q_ref.shape[1]
-    width = CAP * block_len
+    width = 2 * block_len
+    slots = [ref.at[0] for ref in first_refs] + [second_ref.at[j] for j in range(instances)]
+
+    def pair(i, part, h):
+        return jnp.concatenate([slots[2 * i][part, h], slots[2 * i + 1][part, h]], axis=0)
+
     for h in range(heads):
-        for s, codes_ref in enumerate(code_refs):
-            left = s * width
+        for i in range(instances):
+            left = i * width
 
             def store(row, lane, value, h=h, left=left):
                 t_ref[h, row : row + rows, left + lane : left + lane + value.shape[1]] = value
 
             score_tiles(
                 q_ref[h],
-                codes_ref[:, 0, h].reshape(width, codes_ref.shape[-1]),
+                pair(i, 0, h),
                 log_ref.at[:, left : left + width],
                 row_ref[h : h + 1, left : left + width],
                 rows,
@@ -324,10 +342,10 @@
             t_ref[h, at, 0:128] = keep
             t_ref[h, at, 128:256] = 1.0 / total
         mixed = acc_ref[h] * t_ref[h, :, 0:128]
-        for s, codes_ref in enumerate(code_refs):
+        for i in range(instances):
             mixed = mixed + jnp.dot(
-                p_ref[h, :, s * width : (s + 1) * width],
-                codes_ref[:, 1, h].reshape(width, codes_ref.shape[-1]),
+                p_ref[h, :, i * width : (i + 1) * width],
+                pair(i, 1, h),
                 preferred_element_type=jnp.float32,
             )
         result = (mixed * t_ref[h, :, 128:256]).astype(jnp.bfloat16)
@@ -351,20 +369,26 @@
     f32, bf16 = jnp.float32, jnp.bfloat16
 
     block_shape = pool_codes.shape[1:]
-    send = pl.pallas_call(
-        functools.partial(pack_kernel, instances, listed),
-        out_shape=[jax.ShapeDtypeStruct((CAP,) + block_shape, bf16)] * instances,
-        in_specs=[SMEM_SPEC, SMEM_SPEC, HBM_SPEC],
-        out_specs=[VMEM_SPEC] * instances,
-        scratch_shapes=[pltpu.SMEM((slots,), jnp.int32), pltpu.SemaphoreType.DMA((slots,))],
-        compiler_params=pltpu.CompilerParams(
-            vmem_limit_bytes=(2 * slots * math.prod(block_shape) * 2) + 4 * MIB
-        ),
-        cost_estimate=pl.CostEstimate(
-            flops=0, bytes_accessed=2 * slots * math.prod(block_shape) * 2, transcendentals=0
-        ),
-        name="pack_blocks",
-    )(mig_dest, mig_block, pool_codes)
+
+    def pack(rest_only, dests, blocks, codes):
+        count = instances if rest_only else instances + 1
+        return pl.pallas_call(
+            functools.partial(pack_kernel, instances, listed, rest_only),
+            out_shape=[jax.ShapeDtypeStruct((1,) + block_shape, bf16)] * count,
+            in_specs=[SMEM_SPEC, SMEM_SPEC, HBM_SPEC],
+            out_specs=[HBM_SPEC] * count,
+            scratch_shapes=[
+                pltpu.SMEM((count,), jnp.int32),
+                pltpu.VMEM((count,) + block_shape, bf16),
+                pltpu.SemaphoreType.DMA((count,)),
+                pltpu.SemaphoreType.DMA((count,)),
+            ],
+            compiler_params=pltpu.CompilerParams(vmem_limit_bytes=56 * MIB),
+            cost_estimate=pl.CostEstimate(
+                flops=0, bytes_accessed=4 * count * math.prod(block_shape), transcendentals=0
+            ),
+            name="pack_blocks",
+        )(dests, blocks, codes)
 
     def from_shift(value, shift):
         if shift == 0:
@@ -373,15 +397,15 @@
             value, "inst", [(j, (j + shift) % instances) for j in range(instances)]
         )
 
-    mig_dest, mig_block, pool_scales, *send = lax.optimization_barrier(
-        (mig_dest, mig_block, pool_scales, *send)
+    *send, second = pack(False, mig_dest, mig_block, pool_codes)
+    mig_dest, mig_block, pool_scales, second, *send = lax.optimization_barrier(
+        (mig_dest, mig_block, pool_scales, second, *send)
     )
-    codes_in = [from_shift(send[shift], shift) for shift in range(instances)]
+    first_in = [from_shift(send[shift], shift) for shift in range(instances)]
+    second_in = lax.all_gather(second, "inst", axis=0, tiled=True)
     flat_scales = jnp.transpose(pool_scales, (1, 2, 0)).reshape(1, -1).astype(f32)
     lists = jnp.concatenate([mig_dest.astype(f32), mig_block.astype(f32), flat_scales], axis=1)
-    lists_in = jnp.concatenate(
-        [from_shift(lists, shift) for shift in range(instances)], axis=0
-    )
+    lists_in = lax.all_gather(lists, ("groups", "inst"), axis=0, tiled=True)
 
     query_rows = (
         queries.reshape(requests, steps, heads, per_head, head_dim)
@@ -433,27 +457,42 @@
         name="own_blocks",
     )(tables, length, flat_scales, query_rows, fresh, pool_codes)
 
-    moved_to, log_in, rows_in = pl.pallas_call(
+    moved_to, more, log_in, rows_in = pl.pallas_call(
         functools.partial(
-            route_kernel, (pool, heads, instances, listed, block_len, spans, factor)
+            route_kernel,
+            (pool, heads, instances, lax.axis_size("groups"), listed, block_len, spans, factor),
         ),
         out_shape=[
             jax.ShapeDtypeStruct((1, listed), jnp.int32),
+            jax.ShapeDtypeStruct((1,), jnp.int32),
             jax.ShapeDtypeStruct((requests, slots * block_len), f32),
             jax.ShapeDtypeStruct((2 * heads, slots * block_len), f32),
         ],
-        in_specs=[SMEM_SPEC, VMEM_SPEC, VMEM_SPEC],
-        out_specs=[SMEM_SPEC, VMEM_SPEC, VMEM_SPEC],
+        in_specs=[SMEM_SPEC, VMEM_SPEC, VMEM_SPEC, HBM_SPEC],
+        out_specs=[SMEM_SPEC, SMEM_SPEC, VMEM_SPEC, VMEM_SPEC],
         compiler_params=pltpu.CompilerParams(vmem_limit_bytes=8 * MIB),
         name="route_arrivals",
-    )(lists_in, tables, length)
+    )(lists_in, tables, length, top)
+
+    def all_seconds(gathered, dests, blocks, codes):
+        rest = pack(True, dests, blocks, codes)
+        arrived = jnp.concatenate([from_shift(rest[s], s) for s in range(instances)], axis=0)
+        shifts = (lax.axis_index("inst") - jnp.arange(instances)) % instances
+        return jnp.take(arrived, shifts, axis=0)
+
+    second_in = lax.cond(
+        more[0] > 0,
+        all_seconds,
+        lambda gathered, *unused: gathered,
+        second_in, mig_dest, mig_block, pool_codes,
+    )
 
     arrival_bytes = 6 * heads * height * slots * block_len + 8 * math.prod(stat)
     arrival_bytes += 4 * slots * math.prod(block_shape)
     out = pl.pallas_call(
-        functools.partial(arrival_kernel, (heads, rows, block_len), instances),
+        functools.partial(arrival_kernel, (heads, rows, block_len, instances)),
         out_shape=jax.ShapeDtypeStruct((requests, heads, rows, head_dim), bf16),
-        in_specs=[VMEM_SPEC] * (6 + instances),
+        in_specs=[VMEM_SPEC] * (7 + instances),
         out_specs=VMEM_SPEC,
         scratch_shapes=[
             pltpu.VMEM((heads, height, slots * block_len), f32),
@@ -466,7 +505,7 @@
             transcendentals=heads * height * slots * block_len,
         ),
         name="arrived_blocks",
-    )(query_rows, log_in, rows_in, acc, top, total, *codes_in)
+    )(query_rows, log_in, rows_in, acc, top, total, *first_in, second_in)
     out = (
         out.reshape(requests, q_heads, steps, head_dim)
         .transpose(0, 2, 1, 3)

time: 40 us -> 67.8 us (1.69)
  the two profiles are of different devices: /device:TPU:9 before, /device:TPU:0 now
where the time goes in v3:
time: 67.8 us; the launch traced here: 67.4 us
  blocking collectives  33.5 us (49%)
  Pallas kernels  21 us (31%)
  starting transfers between devices  7.27 us (11%)
  waiting for transfers between devices  3.63 us (5%)
  between operations  1.42 us (2%)
    all_gather x1, blocking collectives, shards(): lists_in = lax.all_gather(lists, ('groups', 'inst'), axis=0, tiled=True)  18.6 us
    all_gather x1, blocking collectives, shards(): second_in = lax.all_gather(second, 'inst', axis=0, tiled=True)  14.9 us
    pallas_call x1, Pallas kernels, shards(): pl.pallas_call(functools.partial(own_kernel, (pool, heads, rows, steps, b...  13.7 us
    ppermute x3, starting transfers between devices, from_shift(): lax.ppermute(value, 'inst', [(j, (j + shift) % instances) for j in range(...  7.27 us
    ppermute x3, waiting for transfers between devices, from_shift(): lax.ppermute(value, 'inst', [(j, (j + shift) % instances) for j in range(...  3.63 us
    pallas_call x1, Pallas kernels, pack(): pl.pallas_call(functools.partial(pack_kernel, instances, listed, rest_onl...  2.72 us
    pallas_call x1, Pallas kernels, shards(): pl.pallas_call(functools.partial(arrival_kernel, (heads, rows, block_len,...  2.67 us
    pallas_call x1, Pallas kernels, shards(): pl.pallas_call(functools.partial(route_kernel, (pool, heads, instances, l...  1.89 us
  transfers between devices with their start and end apart: 3, of which 1 were waited for; matrix products, arithmetic and copies ran while one was open for 1% of the time, Pallas kernels for 23%

profile of v3, /device:TPU:0, one launch (start us, length us, event | category | flops | bytes accessed | tf_op | source)
XLA Modules:
  0.0 67.4 jit_solution(12231207661548989467)
XLA Ops:
  0.6 0.0 copy-start.5
  0.6 0.0 copy-start.4
  0.7 0.0 copy-start.6
  0.7 0.0 copy-start.3
  0.7 0.0 copy-start.7
  0.7 0.0 copy-start.2
  0.7 0.0 copy-start.1
  0.7 2.7 %pack_blocks.3 = (bf16[1,2,2,128,128]{4,3,2,1,0:T(8,128)(2,1)}, bf16[1,2,2,128,128]{4,3,2,1,0:T(8,128)(2,1)}, bf16[1,2,2,128,128]{4,3,2,1,0:T(8,128)(2,1)}, bf16...) custom-call(s32[1,4]{1,0:T(1,128)} %dest_ref.1, s32[1,4]{1,0:T(1,128)} %block_ref.1, ...), custom_call_target="tpu_custom_call" | custom-call | bytes 1310720 | tf_op jit(solution)/shard_map/pack_blocks/pallas_call | solution.py:375
  3.4 3.1 %collective-permute-start.3 = (bf16[1,2,2,128,128]{4,3,2,1,0:T(8,128)(2,1)}, bf16[1,2,2,128,128]{4,3,2,1,0:T(8,128)(2,1)S(1)}, u32[]{:S(2)}, u32[]{:S(2)}) collective-permute-start(bf16[1,2,2,128,128]{4,3,2,1,0:T(8,128)(2,1)} %get-tuple-element.53), channel_id=1, source_target_pairs={{0,4},{4,8},{8,12},{12,0},{1,5},{5,9},{9,13},{13,1},{2,6},{6,10},{... | collective-permute-start | bytes 393224 | tf_op jit(solution)/shard_map/ppermute | solution.py:396
  6.5 2.6 %collective-permute-start.4 = (bf16[1,2,2,128,128]{4,3,2,1,0:T(8,128)(2,1)}, bf16[1,2,2,128,128]{4,3,2,1,0:T(8,128)(2,1)S(1)}, u32[]{:S(2)}, u32[]{:S(2)}) collective-permute-start(bf16[1,2,2,128,128]{4,3,2,1,0:T(8,128)(2,1)} %get-tuple-element.54), channel_id=1, source_target_pairs={{0,8},{4,12},{8,0},{12,4},{1,9},{5,13},{9,1},{13,5},{2,10},{6,14},... | collective-permute-start | bytes 393224 | tf_op jit(solution)/shard_map/ppermute | solution.py:396
  9.1 0.0 copy-done.5
  9.1 0.0 copy-done.4
  9.1 0.0 copy-done.3
  9.1 0.1 copy.21.tables_ref
  9.2 0.0 copy-done.7
  9.2 0.1 copy.22.length_ref
  9.3 0.0 copy-done.2
  9.3 0.1 copy.18
  9.3 0.0 copy-done.1
  9.4 0.2 copy.17
  9.6 0.0 copy-done.6
  9.6 0.1 reshape.97.scale_ref
  9.7 0.1 maximum_bitcast_fusion
  9.8 18.6 %all-gather = f32[8,1,200]{2,1,0:T(1,128)S(1)} all-gather(f32[1,1,200]{2,1,0:T(1,128)S(1)} %maximum_bitcast_fusion), channel_id=1, replica_groups=mesh['groups'=2,'inst'=4,'tp'=4] {'groups','inst'}, dimensions={0}, use_global_device_ids=true | all-gather | bytes 7200 | tf_op jit(solution)/shard_map/all_gather | solution.py:408
  28.3 14.9 %all_gather.10 = bf16[4,2,2,128,128]{4,3,2,1,0:T(8,128)(2,1)S(1)} all-gather(bf16[1,2,2,128,128]{4,3,2,1,0:T(8,128)(2,1)} %get-tuple-element.57), channel_id=1, replica_groups=mesh['groups'=2,'inst'=4,'tp'=4] {'inst'}, dimensions={0}, use_global_device_ids=true | all-gather | bytes 655360 | tf_op jit(solution)/shard_map/all_gather | solution.py:405
  43.2 13.7 %own_blocks.1 = (f32[2,512,128]{2,1,0:T(8,128)S(1)}, f32[2,512,128]{2,1,0:T(8,128)S(1)}, f32[2,512,128]{2,1,0:T(8,128)S(1)}) custom-call(s32[32,16]{1,0:T(8,128)S(1)} %copy.21.tables_ref, s32[32,1]{1,0:T(8,128)S(1)} %copy.22.length_ref, f32[1,192]{1,0:T(1,128)S(1)} %reshape.97.scale_ref, bf16[2,512,128]{2,1,0:T(8,128)(2,1)S(1)} %bitcast.22, ...), custom_call_target="tpu_custom_call" | custom-call | flops 3221225472 | bytes 6291456 | tf_op jit(solution)/shard_map/own_blocks/pallas_call | solution.py:427
  56.9 0.0 copy-start
  56.9 1.9 %route_arrivals.1 = (s32[1,4]{1,0:T(1,128)}, s32[1]{0:T(128)}, f32[32,1024]{1,0:T(8,128)S(1)}, f32[4,1024]{1,0:T(4,128)S(1)}) custom-call(f32[8,200]{1,0:T(8,128)S(1)} %bitcast.24, s32[32,16]{1,0:T(8,128)S(1)} %copy.21.tables_ref, s32[32,1]{1,0:T(8,128)S(1)} %copy.22.length_ref, f32[2,512,128]{2,1,0:T(8,128)S(1)} %get-tuple-element.47.own_ref.top_ref), custom_call_target="tpu_custom_call" | custom-call | tf_op jit(solution)/shard_map/route_arrivals/pallas_call | solution.py:460
  59.5 1.6 %collective-permute-start.5 = (bf16[1,2,2,128,128]{4,3,2,1,0:T(8,128)(2,1)}, bf16[1,2,2,128,128]{4,3,2,1,0:T(8,128)(2,1)S(1)}, u32[]{:S(2)}, u32[]{:S(2)}) collective-permute-start(bf16[1,2,2,128,128]{4,3,2,1,0:T(8,128)(2,1)} %get-tuple-element.55), channel_id=1, source_target_pairs={{0,12},{4,0},{8,4},{12,8},{1,13},{5,1},{9,5},{13,9},{2,14},{6,2},{... | collective-permute-start | bytes 393224 | tf_op jit(solution)/shard_map/ppermute | solution.py:396
  61.1 0.0 collective-permute-done.3.rest_1_
  61.1 0.0 collective-permute-done.4.rest_2_
  61.1 3.6 %collective-permute-done.5.rest_3_ = bf16[1,2,2,128,128]{4,3,2,1,0:T(8,128)(2,1)S(1)} collective-permute-done((bf16[1,2,2,128,128]{4,3,2,1,0:T(8,128)(2,1)}, bf16[1,2,2,128,128]{4,3,2,1,0:T(8,128)(2,1)S(1)}, u32[]{:S(2)}, u32[]{:S(2)}) %collective-permute-start.5) | collective-permute-done | bytes 131104 | tf_op jit(solution)/shard_map/ppermute | solution.py:396
  64.7 0.0 copy-done
  64.7 2.7 %arrived_blocks.1 = bf16[32,2,16,128]{3,2,1,0:T(8,128)(2,1)} custom-call(bf16[2,512,128]{2,1,0:T(8,128)(2,1)S(1)} %bitcast.23, f32[32,1024]{1,0:T(8,128)S(1)} %get-tuple-element.48.log_ref, f32[4,1024]{1,0:T(4,128)S(1)} %get-tuple-element.49.row_ref, f32[2,512,128]{2,1,0:T(8,128)S(1)} %get-tuple-element.50.acc_ref, ...), custom_call_target="tpu_custom_call" | custom-call | flops 536870912 | bytes 1048576 | tf_op jit(solution)/shard_map/arrived_blocks/pallas_call | solution.py:492
  (6 shorter events, 0.0 us)
Async XLA Ops:
  0.6 8.5 %copy-start.5 = (s32[1,4]{1,0:T(1,128)S(1)}, s32[1,4]{1,0:T(1,128)}, u32[]{:S(2)}) copy-start(s32[1,4]{1,0:T(1,128)} %dest_ref.1) | copy-start | bytes 52
  0.6 8.5 %copy-start.4 = (s32[1,4]{1,0:T(1,128)S(1)}, s32[1,4]{1,0:T(1,128)}, u32[]{:S(2)}) copy-start(s32[1,4]{1,0:T(1,128)} %block_ref.1) | copy-start | bytes 52
  0.7 8.9 %copy-start.6 = (bf16[48,2,2]{0,2,1:T(2,128)(2,1)S(1)}, bf16[48,2,2]{0,2,1:T(2,128)(2,1)}, u32[]{:S(2)}) copy-start(bf16[48,2,2]{0,2,1:T(2,128)(2,1)} %param.13) | copy-start | bytes 1156
  0.7 8.4 %copy-start.3 = (s32[32,16]{0,1:T(8,128)S(1)}, s32[32,16]{0,1:T(8,128)}, u32[]{:S(2)}) copy-start(s32[32,16]{0,1:T(8,128)} %param.14) | copy-start | bytes 6148
  0.7 8.5 %copy-start.7 = (s32[32]{0:T(128)S(1)}, s32[32]{0:T(128)}, u32[]{:S(2)}) copy-start(s32[32]{0:T(128)} %param.15) | copy-start | bytes 388
  0.7 8.6 %copy-start.2 = (bf16[32,2,2,2,128]{4,3,2,1,0:T(2,128)(2,1)S(1)}, bf16[32,2,2,2,128]{4,3,2,1,0:T(2,128)(2,1)}, u32[]{:S(2)}) copy-start(bf16[32,2,2,2,128]{4,3,2,1,0:T(2,128)(2,1)} %param.11) | copy-start | bytes 196612
  0.7 8.7 %copy-start.1 = (bf16[32,2,16,128]{3,2,1,0:T(8,128)(2,1)S(1)}, bf16[32,2,16,128]{3,2,1,0:T(8,128)(2,1)}, u32[]{:S(2)}) copy-start(bf16[32,2,16,128]{3,2,1,0:T(8,128)(2,1)} %param.10) | copy-start | bytes 786436
  3.4 57.7 %collective-permute-start.3 = (bf16[1,2,2,128,128]{4,3,2,1,0:T(8,128)(2,1)}, bf16[1,2,2,128,128]{4,3,2,1,0:T(8,128)(2,1)S(1)}, u32[]{:S(2)}, u32[]{:S(2)}) collective-permute-start(bf16[1,2,2,128,128]{4,3,2,1,0:T(8,128)(2,1)} %get-tuple-element.53), channel_id=1, source_target_pairs={{0,4},{4,8},{8,12},{12,0},{1,5},{5,9},{9,13},{13,1},{2,6},{6,10},{... | collective-permute-start | bytes 393224 | tf_op jit(solution)/shard_map/ppermute | solution.py:396
  6.5 54.6 %collective-permute-start.4 = (bf16[1,2,2,128,128]{4,3,2,1,0:T(8,128)(2,1)}, bf16[1,2,2,128,128]{4,3,2,1,0:T(8,128)(2,1)S(1)}, u32[]{:S(2)}, u32[]{:S(2)}) collective-permute-start(bf16[1,2,2,128,128]{4,3,2,1,0:T(8,128)(2,1)} %get-tuple-element.54), channel_id=1, source_target_pairs={{0,8},{4,12},{8,0},{12,4},{1,9},{5,13},{9,1},{13,5},{2,10},{6,14},... | collective-permute-start | bytes 393224 | tf_op jit(solution)/shard_map/ppermute | solution.py:396
  56.9 7.8 %copy-start = (bf16[1,2,2,128,128]{4,3,2,1,0:T(8,128)(2,1)S(1)}, bf16[1,2,2,128,128]{4,3,2,1,0:T(8,128)(2,1)}, u32[]{:S(2)}) copy-start(bf16[1,2,2,128,128]{4,3,2,1,0:T(8,128)(2,1)} %get-tuple-element.52.rest_0_) | copy-start | bytes 393220
  59.5 5.2 %collective-permute-start.5 = (bf16[1,2,2,128,128]{4,3,2,1,0:T(8,128)(2,1)}, bf16[1,2,2,128,128]{4,3,2,1,0:T(8,128)(2,1)S(1)}, u32[]{:S(2)}, u32[]{:S(2)}) collective-permute-start(bf16[1,2,2,128,128]{4,3,2,1,0:T(8,128)(2,1)} %get-tuple-element.55), channel_id=1, source_target_pairs={{0,12},{4,0},{8,4},{12,8},{1,13},{5,1},{9,5},{13,9},{2,14},{6,2},{... | collective-permute-start | bytes 393224 | tf_op jit(solution)/shard_map/ppermute | solution.py:396

commit v4 on v3

v4 whole, which is shorter than its diff:
```python
import functools
import math

import jax
import jax.numpy as jnp
from jax import lax
from jax.experimental import pallas as pl
from jax.experimental.pallas import tpu as pltpu
from jax.sharding import PartitionSpec as P

CAP = 2
LOG2E = math.log2(math.e)
MIB = 1 << 20
SMEM_SPEC = pl.BlockSpec(memory_space=pltpu.SMEM)
VMEM_SPEC = pl.BlockSpec(memory_space=pltpu.VMEM)
HBM_SPEC = pl.BlockSpec(memory_space=pltpu.HBM)
NT = (((1,), (1,)), ((), ()))


def loop(count, body, init):
    if count <= 8:
        for i in range(count):
            init = body(i, init)
        return init
    return lax.fori_loop(0, count, body, init)


def pack_kernel(instances, listed, copies, dest_ref, block_ref, pool_ref, *refs):
    count = len(refs) - 4
    send_refs, (index_ref, held_ref, in_sems, out_sems) = refs[:count], refs[count:]
    me = lax.axis_index("inst")
    for entry in range(2 * instances + 1):
        index_ref[entry] = 0

    def place(m, carry):
        dest = dest_ref[0, m]
        rank = loop(
            listed,
            lambda m2, n: n + jnp.where((dest_ref[0, m2] == dest) & (m2 < m), 1, 0),
            jnp.int32(0),
        )
        entry = jnp.bitwise_xor(dest, me) + jnp.where(rank > 0, instances, 0)
        index_ref[entry] = block_ref[0, m]
        index_ref[jnp.where(rank > 0, 2 * instances, entry)] = block_ref[0, m]
        return carry

    loop(listed, place, 0)
    loads, stores = [], []
    for i, (entry, _) in enumerate(copies):
        loads.append(
            pltpu.make_async_copy(pool_ref.at[index_ref[entry]], held_ref.at[i], in_sems.at[i])
        )
        loads[-1].start()
    for i, (_, targets) in enumerate(copies):
        loads[i].wait()
        for output, row in targets:
            stores.append(
                pltpu.make_async_copy(
                    held_ref.at[i], send_refs[output].at[row], out_sems.at[len(stores)]
                )
            )
            stores[-1].start()
    for store in stores:
        store.wait()


def count_log(tables, length, ids, block_len, spans, store):
    requests, width = tables.shape[0], ids.shape[1]
    whole = length // block_len
    rest = length - whole * block_len
    full = jnp.zeros((requests, width), jnp.float32)
    part = jnp.zeros((requests, width), jnp.float32)
    for e in range(spans):
        hit = tables[:, e : e + 1] == ids
        full = full + jnp.where(hit & (whole > e), 1.0, 0.0)
        part = part + jnp.where(hit & (whole == e), 1.0, 0.0)
    inside = lax.broadcasted_iota(jnp.int32, (requests, block_len), 1) < rest
    for b in range(width):
        count = jnp.broadcast_to(full[:, b : b + 1], (requests, block_len)) + jnp.where(
            inside, jnp.broadcast_to(part[:, b : b + 1], (requests, block_len)), 0.0
        )
        store(b, jnp.where(count > 0, jnp.log(jnp.maximum(count, 1.0)) * LOG2E, -jnp.inf))


def score_tiles(query, keys, log_ref, scale_row, rows, store):
    height, wide = min(256, query.shape[0]), min(256, keys.shape[0])
    for top in range(0, query.shape[0], height):
        for left in range(0, keys.shape[0], wide):
            part = lax.dot_general(
                query[top : top + height],
                keys[left : left + wide],
                NT,
                preferred_element_type=jnp.float32,
            )
            scale = scale_row[:, left : left + wide]
            for r in range(height // rows):
                request = top // rows + r
                store(
                    request * rows,
                    left,
                    part[r * rows : (r + 1) * rows] * scale
                    + log_ref[request : request + 1, left : left + wide],
                )


def lane_fold(value, op):
    parts = [value[:, i : i + 128] for i in range(0, value.shape[1], 128)]
    while len(parts) > 1:
        parts = [
            op(parts[i], parts[i + 1]) if i + 1 < len(parts) else parts[i]
            for i in range(0, len(parts), 2)
        ]
    return parts[0]


def spread(column, width):
    return jnp.concatenate([column] * (width // 128), axis=1)


def own_kernel(
    dims,
    tables_ref, length_ref, scale_ref, q_ref, fresh_ref, codes_ref,
    acc_ref, top_ref, total_ref,
    log_ref, row_ref, t_ref, new_ref, p_ref,
):
    head, pool, heads, rows, steps, block_len, spans, factor, group = dims
    phase, chunk = pl.program_id(0), pl.program_id(1)
    chunks = pool // group
    height = q_ref.shape[1]
    width = group * block_len

    @pl.when((phase == 0) & (chunk == 0))
    def _():
        ids = lax.broadcasted_iota(jnp.int32, (1, pool), 1)

        def store(b, value):
            lane = (b % group) * block_len
            log_ref[b // group, :, lane : lane + block_len] = value

        count_log(tables_ref[...], length_ref[...], ids, block_len, spans, store)
        for b in range(pool):
            lane = (b % group) * block_len
            for part, unit in ((0, factor * LOG2E), (1, 1.0)):
                row_ref[b // group, part : part + 1, lane : lane + block_len] = jnp.full(
                    (1, block_len), scale_ref[0, (part * heads + head) * pool + b] * unit
                )
        shape = (height, fresh_ref.shape[2])
        row = lax.broadcasted_iota(jnp.int32, shape, 0)
        col = lax.broadcasted_iota(jnp.int32, shape, 1)
        seen = (col // steps == row // rows) & (col % steps <= row % steps)
        score = lax.dot_general(
            q_ref[0], fresh_ref[0, 0], NT, preferred_element_type=jnp.float32
        )
        score = jnp.where(seen, score * (factor * LOG2E), -jnp.inf)
        new_ref[...] = score
        top_ref[...] = lane_fold(score, jnp.maximum)

    @pl.when(phase == 0)
    def _():
        def store(row, lane, value):
            t_ref[chunk, row : row + rows, lane : lane + value.shape[1]] = value

        score_tiles(
            q_ref[0],
            codes_ref[:, 0, 0].reshape(width, codes_ref.shape[-1]),
            log_ref.at[chunk],
            row_ref[chunk, 0:1, :],
            rows,
            store,
        )
        for row in range(0, height, rows):
            at = pl.ds(row, rows)
            top_ref[at] = jnp.maximum(top_ref[at], lane_fold(t_ref[chunk, at], jnp.maximum))

    @pl.when((phase == 1) & (chunk == 0))
    def _():
        top = jnp.broadcast_to(jnp.max(top_ref[...], axis=1, keepdims=True), (height, 128))
        top_ref[...] = top
        weight = jnp.exp2(new_ref[...] - spread(top, new_ref.shape[1]))
        total_ref[...] = lane_fold(weight, jnp.add)
        acc_ref[...] = jnp.dot(
            weight.astype(jnp.bfloat16), fresh_ref[1, 0], preferred_element_type=jnp.float32
        )

    @pl.when(phase == 1)
    def _():
        scale = row_ref[chunk, 1:2, :]
        for row in range(0, height, rows):
            at = pl.ds(row, rows)
            weight = jnp.exp2(t_ref[chunk, at] - spread(top_ref[at], width))
            total_ref[at] += lane_fold(weight, jnp.add)
            p_ref[at] = (weight * scale).astype(jnp.bfloat16)
        acc_ref[...] += jnp.dot(
            p_ref[...],
            codes_ref[:, 0, 0].reshape(width, codes_ref.shape[-1]),
            preferred_element_type=jnp.float32,
        )

    @pl.when((phase == 1) & (chunk == chunks - 1))
    def _():
        total_ref[...] = jnp.broadcast_to(
            jnp.sum(total_ref[...], axis=1, keepdims=True), (height, 128)
        )


def route_kernel(
    dims, lists_ref, tables_ref, length_ref, own_ref, moved_ref, more_ref, log_ref, row_ref
):
    pool, heads, instances, everyone, listed, block_len, spans, factor = dims
    me = lax.axis_index("inst")

    def dest(row, m):
        return lists_ref[row, m].astype(jnp.int32)

    def count(row, target):
        return loop(
            listed, lambda m, n: n + jnp.where(dest(row, m) == target, 1, 0), jnp.int32(0)
        )

    def rank(row, m):
        target = dest(row, m)
        return loop(
            listed,
            lambda m2, n: n + jnp.where((dest(row, m2) == target) & (m2 < m), 1, 0),
            jnp.int32(0),
        )

    def before(source, target):
        return loop(
            instances,
            lambda k, n: n + jnp.where(jnp.bitwise_xor(me, k) < source, count(k, target), 0),
            jnp.int32(pool),
        )

    def move(m, carry):
        moved_ref[0, m] = before(me, dest(0, m)) + rank(0, m)
        return carry

    loop(listed, move, 0)

    def seconds(row, more):
        found = loop(listed, lambda m, n: n + jnp.minimum(rank(row, m), 1), jnp.int32(0))
        return jnp.maximum(more, jnp.where(found > 1, 1, 0))

    more_ref[0] = loop(everyone, seconds, jnp.int32(0))
    slots = instances * CAP
    lane = lax.broadcasted_iota(jnp.int32, (1, slots), 1)

    def place(k, ids):
        first = before(jnp.bitwise_xor(me, k), me)

        def find(m, carry):
            seen, blocks = carry
            hit = dest(k, m) == me
            block = lists_ref[k, listed + m].astype(jnp.int32)
            blocks = [jnp.where(hit & (seen == r), block, blocks[r]) for r in range(CAP)]
            return seen + jnp.where(hit, 1, 0), blocks

        seen, blocks = loop(listed, find, (jnp.int32(0), [jnp.int32(0)] * CAP))
        for r in range(CAP):
            slot = r * instances + k
            ids = jnp.where(lane == slot, jnp.where(r < seen, first + r, -1), ids)
            at = pl.ds(pl.multiple_of(slot * block_len, block_len), block_len)
            for h in range(heads):
                key = lists_ref[k, 2 * listed + h * pool + blocks[r]]
                value = lists_ref[k, 2 * listed + (heads + h) * pool + blocks[r]]
                row_ref[h : h + 1, at] = jnp.full((1, block_len), key * (factor * LOG2E))
                row_ref[heads + h : heads + h + 1, at] = jnp.full((1, block_len), value)
        return ids

    ids = loop(instances, place, jnp.full((1, slots), -1, jnp.int32))

    def store(b, value):
        log_ref[:, b * block_len : (b + 1) * block_len] = value

    count_log(tables_ref[...], length_ref[...], ids, block_len, spans, store)


def arrival_kernel(dims, places, q_ref, log_ref, row_ref, *refs):
    heads, rows, block_len = dims
    own_refs, refs = refs[: 3 * heads], refs[3 * heads :]
    code_refs, (out_ref, t_ref, p_ref) = refs[:-3], refs[-3:]
    height = q_ref.shape[1]
    width = 2 * block_len
    slots = [code_refs[array].at[row] for array, row in places]
    pairs = len(slots) // 2

    def pair(i, part, h):
        return jnp.concatenate([slots[2 * i][part, h], slots[2 * i + 1][part, h]], axis=0)

    for h in range(heads):
        for i in range(pairs):
            left = i * width

            def store(row, lane, value, h=h, left=left):
                t_ref[h, row : row + rows, left + lane : left + lane + value.shape[1]] = value

            score_tiles(
                q_ref[h],
                pair(i, 0, h),
                log_ref.at[:, left : left + width],
                row_ref[h : h + 1, left : left + width],
                rows,
                store,
            )
    for h in range(heads):
        acc_ref, top_ref, total_ref = own_refs[3 * h : 3 * h + 3]
        scale = row_ref[heads + h : heads + h + 1, :]
        for row in range(0, height, rows):
            at = pl.ds(row, rows)
            score = t_ref[h, at]
            own_top = top_ref[at]
            top = jnp.maximum(
                own_top, jnp.max(lane_fold(score, jnp.maximum), axis=1, keepdims=True)
            )
            weight = jnp.exp2(score - spread(top, score.shape[1]))
            keep = jnp.exp2(own_top - top)
            total = total_ref[at] * keep + jnp.sum(
                lane_fold(weight, jnp.add), axis=1, keepdims=True
            )
            p_ref[h, at] = (weight * scale).astype(jnp.bfloat16)
            t_ref[h, at, 0:128] = keep
            t_ref[h, at, 128:256] = 1.0 / total
        mixed = acc_ref[...] * t_ref[h, :, 0:128]
        for i in range(pairs):
            mixed = mixed + jnp.dot(
                p_ref[h, :, i * width : (i + 1) * width],
                pair(i, 1, h),
                preferred_element_type=jnp.float32,
            )
        result = (mixed * t_ref[h, :, 128:256]).astype(jnp.bfloat16)
        out_ref[:, h] = result.reshape(height // rows, rows, result.shape[-1])


def doubling(bits, value, axis):
    for bit in bits:
        size = lax.axis_size(axis)
        moved = lax.ppermute(value, axis, [(j, j ^ bit) for j in range(size)])
        value = jnp.concatenate([value, moved], axis=0)
    return value


def attend(
    general, queries, new_kv, pool_codes, pool_scales, tables, ctx_len, mig_block, mig_dest
):
    instances, groups = lax.axis_size("inst"), lax.axis_size("groups")
    pool = pool_codes.shape[0]
    requests, steps, q_heads, head_dim = queries.shape
    heads = new_kv.shape[3]
    per_head = q_heads // heads
    spans = tables.shape[1]
    block_len = pool_codes.shape[3]
    listed = mig_dest.shape[1]
    factor = head_dim ** (-0.5)
    rows = per_head * steps
    height = requests * rows
    slots = instances * CAP
    group = 8
    f32, bf16 = jnp.float32, jnp.bfloat16
    block_shape = pool_codes.shape[1:]
    block_bytes = 2 * math.prod(block_shape)
    inst_bits = [1 << i for i in range(instances.bit_length() - 1)]
    group_bits = [1 << i for i in range(groups.bit_length() - 1)]
    assert instances == 1 << len(inst_bits) and groups == 1 << len(group_bits)

    if general:
        sizes = [CAP] * instances
        copies = [(r * instances + k, [(k, r)]) for k in range(instances) for r in range(CAP)]
    else:
        sizes = [1, 2] + [1] * (instances - 1)
        copies = [(2 * instances, [(instances, 0), (1, 1)])]
        copies += [(k, [(k, 0)]) for k in list(range(instances))[::-1]]
    stores = sum(len(targets) for _, targets in copies)
    send = pl.pallas_call(
        functools.partial(pack_kernel, instances, listed, copies),
        out_shape=[jax.ShapeDtypeStruct((size,) + block_shape, bf16) for size in sizes],
        in_specs=[SMEM_SPEC, SMEM_SPEC, HBM_SPEC],
        out_specs=[HBM_SPEC] * len(sizes),
        scratch_shapes=[
            pltpu.SMEM((2 * instances + 1,), jnp.int32),
            pltpu.VMEM((len(copies),) + block_shape, bf16),
            pltpu.SemaphoreType.DMA((len(copies),)),
            pltpu.SemaphoreType.DMA((stores,)),
        ],
        compiler_params=pltpu.CompilerParams(vmem_limit_bytes=56 * MIB),
        cost_estimate=pl.CostEstimate(
            flops=0, bytes_accessed=2 * stores * block_bytes, transcendentals=0
        ),
        name="pack_blocks",
    )(mig_dest, mig_block, pool_codes)
    mig_dest, mig_block, pool_scales, *send = lax.optimization_barrier(
        (mig_dest, mig_block, pool_scales, *send)
    )

    def swap(value, distance):
        return lax.ppermute(value, "inst", [(j, j ^ distance) for j in range(instances)])

    if general:
        arrived = [send[0]] + [swap(send[k], k) for k in range(1, instances)]
        places = [(k, r) for r in range(CAP) for k in range(instances)]
    else:
        second = send.pop()
        seconds = {0: second}
        for bit in inst_bits[:0:-1]:
            for k in list(seconds):
                seconds[k ^ bit] = swap(seconds[k], bit)
        arrived = [send[0]] + [swap(send[k], k) for k in range(1, instances)]
        for k in list(seconds):
            if k:
                seconds[k ^ 1] = swap(seconds[k], 1)
        places = [(k, 0) for k in range(instances)]
        for k in range(instances):
            if k == 1:
                places.append((1, 1))
            else:
                places.append((len(arrived), 0))
                arrived.append(seconds[k])

    flat_scales = jnp.transpose(pool_scales, (1, 2, 0)).reshape(1, -1).astype(f32)
    lists = jnp.concatenate([mig_dest.astype(f32), mig_block.astype(f32), flat_scales], axis=1)
    lists_in = doubling(group_bits, doubling(inst_bits, lists, "inst"), "groups")

    query_rows = (
        queries.reshape(requests, steps, heads, per_head, head_dim)
        .transpose(2, 0, 3, 1, 4)
        .reshape(heads, height, head_dim)
    )
    fresh_len = requests * steps
    fresh = new_kv.transpose(2, 3, 0, 1, 4).reshape(2, heads, fresh_len, head_dim)
    fresh = jnp.pad(fresh, ((0, 0), (0, 0), (0, -fresh_len % 128), (0, 0)))
    fresh_len = fresh.shape[2]
    length = ctx_len[:, None]
    width = group * block_len
    chunks = pool // group
    tokens = pool * block_len

    def whole(shape):
        return pl.BlockSpec(shape, lambda p, c: (0,) * len(shape))

    def own(head):
        return pl.pallas_call(
            functools.partial(
                own_kernel, (head, pool, heads, rows, steps, block_len, spans, factor, group)
            ),
            grid=(2, chunks),
            out_shape=[jax.ShapeDtypeStruct((height, head_dim), f32)] * 3,
            in_specs=[
                whole(tables.shape),
                whole(length.shape),
                SMEM_SPEC,
                pl.BlockSpec((1, height, head_dim), lambda p, c: (head, 0, 0)),
                pl.BlockSpec((2, 1, fresh_len, head_dim), lambda p, c: (0, head, 0, 0)),
                pl.BlockSpec(
                    (group, 1, 1, block_len, head_dim), lambda p, c: (c, p, head, 0, 0)
                ),
            ],
            out_specs=[whole((height, head_dim))] * 3,
            scratch_shapes=[
                pltpu.VMEM((chunks, requests, width), f32),
                pltpu.VMEM((chunks, 2, width), f32),
                pltpu.VMEM((chunks, height, width), f32),
                pltpu.VMEM((height, fresh_len), f32),
                pltpu.VMEM((height, width), bf16),
            ],
            compiler_params=pltpu.CompilerParams(vmem_limit_bytes=32 * MIB),
            cost_estimate=pl.CostEstimate(
                flops=4 * height * tokens * head_dim,
                bytes_accessed=pool_codes.size * 2 // heads,
                transcendentals=height * tokens,
            ),
            name="own_blocks",
        )(tables, length, flat_scales, query_rows, fresh, pool_codes)

    own_parts = [value for head in range(heads) for value in own(head)]

    moved_to, more, log_in, rows_in = pl.pallas_call(
        functools.partial(
            route_kernel,
            (pool, heads, instances, groups * instances, listed, block_len, spans, factor),
        ),
        out_shape=[
            jax.ShapeDtypeStruct((1, listed), jnp.int32),
            jax.ShapeDtypeStruct((1,), jnp.int32),
            jax.ShapeDtypeStruct((requests, slots * block_len), f32),
            jax.ShapeDtypeStruct((2 * heads, slots * block_len), f32),
        ],
        in_specs=[SMEM_SPEC, VMEM_SPEC, VMEM_SPEC, HBM_SPEC],
        out_specs=[SMEM_SPEC, SMEM_SPEC, VMEM_SPEC, VMEM_SPEC],
        compiler_params=pltpu.CompilerParams(vmem_limit_bytes=8 * MIB),
        name="route_arrivals",
    )(lists_in, tables, length, own_parts[-1])

    arrival_bytes = 6 * heads * height * slots * block_len + 2 * 12 * height * head_dim * heads
    arrival_bytes += 2 * slots * block_bytes
    out = pl.pallas_call(
        functools.partial(arrival_kernel, (heads, rows, block_len), places),
        out_shape=jax.ShapeDtypeStruct((requests, heads, rows, head_dim), bf16),
        in_specs=[VMEM_SPEC] * (3 + 3 * heads + len(arrived)),
        out_specs=VMEM_SPEC,
        scratch_shapes=[
            pltpu.VMEM((heads, height, slots * block_len), f32),
            pltpu.VMEM((heads, height, slots * block_len), bf16),
        ],
        compiler_params=pltpu.CompilerParams(vmem_limit_bytes=arrival_bytes + 8 * MIB),
        cost_estimate=pl.CostEstimate(
            flops=4 * heads * height * slots * block_len * head_dim,
            bytes_accessed=slots * block_bytes,
            transcendentals=heads * height * slots * block_len,
        ),
        name="arrived_blocks",
    )(query_rows, log_in, rows_in, *own_parts, *arrived)
    out = (
        out.reshape(requests, q_heads, steps, head_dim)
        .transpose(0, 2, 1, 3)
        .reshape(requests, steps, q_heads * head_dim)
    )
    return out, moved_to, more


def shards(*args):
    out, moved_to, more = attend(False, *args)
    out = lax.cond(
        more[0] > 0,
        lambda out, *args: attend(True, *args)[0],
        lambda out, *args: out,
        out, *args,
    )
    return out, moved_to


def solution(mesh):
    in_specs = (
        P(("groups", "inst"), None, "tp", None),
        P(("groups", "inst"), None, None, "tp", None),
        P(("groups", "inst"), None, "tp", None, None),
        P(("groups", "inst"), None, "tp"),
        P(("groups", "inst"), None),
        P(("groups", "inst")),
        P(("groups", "inst"), None),
        P(("groups", "inst"), None),
    )
    out_specs = (P(("groups", "inst"), None, "tp"), P(("groups", "inst"), None))
    return jax.shard_map(shards, mesh=mesh, in_specs=in_specs, out_specs=out_specs, check_vma=False)
```

time: 67.8 us -> 45.5 us (0.67)
  blocking collectives: 33.5 us -> 0 us
  Pallas kernels: 21 us -> 28.5 us
  starting transfers between devices: 7.27 us -> 11.6 us
  waiting for transfers between devices: 3.63 us -> 1.47 us
  local copies, waits for them, and re-layouts: 0.55 us -> 1.36 us
    all_gather x2 -> x0, blocking collectives: 33.5 us -> none  [the longest x1 18.6 us: shards(): lists_in = lax.all_gather(lists, ('groups', 'inst'), axis=0, tiled=True)]
    pallas_call x4 -> x5, Pallas kernels: 21 us -> 28.5 us  [the longest x2 21.9 us: own(): pl.pallas_call(functools.partial(own_kernel, (head, pool, heads, rows, st...]
    ppermute x3 -> x8, starting transfers between devices: 7.27 us -> 11.6 us  [the longest x5 6.98 us: swap(): lax.ppermute(value, 'inst', [(j, j ^ distance) for j in range(instances)])]
    ppermute x3 -> x8, waiting for transfers between devices: 3.63 us -> 1.47 us  [the longest x3 1.46 us: doubling(): moved = lax.ppermute(value, axis, [(j, j ^ bit) for j in range(size)])]
    unnamed x18 -> x21, local copies, waits for them, and re-layouts: 0.11 us -> 0.81 us
  transfers between devices with their start and end apart: 3 -> 8, of which waited for: 1 -> 1; matrix products, arithmetic and copies ran while one was open for 1% -> 1% of each run, Pallas kernels for 23% -> 53%
where the time goes in v4:
time: 45.5 us; the launch traced here: 45 us
  Pallas kernels  28.5 us (63%)
  starting transfers between devices  11.6 us (25%)
  between operations  1.55 us (3%)
  waiting for transfers between devices  1.47 us (3%)
  local copies, waits for them, and re-layouts  1.36 us (3%)
    pallas_call x2, Pallas kernels, own(): pl.pallas_call(functools.partial(own_kernel, (head, pool, heads, rows, st...  21.9 us
    ppermute x5, starting transfers between devices, swap(): lax.ppermute(value, 'inst', [(j, j ^ distance) for j in range(instances)])  6.98 us
    ppermute x3, starting transfers between devices, doubling(): moved = lax.ppermute(value, axis, [(j, j ^ bit) for j in range(size)])  4.61 us
    pallas_call x1, Pallas kernels, attend(): pl.pallas_call(functools.partial(pack_kernel, instances, listed, copies),...  2.74 us
    pallas_call x1, Pallas kernels, attend(): pl.pallas_call(functools.partial(arrival_kernel, (heads, rows, block_len)...  2.06 us
    pallas_call x1, Pallas kernels, attend(): pl.pallas_call(functools.partial(route_kernel, (pool, heads, instances, g...  1.79 us
    ppermute x3, waiting for transfers between devices, doubling(): moved = lax.ppermute(value, axis, [(j, j ^ bit) for j in range(size)])  1.46 us
  transfers between devices with their start and end apart: 8, of which 1 were waited for; matrix products, arithmetic and copies ran while one was open for 1% of the time, Pallas kernels for 53%

profile of v4, /device:TPU:0, one launch (start us, length us, event | category | flops | bytes accessed | tf_op | source)
XLA Modules:
  0.0 45.0 jit_solution(7628345612356611028)
XLA Ops:
  0.6 0.0 copy-start.10
  0.6 0.0 copy-start.9
  0.7 0.0 copy-start.7
  0.7 0.0 copy-start.8
  0.7 0.0 copy-start.6
  0.7 0.0 copy-start.5
  0.7 0.0 copy-start.3
  0.7 2.7 %pack_blocks.3 = (bf16[1,2,2,128,128]{4,3,2,1,0:T(8,128)(2,1)}, bf16[2,2,2,128,128]{4,3,2,1,0:T(8,128)(2,1)}, bf16[1,2,2,128,128]{4,3,2,1,0:T(8,128)(2,1)}, bf16...) custom-call(s32[1,4]{1,0:T(1,128)} %dest_ref.1, s32[1,4]{1,0:T(1,128)} %block_ref.1, ...), custom_call_target="tpu_custom_call" | custom-call | bytes 1572864 | tf_op jit(solution)/shard_map/pack_blocks/pallas_call | solution.py:374
  3.4 0.0 copy-done.10
  3.5 0.0 copy-done.9
  3.5 0.0 copy-done.7
  3.5 0.1 reshape.81.scale_ref
  3.6 0.1 pad_maximum_fusion.7
  3.7 3.0 %collective-permute-start.6 = (f32[1,200]{1,0:T(1,128)S(1)}, f32[1,200]{1,0:T(1,128)S(1)}, u32[]{:S(2)}, u32[]{:S(2)}) collective-permute-start(f32[1,200]{1,0:T(1,128)S(1)} %pad_maximum_fusion.7), channel_id=1, source_target_pairs={{0,4},{4,0},{8,12},{12,8},{1,5},{5,1},{9,13},{13,9},{2,6},{6,2},{1... | collective-permute-start | bytes 2408 | tf_op jit(solution)/shard_map/ppermute | solution.py:338
  6.7 2.6 %collective-permute-start.10 = (bf16[1,2,2,128,128]{4,3,2,1,0:T(8,128)(2,1)}, bf16[1,2,2,128,128]{4,3,2,1,0:T(8,128)(2,1)S(1)}, u32[]{:S(2)}, u32[]{:S(2)}) collective-permute-start(bf16[1,2,2,128,128]{4,3,2,1,0:T(8,128)(2,1)} %get-tuple-element.97), channel_id=1, source_target_pairs={{0,8},{4,12},{8,0},{12,4},{1,9},{5,13},{9,1},{13,5},{2,10},{6,14},... | collective-permute-start | bytes 393224 | tf_op jit(solution)/shard_map/ppermute | solution.py:396
  9.3 0.0 collective-permute-start.11
  9.3 1.9 %collective-permute-start.12 = (bf16[1,2,2,128,128]{4,3,2,1,0:T(8,128)(2,1)}, bf16[1,2,2,128,128]{4,3,2,1,0:T(8,128)(2,1)S(1)}, u32[]{:S(2)}, u32[]{:S(2)}) collective-permute-start(bf16[1,2,2,128,128]{4,3,2,1,0:T(8,128)(2,1)} %get-tuple-element.99.refs_10_), channel_id=1, source_target_pairs={{0,8},{4,12},{8,0},{12,4},{1,9},{5,13},{9,1},{13,5},{2,10},{6,14},... | collective-permute-start | bytes 393224 | tf_op jit(solution)/shard_map/ppermute | solution.py:396
  11.2 2.5 %collective-permute-start.9 = (bf16[2,2,2,128,128]{4,3,2,1,0:T(8,128)(2,1)}, bf16[2,2,2,128,128]{4,3,2,1,0:T(8,128)(2,1)S(1)}, u32[]{:S(2)}, u32[]{:S(2)}) collective-permute-start(bf16[2,2,2,128,128]{4,3,2,1,0:T(8,128)(2,1)} %get-tuple-element.96), channel_id=1, source_target_pairs={{0,4},{4,0},{8,12},{12,8},{1,5},{5,1},{9,13},{13,9},{2,6},{6,2},{1... | collective-permute-start | bytes 786440 | tf_op jit(solution)/shard_map/ppermute | solution.py:396
  13.7 0.0 copy-done.8
  13.7 0.1 copy.19.length_ref
  13.8 0.0 copy-done.6
  13.8 0.1 copy.18.tables_ref
  13.8 0.0 copy-done.5
  13.8 0.1 copy.15
  13.9 0.0 copy-done.3
  13.9 0.2 copy.14
  14.2 0.0 collective-permute-done.6
  14.2 0.1 pad_maximum_fusion.6
  14.2 0.0 collective-permute-start.7
  14.3 0.0 copy-start.1
  14.3 0.0 copy-start.2
  14.3 11.0 %own_blocks.7 = (f32[512,128]{1,0:T(8,128)S(1)}, f32[512,128]{1,0:T(8,128)S(1)}, f32[512,128]{1,0:T(8,128)S(1)}) custom-call(s32[32,16]{1,0:T(8,128)S(1)} %copy.18.tables_ref, s32[32,1]{1,0:T(8,128)S(1)} %copy.19.length_ref, f32[1,192]{1,0:T(1,128)S(1)} %reshape.81.scale_ref, bf16[2,512,128]{2,1,0:T(8,128)(2,1)S(1)} %bitcast.31, ...), custom_call_target="tpu_custom_call" | custom-call | flops 1610612736 | bytes 3145728 | tf_op jit(solution)/shard_map/own_blocks/pallas_call | solution.py:441
  25.3 1.5 %collective-permute-done.7 = f32[2,200]{1,0:T(2,128)S(1)} collective-permute-done((f32[2,200]{1,0:T(2,128)S(1)}, f32[2,200]{1,0:T(2,128)S(1)}, u32[]{:S(2)}, u32[]{:S(2)}) %collective-permute-start.7) | collective-permute-done | bytes 1632 | tf_op jit(solution)/shard_map/ppermute | solution.py:338
  26.7 0.1 pad_maximum_fusion.5
  26.8 1.6 %collective-permute-start.8 = (f32[4,200]{1,0:T(4,128)S(1)}, f32[4,200]{1,0:T(4,128)S(1)}, u32[]{:S(2)}, u32[]{:S(2)}) collective-permute-start(f32[4,200]{1,0:T(4,128)S(1)} %pad_maximum_fusion.5), channel_id=1, source_target_pairs={{0,16},{16,0},{1,17},{17,1},{2,18},{18,2},{3,19},{19,3},{4,20},{20... | collective-permute-start | bytes 9608 | tf_op jit(solution)/shard_map/ppermute | solution.py:338
  28.4 0.0 collective-permute-done.12.refs_11_
  28.4 0.0 collective-permute-start.13
  28.4 10.9 %own_blocks.6 = (f32[512,128]{1,0:T(8,128)S(1)}, f32[512,128]{1,0:T(8,128)S(1)}, f32[512,128]{1,0:T(8,128)S(1)}) custom-call(s32[32,16]{1,0:T(8,128)S(1)} %copy.18.tables_ref, s32[32,1]{1,0:T(8,128)S(1)} %copy.19.length_ref, f32[1,192]{1,0:T(1,128)S(1)} %reshape.81.scale_ref, bf16[2,512,128]{2,1,0:T(8,128)(2,1)S(1)} %bitcast.32, ...), custom_call_target="tpu_custom_call" | custom-call | flops 1610612736 | bytes 3145728 | tf_op jit(solution)/shard_map/own_blocks/pallas_call | solution.py:441
  39.3 0.0 collective-permute-done.8
  39.3 0.1 pad_maximum_fusion.4.lists_ref
  39.4 1.8 %route_arrivals.3 = (s32[1,4]{1,0:T(1,128)}, s32[1]{0:T(128)}, f32[32,1024]{1,0:T(8,128)S(1)}, f32[4,1024]{1,0:T(4,128)S(1)}) custom-call(f32[8,200]{1,0:T(8,128)S(1)} %pad_maximum_fusion.4.lists_ref, s32[32,16]{1,0:T(8,128)S(1)} %copy.18.tables_ref, s32[32,1]{1,0:T(8,128)S(1)} %copy.19.length_ref, f32[512,128]{1,0:T(8,128)S(1)} %get-tuple-element.86.own_ref.refs_5_), custom_call_target="tpu_custom_call" | custom-call | tf_op jit(solution)/shard_map/route_arrivals/pallas_call | solution.py:476
  41.8 0.0 collective-permute-done.10.refs_8_
  41.8 0.0 collective-permute-done.11.refs_9_
  41.8 0.0 collective-permute-done.13.refs_12_
  41.9 0.0 collective-permute-done.9.refs_7_
  41.9 0.0 copy-done.1
  41.9 0.0 copy-done.2
  41.9 2.1 %arrived_blocks.3 = bf16[32,2,16,128]{3,2,1,0:T(8,128)(2,1)S(1)} custom-call(bf16[2,512,128]{2,1,0:T(8,128)(2,1)S(1)} %bitcast.33, f32[32,1024]{1,0:T(8,128)S(1)} %get-tuple-element.88.log_ref, f32[4,1024]{1,0:T(4,128)S(1)} %get-tuple-element.89.row_ref, f32[512,128]{1,0:T(8,128)S(1)} %get-tuple-element.90.refs_0_, ...), custom_call_target="tpu_custom_call" | custom-call | flops 536870912 | bytes 1048576 | tf_op jit(solution)/shard_map/arrived_blocks/pallas_call | solution.py:495
  44.0 0.3 conditional.1
  44.0 0.1 reshape.78
  44.3 0.0 copy-start.4
  44.3 0.7 %copy-done.4 = bf16[32,2,2048]{2,1,0:T(2,128)(2,1)} copy-done((bf16[32,2,2048]{2,1,0:T(2,128)(2,1)}, bf16[32,2,2048]{2,1,0:T(2,128)(2,1)S(1)}, u32[]{:S(2)}) %copy-start.4) | copy-done | bytes 262168
  (5 shorter events, 0.1 us)
Async XLA Ops:
  0.6 2.8 %copy-start.10 = (s32[1,4]{1,0:T(1,128)S(1)}, s32[1,4]{1,0:T(1,128)}, u32[]{:S(2)}) copy-start(s32[1,4]{1,0:T(1,128)} %dest_ref.1) | copy-start | bytes 52
  0.6 2.8 %copy-start.9 = (s32[1,4]{1,0:T(1,128)S(1)}, s32[1,4]{1,0:T(1,128)}, u32[]{:S(2)}) copy-start(s32[1,4]{1,0:T(1,128)} %block_ref.1) | copy-start | bytes 52
  0.7 2.8 %copy-start.7 = (bf16[48,2,2]{0,2,1:T(2,128)(2,1)S(1)}, bf16[48,2,2]{0,2,1:T(2,128)(2,1)}, u32[]{:S(2)}) copy-start(bf16[48,2,2]{0,2,1:T(2,128)(2,1)} %param.13) | copy-start | bytes 1156
  0.7 13.0 %copy-start.8 = (s32[32]{0:T(128)S(1)}, s32[32]{0:T(128)}, u32[]{:S(2)}) copy-start(s32[32]{0:T(128)} %param.15) | copy-start | bytes 388
  0.7 13.1 %copy-start.6 = (s32[32,16]{0,1:T(8,128)S(1)}, s32[32,16]{0,1:T(8,128)}, u32[]{:S(2)}) copy-start(s32[32,16]{0,1:T(8,128)} %param.14) | copy-start | bytes 6148
  0.7 13.2 %copy-start.5 = (bf16[32,2,2,2,128]{4,3,2,1,0:T(2,128)(2,1)S(1)}, bf16[32,2,2,2,128]{4,3,2,1,0:T(2,128)(2,1)}, u32[]{:S(2)}) copy-start(bf16[32,2,2,2,128]{4,3,2,1,0:T(2,128)(2,1)} %param.11) | copy-start | bytes 196612
  0.7 13.2 %copy-start.3 = (bf16[32,2,16,128]{3,2,1,0:T(8,128)(2,1)S(1)}, bf16[32,2,16,128]{3,2,1,0:T(8,128)(2,1)}, u32[]{:S(2)}) copy-start(bf16[32,2,16,128]{3,2,1,0:T(8,128)(2,1)} %param.10) | copy-start | bytes 786436
  3.7 10.5 %collective-permute-start.6 = (f32[1,200]{1,0:T(1,128)S(1)}, f32[1,200]{1,0:T(1,128)S(1)}, u32[]{:S(2)}, u32[]{:S(2)}) collective-permute-start(f32[1,200]{1,0:T(1,128)S(1)} %pad_maximum_fusion.7), channel_id=1, source_target_pairs={{0,4},{4,0},{8,12},{12,8},{1,5},{5,1},{9,13},{13,9},{2,6},{6,2},{1... | collective-permute-start | bytes 2408 | tf_op jit(solution)/shard_map/ppermute | solution.py:338
  6.7 35.1 %collective-permute-start.10 = (bf16[1,2,2,128,128]{4,3,2,1,0:T(8,128)(2,1)}, bf16[1,2,2,128,128]{4,3,2,1,0:T(8,128)(2,1)S(1)}, u32[]{:S(2)}, u32[]{:S(2)}) collective-permute-start(bf16[1,2,2,128,128]{4,3,2,1,0:T(8,128)(2,1)} %get-tuple-element.97), channel_id=1, source_target_pairs={{0,8},{4,12},{8,0},{12,4},{1,9},{5,13},{9,1},{13,5},{2,10},{6,14},... | collective-permute-start | bytes 393224 | tf_op jit(solution)/shard_map/ppermute | solution.py:396
  9.3 32.5 %collective-permute-start.11 = (bf16[1,2,2,128,128]{4,3,2,1,0:T(8,128)(2,1)}, bf16[1,2,2,128,128]{4,3,2,1,0:T(8,128)(2,1)S(1)}, u32[]{:S(2)}, u32[]{:S(2)}) collective-permute-start(bf16[1,2,2,128,128]{4,3,2,1,0:T(8,128)(2,1)} %get-tuple-element.98), channel_id=1, source_target_pairs={{0,12},{4,8},{8,4},{12,0},{1,13},{5,9},{9,5},{13,1},{2,14},{6,10},... | collective-permute-start | bytes 393224 | tf_op jit(solution)/shard_map/ppermute | solution.py:396
  9.3 19.1 %collective-permute-start.12 = (bf16[1,2,2,128,128]{4,3,2,1,0:T(8,128)(2,1)}, bf16[1,2,2,128,128]{4,3,2,1,0:T(8,128)(2,1)S(1)}, u32[]{:S(2)}, u32[]{:S(2)}) collective-permute-start(bf16[1,2,2,128,128]{4,3,2,1,0:T(8,128)(2,1)} %get-tuple-element.99.refs_10_), channel_id=1, source_target_pairs={{0,8},{4,12},{8,0},{12,4},{1,9},{5,13},{9,1},{13,5},{2,10},{6,14},... | collective-permute-start | bytes 393224 | tf_op jit(solution)/shard_map/ppermute | solution.py:396
  11.2 30.7 %collective-permute-start.9 = (bf16[2,2,2,128,128]{4,3,2,1,0:T(8,128)(2,1)}, bf16[2,2,2,128,128]{4,3,2,1,0:T(8,128)(2,1)S(1)}, u32[]{:S(2)}, u32[]{:S(2)}) collective-permute-start(bf16[2,2,2,128,128]{4,3,2,1,0:T(8,128)(2,1)} %get-tuple-element.96), channel_id=1, source_target_pairs={{0,4},{4,0},{8,12},{12,8},{1,5},{5,1},{9,13},{13,9},{2,6},{6,2},{1... | collective-permute-start | bytes 786440 | tf_op jit(solution)/shard_map/ppermute | solution.py:396
  14.2 12.5 %collective-permute-start.7 = (f32[2,200]{1,0:T(2,128)S(1)}, f32[2,200]{1,0:T(2,128)S(1)}, u32[]{:S(2)}, u32[]{:S(2)}) collective-permute-start(f32[2,200]{1,0:T(2,128)S(1)} %pad_maximum_fusion.6), channel_id=1, source_target_pairs={{0,8},{4,12},{8,0},{12,4},{1,9},{5,13},{9,1},{13,5},{2,10},{6,14},... | collective-permute-start | bytes 4808 | tf_op jit(solution)/shard_map/ppermute | solution.py:338
  14.3 27.6 %copy-start.1 = (bf16[1,2,2,128,128]{4,3,2,1,0:T(8,128)(2,1)S(1)}, bf16[1,2,2,128,128]{4,3,2,1,0:T(8,128)(2,1)}, u32[]{:S(2)}) copy-start(bf16[1,2,2,128,128]{4,3,2,1,0:T(8,128)(2,1)} %get-tuple-element.95.refs_6_) | copy-start | bytes 393220
  14.3 27.6 %copy-start.2 = (bf16[1,2,2,128,128]{4,3,2,1,0:T(8,128)(2,1)S(1)}, bf16[1,2,2,128,128]{4,3,2,1,0:T(8,128)(2,1)}, u32[]{:S(2)}) copy-start(bf16[1,2,2,128,128]{4,3,2,1,0:T(8,128)(2,1)} %get-tuple-element.99.refs_10_) | copy-start | bytes 393220
  26.8 12.5 %collective-permute-start.8 = (f32[4,200]{1,0:T(4,128)S(1)}, f32[4,200]{1,0:T(4,128)S(1)}, u32[]{:S(2)}, u32[]{:S(2)}) collective-permute-start(f32[4,200]{1,0:T(4,128)S(1)} %pad_maximum_fusion.5), channel_id=1, source_target_pairs={{0,16},{16,0},{1,17},{17,1},{2,18},{18,2},{3,19},{19,3},{4,20},{20... | collective-permute-start | bytes 9608 | tf_op jit(solution)/shard_map/ppermute | solution.py:338
  28.4 13.5 %collective-permute-start.13 = (bf16[1,2,2,128,128]{4,3,2,1,0:T(8,128)(2,1)S(1)}, bf16[1,2,2,128,128]{4,3,2,1,0:T(8,128)(2,1)S(1)}, u32[]{:S(2)}, u32[]{:S(2)}) collective-permute-start(bf16[1,2,2,128,128]{4,3,2,1,0:T(8,128)(2,1)S(1)} %collective-permute-done.12.refs_11_), channel_id=1, source_target_pairs={{0,4},{4,0},{8,12},{12,8},{1,5},{5,1},{9,13},{13,9},{2,6},{6,2},{1... | collective-permute-start | bytes 393224 | tf_op jit(solution)/shard_map/ppermute | solution.py:396
  44.3 0.7 %copy-start.4 = (bf16[32,2,2048]{2,1,0:T(2,128)(2,1)}, bf16[32,2,2048]{2,1,0:T(2,128)(2,1)S(1)}, u32[]{:S(2)}) copy-start(bf16[32,2,2048]{2,1,0:T(2,128)(2,1)S(1)} %get-tuple-element.76) | copy-start | bytes 786436

commit v5 on v4

--- a/solution.py
+++ b/solution.py
@@ -64,22 +64,37 @@
         store.wait()
 
 
+def split(value, size):
+    assert size & (size - 1) == 0
+    return lax.shift_right_logical(value, size.bit_length() - 1), value & (size - 1)
+
+
 def count_log(tables, length, ids, block_len, spans, store):
     requests, width = tables.shape[0], ids.shape[1]
-    whole = length // block_len
-    rest = length - whole * block_len
+    whole, rest = split(length, block_len)
+    whole = jnp.broadcast_to(whole, (requests, width))
     full = jnp.zeros((requests, width), jnp.float32)
     part = jnp.zeros((requests, width), jnp.float32)
     for e in range(spans):
-        hit = tables[:, e : e + 1] == ids
+        hit = jnp.broadcast_to(tables[:, e : e + 1], (requests, width)) == ids
         full = full + jnp.where(hit & (whole > e), 1.0, 0.0)
         part = part + jnp.where(hit & (whole == e), 1.0, 0.0)
-    inside = lax.broadcasted_iota(jnp.int32, (requests, block_len), 1) < rest
+
+    def log2(count):
+        return jnp.where(count > 0, jnp.log(jnp.maximum(count, 1.0)) * LOG2E, -jnp.inf)
+
+    beyond, within = log2(full), log2(full + part)
+    shape = (requests, block_len)
+    inside = lax.broadcasted_iota(jnp.int32, shape, 1) < jnp.broadcast_to(rest, shape)
     for b in range(width):
-        count = jnp.broadcast_to(full[:, b : b + 1], (requests, block_len)) + jnp.where(
-            inside, jnp.broadcast_to(part[:, b : b + 1], (requests, block_len)), 0.0
-        )
-        store(b, jnp.where(count > 0, jnp.log(jnp.maximum(count, 1.0)) * LOG2E, -jnp.inf))
+        store(
+            b,
+            jnp.where(
+                inside,
+                jnp.broadcast_to(within[:, b : b + 1], shape),
+                jnp.broadcast_to(beyond[:, b : b + 1], shape),
+            ),
+        )
 
 
 def score_tiles(query, keys, log_ref, scale_row, rows, store):
@@ -147,7 +162,8 @@
         shape = (height, fresh_ref.shape[2])
         row = lax.broadcasted_iota(jnp.int32, shape, 0)
         col = lax.broadcasted_iota(jnp.int32, shape, 1)
-        seen = (col // steps == row // rows) & (col % steps <= row % steps)
+        (request, row_step), (owner, step) = split(row, rows), split(col, steps)
+        seen = (request == owner) & (split(row_step, steps)[1] >= step)
         score = lax.dot_general(
             q_ref[0], fresh_ref[0, 0], NT, preferred_element_type=jnp.float32
         )

time: 45.5 us -> 45.3 us (level)
  transfers between devices with their start and end apart: 8 -> 8, of which waited for: 1 -> 1; matrix products, arithmetic and copies ran while one was open for 1% -> 2% of each run, Pallas kernels for 53% -> 52%
where the time goes in v5:
time: 45.3 us; the launch traced here: 44.9 us
  Pallas kernels  28.3 us (62%)
  starting transfers between devices  11.6 us (26%)
  waiting for transfers between devices  1.56 us (3%)
  between operations  1.55 us (3%)
  local copies, waits for them, and re-layouts  1.36 us (3%)
    pallas_call x2, Pallas kernels, own(): pl.pallas_call(functools.partial(own_kernel, (head, pool, heads, rows, st...  21.7 us
    ppermute x5, starting transfers between devices, swap(): lax.ppermute(value, 'inst', [(j, j ^ distance) for j in range(instances)])  6.98 us
    ppermute x3, starting transfers between devices, doubling(): moved = lax.ppermute(value, axis, [(j, j ^ bit) for j in range(size)])  4.61 us
    pallas_call x1, Pallas kernels, attend(): pl.pallas_call(functools.partial(pack_kernel, instances, listed, copies),...  2.74 us
    pallas_call x1, Pallas kernels, attend(): pl.pallas_call(functools.partial(arrival_kernel, (heads, rows, block_len)...  2.06 us
    pallas_call x1, Pallas kernels, attend(): pl.pallas_call(functools.partial(route_kernel, (pool, heads, instances, g...  1.74 us
    ppermute x3, waiting for transfers between devices, doubling(): moved = lax.ppermute(value, axis, [(j, j ^ bit) for j in range(size)])  1.54 us
  transfers between devices with their start and end apart: 8, of which 1 were waited for; matrix products, arithmetic and copies ran while one was open for 2% of the time, Pallas kernels for 52%

profile of v5, /device:TPU:0, one launch (start us, length us, event | category | flops | bytes accessed | tf_op | source)
XLA Modules:
  0.0 44.9 jit_solution(13356344649588061203)
XLA Ops:
  0.6 0.0 copy-start.10
  0.6 0.0 copy-start.9
  0.7 0.0 copy-start.7
  0.7 0.0 copy-start.8
  0.7 0.0 copy-start.6
  0.7 0.0 copy-start.5
  0.7 0.0 copy-start.3
  0.7 2.7 %pack_blocks.3 = (bf16[1,2,2,128,128]{4,3,2,1,0:T(8,128)(2,1)}, bf16[2,2,2,128,128]{4,3,2,1,0:T(8,128)(2,1)}, bf16[1,2,2,128,128]{4,3,2,1,0:T(8,128)(2,1)}, bf16...) custom-call(s32[1,4]{1,0:T(1,128)} %dest_ref.1, s32[1,4]{1,0:T(1,128)} %block_ref.1, ...), custom_call_target="tpu_custom_call" | custom-call | bytes 1572864 | tf_op jit(solution)/shard_map/pack_blocks/pallas_call | solution.py:390
  3.4 0.0 copy-done.10
  3.5 0.0 copy-done.9
  3.5 0.0 copy-done.7
  3.5 0.1 reshape.81.scale_ref
  3.6 0.1 pad_maximum_fusion.7
  3.7 3.0 %collective-permute-start.6 = (f32[1,200]{1,0:T(1,128)S(1)}, f32[1,200]{1,0:T(1,128)S(1)}, u32[]{:S(2)}, u32[]{:S(2)}) collective-permute-start(f32[1,200]{1,0:T(1,128)S(1)} %pad_maximum_fusion.7), channel_id=1, source_target_pairs={{0,4},{4,0},{8,12},{12,8},{1,5},{5,1},{9,13},{13,9},{2,6},{6,2},{1... | collective-permute-start | bytes 2408 | tf_op jit(solution)/shard_map/ppermute | solution.py:354
  6.7 2.6 %collective-permute-start.10 = (bf16[1,2,2,128,128]{4,3,2,1,0:T(8,128)(2,1)}, bf16[1,2,2,128,128]{4,3,2,1,0:T(8,128)(2,1)S(1)}, u32[]{:S(2)}, u32[]{:S(2)}) collective-permute-start(bf16[1,2,2,128,128]{4,3,2,1,0:T(8,128)(2,1)} %get-tuple-element.97), channel_id=1, source_target_pairs={{0,8},{4,12},{8,0},{12,4},{1,9},{5,13},{9,1},{13,5},{2,10},{6,14},... | collective-permute-start | bytes 393224 | tf_op jit(solution)/shard_map/ppermute | solution.py:412
  9.3 0.0 collective-permute-start.11
  9.3 1.9 %collective-permute-start.12 = (bf16[1,2,2,128,128]{4,3,2,1,0:T(8,128)(2,1)}, bf16[1,2,2,128,128]{4,3,2,1,0:T(8,128)(2,1)S(1)}, u32[]{:S(2)}, u32[]{:S(2)}) collective-permute-start(bf16[1,2,2,128,128]{4,3,2,1,0:T(8,128)(2,1)} %get-tuple-element.99.refs_10_), channel_id=1, source_target_pairs={{0,8},{4,12},{8,0},{12,4},{1,9},{5,13},{9,1},{13,5},{2,10},{6,14},... | collective-permute-start | bytes 393224 | tf_op jit(solution)/shard_map/ppermute | solution.py:412
  11.2 2.5 %collective-permute-start.9 = (bf16[2,2,2,128,128]{4,3,2,1,0:T(8,128)(2,1)}, bf16[2,2,2,128,128]{4,3,2,1,0:T(8,128)(2,1)S(1)}, u32[]{:S(2)}, u32[]{:S(2)}) collective-permute-start(bf16[2,2,2,128,128]{4,3,2,1,0:T(8,128)(2,1)} %get-tuple-element.96), channel_id=1, source_target_pairs={{0,4},{4,0},{8,12},{12,8},{1,5},{5,1},{9,13},{13,9},{2,6},{6,2},{1... | collective-permute-start | bytes 786440 | tf_op jit(solution)/shard_map/ppermute | solution.py:412
  13.7 0.0 copy-done.8
  13.7 0.1 copy.19.length_ref
  13.8 0.0 copy-done.6
  13.8 0.1 copy.18.tables_ref
  13.8 0.0 copy-done.5
  13.8 0.1 copy.15
  13.9 0.0 copy-done.3
  13.9 0.2 copy.14
  14.2 0.0 collective-permute-done.6
  14.2 0.1 pad_maximum_fusion.6
  14.2 0.0 collective-permute-start.7
  14.3 0.0 copy-start.1
  14.3 0.0 copy-start.2
  14.3 10.9 %own_blocks.7 = (f32[512,128]{1,0:T(8,128)S(1)}, f32[512,128]{1,0:T(8,128)S(1)}, f32[512,128]{1,0:T(8,128)S(1)}) custom-call(s32[32,16]{1,0:T(8,128)S(1)} %copy.18.tables_ref, s32[32,1]{1,0:T(8,128)S(1)} %copy.19.length_ref, f32[1,192]{1,0:T(1,128)S(1)} %reshape.81.scale_ref, bf16[2,512,128]{2,1,0:T(8,128)(2,1)S(1)} %bitcast.31, ...), custom_call_target="tpu_custom_call" | custom-call | flops 1610612736 | bytes 3145728 | tf_op jit(solution)/shard_map/own_blocks/pallas_call | solution.py:457
  25.2 1.5 %collective-permute-done.7 = f32[2,200]{1,0:T(2,128)S(1)} collective-permute-done((f32[2,200]{1,0:T(2,128)S(1)}, f32[2,200]{1,0:T(2,128)S(1)}, u32[]{:S(2)}, u32[]{:S(2)}) %collective-permute-start.7) | collective-permute-done | bytes 1632 | tf_op jit(solution)/shard_map/ppermute | solution.py:354
  26.7 0.1 pad_maximum_fusion.5
  26.8 1.6 %collective-permute-start.8 = (f32[4,200]{1,0:T(4,128)S(1)}, f32[4,200]{1,0:T(4,128)S(1)}, u32[]{:S(2)}, u32[]{:S(2)}) collective-permute-start(f32[4,200]{1,0:T(4,128)S(1)} %pad_maximum_fusion.5), channel_id=1, source_target_pairs={{0,16},{16,0},{1,17},{17,1},{2,18},{18,2},{3,19},{19,3},{4,20},{20... | collective-permute-start | bytes 9608 | tf_op jit(solution)/shard_map/ppermute | solution.py:354
  28.4 0.0 collective-permute-done.12.refs_11_
  28.4 0.0 collective-permute-start.13
  28.4 10.8 %own_blocks.6 = (f32[512,128]{1,0:T(8,128)S(1)}, f32[512,128]{1,0:T(8,128)S(1)}, f32[512,128]{1,0:T(8,128)S(1)}) custom-call(s32[32,16]{1,0:T(8,128)S(1)} %copy.18.tables_ref, s32[32,1]{1,0:T(8,128)S(1)} %copy.19.length_ref, f32[1,192]{1,0:T(1,128)S(1)} %reshape.81.scale_ref, bf16[2,512,128]{2,1,0:T(8,128)(2,1)S(1)} %bitcast.32, ...), custom_call_target="tpu_custom_call" | custom-call | flops 1610612736 | bytes 3145728 | tf_op jit(solution)/shard_map/own_blocks/pallas_call | solution.py:457
  39.2 0.0 collective-permute-done.8
  39.2 0.1 pad_maximum_fusion.4.lists_ref
  39.3 1.7 %route_arrivals.3 = (s32[1,4]{1,0:T(1,128)}, s32[1]{0:T(128)}, f32[32,1024]{1,0:T(8,128)S(1)}, f32[4,1024]{1,0:T(4,128)S(1)}) custom-call(f32[8,200]{1,0:T(8,128)S(1)} %pad_maximum_fusion.4.lists_ref, s32[32,16]{1,0:T(8,128)S(1)} %copy.18.tables_ref, s32[32,1]{1,0:T(8,128)S(1)} %copy.19.length_ref, f32[512,128]{1,0:T(8,128)S(1)} %get-tuple-element.86.own_ref.refs_5_), custom_call_target="tpu_custom_call" | custom-call | tf_op jit(solution)/shard_map/route_arrivals/pallas_call | solution.py:492
  41.7 0.0 collective-permute-done.10.refs_8_
  41.7 0.0 collective-permute-done.11.refs_9_
  41.7 0.0 collective-permute-done.13.refs_12_
  41.7 0.0 collective-permute-done.9.refs_7_
  41.7 0.0 copy-done.1
  41.7 0.0 copy-done.2
  41.8 2.1 %arrived_blocks.3 = bf16[32,2,16,128]{3,2,1,0:T(8,128)(2,1)S(1)} custom-call(bf16[2,512,128]{2,1,0:T(8,128)(2,1)S(1)} %bitcast.33, f32[32,1024]{1,0:T(8,128)S(1)} %get-tuple-element.88.log_ref, f32[4,1024]{1,0:T(4,128)S(1)} %get-tuple-element.89.row_ref, f32[512,128]{1,0:T(8,128)S(1)} %get-tuple-element.90.refs_0_, ...), custom_call_target="tpu_custom_call" | custom-call | flops 536870912 | bytes 1048576 | tf_op jit(solution)/shard_map/arrived_blocks/pallas_call | solution.py:511
  43.9 0.3 conditional.1
  43.9 0.1 reshape.78
  44.1 0.0 copy-start.4
  44.2 0.7 %copy-done.4 = bf16[32,2,2048]{2,1,0:T(2,128)(2,1)} copy-done((bf16[32,2,2048]{2,1,0:T(2,128)(2,1)}, bf16[32,2,2048]{2,1,0:T(2,128)(2,1)S(1)}, u32[]{:S(2)}) %copy-start.4) | copy-done | bytes 262168
  (5 shorter events, 0.1 us)
Async XLA Ops:
  0.6 2.8 %copy-start.10 = (s32[1,4]{1,0:T(1,128)S(1)}, s32[1,4]{1,0:T(1,128)}, u32[]{:S(2)}) copy-start(s32[1,4]{1,0:T(1,128)} %dest_ref.1) | copy-start | bytes 52
  0.6 2.8 %copy-start.9 = (s32[1,4]{1,0:T(1,128)S(1)}, s32[1,4]{1,0:T(1,128)}, u32[]{:S(2)}) copy-start(s32[1,4]{1,0:T(1,128)} %block_ref.1) | copy-start | bytes 52
  0.7 2.8 %copy-start.7 = (bf16[48,2,2]{0,2,1:T(2,128)(2,1)S(1)}, bf16[48,2,2]{0,2,1:T(2,128)(2,1)}, u32[]{:S(2)}) copy-start(bf16[48,2,2]{0,2,1:T(2,128)(2,1)} %param.13) | copy-start | bytes 1156
  0.7 13.0 %copy-start.8 = (s32[32]{0:T(128)S(1)}, s32[32]{0:T(128)}, u32[]{:S(2)}) copy-start(s32[32]{0:T(128)} %param.15) | copy-start | bytes 388
  0.7 13.1 %copy-start.6 = (s32[32,16]{0,1:T(8,128)S(1)}, s32[32,16]{0,1:T(8,128)}, u32[]{:S(2)}) copy-start(s32[32,16]{0,1:T(8,128)} %param.14) | copy-start | bytes 6148
  0.7 13.2 %copy-start.5 = (bf16[32,2,2,2,128]{4,3,2,1,0:T(2,128)(2,1)S(1)}, bf16[32,2,2,2,128]{4,3,2,1,0:T(2,128)(2,1)}, u32[]{:S(2)}) copy-start(bf16[32,2,2,2,128]{4,3,2,1,0:T(2,128)(2,1)} %param.11) | copy-start | bytes 196612
  0.7 13.2 %copy-start.3 = (bf16[32,2,16,128]{3,2,1,0:T(8,128)(2,1)S(1)}, bf16[32,2,16,128]{3,2,1,0:T(8,128)(2,1)}, u32[]{:S(2)}) copy-start(bf16[32,2,16,128]{3,2,1,0:T(8,128)(2,1)} %param.10) | copy-start | bytes 786436
  3.7 10.5 %collective-permute-start.6 = (f32[1,200]{1,0:T(1,128)S(1)}, f32[1,200]{1,0:T(1,128)S(1)}, u32[]{:S(2)}, u32[]{:S(2)}) collective-permute-start(f32[1,200]{1,0:T(1,128)S(1)} %pad_maximum_fusion.7), channel_id=1, source_target_pairs={{0,4},{4,0},{8,12},{12,8},{1,5},{5,1},{9,13},{13,9},{2,6},{6,2},{1... | collective-permute-start | bytes 2408 | tf_op jit(solution)/shard_map/ppermute | solution.py:354
  6.7 35.0 %collective-permute-start.10 = (bf16[1,2,2,128,128]{4,3,2,1,0:T(8,128)(2,1)}, bf16[1,2,2,128,128]{4,3,2,1,0:T(8,128)(2,1)S(1)}, u32[]{:S(2)}, u32[]{:S(2)}) collective-permute-start(bf16[1,2,2,128,128]{4,3,2,1,0:T(8,128)(2,1)} %get-tuple-element.97), channel_id=1, source_target_pairs={{0,8},{4,12},{8,0},{12,4},{1,9},{5,13},{9,1},{13,5},{2,10},{6,14},... | collective-permute-start | bytes 393224 | tf_op jit(solution)/shard_map/ppermute | solution.py:412
  9.3 32.4 %collective-permute-start.11 = (bf16[1,2,2,128,128]{4,3,2,1,0:T(8,128)(2,1)}, bf16[1,2,2,128,128]{4,3,2,1,0:T(8,128)(2,1)S(1)}, u32[]{:S(2)}, u32[]{:S(2)}) collective-permute-start(bf16[1,2,2,128,128]{4,3,2,1,0:T(8,128)(2,1)} %get-tuple-element.98), channel_id=1, source_target_pairs={{0,12},{4,8},{8,4},{12,0},{1,13},{5,9},{9,5},{13,1},{2,14},{6,10},... | collective-permute-start | bytes 393224 | tf_op jit(solution)/shard_map/ppermute | solution.py:412
  9.3 19.1 %collective-permute-start.12 = (bf16[1,2,2,128,128]{4,3,2,1,0:T(8,128)(2,1)}, bf16[1,2,2,128,128]{4,3,2,1,0:T(8,128)(2,1)S(1)}, u32[]{:S(2)}, u32[]{:S(2)}) collective-permute-start(bf16[1,2,2,128,128]{4,3,2,1,0:T(8,128)(2,1)} %get-tuple-element.99.refs_10_), channel_id=1, source_target_pairs={{0,8},{4,12},{8,0},{12,4},{1,9},{5,13},{9,1},{13,5},{2,10},{6,14},... | collective-permute-start | bytes 393224 | tf_op jit(solution)/shard_map/ppermute | solution.py:412
  11.2 30.5 %collective-permute-start.9 = (bf16[2,2,2,128,128]{4,3,2,1,0:T(8,128)(2,1)}, bf16[2,2,2,128,128]{4,3,2,1,0:T(8,128)(2,1)S(1)}, u32[]{:S(2)}, u32[]{:S(2)}) collective-permute-start(bf16[2,2,2,128,128]{4,3,2,1,0:T(8,128)(2,1)} %get-tuple-element.96), channel_id=1, source_target_pairs={{0,4},{4,0},{8,12},{12,8},{1,5},{5,1},{9,13},{13,9},{2,6},{6,2},{1... | collective-permute-start | bytes 786440 | tf_op jit(solution)/shard_map/ppermute | solution.py:412
  14.2 12.5 %collective-permute-start.7 = (f32[2,200]{1,0:T(2,128)S(1)}, f32[2,200]{1,0:T(2,128)S(1)}, u32[]{:S(2)}, u32[]{:S(2)}) collective-permute-start(f32[2,200]{1,0:T(2,128)S(1)} %pad_maximum_fusion.6), channel_id=1, source_target_pairs={{0,8},{4,12},{8,0},{12,4},{1,9},{5,13},{9,1},{13,5},{2,10},{6,14},... | collective-permute-start | bytes 4808 | tf_op jit(solution)/shard_map/ppermute | solution.py:354
  14.3 27.5 %copy-start.1 = (bf16[1,2,2,128,128]{4,3,2,1,0:T(8,128)(2,1)S(1)}, bf16[1,2,2,128,128]{4,3,2,1,0:T(8,128)(2,1)}, u32[]{:S(2)}) copy-start(bf16[1,2,2,128,128]{4,3,2,1,0:T(8,128)(2,1)} %get-tuple-element.95.refs_6_) | copy-start | bytes 393220
  14.3 27.5 %copy-start.2 = (bf16[1,2,2,128,128]{4,3,2,1,0:T(8,128)(2,1)S(1)}, bf16[1,2,2,128,128]{4,3,2,1,0:T(8,128)(2,1)}, u32[]{:S(2)}) copy-start(bf16[1,2,2,128,128]{4,3,2,1,0:T(8,128)(2,1)} %get-tuple-element.99.refs_10_) | copy-start | bytes 393220
  26.8 12.4 %collective-permute-start.8 = (f32[4,200]{1,0:T(4,128)S(1)}, f32[4,200]{1,0:T(4,128)S(1)}, u32[]{:S(2)}, u32[]{:S(2)}) collective-permute-start(f32[4,200]{1,0:T(4,128)S(1)} %pad_maximum_fusion.5), channel_id=1, source_target_pairs={{0,16},{16,0},{1,17},{17,1},{2,18},{18,2},{3,19},{19,3},{4,20},{20... | collective-permute-start | bytes 9608 | tf_op jit(solution)/shard_map/ppermute | solution.py:354
  28.4 13.3 %collective-permute-start.13 = (bf16[1,2,2,128,128]{4,3,2,1,0:T(8,128)(2,1)S(1)}, bf16[1,2,2,128,128]{4,3,2,1,0:T(8,128)(2,1)S(1)}, u32[]{:S(2)}, u32[]{:S(2)}) collective-permute-start(bf16[1,2,2,128,128]{4,3,2,1,0:T(8,128)(2,1)S(1)} %collective-permute-done.12.refs_11_), channel_id=1, source_target_pairs={{0,4},{4,0},{8,12},{12,8},{1,5},{5,1},{9,13},{13,9},{2,6},{6,2},{1... | collective-permute-start | bytes 393224 | tf_op jit(solution)/shard_map/ppermute | solution.py:412
  44.1 0.7 %copy-start.4 = (bf16[32,2,2048]{2,1,0:T(2,128)(2,1)}, bf16[32,2,2048]{2,1,0:T(2,128)(2,1)S(1)}, u32[]{:S(2)}) copy-start(bf16[32,2,2048]{2,1,0:T(2,128)(2,1)S(1)} %get-tuple-element.76) | copy-start | bytes 786436

commit v6 on v5

--- a/solution.py
+++ b/solution.py
@@ -134,51 +134,60 @@
 
 def own_kernel(
     dims,
-    tables_ref, length_ref, scale_ref, q_ref, fresh_ref, codes_ref,
+    tables_ref, length_ref, scale_ref, q_ref, fresh_ref, pool_ref,
     acc_ref, top_ref, total_ref,
-    log_ref, row_ref, t_ref, new_ref, p_ref,
+    log_ref, row_ref, t_ref, p_ref, codes_ref, sems,
 ):
     head, pool, heads, rows, steps, block_len, spans, factor, group = dims
-    phase, chunk = pl.program_id(0), pl.program_id(1)
     chunks = pool // group
-    height = q_ref.shape[1]
+    height, head_dim = q_ref.shape[1:]
     width = group * block_len
 
-    @pl.when((phase == 0) & (chunk == 0))
-    def _():
-        ids = lax.broadcasted_iota(jnp.int32, (1, pool), 1)
-
-        def store(b, value):
-            lane = (b % group) * block_len
-            log_ref[b // group, :, lane : lane + block_len] = value
-
-        count_log(tables_ref[...], length_ref[...], ids, block_len, spans, store)
-        for b in range(pool):
-            lane = (b % group) * block_len
-            for part, unit in ((0, factor * LOG2E), (1, 1.0)):
-                row_ref[b // group, part : part + 1, lane : lane + block_len] = jnp.full(
-                    (1, block_len), scale_ref[0, (part * heads + head) * pool + b] * unit
-                )
-        shape = (height, fresh_ref.shape[2])
-        row = lax.broadcasted_iota(jnp.int32, shape, 0)
-        col = lax.broadcasted_iota(jnp.int32, shape, 1)
-        (request, row_step), (owner, step) = split(row, rows), split(col, steps)
-        seen = (request == owner) & (split(row_step, steps)[1] >= step)
-        score = lax.dot_general(
-            q_ref[0], fresh_ref[0, 0], NT, preferred_element_type=jnp.float32
-        )
-        score = jnp.where(seen, score * (factor * LOG2E), -jnp.inf)
-        new_ref[...] = score
-        top_ref[...] = lane_fold(score, jnp.maximum)
-
-    @pl.when(phase == 0)
-    def _():
+    def load(part, chunk):
+        return pltpu.make_async_copy(
+            pool_ref.at[pl.ds(chunk * group, group), part, head],
+            codes_ref.at[part, chunk],
+            sems.at[part, chunk],
+        )
+
+    for part in range(2):
+        for chunk in range(chunks):
+            load(part, chunk).start()
+
+    ids = lax.broadcasted_iota(jnp.int32, (1, pool), 1)
+
+    def store_log(b, value):
+        lane = (b % group) * block_len
+        log_ref[b // group, :, lane : lane + block_len] = value
+
+    count_log(tables_ref[...], length_ref[...], ids, block_len, spans, store_log)
+    for b in range(pool):
+        lane = (b % group) * block_len
+        for part, unit in ((0, factor * LOG2E), (1, 1.0)):
+            row_ref[b // group, part : part + 1, lane : lane + block_len] = jnp.full(
+                (1, block_len), scale_ref[0, (part * heads + head) * pool + b] * unit
+            )
+    shape = (height, fresh_ref.shape[2])
+    row = lax.broadcasted_iota(jnp.int32, shape, 0)
+    col = lax.broadcasted_iota(jnp.int32, shape, 1)
+    (request, row_step), (owner, step) = split(row, rows), split(col, steps)
+    seen = (request == owner) & (split(row_step, steps)[1] >= step)
+    new_score = lax.dot_general(
+        q_ref[head], fresh_ref[0, head], NT, preferred_element_type=jnp.float32
+    )
+    new_score = jnp.where(seen, new_score * (factor * LOG2E), -jnp.inf)
+    acc_ref[...] = new_score
+    top_ref[...] = lane_fold(new_score, jnp.maximum)
+
+    def score(chunk, carry):
+        load(0, chunk).wait()
+
         def store(row, lane, value):
             t_ref[chunk, row : row + rows, lane : lane + value.shape[1]] = value
 
         score_tiles(
-            q_ref[0],
-            codes_ref[:, 0, 0].reshape(width, codes_ref.shape[-1]),
+            q_ref[head],
+            codes_ref[0, chunk].reshape(width, head_dim),
             log_ref.at[chunk],
             row_ref[chunk, 0:1, :],
             rows,
@@ -187,19 +196,20 @@
         for row in range(0, height, rows):
             at = pl.ds(row, rows)
             top_ref[at] = jnp.maximum(top_ref[at], lane_fold(t_ref[chunk, at], jnp.maximum))
-
-    @pl.when((phase == 1) & (chunk == 0))
-    def _():
-        top = jnp.broadcast_to(jnp.max(top_ref[...], axis=1, keepdims=True), (height, 128))
-        top_ref[...] = top
-        weight = jnp.exp2(new_ref[...] - spread(top, new_ref.shape[1]))
-        total_ref[...] = lane_fold(weight, jnp.add)
-        acc_ref[...] = jnp.dot(
-            weight.astype(jnp.bfloat16), fresh_ref[1, 0], preferred_element_type=jnp.float32
-        )
-
-    @pl.when(phase == 1)
-    def _():
+        return carry
+
+    lax.fori_loop(0, chunks, score, 0)
+
+    top = jnp.broadcast_to(jnp.max(top_ref[...], axis=1, keepdims=True), (height, 128))
+    top_ref[...] = top
+    weight = jnp.exp2(acc_ref[...] - spread(top, acc_ref.shape[1]))
+    total_ref[...] = lane_fold(weight, jnp.add)
+    acc_ref[...] = jnp.dot(
+        weight.astype(jnp.bfloat16), fresh_ref[1, head], preferred_element_type=jnp.float32
+    )
+
+    def apply(chunk, carry):
+        load(1, chunk).wait()
         scale = row_ref[chunk, 1:2, :]
         for row in range(0, height, rows):
             at = pl.ds(row, rows)
@@ -208,15 +218,15 @@
             p_ref[at] = (weight * scale).astype(jnp.bfloat16)
         acc_ref[...] += jnp.dot(
             p_ref[...],
-            codes_ref[:, 0, 0].reshape(width, codes_ref.shape[-1]),
+            codes_ref[1, chunk].reshape(width, head_dim),
             preferred_element_type=jnp.float32,
         )
-
-    @pl.when((phase == 1) & (chunk == chunks - 1))
-    def _():
-        total_ref[...] = jnp.broadcast_to(
-            jnp.sum(total_ref[...], axis=1, keepdims=True), (height, 128)
-        )
+        return carry
+
+    lax.fori_loop(0, chunks, apply, 0)
+    total_ref[...] = jnp.broadcast_to(
+        jnp.sum(total_ref[...], axis=1, keepdims=True), (height, 128)
+    )
 
 
 def route_kernel(
@@ -444,39 +454,27 @@
     fresh_len = requests * steps
     fresh = new_kv.transpose(2, 3, 0, 1, 4).reshape(2, heads, fresh_len, head_dim)
     fresh = jnp.pad(fresh, ((0, 0), (0, 0), (0, -fresh_len % 128), (0, 0)))
-    fresh_len = fresh.shape[2]
+    assert fresh.shape[2] == head_dim
     length = ctx_len[:, None]
     width = group * block_len
     chunks = pool // group
     tokens = pool * block_len
-
-    def whole(shape):
-        return pl.BlockSpec(shape, lambda p, c: (0,) * len(shape))
 
     def own(head):
         return pl.pallas_call(
             functools.partial(
                 own_kernel, (head, pool, heads, rows, steps, block_len, spans, factor, group)
             ),
-            grid=(2, chunks),
             out_shape=[jax.ShapeDtypeStruct((height, head_dim), f32)] * 3,
-            in_specs=[
-                whole(tables.shape),
-                whole(length.shape),
-                SMEM_SPEC,
-                pl.BlockSpec((1, height, head_dim), lambda p, c: (head, 0, 0)),
-                pl.BlockSpec((2, 1, fresh_len, head_dim), lambda p, c: (0, head, 0, 0)),
-                pl.BlockSpec(
-                    (group, 1, 1, block_len, head_dim), lambda p, c: (c, p, head, 0, 0)
-                ),
-            ],
-            out_specs=[whole((height, head_dim))] * 3,
+            in_specs=[VMEM_SPEC, VMEM_SPEC, SMEM_SPEC, VMEM_SPEC, VMEM_SPEC, HBM_SPEC],
+            out_specs=[VMEM_SPEC] * 3,
             scratch_shapes=[
                 pltpu.VMEM((chunks, requests, width), f32),
                 pltpu.VMEM((chunks, 2, width), f32),
                 pltpu.VMEM((chunks, height, width), f32),
-                pltpu.VMEM((height, fresh_len), f32),
                 pltpu.VMEM((height, width), bf16),
+                pltpu.VMEM((2, chunks, group, block_len, head_dim), bf16),
+                pltpu.SemaphoreType.DMA((2, chunks)),
             ],
             compiler_params=pltpu.CompilerParams(vmem_limit_bytes=32 * MIB),
             cost_estimate=pl.CostEstimate(

time: 45.3 us -> 42.6 us (0.940)
  Pallas kernels: 28.3 us -> 23.4 us
  waiting for transfers between devices: 1.56 us -> 4.03 us
    pallas_call x2, Pallas kernels: 21.7 us -> 16.9 us  [own(): pl.pallas_call(functools.partial(own_kernel, (head, pool, heads, rows, st...]
    ppermute x3, waiting for transfers between devices: 1.54 us -> 4.01 us  [doubling(): moved = lax.ppermute(value, axis, [(j, j ^ bit) for j in range(size)])]
  transfers between devices with their start and end apart: 8 -> 8, of which waited for: 1 -> 1; matrix products, arithmetic and copies ran while one was open for 2% -> 2% of each run, Pallas kernels for 52% -> 44%
where the time goes in v6:
time: 42.6 us; the launch traced here: 42.4 us
  Pallas kernels  23.4 us (55%)
  starting transfers between devices  11.6 us (27%)
  waiting for transfers between devices  4.03 us (9%)
  between operations  1.55 us (4%)
  local copies, waits for them, and re-layouts  1.36 us (3%)
    pallas_call x2, Pallas kernels, own(): pl.pallas_call(functools.partial(own_kernel, (head, pool, heads, rows, st...  16.9 us
    ppermute x5, starting transfers between devices, swap(): lax.ppermute(value, 'inst', [(j, j ^ distance) for j in range(instances)])  6.98 us
    ppermute x3, starting transfers between devices, doubling(): moved = lax.ppermute(value, axis, [(j, j ^ bit) for j in range(size)])  4.61 us
    ppermute x3, waiting for transfers between devices, doubling(): moved = lax.ppermute(value, axis, [(j, j ^ bit) for j in range(size)])  4.01 us
    pallas_call x1, Pallas kernels, attend(): pl.pallas_call(functools.partial(pack_kernel, instances, listed, copies),...  2.74 us
    pallas_call x1, Pallas kernels, attend(): pl.pallas_call(functools.partial(arrival_kernel, (heads, rows, block_len)...  2.06 us
    pallas_call x1, Pallas kernels, attend(): pl.pallas_call(functools.partial(route_kernel, (pool, heads, instances, g...  1.74 us
  transfers between devices with their start and end apart: 8, of which 1 were waited for; matrix products, arithmetic and copies ran while one was open for 2% of the time, Pallas kernels for 44%

profile of v6, /device:TPU:0, one launch (start us, length us, event | category | flops | bytes accessed | tf_op | source)
XLA Modules:
  0.0 42.4 jit_solution(14492827004612497974)
XLA Ops:
  0.6 0.0 copy-start.10
  0.6 0.0 copy-start.9
  0.7 0.0 copy-start.7
  0.7 0.0 copy-start.8
  0.7 0.0 copy-start.6
  0.7 0.0 copy-start.5
  0.7 0.0 copy-start.3
  0.7 2.7 %pack_blocks.3 = (bf16[1,2,2,128,128]{4,3,2,1,0:T(8,128)(2,1)}, bf16[2,2,2,128,128]{4,3,2,1,0:T(8,128)(2,1)}, bf16[1,2,2,128,128]{4,3,2,1,0:T(8,128)(2,1)}, bf16...) custom-call(s32[1,4]{1,0:T(1,128)} %dest_ref.1, s32[1,4]{1,0:T(1,128)} %block_ref.1, ...), custom_call_target="tpu_custom_call" | custom-call | bytes 1572864 | tf_op jit(solution)/shard_map/pack_blocks/pallas_call | solution.py:400
  3.4 0.0 copy-done.10
  3.5 0.0 copy-done.9
  3.5 0.0 copy-done.7
  3.5 0.1 reshape.81.scale_ref
  3.6 0.1 pad_maximum_fusion.7
  3.7 3.0 %collective-permute-start.6 = (f32[1,200]{1,0:T(1,128)S(1)}, f32[1,200]{1,0:T(1,128)S(1)}, u32[]{:S(2)}, u32[]{:S(2)}) collective-permute-start(f32[1,200]{1,0:T(1,128)S(1)} %pad_maximum_fusion.7), channel_id=1, source_target_pairs={{0,4},{4,0},{8,12},{12,8},{1,5},{5,1},{9,13},{13,9},{2,6},{6,2},{1... | collective-permute-start | bytes 2408 | tf_op jit(solution)/shard_map/ppermute | solution.py:364
  6.7 2.6 %collective-permute-start.10 = (bf16[1,2,2,128,128]{4,3,2,1,0:T(8,128)(2,1)}, bf16[1,2,2,128,128]{4,3,2,1,0:T(8,128)(2,1)S(1)}, u32[]{:S(2)}, u32[]{:S(2)}) collective-permute-start(bf16[1,2,2,128,128]{4,3,2,1,0:T(8,128)(2,1)} %get-tuple-element.97), channel_id=1, source_target_pairs={{0,8},{4,12},{8,0},{12,4},{1,9},{5,13},{9,1},{13,5},{2,10},{6,14},... | collective-permute-start | bytes 393224 | tf_op jit(solution)/shard_map/ppermute | solution.py:422
  9.3 0.0 collective-permute-start.11
  9.3 1.9 %collective-permute-start.12 = (bf16[1,2,2,128,128]{4,3,2,1,0:T(8,128)(2,1)}, bf16[1,2,2,128,128]{4,3,2,1,0:T(8,128)(2,1)S(1)}, u32[]{:S(2)}, u32[]{:S(2)}) collective-permute-start(bf16[1,2,2,128,128]{4,3,2,1,0:T(8,128)(2,1)} %get-tuple-element.99.refs_10_), channel_id=1, source_target_pairs={{0,8},{4,12},{8,0},{12,4},{1,9},{5,13},{9,1},{13,5},{2,10},{6,14},... | collective-permute-start | bytes 393224 | tf_op jit(solution)/shard_map/ppermute | solution.py:422
  11.2 2.5 %collective-permute-start.9 = (bf16[2,2,2,128,128]{4,3,2,1,0:T(8,128)(2,1)}, bf16[2,2,2,128,128]{4,3,2,1,0:T(8,128)(2,1)S(1)}, u32[]{:S(2)}, u32[]{:S(2)}) collective-permute-start(bf16[2,2,2,128,128]{4,3,2,1,0:T(8,128)(2,1)} %get-tuple-element.96), channel_id=1, source_target_pairs={{0,4},{4,0},{8,12},{12,8},{1,5},{5,1},{9,13},{13,9},{2,6},{6,2},{1... | collective-permute-start | bytes 786440 | tf_op jit(solution)/shard_map/ppermute | solution.py:422
  13.7 0.0 copy-done.8
  13.7 0.1 copy.19.length_ref
  13.8 0.0 copy-done.6
  13.8 0.1 copy.18.tables_ref
  13.8 0.0 copy-done.5
  13.8 0.1 copy.15
  13.9 0.0 copy-done.3
  13.9 0.2 copy.14
  14.2 0.0 collective-permute-done.6
  14.2 0.1 pad_maximum_fusion.6
  14.2 0.0 collective-permute-start.7
  14.3 0.0 copy-start.1
  14.3 0.0 copy-start.2
  14.3 8.4 %own_blocks.7 = (f32[512,128]{1,0:T(8,128)S(1)}, f32[512,128]{1,0:T(8,128)S(1)}, f32[512,128]{1,0:T(8,128)S(1)}) custom-call(s32[32,16]{1,0:T(8,128)S(1)} %copy.18.tables_ref, s32[32,1]{1,0:T(8,128)S(1)} %copy.19.length_ref, f32[1,192]{1,0:T(1,128)S(1)} %reshape.81.scale_ref, bf16[2,512,128]{2,1,0:T(8,128)(2,1)S(1)} %bitcast.31, ...), custom_call_target="tpu_custom_call" | custom-call | flops 1610612736 | bytes 3145728 | tf_op jit(solution)/shard_map/own_blocks/pallas_call | solution.py:464
  22.7 4.0 %collective-permute-done.7 = f32[2,200]{1,0:T(2,128)S(1)} collective-permute-done((f32[2,200]{1,0:T(2,128)S(1)}, f32[2,200]{1,0:T(2,128)S(1)}, u32[]{:S(2)}, u32[]{:S(2)}) %collective-permute-start.7) | collective-permute-done | bytes 1632 | tf_op jit(solution)/shard_map/ppermute | solution.py:364
  26.7 0.1 pad_maximum_fusion.5
  26.8 1.6 %collective-permute-start.8 = (f32[4,200]{1,0:T(4,128)S(1)}, f32[4,200]{1,0:T(4,128)S(1)}, u32[]{:S(2)}, u32[]{:S(2)}) collective-permute-start(f32[4,200]{1,0:T(4,128)S(1)} %pad_maximum_fusion.5), channel_id=1, source_target_pairs={{0,16},{16,0},{1,17},{17,1},{2,18},{18,2},{3,19},{19,3},{4,20},{20... | collective-permute-start | bytes 9608 | tf_op jit(solution)/shard_map/ppermute | solution.py:364
  28.4 0.0 collective-permute-done.12.refs_11_
  28.4 0.0 collective-permute-start.13
  28.4 8.4 %own_blocks.6 = (f32[512,128]{1,0:T(8,128)S(1)}, f32[512,128]{1,0:T(8,128)S(1)}, f32[512,128]{1,0:T(8,128)S(1)}) custom-call(s32[32,16]{1,0:T(8,128)S(1)} %copy.18.tables_ref, s32[32,1]{1,0:T(8,128)S(1)} %copy.19.length_ref, f32[1,192]{1,0:T(1,128)S(1)} %reshape.81.scale_ref, bf16[2,512,128]{2,1,0:T(8,128)(2,1)S(1)} %bitcast.32, ...), custom_call_target="tpu_custom_call" | custom-call | flops 1610612736 | bytes 3145728 | tf_op jit(solution)/shard_map/own_blocks/pallas_call | solution.py:464
  36.8 0.0 collective-permute-done.8
  36.8 0.1 pad_maximum_fusion.4.lists_ref
  36.9 1.7 %route_arrivals.3 = (s32[1,4]{1,0:T(1,128)}, s32[1]{0:T(128)}, f32[32,1024]{1,0:T(8,128)S(1)}, f32[4,1024]{1,0:T(4,128)S(1)}) custom-call(f32[8,200]{1,0:T(8,128)S(1)} %pad_maximum_fusion.4.lists_ref, s32[32,16]{1,0:T(8,128)S(1)} %copy.18.tables_ref, s32[32,1]{1,0:T(8,128)S(1)} %copy.19.length_ref, f32[512,128]{1,0:T(8,128)S(1)} %get-tuple-element.86.own_ref.refs_5_), custom_call_target="tpu_custom_call" | custom-call | tf_op jit(solution)/shard_map/route_arrivals/pallas_call | solution.py:490
  39.3 0.0 collective-permute-done.10.refs_8_
  39.3 0.0 collective-permute-done.11.refs_9_
  39.3 0.0 collective-permute-done.13.refs_12_
  39.3 0.0 collective-permute-done.9.refs_7_
  39.3 0.0 copy-done.1
  39.3 0.0 copy-done.2
  39.4 2.1 %arrived_blocks.3 = bf16[32,2,16,128]{3,2,1,0:T(8,128)(2,1)S(1)} custom-call(bf16[2,512,128]{2,1,0:T(8,128)(2,1)S(1)} %bitcast.33, f32[32,1024]{1,0:T(8,128)S(1)} %get-tuple-element.88.log_ref, f32[4,1024]{1,0:T(4,128)S(1)} %get-tuple-element.89.row_ref, f32[512,128]{1,0:T(8,128)S(1)} %get-tuple-element.90.refs_0_, ...), custom_call_target="tpu_custom_call" | custom-call | flops 536870912 | bytes 1048576 | tf_op jit(solution)/shard_map/arrived_blocks/pallas_call | solution.py:509
  41.5 0.3 conditional.1
  41.5 0.1 reshape.78
  41.7 0.0 copy-start.4
  41.7 0.7 %copy-done.4 = bf16[32,2,2048]{2,1,0:T(2,128)(2,1)} copy-done((bf16[32,2,2048]{2,1,0:T(2,128)(2,1)}, bf16[32,2,2048]{2,1,0:T(2,128)(2,1)S(1)}, u32[]{:S(2)}) %copy-start.4) | copy-done | bytes 262168
  (5 shorter events, 0.1 us)
Async XLA Ops:
  0.6 2.8 %copy-start.10 = (s32[1,4]{1,0:T(1,128)S(1)}, s32[1,4]{1,0:T(1,128)}, u32[]{:S(2)}) copy-start(s32[1,4]{1,0:T(1,128)} %dest_ref.1) | copy-start | bytes 52
  0.6 2.8 %copy-start.9 = (s32[1,4]{1,0:T(1,128)S(1)}, s32[1,4]{1,0:T(1,128)}, u32[]{:S(2)}) copy-start(s32[1,4]{1,0:T(1,128)} %block_ref.1) | copy-start | bytes 52
  0.7 2.8 %copy-start.7 = (bf16[48,2,2]{0,2,1:T(2,128)(2,1)S(1)}, bf16[48,2,2]{0,2,1:T(2,128)(2,1)}, u32[]{:S(2)}) copy-start(bf16[48,2,2]{0,2,1:T(2,128)(2,1)} %param.13) | copy-start | bytes 1156
  0.7 13.0 %copy-start.8 = (s32[32]{0:T(128)S(1)}, s32[32]{0:T(128)}, u32[]{:S(2)}) copy-start(s32[32]{0:T(128)} %param.15) | copy-start | bytes 388
  0.7 13.1 %copy-start.6 = (s32[32,16]{0,1:T(8,128)S(1)}, s32[32,16]{0,1:T(8,128)}, u32[]{:S(2)}) copy-start(s32[32,16]{0,1:T(8,128)} %param.14) | copy-start | bytes 6148
  0.7 13.2 %copy-start.5 = (bf16[32,2,2,2,128]{4,3,2,1,0:T(2,128)(2,1)S(1)}, bf16[32,2,2,2,128]{4,3,2,1,0:T(2,128)(2,1)}, u32[]{:S(2)}) copy-start(bf16[32,2,2,2,128]{4,3,2,1,0:T(2,128)(2,1)} %param.11) | copy-start | bytes 196612
  0.7 13.2 %copy-start.3 = (bf16[32,2,16,128]{3,2,1,0:T(8,128)(2,1)S(1)}, bf16[32,2,16,128]{3,2,1,0:T(8,128)(2,1)}, u32[]{:S(2)}) copy-start(bf16[32,2,16,128]{3,2,1,0:T(8,128)(2,1)} %param.10) | copy-start | bytes 786436
  3.7 10.5 %collective-permute-start.6 = (f32[1,200]{1,0:T(1,128)S(1)}, f32[1,200]{1,0:T(1,128)S(1)}, u32[]{:S(2)}, u32[]{:S(2)}) collective-permute-start(f32[1,200]{1,0:T(1,128)S(1)} %pad_maximum_fusion.7), channel_id=1, source_target_pairs={{0,4},{4,0},{8,12},{12,8},{1,5},{5,1},{9,13},{13,9},{2,6},{6,2},{1... | collective-permute-start | bytes 2408 | tf_op jit(solution)/shard_map/ppermute | solution.py:364
  6.7 32.6 %collective-permute-start.10 = (bf16[1,2,2,128,128]{4,3,2,1,0:T(8,128)(2,1)}, bf16[1,2,2,128,128]{4,3,2,1,0:T(8,128)(2,1)S(1)}, u32[]{:S(2)}, u32[]{:S(2)}) collective-permute-start(bf16[1,2,2,128,128]{4,3,2,1,0:T(8,128)(2,1)} %get-tuple-element.97), channel_id=1, source_target_pairs={{0,8},{4,12},{8,0},{12,4},{1,9},{5,13},{9,1},{13,5},{2,10},{6,14},... | collective-permute-start | bytes 393224 | tf_op jit(solution)/shard_map/ppermute | solution.py:422
  9.3 30.0 %collective-permute-start.11 = (bf16[1,2,2,128,128]{4,3,2,1,0:T(8,128)(2,1)}, bf16[1,2,2,128,128]{4,3,2,1,0:T(8,128)(2,1)S(1)}, u32[]{:S(2)}, u32[]{:S(2)}) collective-permute-start(bf16[1,2,2,128,128]{4,3,2,1,0:T(8,128)(2,1)} %get-tuple-element.98), channel_id=1, source_target_pairs={{0,12},{4,8},{8,4},{12,0},{1,13},{5,9},{9,5},{13,1},{2,14},{6,10},... | collective-permute-start | bytes 393224 | tf_op jit(solution)/shard_map/ppermute | solution.py:422
  9.3 19.1 %collective-permute-start.12 = (bf16[1,2,2,128,128]{4,3,2,1,0:T(8,128)(2,1)}, bf16[1,2,2,128,128]{4,3,2,1,0:T(8,128)(2,1)S(1)}, u32[]{:S(2)}, u32[]{:S(2)}) collective-permute-start(bf16[1,2,2,128,128]{4,3,2,1,0:T(8,128)(2,1)} %get-tuple-element.99.refs_10_), channel_id=1, source_target_pairs={{0,8},{4,12},{8,0},{12,4},{1,9},{5,13},{9,1},{13,5},{2,10},{6,14},... | collective-permute-start | bytes 393224 | tf_op jit(solution)/shard_map/ppermute | solution.py:422
  11.2 28.1 %collective-permute-start.9 = (bf16[2,2,2,128,128]{4,3,2,1,0:T(8,128)(2,1)}, bf16[2,2,2,128,128]{4,3,2,1,0:T(8,128)(2,1)S(1)}, u32[]{:S(2)}, u32[]{:S(2)}) collective-permute-start(bf16[2,2,2,128,128]{4,3,2,1,0:T(8,128)(2,1)} %get-tuple-element.96), channel_id=1, source_target_pairs={{0,4},{4,0},{8,12},{12,8},{1,5},{5,1},{9,13},{13,9},{2,6},{6,2},{1... | collective-permute-start | bytes 786440 | tf_op jit(solution)/shard_map/ppermute | solution.py:422
  14.2 12.5 %collective-permute-start.7 = (f32[2,200]{1,0:T(2,128)S(1)}, f32[2,200]{1,0:T(2,128)S(1)}, u32[]{:S(2)}, u32[]{:S(2)}) collective-permute-start(f32[2,200]{1,0:T(2,128)S(1)} %pad_maximum_fusion.6), channel_id=1, source_target_pairs={{0,8},{4,12},{8,0},{12,4},{1,9},{5,13},{9,1},{13,5},{2,10},{6,14},... | collective-permute-start | bytes 4808 | tf_op jit(solution)/shard_map/ppermute | solution.py:364
  14.3 25.1 %copy-start.1 = (bf16[1,2,2,128,128]{4,3,2,1,0:T(8,128)(2,1)S(1)}, bf16[1,2,2,128,128]{4,3,2,1,0:T(8,128)(2,1)}, u32[]{:S(2)}) copy-start(bf16[1,2,2,128,128]{4,3,2,1,0:T(8,128)(2,1)} %get-tuple-element.95.refs_6_) | copy-start | bytes 393220
  14.3 25.1 %copy-start.2 = (bf16[1,2,2,128,128]{4,3,2,1,0:T(8,128)(2,1)S(1)}, bf16[1,2,2,128,128]{4,3,2,1,0:T(8,128)(2,1)}, u32[]{:S(2)}) copy-start(bf16[1,2,2,128,128]{4,3,2,1,0:T(8,128)(2,1)} %get-tuple-element.99.refs_10_) | copy-start | bytes 393220
  26.8 10.0 %collective-permute-start.8 = (f32[4,200]{1,0:T(4,128)S(1)}, f32[4,200]{1,0:T(4,128)S(1)}, u32[]{:S(2)}, u32[]{:S(2)}) collective-permute-start(f32[4,200]{1,0:T(4,128)S(1)} %pad_maximum_fusion.5), channel_id=1, source_target_pairs={{0,16},{16,0},{1,17},{17,1},{2,18},{18,2},{3,19},{19,3},{4,20},{20... | collective-permute-start | bytes 9608 | tf_op jit(solution)/shard_map/ppermute | solution.py:364
  28.4 10.9 %collective-permute-start.13 = (bf16[1,2,2,128,128]{4,3,2,1,0:T(8,128)(2,1)S(1)}, bf16[1,2,2,128,128]{4,3,2,1,0:T(8,128)(2,1)S(1)}, u32[]{:S(2)}, u32[]{:S(2)}) collective-permute-start(bf16[1,2,2,128,128]{4,3,2,1,0:T(8,128)(2,1)S(1)} %collective-permute-done.12.refs_11_), channel_id=1, source_target_pairs={{0,4},{4,0},{8,12},{12,8},{1,5},{5,1},{9,13},{13,9},{2,6},{6,2},{1... | collective-permute-start | bytes 393224 | tf_op jit(solution)/shard_map/ppermute | solution.py:422
  41.7 0.7 %copy-start.4 = (bf16[32,2,2048]{2,1,0:T(2,128)(2,1)}, bf16[32,2,2048]{2,1,0:T(2,128)(2,1)S(1)}, u32[]{:S(2)}) copy-start(bf16[32,2,2048]{2,1,0:T(2,128)(2,1)S(1)} %get-tuple-element.76) | copy-start | bytes 786436

commit v7 on v6

v7 whole, which is shorter than its diff:
```python
import functools
import math

import jax
import jax.numpy as jnp
from jax import lax
from jax.experimental import pallas as pl
from jax.experimental.pallas import tpu as pltpu
from jax.sharding import PartitionSpec as P

CAP = 2
LOG2E = math.log2(math.e)
MIB = 1 << 20
SMEM_SPEC = pl.BlockSpec(memory_space=pltpu.SMEM)
VMEM_SPEC = pl.BlockSpec(memory_space=pltpu.VMEM)
HBM_SPEC = pl.BlockSpec(memory_space=pltpu.HBM)
NT = (((1,), (1,)), ((), ()))


def loop(count, body, init):
    if count <= 8:
        for i in range(count):
            init = body(i, init)
        return init
    return lax.fori_loop(0, count, body, init)


def pack_kernel(instances, listed, dest_ref, block_ref, pool_ref, *refs):
    send_refs, (index_ref, held_ref, in_sems, out_sems) = refs[:instances], refs[instances:]
    slots = instances * CAP
    me = lax.axis_index("inst")
    for slot in range(slots):
        index_ref[slot] = 0

    def place(m, carry):
        dest = dest_ref[0, m]
        rank = loop(
            listed,
            lambda m2, n: n + jnp.where((dest_ref[0, m2] == dest) & (m2 < m), 1, 0),
            jnp.int32(0),
        )
        index_ref[jnp.bitwise_xor(dest, me) * CAP + jnp.minimum(rank, CAP - 1)] = block_ref[0, m]
        return carry

    loop(listed, place, 0)
    order = list(range(slots))[::-1]
    loads, stores = {}, []
    for i in order:
        loads[i] = pltpu.make_async_copy(
            pool_ref.at[index_ref[i]], held_ref.at[i], in_sems.at[i]
        )
        loads[i].start()
    for i in order:
        loads[i].wait()
        stores.append(
            pltpu.make_async_copy(
                held_ref.at[i], send_refs[i // CAP].at[i % CAP], out_sems.at[i]
            )
        )
        stores[-1].start()
    for store in stores:
        store.wait()


def split(value, size):
    assert size & (size - 1) == 0
    return lax.shift_right_logical(value, size.bit_length() - 1), value & (size - 1)


def count_log(tables, length, ids, block_len, spans, store):
    requests, width = tables.shape[0], ids.shape[1]
    whole, rest = split(length, block_len)
    whole = jnp.broadcast_to(whole, (requests, width))
    full = jnp.zeros((requests, width), jnp.float32)
    part = jnp.zeros((requests, width), jnp.float32)
    for e in range(spans):
        hit = jnp.broadcast_to(tables[:, e : e + 1], (requests, width)) == ids
        full = full + jnp.where(hit & (whole > e), 1.0, 0.0)
        part = part + jnp.where(hit & (whole == e), 1.0, 0.0)

    def log2(count):
        return jnp.where(count > 0, jnp.log(jnp.maximum(count, 1.0)) * LOG2E, -jnp.inf)

    beyond, within = log2(full), log2(full + part)
    shape = (requests, block_len)
    inside = lax.broadcasted_iota(jnp.int32, shape, 1) < jnp.broadcast_to(rest, shape)
    for b in range(width):
        store(
            b,
            jnp.where(
                inside,
                jnp.broadcast_to(within[:, b : b + 1], shape),
                jnp.broadcast_to(beyond[:, b : b + 1], shape),
            ),
        )


def score_tiles(query, keys, log_ref, scale_row, rows, store):
    height, wide = min(256, query.shape[0]), min(256, keys.shape[0])
    for top in range(0, query.shape[0], height):
        for left in range(0, keys.shape[0], wide):
            part = lax.dot_general(
                query[top : top + height],
                keys[left : left + wide],
                NT,
                preferred_element_type=jnp.float32,
            )
            scale = scale_row[:, left : left + wide]
            for r in range(height // rows):
                request = top // rows + r
                store(
                    request * rows,
                    left,
                    part[r * rows : (r + 1) * rows] * scale
                    + log_ref[request : request + 1, left : left + wide],
                )


def lane_fold(value, op):
    parts = [value[:, i : i + 128] for i in range(0, value.shape[1], 128)]
    while len(parts) > 1:
        parts = [
            op(parts[i], parts[i + 1]) if i + 1 < len(parts) else parts[i]
            for i in range(0, len(parts), 2)
        ]
    return parts[0]


def spread(column, width):
    return jnp.concatenate([column] * (width // 128), axis=1)


def own_kernel(
    dims,
    tables_ref, length_ref, scale_ref, q_ref, fresh_ref, pool_ref,
    acc_ref, top_ref, total_ref,
    log_ref, row_ref, t_ref, p_ref, codes_ref, sems,
):
    pool, heads, rows, steps, block_len, spans, factor, group = dims
    chunks = pool // group
    height, head_dim = q_ref.shape[1:]
    width = group * block_len

    def load(part, chunk):
        return pltpu.make_async_copy(
            pool_ref.at[pl.ds(chunk * group, group), part],
            codes_ref.at[part, chunk],
            sems.at[part, chunk],
        )

    for part in range(2):
        for chunk in range(chunks):
            load(part, chunk).start()

    ids = lax.broadcasted_iota(jnp.int32, (1, pool), 1)

    def store_log(b, value):
        lane = (b % group) * block_len
        log_ref[b // group, :, lane : lane + block_len] = value

    count_log(tables_ref[...], length_ref[...], ids, block_len, spans, store_log)
    for b in range(pool):
        lane = (b % group) * block_len
        for row in range(2 * heads):
            unit = factor * LOG2E if row < heads else 1.0
            row_ref[b // group, row : row + 1, lane : lane + block_len] = jnp.full(
                (1, block_len), scale_ref[0, row * pool + b] * unit
            )
    shape = (height, fresh_ref.shape[2])
    row = lax.broadcasted_iota(jnp.int32, shape, 0)
    col = lax.broadcasted_iota(jnp.int32, shape, 1)
    (request, row_step), (owner, step) = split(row, rows), split(col, steps)
    seen = (request == owner) & (split(row_step, steps)[1] >= step)
    for h in range(heads):
        new_score = lax.dot_general(
            q_ref[h], fresh_ref[0, h], NT, preferred_element_type=jnp.float32
        )
        new_score = jnp.where(seen, new_score * (factor * LOG2E), -jnp.inf)
        acc_ref[h] = new_score
        top_ref[h] = lane_fold(new_score, jnp.maximum)

    def score(chunk, carry):
        load(0, chunk).wait()
        for h in range(heads):

            def store(row, lane, value, h=h):
                t_ref[h, chunk, row : row + rows, lane : lane + value.shape[1]] = value

            score_tiles(
                q_ref[h],
                codes_ref[0, chunk, :, h].reshape(width, head_dim),
                log_ref.at[chunk],
                row_ref[chunk, h : h + 1, :],
                rows,
                store,
            )
            for row in range(0, height, rows):
                at = pl.ds(row, rows)
                top_ref[h, at] = jnp.maximum(
                    top_ref[h, at], lane_fold(t_ref[h, chunk, at], jnp.maximum)
                )
        return carry

    lax.fori_loop(0, chunks, score, 0)

    for h in range(heads):
        top = jnp.broadcast_to(jnp.max(top_ref[h], axis=1, keepdims=True), (height, 128))
        top_ref[h] = top
        weight = jnp.exp2(acc_ref[h] - spread(top, acc_ref.shape[2]))
        total_ref[h] = lane_fold(weight, jnp.add)
        acc_ref[h] = jnp.dot(
            weight.astype(jnp.bfloat16), fresh_ref[1, h], preferred_element_type=jnp.float32
        )

    def apply(chunk, carry):
        load(1, chunk).wait()
        for h in range(heads):
            scale = row_ref[chunk, heads + h : heads + h + 1, :]
            for row in range(0, height, rows):
                at = pl.ds(row, rows)
                weight = jnp.exp2(t_ref[h, chunk, at] - spread(top_ref[h, at], width))
                total_ref[h, at] += lane_fold(weight, jnp.add)
                p_ref[h, at] = (weight * scale).astype(jnp.bfloat16)
            acc_ref[h] += jnp.dot(
                p_ref[h],
                codes_ref[1, chunk, :, h].reshape(width, head_dim),
                preferred_element_type=jnp.float32,
            )
        return carry

    lax.fori_loop(0, chunks, apply, 0)
    for h in range(heads):
        total_ref[h] = jnp.broadcast_to(
            jnp.sum(total_ref[h], axis=1, keepdims=True), (height, 128)
        )


def route_kernel(
    dims, lists_ref, tables_ref, length_ref, own_ref, moved_ref, log_ref, row_ref
):
    pool, heads, instances, listed, block_len, spans, factor = dims
    me = lax.axis_index("inst")

    def dest(row, m):
        return lists_ref[row, m].astype(jnp.int32)

    def count(row, target):
        return loop(
            listed, lambda m, n: n + jnp.where(dest(row, m) == target, 1, 0), jnp.int32(0)
        )

    def rank(row, m):
        target = dest(row, m)
        return loop(
            listed,
            lambda m2, n: n + jnp.where((dest(row, m2) == target) & (m2 < m), 1, 0),
            jnp.int32(0),
        )

    def before(source, target):
        return loop(
            instances,
            lambda k, n: n + jnp.where(jnp.bitwise_xor(me, k) < source, count(k, target), 0),
            jnp.int32(pool),
        )

    def move(m, carry):
        moved_ref[0, m] = before(me, dest(0, m)) + rank(0, m)
        return carry

    loop(listed, move, 0)

    slots = instances * CAP
    lane = lax.broadcasted_iota(jnp.int32, (1, slots), 1)

    def place(k, ids):
        first = before(jnp.bitwise_xor(me, k), me)

        def find(m, carry):
            seen, blocks = carry
            hit = dest(k, m) == me
            block = lists_ref[k, listed + m].astype(jnp.int32)
            blocks = [jnp.where(hit & (seen == r), block, blocks[r]) for r in range(CAP)]
            return seen + jnp.where(hit, 1, 0), blocks

        seen, blocks = loop(listed, find, (jnp.int32(0), [jnp.int32(0)] * CAP))
        for r in range(CAP):
            slot = r * instances + k
            ids = jnp.where(lane == slot, jnp.where(r < seen, first + r, -1), ids)
            at = pl.ds(pl.multiple_of(slot * block_len, block_len), block_len)
            for h in range(heads):
                key = lists_ref[k, 2 * listed + h * pool + blocks[r]]
                value = lists_ref[k, 2 * listed + (heads + h) * pool + blocks[r]]
                row_ref[h : h + 1, at] = jnp.full((1, block_len), key * (factor * LOG2E))
                row_ref[heads + h : heads + h + 1, at] = jnp.full((1, block_len), value)
        return ids

    ids = loop(instances, place, jnp.full((1, slots), -1, jnp.int32))

    def store(b, value):
        log_ref[:, b * block_len : (b + 1) * block_len] = value

    count_log(tables_ref[...], length_ref[...], ids, block_len, spans, store)


def arrival_kernel(dims, places, q_ref, log_ref, row_ref, *refs):
    heads, rows, block_len = dims
    (acc_ref, top_ref, total_ref), refs = refs[:3], refs[3:]
    code_refs, (out_ref, t_ref, p_ref) = refs[:-3], refs[-3:]
    height = q_ref.shape[1]
    width = 2 * block_len
    slots = [code_refs[array].at[row] for array, row in places]
    pairs = len(slots) // 2

    def pair(i, part, h):
        return jnp.concatenate([slots[2 * i][part, h], slots[2 * i + 1][part, h]], axis=0)

    for h in range(heads):
        for i in range(pairs):
            left = i * width

            def store(row, lane, value, h=h, left=left):
                t_ref[h, row : row + rows, left + lane : left + lane + value.shape[1]] = value

            score_tiles(
                q_ref[h],
                pair(i, 0, h),
                log_ref.at[:, left : left + width],
                row_ref[h : h + 1, left : left + width],
                rows,
                store,
            )
    for h in range(heads):
        scale = row_ref[heads + h : heads + h + 1, :]
        for row in range(0, height, rows):
            at = pl.ds(row, rows)
            score = t_ref[h, at]
            own_top = top_ref[h, at]
            top = jnp.maximum(
                own_top, jnp.max(lane_fold(score, jnp.maximum), axis=1, keepdims=True)
            )
            weight = jnp.exp2(score - spread(top, score.shape[1]))
            keep = jnp.exp2(own_top - top)
            total = total_ref[h, at] * keep + jnp.sum(
                lane_fold(weight, jnp.add), axis=1, keepdims=True
            )
            p_ref[h, at] = (weight * scale).astype(jnp.bfloat16)
            t_ref[h, at, 0:128] = keep
            t_ref[h, at, 128:256] = 1.0 / total
        mixed = acc_ref[h] * t_ref[h, :, 0:128]
        for i in range(pairs):
            mixed = mixed + jnp.dot(
                p_ref[h, :, i * width : (i + 1) * width],
                pair(i, 1, h),
                preferred_element_type=jnp.float32,
            )
        result = (mixed * t_ref[h, :, 128:256]).astype(jnp.bfloat16)
        out_ref[:, h] = result.reshape(height // rows, rows, result.shape[-1])


def shards(queries, new_kv, pool_codes, pool_scales, tables, ctx_len, mig_block, mig_dest):
    instances = lax.axis_size("inst")
    pool = pool_codes.shape[0]
    requests, steps, q_heads, head_dim = queries.shape
    heads = new_kv.shape[3]
    per_head = q_heads // heads
    spans = tables.shape[1]
    block_len = pool_codes.shape[3]
    listed = mig_dest.shape[1]
    factor = head_dim ** (-0.5)
    rows = per_head * steps
    height = requests * rows
    slots = instances * CAP
    group = 8
    f32, bf16 = jnp.float32, jnp.bfloat16
    block_shape = pool_codes.shape[1:]
    block_bytes = 2 * math.prod(block_shape)
    assert instances & (instances - 1) == 0

    send = pl.pallas_call(
        functools.partial(pack_kernel, instances, listed),
        out_shape=[jax.ShapeDtypeStruct((CAP,) + block_shape, bf16)] * instances,
        in_specs=[SMEM_SPEC, SMEM_SPEC, HBM_SPEC],
        out_specs=[HBM_SPEC] * instances,
        scratch_shapes=[
            pltpu.SMEM((slots,), jnp.int32),
            pltpu.VMEM((slots,) + block_shape, bf16),
            pltpu.SemaphoreType.DMA((slots,)),
            pltpu.SemaphoreType.DMA((slots,)),
        ],
        compiler_params=pltpu.CompilerParams(vmem_limit_bytes=56 * MIB),
        cost_estimate=pl.CostEstimate(
            flops=0, bytes_accessed=2 * slots * block_bytes, transcendentals=0
        ),
        name="pack_blocks",
    )(mig_dest, mig_block, pool_codes)
    mig_dest, mig_block, pool_scales, *send = lax.optimization_barrier(
        (mig_dest, mig_block, pool_scales, *send)
    )

    def swap(value, distance):
        return lax.ppermute(value, "inst", [(j, j ^ distance) for j in range(instances)])

    arrived = [send[0]] + [swap(send[k], k) for k in range(1, instances)]
    places = [(k, r) for r in range(CAP) for k in range(instances)]

    flat_scales = jnp.transpose(pool_scales, (1, 2, 0)).reshape(1, -1).astype(f32)
    lists = jnp.concatenate([mig_dest.astype(f32), mig_block.astype(f32), flat_scales], axis=1)
    lists_in = jnp.concatenate([lists] + [swap(lists, k) for k in range(1, instances)], axis=0)

    query_rows = (
        queries.reshape(requests, steps, heads, per_head, head_dim)
        .transpose(2, 0, 3, 1, 4)
        .reshape(heads, height, head_dim)
    )
    fresh_len = requests * steps
    fresh = new_kv.transpose(2, 3, 0, 1, 4).reshape(2, heads, fresh_len, head_dim)
    fresh = jnp.pad(fresh, ((0, 0), (0, 0), (0, -fresh_len % 128), (0, 0)))
    assert fresh.shape[2] == head_dim
    length = ctx_len[:, None]
    width = group * block_len
    chunks = pool // group
    tokens = pool * block_len

    stat = (heads, height, head_dim)
    own_parts = pl.pallas_call(
        functools.partial(
            own_kernel, (pool, heads, rows, steps, block_len, spans, factor, group)
        ),
        out_shape=[jax.ShapeDtypeStruct(stat, f32)] * 3,
        in_specs=[VMEM_SPEC, VMEM_SPEC, SMEM_SPEC, VMEM_SPEC, VMEM_SPEC, HBM_SPEC],
        out_specs=[VMEM_SPEC] * 3,
        scratch_shapes=[
            pltpu.VMEM((chunks, requests, width), f32),
            pltpu.VMEM((chunks, 2 * heads, width), f32),
            pltpu.VMEM((heads, chunks, height, width), f32),
            pltpu.VMEM((heads, height, width), bf16),
            pltpu.VMEM((2, chunks, group, heads, block_len, head_dim), bf16),
            pltpu.SemaphoreType.DMA((2, chunks)),
        ],
        compiler_params=pltpu.CompilerParams(vmem_limit_bytes=48 * MIB),
        cost_estimate=pl.CostEstimate(
            flops=4 * heads * height * tokens * head_dim,
            bytes_accessed=pool_codes.size * 2,
            transcendentals=heads * height * tokens,
        ),
        name="own_blocks",
    )(tables, length, flat_scales, query_rows, fresh, pool_codes)

    moved_to, log_in, rows_in = pl.pallas_call(
        functools.partial(
            route_kernel,
            (pool, heads, instances, listed, block_len, spans, factor),
        ),
        out_shape=[
            jax.ShapeDtypeStruct((1, listed), jnp.int32),
            jax.ShapeDtypeStruct((requests, slots * block_len), f32),
            jax.ShapeDtypeStruct((2 * heads, slots * block_len), f32),
        ],
        in_specs=[SMEM_SPEC, VMEM_SPEC, VMEM_SPEC, HBM_SPEC],
        out_specs=[SMEM_SPEC, VMEM_SPEC, VMEM_SPEC],
        compiler_params=pltpu.CompilerParams(vmem_limit_bytes=8 * MIB),
        name="route_arrivals",
    )(lists_in, tables, length, own_parts[2])

    arrival_bytes = 6 * heads * height * slots * block_len + 2 * 12 * height * head_dim * heads
    arrival_bytes += 2 * slots * block_bytes
    out = pl.pallas_call(
        functools.partial(arrival_kernel, (heads, rows, block_len), places),
        out_shape=jax.ShapeDtypeStruct((requests, heads, rows, head_dim), bf16),
        in_specs=[VMEM_SPEC] * (6 + len(arrived)),
        out_specs=VMEM_SPEC,
        scratch_shapes=[
            pltpu.VMEM((heads, height, slots * block_len), f32),
            pltpu.VMEM((heads, height, slots * block_len), bf16),
        ],
        compiler_params=pltpu.CompilerParams(vmem_limit_bytes=arrival_bytes + 8 * MIB),
        cost_estimate=pl.CostEstimate(
            flops=4 * heads * height * slots * block_len * head_dim,
            bytes_accessed=slots * block_bytes,
            transcendentals=heads * height * slots * block_len,
        ),
        name="arrived_blocks",
    )(query_rows, log_in, rows_in, *own_parts, *arrived)
    out = (
        out.reshape(requests, q_heads, steps, head_dim)
        .transpose(0, 2, 1, 3)
        .reshape(requests, steps, q_heads * head_dim)
    )
    return out, moved_to


def solution(mesh):
    in_specs = (
        P(("groups", "inst"), None, "tp", None),
        P(("groups", "inst"), None, None, "tp", None),
        P(("groups", "inst"), None, "tp", None, None),
        P(("groups", "inst"), None, "tp"),
        P(("groups", "inst"), None),
        P(("groups", "inst")),
        P(("groups", "inst"), None),
        P(("groups", "inst"), None),
    )
    out_specs = (P(("groups", "inst"), None, "tp"), P(("groups", "inst"), None))
    return jax.shard_map(shards, mesh=mesh, in_specs=in_specs, out_specs=out_specs, check_vma=False)
```

time: 42.6 us -> 36.9 us (0.87)
  the two profiles are of different devices: /device:TPU:0 before, /device:TPU:8 now
where the time goes in v7:
time: 36.9 us; the launch traced here: 36.7 us
  Pallas kernels  20.2 us (55%)
  starting transfers between devices  7.59 us (21%)
  waiting for transfers between devices  7.38 us (20%)
  between operations  0.84 us (2%)
  local copies, waits for them, and re-layouts  0.55 us (1%)
    pallas_call x1, Pallas kernels, shards(): pl.pallas_call(functools.partial(own_kernel, (pool, heads, rows, steps, b...  12.6 us
    ppermute x6, starting transfers between devices, swap(): lax.ppermute(value, 'inst', [(j, j ^ distance) for j in range(instances)])  7.59 us
    ppermute x6, waiting for transfers between devices, swap(): lax.ppermute(value, 'inst', [(j, j ^ distance) for j in range(instances)])  7.38 us
    pallas_call x1, Pallas kernels, shards(): pl.pallas_call(functools.partial(pack_kernel, instances, listed), out_sha...  3.17 us
    pallas_call x1, Pallas kernels, shards(): pl.pallas_call(functools.partial(arrival_kernel, (heads, rows, block_len)...  2.83 us
    pallas_call x1, Pallas kernels, shards(): pl.pallas_call(functools.partial(route_kernel, (pool, heads, instances, l...  1.54 us
  transfers between devices with their start and end apart: 6, of which 2 were waited for; matrix products, arithmetic and copies ran while one was open for 1% of the time, Pallas kernels for 39%

profile of v7, /device:TPU:8, one launch (start us, length us, event | category | flops | bytes accessed | tf_op | source)
XLA Modules:
  0.0 36.7 jit_solution(3734294577012268726)
XLA Ops:
  0.6 0.0 copy-start.6
  0.6 0.0 copy-start.7
  0.7 0.0 copy-start.4
  0.7 0.0 copy-start.3
  0.7 0.0 copy-start.5
  0.7 0.0 copy-start.2
  0.7 0.0 copy-start.1
  0.7 3.2 %pack_blocks.1 = (bf16[2,2,2,128,128]{4,3,2,1,0:T(8,128)(2,1)}, bf16[2,2,2,128,128]{4,3,2,1,0:T(8,128)(2,1)}, bf16[2,2,2,128,128]{4,3,2,1,0:T(8,128)(2,1)}, bf16[2,2,2,128,128]{4,3,2,1,0:T(8,128)(2,1)}) custom-call(s32[1,4]{1,0:T(1,128)} %dest_ref.1, s32[1,4]{1,0:T(1,128)} %block_ref.1, bf16[48,2,2,128,128]{4,3,2,1,0:T(8,128)(2,1)} %pool_ref.3), custom_call_target="tpu_custom_call" | custom-call | bytes 2097152 | tf_op jit(solution)/shard_map/pack_blocks/pallas_call | solution.py:380
  3.9 0.0 copy-done.6
  3.9 0.0 copy-done.7
  3.9 0.0 copy-done.4
  3.9 0.1 reshape.39.scale_ref
  4.0 0.1 pad_maximum_fusion.1
  4.1 1.6 %collective-permute-start.2 = (f32[1,200]{1,0:T(1,128)S(1)}, f32[1,200]{1,0:T(1,128)S(1)}, u32[]{:S(2)}, u32[]{:S(2)}) collective-permute-start(f32[1,200]{1,0:T(1,128)S(1)} %pad_maximum_fusion.1), channel_id=1, source_target_pairs={{0,12},{4,8},{8,4},{12,0},{1,13},{5,9},{9,5},{13,1},{2,14},{6,10},... | collective-permute-start | bytes 2408 | tf_op jit(solution)/shard_map/ppermute | solution.py:402
  5.7 1.1 %collective-permute-start.1 = (f32[1,200]{1,0:T(1,128)S(1)}, f32[1,200]{1,0:T(1,128)S(1)}, u32[]{:S(2)}, u32[]{:S(2)}) collective-permute-start(f32[1,200]{1,0:T(1,128)S(1)} %pad_maximum_fusion.1), channel_id=1, source_target_pairs={{0,8},{4,12},{8,0},{12,4},{1,9},{5,13},{9,1},{13,5},{2,10},{6,14},... | collective-permute-start | bytes 2408 | tf_op jit(solution)/shard_map/ppermute | solution.py:402
  6.8 1.4 %collective-permute-start = (f32[1,200]{1,0:T(1,128)S(1)}, f32[1,200]{1,0:T(1,128)S(1)}, u32[]{:S(2)}, u32[]{:S(2)}) collective-permute-start(f32[1,200]{1,0:T(1,128)S(1)} %pad_maximum_fusion.1), channel_id=1, source_target_pairs={{0,4},{4,0},{8,12},{12,8},{1,5},{5,1},{9,13},{13,9},{2,6},{6,2},{1... | collective-permute-start | bytes 2408 | tf_op jit(solution)/shard_map/ppermute | solution.py:402
  8.1 0.6 %collective-permute-start.3 = (bf16[2,2,2,128,128]{4,3,2,1,0:T(8,128)(2,1)}, bf16[2,2,2,128,128]{4,3,2,1,0:T(8,128)(2,1)S(1)}, u32[]{:S(2)}, u32[]{:S(2)}) collective-permute-start(bf16[2,2,2,128,128]{4,3,2,1,0:T(8,128)(2,1)} %get-tuple-element.32), channel_id=1, source_target_pairs={{0,4},{4,0},{8,12},{12,8},{1,5},{5,1},{9,13},{13,9},{2,6},{6,2},{1... | collective-permute-start | bytes 786440 | tf_op jit(solution)/shard_map/ppermute | solution.py:402
  8.8 2.3 %collective-permute-start.4 = (bf16[2,2,2,128,128]{4,3,2,1,0:T(8,128)(2,1)}, bf16[2,2,2,128,128]{4,3,2,1,0:T(8,128)(2,1)S(1)}, u32[]{:S(2)}, u32[]{:S(2)}) collective-permute-start(bf16[2,2,2,128,128]{4,3,2,1,0:T(8,128)(2,1)} %get-tuple-element.33), channel_id=1, source_target_pairs={{0,8},{4,12},{8,0},{12,4},{1,9},{5,13},{9,1},{13,5},{2,10},{6,14},... | collective-permute-start | bytes 786440 | tf_op jit(solution)/shard_map/ppermute | solution.py:402
  11.1 0.0 copy-done.3
  11.1 0.1 copy.14.tables_ref
  11.2 0.0 copy-done.5
  11.2 0.1 copy.15.length_ref
  11.3 0.0 copy-done.2
  11.3 0.1 copy.11
  11.3 0.0 copy-done.1
  11.3 0.2 copy.10
  11.6 0.0 copy-start
  11.6 0.0 collective-permute-done.2
  11.6 0.6 %collective-permute-start.5 = (bf16[2,2,2,128,128]{4,3,2,1,0:T(8,128)(2,1)}, bf16[2,2,2,128,128]{4,3,2,1,0:T(8,128)(2,1)S(1)}, u32[]{:S(2)}, u32[]{:S(2)}) collective-permute-start(bf16[2,2,2,128,128]{4,3,2,1,0:T(8,128)(2,1)} %get-tuple-element.34), channel_id=1, source_target_pairs={{0,12},{4,8},{8,4},{12,0},{1,13},{5,9},{9,5},{13,1},{2,14},{6,10},... | collective-permute-start | bytes 786440 | tf_op jit(solution)/shard_map/ppermute | solution.py:402
  12.2 12.6 %own_blocks.1 = (f32[2,512,128]{2,1,0:T(8,128)S(1)}, f32[2,512,128]{2,1,0:T(8,128)S(1)}, f32[2,512,128]{2,1,0:T(8,128)S(1)}) custom-call(s32[32,16]{1,0:T(8,128)S(1)} %copy.14.tables_ref, s32[32,1]{1,0:T(8,128)S(1)} %copy.15.length_ref, f32[1,192]{1,0:T(1,128)S(1)} %reshape.39.scale_ref, bf16[2,512,128]{2,1,0:T(8,128)(2,1)S(1)} %bitcast.14, ...), custom_call_target="tpu_custom_call" | custom-call | flops 3221225472 | bytes 6291456 | tf_op jit(solution)/shard_map/own_blocks/pallas_call | solution.py:426
  24.8 0.0 collective-permute-done.1
  24.9 0.0 collective-permute-done
  24.9 0.1 pad_maximum_fusion.lists_ref
  24.9 1.5 %route_arrivals.1 = (s32[1,4]{1,0:T(1,128)}, f32[32,1024]{1,0:T(8,128)S(1)}, f32[4,1024]{1,0:T(4,128)S(1)}) custom-call(f32[4,200]{1,0:T(4,128)S(1)} %pad_maximum_fusion.lists_ref, s32[32,16]{1,0:T(8,128)S(1)} %copy.14.tables_ref, s32[32,1]{1,0:T(8,128)S(1)} %copy.15.length_ref, f32[2,512,128]{2,1,0:T(8,128)S(1)} %get-tuple-element.26.own_ref.refs_2_), custom_call_target="tpu_custom_call" | custom-call | tf_op jit(solution)/shard_map/route_arrivals/pallas_call | solution.py:450
  26.5 0.0 collective-permute-done.3.refs_4_
  26.5 2.9 %collective-permute-done.4.refs_5_ = bf16[2,2,2,128,128]{4,3,2,1,0:T(8,128)(2,1)S(1)} collective-permute-done((bf16[2,2,2,128,128]{4,3,2,1,0:T(8,128)(2,1)}, bf16[2,2,2,128,128]{4,3,2,1,0:T(8,128)(2,1)S(1)}, u32[]{:S(2)}, u32[]{:S(2)}) %collective-permute-start.4) | collective-permute-done | bytes 262176 | tf_op jit(solution)/shard_map/ppermute | solution.py:402
  29.4 4.5 %collective-permute-done.5.refs_6_ = bf16[2,2,2,128,128]{4,3,2,1,0:T(8,128)(2,1)S(1)} collective-permute-done((bf16[2,2,2,128,128]{4,3,2,1,0:T(8,128)(2,1)}, bf16[2,2,2,128,128]{4,3,2,1,0:T(8,128)(2,1)S(1)}, u32[]{:S(2)}, u32[]{:S(2)}) %collective-permute-start.5) | collective-permute-done | bytes 262176 | tf_op jit(solution)/shard_map/ppermute | solution.py:402
  33.9 0.0 copy-done
  33.9 2.8 %arrived_blocks.1 = bf16[32,2,16,128]{3,2,1,0:T(8,128)(2,1)} custom-call(bf16[2,512,128]{2,1,0:T(8,128)(2,1)S(1)} %bitcast.15, f32[32,1024]{1,0:T(8,128)S(1)} %get-tuple-element.27.log_ref, f32[4,1024]{1,0:T(4,128)S(1)} %get-tuple-element.28.row_ref, f32[2,512,128]{2,1,0:T(8,128)S(1)} %get-tuple-element.29.refs_0_, ...), custom_call_target="tpu_custom_call" | custom-call | flops 536870912 | bytes 1048576 | tf_op jit(solution)/shard_map/arrived_blocks/pallas_call | solution.py:468
  (4 shorter events, 0.0 us)
Async XLA Ops:
  0.6 3.3 %copy-start.6 = (s32[1,4]{1,0:T(1,128)S(1)}, s32[1,4]{1,0:T(1,128)}, u32[]{:S(2)}) copy-start(s32[1,4]{1,0:T(1,128)} %dest_ref.1) | copy-start | bytes 52
  0.6 3.3 %copy-start.7 = (s32[1,4]{1,0:T(1,128)S(1)}, s32[1,4]{1,0:T(1,128)}, u32[]{:S(2)}) copy-start(s32[1,4]{1,0:T(1,128)} %block_ref.1) | copy-start | bytes 52
  0.7 3.3 %copy-start.4 = (bf16[48,2,2]{0,2,1:T(2,128)(2,1)S(1)}, bf16[48,2,2]{0,2,1:T(2,128)(2,1)}, u32[]{:S(2)}) copy-start(bf16[48,2,2]{0,2,1:T(2,128)(2,1)} %param.11) | copy-start | bytes 1156
  0.7 10.4 %copy-start.3 = (s32[32,16]{0,1:T(8,128)S(1)}, s32[32,16]{0,1:T(8,128)}, u32[]{:S(2)}) copy-start(s32[32,16]{0,1:T(8,128)} %param.12) | copy-start | bytes 6148
  0.7 10.5 %copy-start.5 = (s32[32]{0:T(128)S(1)}, s32[32]{0:T(128)}, u32[]{:S(2)}) copy-start(s32[32]{0:T(128)} %param.13) | copy-start | bytes 388
  0.7 10.6 %copy-start.2 = (bf16[32,2,2,2,128]{4,3,2,1,0:T(2,128)(2,1)S(1)}, bf16[32,2,2,2,128]{4,3,2,1,0:T(2,128)(2,1)}, u32[]{:S(2)}) copy-start(bf16[32,2,2,2,128]{4,3,2,1,0:T(2,128)(2,1)} %param.9) | copy-start | bytes 196612
  0.7 10.6 %copy-start.1 = (bf16[32,2,16,128]{3,2,1,0:T(8,128)(2,1)S(1)}, bf16[32,2,16,128]{3,2,1,0:T(8,128)(2,1)}, u32[]{:S(2)}) copy-start(bf16[32,2,16,128]{3,2,1,0:T(8,128)(2,1)} %param.8) | copy-start | bytes 786436
  4.1 7.5 %collective-permute-start.2 = (f32[1,200]{1,0:T(1,128)S(1)}, f32[1,200]{1,0:T(1,128)S(1)}, u32[]{:S(2)}, u32[]{:S(2)}) collective-permute-start(f32[1,200]{1,0:T(1,128)S(1)} %pad_maximum_fusion.1), channel_id=1, source_target_pairs={{0,12},{4,8},{8,4},{12,0},{1,13},{5,9},{9,5},{13,1},{2,14},{6,10},... | collective-permute-start | bytes 2408 | tf_op jit(solution)/shard_map/ppermute | solution.py:402
  5.7 19.2 %collective-permute-start.1 = (f32[1,200]{1,0:T(1,128)S(1)}, f32[1,200]{1,0:T(1,128)S(1)}, u32[]{:S(2)}, u32[]{:S(2)}) collective-permute-start(f32[1,200]{1,0:T(1,128)S(1)} %pad_maximum_fusion.1), channel_id=1, source_target_pairs={{0,8},{4,12},{8,0},{12,4},{1,9},{5,13},{9,1},{13,5},{2,10},{6,14},... | collective-permute-start | bytes 2408 | tf_op jit(solution)/shard_map/ppermute | solution.py:402
  6.8 18.1 %collective-permute-start = (f32[1,200]{1,0:T(1,128)S(1)}, f32[1,200]{1,0:T(1,128)S(1)}, u32[]{:S(2)}, u32[]{:S(2)}) collective-permute-start(f32[1,200]{1,0:T(1,128)S(1)} %pad_maximum_fusion.1), channel_id=1, source_target_pairs={{0,4},{4,0},{8,12},{12,8},{1,5},{5,1},{9,13},{13,9},{2,6},{6,2},{1... | collective-permute-start | bytes 2408 | tf_op jit(solution)/shard_map/ppermute | solution.py:402
  8.1 18.4 %collective-permute-start.3 = (bf16[2,2,2,128,128]{4,3,2,1,0:T(8,128)(2,1)}, bf16[2,2,2,128,128]{4,3,2,1,0:T(8,128)(2,1)S(1)}, u32[]{:S(2)}, u32[]{:S(2)}) collective-permute-start(bf16[2,2,2,128,128]{4,3,2,1,0:T(8,128)(2,1)} %get-tuple-element.32), channel_id=1, source_target_pairs={{0,4},{4,0},{8,12},{12,8},{1,5},{5,1},{9,13},{13,9},{2,6},{6,2},{1... | collective-permute-start | bytes 786440 | tf_op jit(solution)/shard_map/ppermute | solution.py:402
  8.8 20.6 %collective-permute-start.4 = (bf16[2,2,2,128,128]{4,3,2,1,0:T(8,128)(2,1)}, bf16[2,2,2,128,128]{4,3,2,1,0:T(8,128)(2,1)S(1)}, u32[]{:S(2)}, u32[]{:S(2)}) collective-permute-start(bf16[2,2,2,128,128]{4,3,2,1,0:T(8,128)(2,1)} %get-tuple-element.33), channel_id=1, source_target_pairs={{0,8},{4,12},{8,0},{12,4},{1,9},{5,13},{9,1},{13,5},{2,10},{6,14},... | collective-permute-start | bytes 786440 | tf_op jit(solution)/shard_map/ppermute | solution.py:402
  11.6 22.3 %copy-start = (bf16[2,2,2,128,128]{4,3,2,1,0:T(8,128)(2,1)S(1)}, bf16[2,2,2,128,128]{4,3,2,1,0:T(8,128)(2,1)}, u32[]{:S(2)}) copy-start(bf16[2,2,2,128,128]{4,3,2,1,0:T(8,128)(2,1)} %get-tuple-element.31.refs_3_) | copy-start | bytes 786436
  11.6 22.3 %collective-permute-start.5 = (bf16[2,2,2,128,128]{4,3,2,1,0:T(8,128)(2,1)}, bf16[2,2,2,128,128]{4,3,2,1,0:T(8,128)(2,1)S(1)}, u32[]{:S(2)}, u32[]{:S(2)}) collective-permute-start(bf16[2,2,2,128,128]{4,3,2,1,0:T(8,128)(2,1)} %get-tuple-element.34), channel_id=1, source_target_pairs={{0,12},{4,8},{8,4},{12,0},{1,13},{5,9},{9,5},{13,1},{2,14},{6,10},... | collective-permute-start | bytes 786440 | tf_op jit(solution)/shard_map/ppermute | solution.py:402

commit v8 on v7

--- a/solution.py
+++ b/solution.py
@@ -9,6 +9,7 @@
 from jax.sharding import PartitionSpec as P
 
 CAP = 2
+EXTRA = 16
 LOG2E = math.log2(math.e)
 MIB = 1 << 20
 SMEM_SPEC = pl.BlockSpec(memory_space=pltpu.SMEM)
@@ -25,9 +26,14 @@
     return lax.fori_loop(0, count, body, init)
 
 
-def pack_kernel(instances, listed, dest_ref, block_ref, pool_ref, *refs):
-    send_refs, (index_ref, held_ref, in_sems, out_sems) = refs[:instances], refs[instances:]
+def pack_kernel(dims, dest_ref, block_ref, scale_ref, pool_ref, *refs):
+    instances, listed, heads, pool = dims
+    send_refs, (index_ref, extra_ref, held_ref, in_sems, out_sems) = (
+        refs[:instances],
+        refs[instances:],
+    )
     slots = instances * CAP
+    code_rows = held_ref.shape[1] - EXTRA
     me = lax.axis_index("inst")
     for slot in range(slots):
         index_ref[slot] = 0
@@ -47,9 +53,32 @@
     loads, stores = {}, []
     for i in order:
         loads[i] = pltpu.make_async_copy(
-            pool_ref.at[index_ref[i]], held_ref.at[i], in_sems.at[i]
+            pool_ref.at[index_ref[i]], held_ref.at[i, pl.ds(0, code_rows)], in_sems.at[i]
         )
         loads[i].start()
+    lane = lax.broadcasted_iota(jnp.int32, (1, 128), 1)
+
+    def spell(m, row):
+        return jnp.where(lane == m, dest_ref[0, m].astype(jnp.float32), row)
+
+    extra_ref[...] = jnp.zeros_like(extra_ref)
+    extra_ref[2 * heads : 2 * heads + 1, :] = loop(
+        listed, spell, jnp.zeros((1, 128), jnp.float32)
+    )
+    scales = [
+        [scale_ref[part, h : h + 1, :].astype(jnp.float32) for h in range(heads)]
+        for part in range(2)
+    ]
+    column = lax.broadcasted_iota(jnp.int32, (1, pool), 1)
+    for i in order:
+        for part in range(2):
+            for h in range(heads):
+                one = jnp.where(column == index_ref[i], scales[part][h], 0.0)
+                row = part * heads + h
+                extra_ref[row : row + 1, :] = jnp.broadcast_to(
+                    jnp.sum(one, axis=1, keepdims=True), (1, 128)
+                )
+        held_ref[i, pl.ds(code_rows, EXTRA)] = extra_ref[...].astype(jnp.bfloat16)
     for i in order:
         loads[i].wait()
         stores.append(
@@ -140,10 +169,11 @@
     chunks = pool // group
     height, head_dim = q_ref.shape[1:]
     width = group * block_len
+    part_rows = heads * block_len
 
     def load(part, chunk):
         return pltpu.make_async_copy(
-            pool_ref.at[pl.ds(chunk * group, group), part],
+            pool_ref.at[pl.ds(chunk * group, group), pl.ds(part * part_rows, part_rows)],
             codes_ref.at[part, chunk],
             sems.at[part, chunk],
         )
@@ -188,7 +218,7 @@
 
             score_tiles(
                 q_ref[h],
-                codes_ref[0, chunk, :, h].reshape(width, head_dim),
+                codes_ref[0, chunk, :, h * block_len : (h + 1) * block_len].reshape(width, head_dim),
                 log_ref.at[chunk],
                 row_ref[chunk, h : h + 1, :],
                 rows,
@@ -223,7 +253,7 @@
                 p_ref[h, at] = (weight * scale).astype(jnp.bfloat16)
             acc_ref[h] += jnp.dot(
                 p_ref[h],
-                codes_ref[1, chunk, :, h].reshape(width, head_dim),
+                codes_ref[1, chunk, :, h * block_len : (h + 1) * block_len].reshape(width, head_dim),
                 preferred_element_type=jnp.float32,
             )
         return carry
@@ -235,87 +265,68 @@
         )
 
 
-def route_kernel(
-    dims, lists_ref, tables_ref, length_ref, own_ref, moved_ref, log_ref, row_ref
-):
-    pool, heads, instances, listed, block_len, spans, factor = dims
-    me = lax.axis_index("inst")
-
-    def dest(row, m):
-        return lists_ref[row, m].astype(jnp.int32)
-
-    def count(row, target):
-        return loop(
-            listed, lambda m, n: n + jnp.where(dest(row, m) == target, 1, 0), jnp.int32(0)
-        )
-
-    def rank(row, m):
-        target = dest(row, m)
-        return loop(
-            listed,
-            lambda m2, n: n + jnp.where((dest(row, m2) == target) & (m2 < m), 1, 0),
-            jnp.int32(0),
-        )
-
-    def before(source, target):
-        return loop(
-            instances,
-            lambda k, n: n + jnp.where(jnp.bitwise_xor(me, k) < source, count(k, target), 0),
-            jnp.int32(pool),
-        )
-
-    def move(m, carry):
-        moved_ref[0, m] = before(me, dest(0, m)) + rank(0, m)
-        return carry
-
-    loop(listed, move, 0)
-
-    slots = instances * CAP
-    lane = lax.broadcasted_iota(jnp.int32, (1, slots), 1)
-
-    def place(k, ids):
-        first = before(jnp.bitwise_xor(me, k), me)
-
-        def find(m, carry):
-            seen, blocks = carry
-            hit = dest(k, m) == me
-            block = lists_ref[k, listed + m].astype(jnp.int32)
-            blocks = [jnp.where(hit & (seen == r), block, blocks[r]) for r in range(CAP)]
-            return seen + jnp.where(hit, 1, 0), blocks
-
-        seen, blocks = loop(listed, find, (jnp.int32(0), [jnp.int32(0)] * CAP))
+def arrival_ids(me, pool, lists, listed):
+    instances = len(lists)
+    lane = lax.broadcasted_iota(jnp.int32, (1, 128), 1)
+    counts = [
+        jnp.sum(
+            jnp.where((row == me.astype(jnp.float32)) & (lane < listed), 1.0, 0.0),
+            axis=1,
+            keepdims=True,
+        )
+        for row in lists
+    ]
+    slot = lax.broadcasted_iota(jnp.int32, (1, instances * CAP), 1)
+    ids = jnp.full(slot.shape, -1.0)
+    for k in range(instances):
+        first = jnp.full((1, 1), float(pool))
+        for j in range(instances):
+            lower = jnp.bitwise_xor(me, j) < jnp.bitwise_xor(me, k)
+            first = first + jnp.where(lower, counts[j], 0.0)
         for r in range(CAP):
-            slot = r * instances + k
-            ids = jnp.where(lane == slot, jnp.where(r < seen, first + r, -1), ids)
-            at = pl.ds(pl.multiple_of(slot * block_len, block_len), block_len)
-            for h in range(heads):
-                key = lists_ref[k, 2 * listed + h * pool + blocks[r]]
-                value = lists_ref[k, 2 * listed + (heads + h) * pool + blocks[r]]
-                row_ref[h : h + 1, at] = jnp.full((1, block_len), key * (factor * LOG2E))
-                row_ref[heads + h : heads + h + 1, at] = jnp.full((1, block_len), value)
-        return ids
-
-    ids = loop(instances, place, jnp.full((1, slots), -1, jnp.int32))
-
-    def store(b, value):
-        log_ref[:, b * block_len : (b + 1) * block_len] = value
-
-    count_log(tables_ref[...], length_ref[...], ids, block_len, spans, store)
-
-
-def arrival_kernel(dims, places, q_ref, log_ref, row_ref, *refs):
-    heads, rows, block_len = dims
-    (acc_ref, top_ref, total_ref), refs = refs[:3], refs[3:]
-    code_refs, (out_ref, t_ref, p_ref) = refs[:-3], refs[-3:]
+            name = jnp.where(counts[k] > r, first + r, -1.0)
+            ids = jnp.where(slot == r * instances + k, jnp.broadcast_to(name, slot.shape), ids)
+    moved = jnp.full((1, 128), float(pool))
+    for j in range(instances):
+        for m in range(listed):
+            same = jnp.broadcast_to(lists[j][:, m : m + 1], (1, 128)) == lists[0]
+            ahead = jnp.bitwise_xor(me, j) < me if j else lane > m
+            moved = moved + jnp.where(same & ahead, 1.0, 0.0)
+    return ids.astype(jnp.int32), moved[:, :listed].astype(jnp.int32)
+
+
+def arrival_kernel(dims, q_ref, tables_ref, length_ref, acc_ref, top_ref, total_ref, *refs):
+    pool, heads, rows, block_len, spans, listed, factor = dims
+    code_refs, (out_ref, moved_ref, log_ref, t_ref, p_ref) = refs[:-5], refs[-5:]
+    instances = len(code_refs)
     height = q_ref.shape[1]
     width = 2 * block_len
-    slots = [code_refs[array].at[row] for array, row in places]
+    extra = 2 * heads * block_len
+    slots = [(ref, r) for r in range(CAP) for ref in code_refs]
     pairs = len(slots) // 2
 
     def pair(i, part, h):
-        return jnp.concatenate([slots[2 * i][part, h], slots[2 * i + 1][part, h]], axis=0)
-
+        at = pl.ds((part * heads + h) * block_len, block_len)
+        return jnp.concatenate([ref[r, at] for ref, r in slots[2 * i : 2 * i + 2]], axis=0)
+
+    lists, scale_rows = [], []
+    for ref, r in slots:
+        values = ref[r, pl.ds(extra, EXTRA)].astype(jnp.float32)
+        scale_rows.append(values)
+        if r == 0:
+            lists.append(values[2 * heads : 2 * heads + 1])
+
+    def scale_row(row):
+        return jnp.concatenate([values[row : row + 1] for values in scale_rows], axis=1)
+
+    ids, moved_ref[...] = arrival_ids(lax.axis_index("inst"), pool, lists, listed)
+
+    def store_log(b, value):
+        log_ref[:, b * block_len : (b + 1) * block_len] = value
+
+    count_log(tables_ref[...], length_ref[...], ids, block_len, spans, store_log)
     for h in range(heads):
+        key_scale = scale_row(h) * (factor * LOG2E)
         for i in range(pairs):
             left = i * width
 
@@ -326,12 +337,12 @@
                 q_ref[h],
                 pair(i, 0, h),
                 log_ref.at[:, left : left + width],
-                row_ref[h : h + 1, left : left + width],
+                key_scale[:, left : left + width],
                 rows,
                 store,
             )
     for h in range(heads):
-        scale = row_ref[heads + h : heads + h + 1, :]
+        scale = scale_row(heads + h)
         for row in range(0, height, rows):
             at = pl.ds(row, rows)
             score = t_ref[h, at]
@@ -373,40 +384,38 @@
     slots = instances * CAP
     group = 8
     f32, bf16 = jnp.float32, jnp.bfloat16
-    block_shape = pool_codes.shape[1:]
-    block_bytes = 2 * math.prod(block_shape)
-    assert instances & (instances - 1) == 0
+    code_rows = 2 * heads * block_len
+    pool_rows = pool_codes.reshape(pool, code_rows, head_dim)
+    sent_shape = (CAP, code_rows + EXTRA, head_dim)
+    sent_bytes = 2 * math.prod(sent_shape)
+    part_scales = jnp.transpose(pool_scales, (1, 2, 0))
+    assert instances & (instances - 1) == 0 and 2 * heads < EXTRA and head_dim == 128
 
     send = pl.pallas_call(
-        functools.partial(pack_kernel, instances, listed),
-        out_shape=[jax.ShapeDtypeStruct((CAP,) + block_shape, bf16)] * instances,
-        in_specs=[SMEM_SPEC, SMEM_SPEC, HBM_SPEC],
+        functools.partial(pack_kernel, (instances, listed, heads, pool)),
+        out_shape=[jax.ShapeDtypeStruct(sent_shape, bf16)] * instances,
+        in_specs=[SMEM_SPEC, SMEM_SPEC, VMEM_SPEC, HBM_SPEC],
         out_specs=[HBM_SPEC] * instances,
         scratch_shapes=[
             pltpu.SMEM((slots,), jnp.int32),
-            pltpu.VMEM((slots,) + block_shape, bf16),
+            pltpu.VMEM((EXTRA, head_dim), f32),
+            pltpu.VMEM((slots,) + sent_shape[1:], bf16),
             pltpu.SemaphoreType.DMA((slots,)),
             pltpu.SemaphoreType.DMA((slots,)),
         ],
         compiler_params=pltpu.CompilerParams(vmem_limit_bytes=56 * MIB),
         cost_estimate=pl.CostEstimate(
-            flops=0, bytes_accessed=2 * slots * block_bytes, transcendentals=0
+            flops=0, bytes_accessed=2 * instances * sent_bytes, transcendentals=0
         ),
         name="pack_blocks",
-    )(mig_dest, mig_block, pool_codes)
-    mig_dest, mig_block, pool_scales, *send = lax.optimization_barrier(
-        (mig_dest, mig_block, pool_scales, *send)
-    )
+    )(mig_dest, mig_block, part_scales, pool_rows)
+    part_scales, *send = lax.optimization_barrier((part_scales, *send))
 
     def swap(value, distance):
         return lax.ppermute(value, "inst", [(j, j ^ distance) for j in range(instances)])
 
     arrived = [send[0]] + [swap(send[k], k) for k in range(1, instances)]
-    places = [(k, r) for r in range(CAP) for k in range(instances)]
-
-    flat_scales = jnp.transpose(pool_scales, (1, 2, 0)).reshape(1, -1).astype(f32)
-    lists = jnp.concatenate([mig_dest.astype(f32), mig_block.astype(f32), flat_scales], axis=1)
-    lists_in = jnp.concatenate([lists] + [swap(lists, k) for k in range(1, instances)], axis=0)
+    flat_scales = part_scales.reshape(1, -1).astype(f32)
 
     query_rows = (
         queries.reshape(requests, steps, heads, per_head, head_dim)
@@ -435,7 +444,7 @@
             pltpu.VMEM((chunks, 2 * heads, width), f32),
             pltpu.VMEM((heads, chunks, height, width), f32),
             pltpu.VMEM((heads, height, width), bf16),
-            pltpu.VMEM((2, chunks, group, heads, block_len, head_dim), bf16),
+            pltpu.VMEM((2, chunks, group, heads * block_len, head_dim), bf16),
             pltpu.SemaphoreType.DMA((2, chunks)),
         ],
         compiler_params=pltpu.CompilerParams(vmem_limit_bytes=48 * MIB),
@@ -445,43 +454,33 @@
             transcendentals=heads * height * tokens,
         ),
         name="own_blocks",
-    )(tables, length, flat_scales, query_rows, fresh, pool_codes)
-
-    moved_to, log_in, rows_in = pl.pallas_call(
+    )(tables, length, flat_scales, query_rows, fresh, pool_rows)
+
+    arrival_bytes = 6 * heads * height * slots * block_len + 2 * 12 * height * head_dim * heads
+    arrival_bytes += 2 * instances * sent_bytes + 4 * requests * slots * block_len
+    out, moved_to = pl.pallas_call(
         functools.partial(
-            route_kernel,
-            (pool, heads, instances, listed, block_len, spans, factor),
+            arrival_kernel, (pool, heads, rows, block_len, spans, listed, factor)
         ),
         out_shape=[
+            jax.ShapeDtypeStruct((requests, heads, rows, head_dim), bf16),
             jax.ShapeDtypeStruct((1, listed), jnp.int32),
-            jax.ShapeDtypeStruct((requests, slots * block_len), f32),
-            jax.ShapeDtypeStruct((2 * heads, slots * block_len), f32),
         ],
-        in_specs=[SMEM_SPEC, VMEM_SPEC, VMEM_SPEC, HBM_SPEC],
-        out_specs=[SMEM_SPEC, VMEM_SPEC, VMEM_SPEC],
-        compiler_params=pltpu.CompilerParams(vmem_limit_bytes=8 * MIB),
-        name="route_arrivals",
-    )(lists_in, tables, length, own_parts[2])
-
-    arrival_bytes = 6 * heads * height * slots * block_len + 2 * 12 * height * head_dim * heads
-    arrival_bytes += 2 * slots * block_bytes
-    out = pl.pallas_call(
-        functools.partial(arrival_kernel, (heads, rows, block_len), places),
-        out_shape=jax.ShapeDtypeStruct((requests, heads, rows, head_dim), bf16),
-        in_specs=[VMEM_SPEC] * (6 + len(arrived)),
-        out_specs=VMEM_SPEC,
+        in_specs=[VMEM_SPEC] * (6 + instances),
+        out_specs=[VMEM_SPEC, VMEM_SPEC],
         scratch_shapes=[
+            pltpu.VMEM((requests, slots * block_len), f32),
             pltpu.VMEM((heads, height, slots * block_len), f32),
             pltpu.VMEM((heads, height, slots * block_len), bf16),
         ],
         compiler_params=pltpu.CompilerParams(vmem_limit_bytes=arrival_bytes + 8 * MIB),
         cost_estimate=pl.CostEstimate(
             flops=4 * heads * height * slots * block_len * head_dim,
-            bytes_accessed=slots * block_bytes,
+            bytes_accessed=instances * sent_bytes,
             transcendentals=heads * height * slots * block_len,
         ),
         name="arrived_blocks",
-    )(query_rows, log_in, rows_in, *own_parts, *arrived)
+    )(query_rows, tables, length, *own_parts, *arrived)
     out = (
         out.reshape(requests, q_heads, steps, head_dim)
         .transpose(0, 2, 1, 3)

time: 36.9 us -> 34.1 us (0.924)
  starting transfers between devices: 7.59 us -> 3.55 us
  waiting for transfers between devices: 7.38 us -> 10.3 us
  Pallas kernels: 20.2 us -> 18.7 us
    ppermute x6 -> x3, starting transfers between devices: 7.59 us -> 3.55 us  [swap(): lax.ppermute(value, 'inst', [(j, j ^ distance) for j in range(instances)])]
    ppermute x6 -> x3, waiting for transfers between devices: 7.38 us -> 10.3 us  [swap(): lax.ppermute(value, 'inst', [(j, j ^ distance) for j in range(instances)])]
    pallas_call x3 -> x2, Pallas kernels: 7.54 us -> 6.09 us  [the longest x1 3.18 us: shards(): pl.pallas_call(functools.partial(pack_kernel, (instances, listed, heads,...]
  transfers between devices with their start and end apart: 6 -> 3, of which waited for: 2 -> 2; matrix products, arithmetic and copies ran while one was open for 1% -> 2% of each run, Pallas kernels for 39% -> 37%
where the time goes in v8:
time: 34.1 us; the launch traced here: 33.9 us
  Pallas kernels  18.7 us (55%)
  waiting for transfers between devices  10.3 us (30%)
  starting transfers between devices  3.55 us (10%)
  between operations  0.75 us (2%)
  local copies, waits for them, and re-layouts  0.54 us (2%)
    pallas_call x1, Pallas kernels, shards(): pl.pallas_call(functools.partial(own_kernel, (pool, heads, rows, steps, b...  12.7 us
    ppermute x3, waiting for transfers between devices, swap(): lax.ppermute(value, 'inst', [(j, j ^ distance) for j in range(instances)])  10.3 us
    ppermute x3, starting transfers between devices, swap(): lax.ppermute(value, 'inst', [(j, j ^ distance) for j in range(instances)])  3.55 us
    pallas_call x1, Pallas kernels, shards(): pl.pallas_call(functools.partial(pack_kernel, (instances, listed, heads,...  3.18 us
    pallas_call x1, Pallas kernels, shards(): pl.pallas_call(functools.partial(arrival_kernel, (pool, heads, rows, bloc...  2.91 us
  transfers between devices with their start and end apart: 3, of which 2 were waited for; matrix products, arithmetic and copies ran while one was open for 2% of the time, Pallas kernels for 37%

profile of v8, /device:TPU:8, one launch (start us, length us, event | category | flops | bytes accessed | tf_op | source)
XLA Modules:
  0.0 33.9 jit_solution(12211219848695773815)
XLA Ops:
  0.6 0.0 copy-start.4
  0.6 0.0 copy-start.3
  0.7 0.0 copy-start.5
  0.7 0.0 copy-start.2
  0.7 0.0 copy-start.1
  0.7 3.2 %pack_blocks.1 = (bf16[2,528,128]{2,1,0:T(8,128)(2,1)}, bf16[2,528,128]{2,1,0:T(8,128)(2,1)}, bf16[2,528,128]{2,1,0:T(8,128)(2,1)}, bf16[2,528,128]{2,1,0:T(8,128)(2,1)}) custom-call(s32[1,4]{1,0:T(1,128)} %dest_ref.1, s32[1,4]{1,0:T(1,128)} %block_ref.1, bf16[2,2,48]{2,1,0:T(2,128)(2,1)} %bitcast.21, bf16[48,512,128]{2,1,0:T(8,128)(2,1)} %bitcast.16), custom_call_target="tpu_custom_call" | custom-call | bytes 2162688 | tf_op jit(solution)/shard_map/pack_blocks/pallas_call | solution.py:394
  3.9 0.1 collective-permute-start
  3.9 2.8 %collective-permute-start.1 = (bf16[2,528,128]{2,1,0:T(8,128)(2,1)}, bf16[2,528,128]{2,1,0:T(8,128)(2,1)S(1)}, u32[]{:S(2)}, u32[]{:S(2)}) collective-permute-start(bf16[2,528,128]{2,1,0:T(8,128)(2,1)} %get-tuple-element.26), channel_id=1, source_target_pairs={{0,8},{4,12},{8,0},{12,4},{1,9},{5,13},{9,1},{13,5},{2,10},{6,14},... | collective-permute-start | bytes 811016 | tf_op jit(solution)/shard_map/ppermute | solution.py:415
  6.7 0.7 %collective-permute-start.2 = (bf16[2,528,128]{2,1,0:T(8,128)(2,1)}, bf16[2,528,128]{2,1,0:T(8,128)(2,1)S(1)}, u32[]{:S(2)}, u32[]{:S(2)}) collective-permute-start(bf16[2,528,128]{2,1,0:T(8,128)(2,1)} %get-tuple-element.27), channel_id=1, source_target_pairs={{0,12},{4,8},{8,4},{12,0},{1,13},{5,9},{9,5},{13,1},{2,14},{6,10},... | collective-permute-start | bytes 811016 | tf_op jit(solution)/shard_map/ppermute | solution.py:415
  7.4 0.0 copy-done.3
  7.4 0.1 copy.14.tables_ref
  7.5 0.0 copy-done.5
  7.5 0.1 copy.15.length_ref
  7.6 0.0 copy-done.2
  7.6 0.1 copy.11
  7.7 0.0 copy-done.1
  7.7 0.0 copy-start
  7.7 0.2 copy.10
  7.9 0.0 copy-done.4
  7.9 0.1 reshape.43.scale_ref
  8.0 12.7 %own_blocks.1 = (f32[2,512,128]{2,1,0:T(8,128)S(1)}, f32[2,512,128]{2,1,0:T(8,128)S(1)}, f32[2,512,128]{2,1,0:T(8,128)S(1)}) custom-call(s32[32,16]{1,0:T(8,128)S(1)} %copy.14.tables_ref, s32[32,1]{1,0:T(8,128)S(1)} %copy.15.length_ref, f32[1,192]{1,0:T(1,128)S(1)} %reshape.43.scale_ref, bf16[2,512,128]{2,1,0:T(8,128)(2,1)S(1)} %bitcast.14, ...), custom_call_target="tpu_custom_call" | custom-call | flops 3221225472 | bytes 6291456 | tf_op jit(solution)/shard_map/own_blocks/pallas_call | solution.py:435
  20.7 0.0 collective-permute-done.refs_1_
  20.7 4.9 %collective-permute-done.1.refs_2_ = bf16[2,528,128]{2,1,0:T(8,128)(2,1)S(1)} collective-permute-done((bf16[2,528,128]{2,1,0:T(8,128)(2,1)}, bf16[2,528,128]{2,1,0:T(8,128)(2,1)S(1)}, u32[]{:S(2)}, u32[]{:S(2)}) %collective-permute-start.1) | collective-permute-done | bytes 270368 | tf_op jit(solution)/shard_map/ppermute | solution.py:415
  25.6 5.4 %collective-permute-done.2.refs_3_ = bf16[2,528,128]{2,1,0:T(8,128)(2,1)S(1)} collective-permute-done((bf16[2,528,128]{2,1,0:T(8,128)(2,1)}, bf16[2,528,128]{2,1,0:T(8,128)(2,1)S(1)}, u32[]{:S(2)}, u32[]{:S(2)}) %collective-permute-start.2) | collective-permute-done | bytes 270368 | tf_op jit(solution)/shard_map/ppermute | solution.py:415
  31.0 0.0 copy-done
  31.0 2.9 %arrived_blocks.1 = (bf16[32,2,16,128]{3,2,1,0:T(8,128)(2,1)}, s32[1,4]{1,0:T(1,128)}) custom-call(bf16[2,512,128]{2,1,0:T(8,128)(2,1)S(1)} %bitcast.15, s32[32,16]{1,0:T(8,128)S(1)} %copy.14.tables_ref, s32[32,1]{1,0:T(8,128)S(1)} %copy.15.length_ref, f32[2,512,128]{2,1,0:T(8,128)S(1)} %get-tuple-element.21.acc_ref, ...), custom_call_target="tpu_custom_call" | custom-call | flops 536870912 | bytes 1081344 | tf_op jit(solution)/shard_map/arrived_blocks/pallas_call | solution.py:461
  (1 shorter events, 0.0 us)
Async XLA Ops:
  0.6 7.3 %copy-start.4 = (bf16[48,2,2]{0,2,1:T(2,128)(2,1)S(1)}, bf16[48,2,2]{0,2,1:T(2,128)(2,1)}, u32[]{:S(2)}) copy-start(bf16[48,2,2]{0,2,1:T(2,128)(2,1)} %param.11) | copy-start | bytes 1156
  0.6 6.8 %copy-start.3 = (s32[32,16]{0,1:T(8,128)S(1)}, s32[32,16]{0,1:T(8,128)}, u32[]{:S(2)}) copy-start(s32[32,16]{0,1:T(8,128)} %param.12) | copy-start | bytes 6148
  0.7 6.9 %copy-start.5 = (s32[32]{0:T(128)S(1)}, s32[32]{0:T(128)}, u32[]{:S(2)}) copy-start(s32[32]{0:T(128)} %param.13) | copy-start | bytes 388
  0.7 6.9 %copy-start.2 = (bf16[32,2,2,2,128]{4,3,2,1,0:T(2,128)(2,1)S(1)}, bf16[32,2,2,2,128]{4,3,2,1,0:T(2,128)(2,1)}, u32[]{:S(2)}) copy-start(bf16[32,2,2,2,128]{4,3,2,1,0:T(2,128)(2,1)} %param.9) | copy-start | bytes 196612
  0.7 7.0 %copy-start.1 = (bf16[32,2,16,128]{3,2,1,0:T(8,128)(2,1)S(1)}, bf16[32,2,16,128]{3,2,1,0:T(8,128)(2,1)}, u32[]{:S(2)}) copy-start(bf16[32,2,16,128]{3,2,1,0:T(8,128)(2,1)} %param.8) | copy-start | bytes 786436
  3.9 16.8 %collective-permute-start = (bf16[2,528,128]{2,1,0:T(8,128)(2,1)}, bf16[2,528,128]{2,1,0:T(8,128)(2,1)S(1)}, u32[]{:S(2)}, u32[]{:S(2)}) collective-permute-start(bf16[2,528,128]{2,1,0:T(8,128)(2,1)} %get-tuple-element.25), channel_id=1, source_target_pairs={{0,4},{4,0},{8,12},{12,8},{1,5},{5,1},{9,13},{13,9},{2,6},{6,2},{1... | collective-permute-start | bytes 811016 | tf_op jit(solution)/shard_map/ppermute | solution.py:415
  3.9 21.6 %collective-permute-start.1 = (bf16[2,528,128]{2,1,0:T(8,128)(2,1)}, bf16[2,528,128]{2,1,0:T(8,128)(2,1)S(1)}, u32[]{:S(2)}, u32[]{:S(2)}) collective-permute-start(bf16[2,528,128]{2,1,0:T(8,128)(2,1)} %get-tuple-element.26), channel_id=1, source_target_pairs={{0,8},{4,12},{8,0},{12,4},{1,9},{5,13},{9,1},{13,5},{2,10},{6,14},... | collective-permute-start | bytes 811016 | tf_op jit(solution)/shard_map/ppermute | solution.py:415
  6.7 24.2 %collective-permute-start.2 = (bf16[2,528,128]{2,1,0:T(8,128)(2,1)}, bf16[2,528,128]{2,1,0:T(8,128)(2,1)S(1)}, u32[]{:S(2)}, u32[]{:S(2)}) collective-permute-start(bf16[2,528,128]{2,1,0:T(8,128)(2,1)} %get-tuple-element.27), channel_id=1, source_target_pairs={{0,12},{4,8},{8,4},{12,0},{1,13},{5,9},{9,5},{13,1},{2,14},{6,10},... | collective-permute-start | bytes 811016 | tf_op jit(solution)/shard_map/ppermute | solution.py:415
  7.7 23.3 %copy-start = (bf16[2,528,128]{2,1,0:T(8,128)(2,1)S(1)}, bf16[2,528,128]{2,1,0:T(8,128)(2,1)}, u32[]{:S(2)}) copy-start(bf16[2,528,128]{2,1,0:T(8,128)(2,1)} %get-tuple-element.24.refs_0_) | copy-start | bytes 811012

commit v9 on v8

--- a/solution.py
+++ b/solution.py
@@ -27,16 +27,12 @@
 
 
 def pack_kernel(dims, dest_ref, block_ref, scale_ref, pool_ref, *refs):
-    instances, listed, heads, pool = dims
-    send_refs, (index_ref, extra_ref, held_ref, in_sems, out_sems) = (
-        refs[:instances],
-        refs[instances:],
-    )
-    slots = instances * CAP
+    instances, listed, heads, pool, copies = dims
+    send_refs, (index_ref, extra_ref, held_ref, in_sems, out_sems) = refs[:-5], refs[-5:]
     code_rows = held_ref.shape[1] - EXTRA
     me = lax.axis_index("inst")
-    for slot in range(slots):
-        index_ref[slot] = 0
+    for entry in range(CAP * instances + 1):
+        index_ref[entry] = 0
 
     def place(m, carry):
         dest = dest_ref[0, m]
@@ -45,15 +41,18 @@
             lambda m2, n: n + jnp.where((dest_ref[0, m2] == dest) & (m2 < m), 1, 0),
             jnp.int32(0),
         )
-        index_ref[jnp.bitwise_xor(dest, me) * CAP + jnp.minimum(rank, CAP - 1)] = block_ref[0, m]
+        entry = jnp.bitwise_xor(dest, me) + jnp.where(rank > 0, instances, 0)
+        index_ref[entry] = block_ref[0, m]
+        index_ref[jnp.where(rank > 0, CAP * instances, entry)] = block_ref[0, m]
         return carry
 
     loop(listed, place, 0)
-    order = list(range(slots))[::-1]
-    loads, stores = {}, []
-    for i in order:
-        loads[i] = pltpu.make_async_copy(
-            pool_ref.at[index_ref[i]], held_ref.at[i, pl.ds(0, code_rows)], in_sems.at[i]
+    loads, stores = [], []
+    for i, (entry, _) in enumerate(copies):
+        loads.append(
+            pltpu.make_async_copy(
+                pool_ref.at[index_ref[entry]], held_ref.at[i, pl.ds(0, code_rows)], in_sems.at[i]
+            )
         )
         loads[i].start()
     lane = lax.broadcasted_iota(jnp.int32, (1, 128), 1)
@@ -70,23 +69,24 @@
         for part in range(2)
     ]
     column = lax.broadcasted_iota(jnp.int32, (1, pool), 1)
-    for i in order:
+    for i, (entry, _) in enumerate(copies):
         for part in range(2):
             for h in range(heads):
-                one = jnp.where(column == index_ref[i], scales[part][h], 0.0)
+                one = jnp.where(column == index_ref[entry], scales[part][h], 0.0)
                 row = part * heads + h
                 extra_ref[row : row + 1, :] = jnp.broadcast_to(
                     jnp.sum(one, axis=1, keepdims=True), (1, 128)
                 )
         held_ref[i, pl.ds(code_rows, EXTRA)] = extra_ref[...].astype(jnp.bfloat16)
-    for i in order:
+    for i, (_, targets) in enumerate(copies):
         loads[i].wait()
-        stores.append(
-            pltpu.make_async_copy(
-                held_ref.at[i], send_refs[i // CAP].at[i % CAP], out_sems.at[i]
-            )
-        )
-        stores[-1].start()
+        for output, row in targets:
+            stores.append(
+                pltpu.make_async_copy(
+                    held_ref.at[i], send_refs[output].at[row], out_sems.at[len(stores)]
+                )
+            )
+            stores[-1].start()
     for store in stores:
         store.wait()
 
@@ -292,17 +292,23 @@
             same = jnp.broadcast_to(lists[j][:, m : m + 1], (1, 128)) == lists[0]
             ahead = jnp.bitwise_xor(me, j) < me if j else lane > m
             moved = moved + jnp.where(same & ahead, 1.0, 0.0)
-    return ids.astype(jnp.int32), moved[:, :listed].astype(jnp.int32)
-
-
-def arrival_kernel(dims, q_ref, tables_ref, length_ref, acc_ref, top_ref, total_ref, *refs):
+    more = jnp.zeros((1, 128))
+    for row in lists:
+        again = jnp.zeros((1, 128))
+        for m in range(listed):
+            same = jnp.broadcast_to(row[:, m : m + 1], (1, 128)) == row
+            again = again + jnp.where(same & (lane > m) & (lane < listed), 1.0, 0.0)
+        more = jnp.maximum(more, jnp.sum(again, axis=1, keepdims=True))
+    return ids.astype(jnp.int32), moved[:, :listed].astype(jnp.int32), more
+
+
+def arrival_kernel(dims, places, q_ref, tables_ref, length_ref, acc_ref, top_ref, total_ref, *refs):
     pool, heads, rows, block_len, spans, listed, factor = dims
-    code_refs, (out_ref, moved_ref, log_ref, t_ref, p_ref) = refs[:-5], refs[-5:]
-    instances = len(code_refs)
+    code_refs, (out_ref, moved_ref, more_ref, log_ref, t_ref, p_ref) = refs[:-6], refs[-6:]
     height = q_ref.shape[1]
     width = 2 * block_len
     extra = 2 * heads * block_len
-    slots = [(ref, r) for r in range(CAP) for ref in code_refs]
+    slots = [(code_refs[array], row) for array, row in places]
     pairs = len(slots) // 2
 
     def pair(i, part, h):
@@ -313,13 +319,14 @@
     for ref, r in slots:
         values = ref[r, pl.ds(extra, EXTRA)].astype(jnp.float32)
         scale_rows.append(values)
-        if r == 0:
+        if len(lists) < len(slots) // CAP:
             lists.append(values[2 * heads : 2 * heads + 1])
 
     def scale_row(row):
         return jnp.concatenate([values[row : row + 1] for values in scale_rows], axis=1)
 
-    ids, moved_ref[...] = arrival_ids(lax.axis_index("inst"), pool, lists, listed)
+    ids, moved_ref[...], more = arrival_ids(lax.axis_index("inst"), pool, lists, listed)
+    more_ref[0] = jnp.max(more).astype(jnp.int32)
 
     def store_log(b, value):
         log_ref[:, b * block_len : (b + 1) * block_len] = value
@@ -369,7 +376,9 @@
         out_ref[:, h] = result.reshape(height // rows, rows, result.shape[-1])
 
 
-def shards(queries, new_kv, pool_codes, pool_scales, tables, ctx_len, mig_block, mig_dest):
+def attend(
+    general, queries, new_kv, pool_codes, pool_scales, tables, ctx_len, mig_block, mig_dest
+):
     instances = lax.axis_size("inst")
     pool = pool_codes.shape[0]
     requests, steps, q_heads, head_dim = queries.shape
@@ -386,26 +395,34 @@
     f32, bf16 = jnp.float32, jnp.bfloat16
     code_rows = 2 * heads * block_len
     pool_rows = pool_codes.reshape(pool, code_rows, head_dim)
-    sent_shape = (CAP, code_rows + EXTRA, head_dim)
+    sent_shape = (code_rows + EXTRA, head_dim)
     sent_bytes = 2 * math.prod(sent_shape)
     part_scales = jnp.transpose(pool_scales, (1, 2, 0))
     assert instances & (instances - 1) == 0 and 2 * heads < EXTRA and head_dim == 128
 
+    if general:
+        sizes = [CAP] * instances
+        copies = [(r * instances + k, [(k, r)]) for k in range(instances) for r in range(CAP)]
+    else:
+        sizes = [1, 2] + [1] * (instances - 1)
+        copies = [(CAP * instances, [(instances, 0), (1, 1)])]
+        copies += [(k, [(k, 0)]) for k in list(range(instances))[::-1]]
+    stores = sum(len(targets) for _, targets in copies)
     send = pl.pallas_call(
-        functools.partial(pack_kernel, (instances, listed, heads, pool)),
-        out_shape=[jax.ShapeDtypeStruct(sent_shape, bf16)] * instances,
+        functools.partial(pack_kernel, (instances, listed, heads, pool, copies)),
+        out_shape=[jax.ShapeDtypeStruct((size,) + sent_shape, bf16) for size in sizes],
         in_specs=[SMEM_SPEC, SMEM_SPEC, VMEM_SPEC, HBM_SPEC],
-        out_specs=[HBM_SPEC] * instances,
+        out_specs=[HBM_SPEC] * len(sizes),
         scratch_shapes=[
-            pltpu.SMEM((slots,), jnp.int32),
+            pltpu.SMEM((CAP * instances + 1,), jnp.int32),
             pltpu.VMEM((EXTRA, head_dim), f32),
-            pltpu.VMEM((slots,) + sent_shape[1:], bf16),
-            pltpu.SemaphoreType.DMA((slots,)),
-            pltpu.SemaphoreType.DMA((slots,)),
+            pltpu.VMEM((len(copies),) + sent_shape, bf16),
+            pltpu.SemaphoreType.DMA((len(copies),)),
+            pltpu.SemaphoreType.DMA((stores,)),
         ],
         compiler_params=pltpu.CompilerParams(vmem_limit_bytes=56 * MIB),
         cost_estimate=pl.CostEstimate(
-            flops=0, bytes_accessed=2 * instances * sent_bytes, transcendentals=0
+            flops=0, bytes_accessed=2 * stores * sent_bytes, transcendentals=0
         ),
         name="pack_blocks",
     )(mig_dest, mig_block, part_scales, pool_rows)
@@ -414,7 +431,17 @@
     def swap(value, distance):
         return lax.ppermute(value, "inst", [(j, j ^ distance) for j in range(instances)])
 
-    arrived = [send[0]] + [swap(send[k], k) for k in range(1, instances)]
+    if general:
+        arrived = [send[0]] + [swap(send[k], k) for k in range(1, instances)]
+        places = [(k, r) for r in range(CAP) for k in range(instances)]
+    else:
+        seconds = {0: send.pop()}
+        bit = instances // 2
+        while bit > 1:
+            for k in list(seconds):
+                seconds[k ^ bit] = swap(seconds[k], bit)
+            bit //= 2
+        arrived = [send[0]] + [swap(send[k], k) for k in range(1, instances)]
     flat_scales = part_scales.reshape(1, -1).astype(f32)
 
     query_rows = (
@@ -456,18 +483,32 @@
         name="own_blocks",
     )(tables, length, flat_scales, query_rows, fresh, pool_rows)
 
+    if not general:
+        held = {k: second for k, second in seconds.items() if k}
+        held, own_parts = lax.optimization_barrier((held, own_parts))
+        for k in held:
+            seconds[k ^ 1] = swap(held[k], 1)
+        places = [(k, 0) for k in range(instances)]
+        for k in range(instances):
+            if k == 1:
+                places.append((1, 1))
+            else:
+                places.append((len(arrived), 0))
+                arrived.append(seconds[k])
+
     arrival_bytes = 6 * heads * height * slots * block_len + 2 * 12 * height * head_dim * heads
-    arrival_bytes += 2 * instances * sent_bytes + 4 * requests * slots * block_len
-    out, moved_to = pl.pallas_call(
+    arrival_bytes += 2 * slots * sent_bytes + 4 * requests * slots * block_len
+    out, moved_to, more = pl.pallas_call(
         functools.partial(
-            arrival_kernel, (pool, heads, rows, block_len, spans, listed, factor)
+            arrival_kernel, (pool, heads, rows, block_len, spans, listed, factor), places
         ),
         out_shape=[
             jax.ShapeDtypeStruct((requests, heads, rows, head_dim), bf16),
             jax.ShapeDtypeStruct((1, listed), jnp.int32),
+            jax.ShapeDtypeStruct((1,), jnp.int32),
         ],
-        in_specs=[VMEM_SPEC] * (6 + instances),
-        out_specs=[VMEM_SPEC, VMEM_SPEC],
+        in_specs=[VMEM_SPEC] * (6 + len(arrived)),
+        out_specs=[VMEM_SPEC, VMEM_SPEC, SMEM_SPEC],
         scratch_shapes=[
             pltpu.VMEM((requests, slots * block_len), f32),
             pltpu.VMEM((heads, height, slots * block_len), f32),
@@ -476,7 +517,7 @@
         compiler_params=pltpu.CompilerParams(vmem_limit_bytes=arrival_bytes + 8 * MIB),
         cost_estimate=pl.CostEstimate(
             flops=4 * heads * height * slots * block_len * head_dim,
-            bytes_accessed=instances * sent_bytes,
+            bytes_accessed=slots * sent_bytes,
             transcendentals=heads * height * slots * block_len,
         ),
         name="arrived_blocks",
@@ -485,6 +526,17 @@
         out.reshape(requests, q_heads, steps, head_dim)
         .transpose(0, 2, 1, 3)
         .reshape(requests, steps, q_heads * head_dim)
+    )
+    return out, moved_to, more
+
+
+def shards(*args):
+    out, moved_to, more = attend(False, *args)
+    out = lax.cond(
+        more[0] > 1,
+        lambda out, *args: attend(True, *args)[0],
+        lambda out, *args: out,
+        out, *args,
     )
     return out, moved_to
 

time: 34.1 us -> 35.2 us (1.032)
  the two profiles are of different devices: /device:TPU:8 before, /device:TPU:0 now
where the time goes in v9:
time: 35.2 us; the launch traced here: 35 us
  Pallas kernels  17.6 us (50%)
  starting transfers between devices  9.32 us (26%)
  waiting for transfers between devices  5.23 us (15%)
  between operations  1.45 us (4%)
  local copies, waits for them, and re-layouts  1.36 us (4%)
    pallas_call x1, Pallas kernels, attend(): pl.pallas_call(functools.partial(own_kernel, (pool, heads, rows, steps, b...  12.3 us
    ppermute x5, starting transfers between devices, swap(): lax.ppermute(value, 'inst', [(j, j ^ distance) for j in range(instances)])  9.32 us
    ppermute x5, waiting for transfers between devices, swap(): lax.ppermute(value, 'inst', [(j, j ^ distance) for j in range(instances)])  5.23 us
    pallas_call x1, Pallas kernels, attend(): pl.pallas_call(functools.partial(pack_kernel, (instances, listed, heads,...  2.75 us
    pallas_call x1, Pallas kernels, attend(): pl.pallas_call(functools.partial(arrival_kernel, (pool, heads, rows, bloc...  2.6 us
    reshape x1, local copies, waits for them, and re-layouts, attend(): out = out.reshape(requests, q_heads, steps, head_dim).transpose(0, 2, 1,...  0.77 us
  transfers between devices with their start and end apart: 5, of which 2 were waited for; matrix products, arithmetic and copies ran while one was open for 1% of the time, Pallas kernels for 35%

profile of v9, /device:TPU:0, one launch (start us, length us, event | category | flops | bytes accessed | tf_op | source)
XLA Modules:
  0.0 35.0 jit_solution(17556028472057526336)
XLA Ops:
  0.6 0.0 copy-start.6
  0.6 0.0 copy-start.9
  0.7 0.0 copy-start.5
  0.7 0.0 copy-start.4
  0.7 0.0 copy-start.3
  0.7 2.8 %pack_blocks.3 = (bf16[1,528,128]{2,1,0:T(8,128)(2,1)}, bf16[2,528,128]{2,1,0:T(8,128)(2,1)}, bf16[1,528,128]{2,1,0:T(8,128)(2,1)}, bf16[1,528,128]{2,1,0:T(8,128)(2,1)}, bf16[1,528,128]{2,1,0:T(8,128)(2,1)}) custom-call(s32[1,4]{1,0:T(1,128)} %dest_ref.1, s32[1,4]{1,0:T(1,128)} %block_ref.1, bf16[2,2,48]{2,1,0:T(2,128)(2,1)} %bitcast.47, ...), custom_call_target="tpu_custom_call" | custom-call | bytes 1622016 | tf_op jit(solution)/shard_map/pack_blocks/pallas_call | solution.py:411
  3.4 4.1 %collective-permute-start.5 = (bf16[1,528,128]{2,1,0:T(8,128)(2,1)}, bf16[1,528,128]{2,1,0:T(8,128)(2,1)S(1)}, u32[]{:S(2)}, u32[]{:S(2)}) collective-permute-start(bf16[1,528,128]{2,1,0:T(8,128)(2,1)} %get-tuple-element.85), channel_id=1, source_target_pairs={{0,8},{4,12},{8,0},{12,4},{1,9},{5,13},{9,1},{13,5},{2,10},{6,14},... | collective-permute-start | bytes 405512 | tf_op jit(solution)/shard_map/ppermute | solution.py:432
  7.5 1.3 %collective-permute-start.6 = (bf16[1,528,128]{2,1,0:T(8,128)(2,1)}, bf16[1,528,128]{2,1,0:T(8,128)(2,1)S(1)}, u32[]{:S(2)}, u32[]{:S(2)}) collective-permute-start(bf16[1,528,128]{2,1,0:T(8,128)(2,1)} %get-tuple-element.86), channel_id=1, source_target_pairs={{0,12},{4,8},{8,4},{12,0},{1,13},{5,9},{9,5},{13,1},{2,14},{6,10},... | collective-permute-start | bytes 405512 | tf_op jit(solution)/shard_map/ppermute | solution.py:432
  8.9 1.7 %collective-permute-start.3 = (bf16[1,528,128]{2,1,0:T(8,128)(2,1)}, bf16[1,528,128]{2,1,0:T(8,128)(2,1)S(1)}, u32[]{:S(2)}, u32[]{:S(2)}) collective-permute-start(bf16[1,528,128]{2,1,0:T(8,128)(2,1)} %get-tuple-element.75.refs_4_), channel_id=1, source_target_pairs={{0,8},{4,12},{8,0},{12,4},{1,9},{5,13},{9,1},{13,5},{2,10},{6,14},... | collective-permute-start | bytes 405512 | tf_op jit(solution)/shard_map/ppermute | solution.py:432
  10.6 1.3 %collective-permute-start.4 = (bf16[2,528,128]{2,1,0:T(8,128)(2,1)}, bf16[2,528,128]{2,1,0:T(8,128)(2,1)S(1)}, u32[]{:S(2)}, u32[]{:S(2)}) collective-permute-start(bf16[2,528,128]{2,1,0:T(8,128)(2,1)} %get-tuple-element.84), channel_id=1, source_target_pairs={{0,4},{4,0},{8,12},{12,8},{1,5},{5,1},{9,13},{13,9},{2,6},{6,2},{1... | collective-permute-start | bytes 811016 | tf_op jit(solution)/shard_map/ppermute | solution.py:432
  11.9 0.0 copy-done.9
  11.9 0.1 copy.18.length_ref
  12.0 0.0 copy-done.5
  12.0 0.1 copy.17.tables_ref
  12.1 0.0 copy-done.4
  12.1 0.1 copy.14
  12.2 0.0 copy-done.3
  12.2 0.0 copy-start.1
  12.2 0.0 copy-start.2
  12.2 0.2 copy.13
  12.4 0.0 copy-done.6
  12.4 0.1 reshape.88.scale_ref
  12.5 0.0 copy-start.7
  12.5 0.0 copy-start.8
  12.5 12.3 %own_blocks.3 = (f32[2,512,128]{2,1,0:T(8,128)S(1)}, f32[2,512,128]{2,1,0:T(8,128)S(1)}, f32[2,512,128]{2,1,0:T(8,128)S(1)}) custom-call(s32[32,16]{1,0:T(8,128)S(1)} %copy.17.tables_ref, s32[32,1]{1,0:T(8,128)S(1)} %copy.18.length_ref, f32[1,192]{1,0:T(1,128)S(1)} %reshape.88.scale_ref, bf16[2,512,128]{2,1,0:T(8,128)(2,1)S(1)} %bitcast.31, ...), custom_call_target="tpu_custom_call" | custom-call | flops 3221225472 | bytes 6291456 | tf_op jit(solution)/shard_map/own_blocks/pallas_call | solution.py:462
  24.8 1.1 %collective-permute-done.3.refs_5_ = bf16[1,528,128]{2,1,0:T(8,128)(2,1)S(1)} collective-permute-done((bf16[1,528,128]{2,1,0:T(8,128)(2,1)}, bf16[1,528,128]{2,1,0:T(8,128)(2,1)S(1)}, u32[]{:S(2)}, u32[]{:S(2)}) %collective-permute-start.3) | collective-permute-done | bytes 135200 | tf_op jit(solution)/shard_map/ppermute | solution.py:432
  25.9 0.8 %collective-permute-start.7 = (bf16[1,528,128]{2,1,0:T(8,128)(2,1)S(1)}, bf16[1,528,128]{2,1,0:T(8,128)(2,1)S(1)}, u32[]{:S(2)}, u32[]{:S(2)}) collective-permute-start(bf16[1,528,128]{2,1,0:T(8,128)(2,1)S(1)} %collective-permute-done.3.refs_5_), channel_id=1, source_target_pairs={{0,4},{4,0},{8,12},{12,8},{1,5},{5,1},{9,13},{13,9},{2,6},{6,2},{1... | collective-permute-start | bytes 405512 | tf_op jit(solution)/shard_map/ppermute | solution.py:432
  26.7 0.0 collective-permute-done.5.refs_2_
  26.7 0.0 collective-permute-done.6.refs_3_
  26.7 0.0 collective-permute-done.4.refs_1_
  26.7 4.2 %collective-permute-done.7.refs_6_ = bf16[1,528,128]{2,1,0:T(8,128)(2,1)S(1)} collective-permute-done((bf16[1,528,128]{2,1,0:T(8,128)(2,1)S(1)}, bf16[1,528,128]{2,1,0:T(8,128)(2,1)S(1)}, u32[]{:S(2)}, u32[]{:S(2)}) %collective-permute-start.7) | collective-permute-done | bytes 135200 | tf_op jit(solution)/shard_map/ppermute | solution.py:432
  30.9 0.0 copy-done.1
  30.9 0.0 copy-done.2
  30.9 2.6 %arrived_blocks.3 = (bf16[32,2,16,128]{3,2,1,0:T(8,128)(2,1)S(1)}, s32[1,4]{1,0:T(1,128)}, s32[1]{0:T(128)}) custom-call(bf16[2,512,128]{2,1,0:T(8,128)(2,1)S(1)} %bitcast.32, s32[32,16]{1,0:T(8,128)S(1)} %copy.17.tables_ref, s32[32,1]{1,0:T(8,128)S(1)} %copy.18.length_ref, f32[2,512,128]{2,1,0:T(8,128)S(1)} %get-tuple-element.80.acc_ref, ...), custom_call_target="tpu_custom_call" | custom-call | flops 536870912 | bytes 1081344 | tf_op jit(solution)/shard_map/arrived_blocks/pallas_call | solution.py:501
  34.2 0.0 copy-done.7
  34.2 0.0 copy-done.8
  34.2 0.8 %conditional.1 = (bf16[32,2,2048]{2,1,0:T(2,128)(2,1)}) conditional(s32[]{:T(128)} %bitcast.24, bf16[32,2,16,128]{3,2,1,0:T(8,128)(2,1)S(1)} %bitcast.42, (bf16[32,2,16,128]{3,2,1,0:T(8,128)(2,1)S(1)}, s32[32]{0:T(128)S(1)}, bf16[48,2,2]{0,2,1:T(2,128)(2,1)S(1)}, bf16[48,2,2,128,128]{4,3,2,1,0:T(8,128)(2,1)}, s32[1,4]{1,0:T(1,128)S(1)}, ...), branch_computations={%region_0.1_spmd, %region_1.2_spmd} | conditional | flops 3758096384 | bytes 14718494 | solution.py:535
  34.2 0.8 %reshape.85 = bf16[32,2,2048]{2,1,0:T(2,128)(2,1)} reshape(bf16[32,2,16,128]{3,2,1,0:T(8,128)(2,1)S(1)} %param) | data formatting | bytes 524288 | tf_op jit(solution)/shard_map/reshape | solution.py:528
  (2 shorter events, 0.1 us)
Async XLA Ops:
  0.6 11.8 %copy-start.6 = (bf16[48,2,2]{0,2,1:T(2,128)(2,1)S(1)}, bf16[48,2,2]{0,2,1:T(2,128)(2,1)}, u32[]{:S(2)}) copy-start(bf16[48,2,2]{0,2,1:T(2,128)(2,1)} %param.13) | copy-start | bytes 1156
  0.6 11.3 %copy-start.9 = (s32[32]{0:T(128)S(1)}, s32[32]{0:T(128)}, u32[]{:S(2)}) copy-start(s32[32]{0:T(128)} %param.15) | copy-start | bytes 388
  0.7 11.4 %copy-start.5 = (s32[32,16]{0,1:T(8,128)S(1)}, s32[32,16]{0,1:T(8,128)}, u32[]{:S(2)}) copy-start(s32[32,16]{0,1:T(8,128)} %param.14) | copy-start | bytes 6148
  0.7 11.4 %copy-start.4 = (bf16[32,2,2,2,128]{4,3,2,1,0:T(2,128)(2,1)S(1)}, bf16[32,2,2,2,128]{4,3,2,1,0:T(2,128)(2,1)}, u32[]{:S(2)}) copy-start(bf16[32,2,2,2,128]{4,3,2,1,0:T(2,128)(2,1)} %param.11) | copy-start | bytes 196612
  0.7 11.5 %copy-start.3 = (bf16[32,2,16,128]{3,2,1,0:T(8,128)(2,1)S(1)}, bf16[32,2,16,128]{3,2,1,0:T(8,128)(2,1)}, u32[]{:S(2)}) copy-start(bf16[32,2,16,128]{3,2,1,0:T(8,128)(2,1)} %param.10) | copy-start | bytes 786436
  3.4 23.3 %collective-permute-start.5 = (bf16[1,528,128]{2,1,0:T(8,128)(2,1)}, bf16[1,528,128]{2,1,0:T(8,128)(2,1)S(1)}, u32[]{:S(2)}, u32[]{:S(2)}) collective-permute-start(bf16[1,528,128]{2,1,0:T(8,128)(2,1)} %get-tuple-element.85), channel_id=1, source_target_pairs={{0,8},{4,12},{8,0},{12,4},{1,9},{5,13},{9,1},{13,5},{2,10},{6,14},... | collective-permute-start | bytes 405512 | tf_op jit(solution)/shard_map/ppermute | solution.py:432
  7.5 19.2 %collective-permute-start.6 = (bf16[1,528,128]{2,1,0:T(8,128)(2,1)}, bf16[1,528,128]{2,1,0:T(8,128)(2,1)S(1)}, u32[]{:S(2)}, u32[]{:S(2)}) collective-permute-start(bf16[1,528,128]{2,1,0:T(8,128)(2,1)} %get-tuple-element.86), channel_id=1, source_target_pairs={{0,12},{4,8},{8,4},{12,0},{1,13},{5,9},{9,5},{13,1},{2,14},{6,10},... | collective-permute-start | bytes 405512 | tf_op jit(solution)/shard_map/ppermute | solution.py:432
  8.9 17.0 %collective-permute-start.3 = (bf16[1,528,128]{2,1,0:T(8,128)(2,1)}, bf16[1,528,128]{2,1,0:T(8,128)(2,1)S(1)}, u32[]{:S(2)}, u32[]{:S(2)}) collective-permute-start(bf16[1,528,128]{2,1,0:T(8,128)(2,1)} %get-tuple-element.75.refs_4_), channel_id=1, source_target_pairs={{0,8},{4,12},{8,0},{12,4},{1,9},{5,13},{9,1},{13,5},{2,10},{6,14},... | collective-permute-start | bytes 405512 | tf_op jit(solution)/shard_map/ppermute | solution.py:432
  10.6 16.1 %collective-permute-start.4 = (bf16[2,528,128]{2,1,0:T(8,128)(2,1)}, bf16[2,528,128]{2,1,0:T(8,128)(2,1)S(1)}, u32[]{:S(2)}, u32[]{:S(2)}) collective-permute-start(bf16[2,528,128]{2,1,0:T(8,128)(2,1)} %get-tuple-element.84), channel_id=1, source_target_pairs={{0,4},{4,0},{8,12},{12,8},{1,5},{5,1},{9,13},{13,9},{2,6},{6,2},{1... | collective-permute-start | bytes 811016 | tf_op jit(solution)/shard_map/ppermute | solution.py:432
  12.2 18.7 %copy-start.1 = (bf16[1,528,128]{2,1,0:T(8,128)(2,1)S(1)}, bf16[1,528,128]{2,1,0:T(8,128)(2,1)}, u32[]{:S(2)}) copy-start(bf16[1,528,128]{2,1,0:T(8,128)(2,1)} %get-tuple-element.83.refs_0_) | copy-start | bytes 405508
  12.2 18.7 %copy-start.2 = (bf16[1,528,128]{2,1,0:T(8,128)(2,1)S(1)}, bf16[1,528,128]{2,1,0:T(8,128)(2,1)}, u32[]{:S(2)}) copy-start(bf16[1,528,128]{2,1,0:T(8,128)(2,1)} %get-tuple-element.75.refs_4_) | copy-start | bytes 405508
  12.5 21.7 %copy-start.7 = (s32[1,4]{1,0:T(1,128)S(1)}, s32[1,4]{1,0:T(1,128)}, u32[]{:S(2)}) copy-start(s32[1,4]{1,0:T(1,128)} %dest_ref.1) | copy-start | bytes 52
  12.5 21.7 %copy-start.8 = (s32[1,4]{1,0:T(1,128)S(1)}, s32[1,4]{1,0:T(1,128)}, u32[]{:S(2)}) copy-start(s32[1,4]{1,0:T(1,128)} %block_ref.1) | copy-start | bytes 52
  25.9 5.0 %collective-permute-start.7 = (bf16[1,528,128]{2,1,0:T(8,128)(2,1)S(1)}, bf16[1,528,128]{2,1,0:T(8,128)(2,1)S(1)}, u32[]{:S(2)}, u32[]{:S(2)}) collective-permute-start(bf16[1,528,128]{2,1,0:T(8,128)(2,1)S(1)} %collective-permute-done.3.refs_5_), channel_id=1, source_target_pairs={{0,4},{4,0},{8,12},{12,8},{1,5},{5,1},{9,13},{13,9},{2,6},{6,2},{1... | collective-permute-start | bytes 405512 | tf_op jit(solution)/shard_map/ppermute | solution.py:432

commit v10 on v8

--- a/solution.py
+++ b/solution.py
@@ -28,12 +28,9 @@
 
 def pack_kernel(dims, dest_ref, block_ref, scale_ref, pool_ref, *refs):
     instances, listed, heads, pool = dims
-    send_refs, (index_ref, extra_ref, held_ref, in_sems, out_sems) = (
-        refs[:instances],
-        refs[instances:],
-    )
+    send_refs, (index_ref, extra_ref, sems) = refs[:instances], refs[instances:]
     slots = instances * CAP
-    code_rows = held_ref.shape[1] - EXTRA
+    code_rows = send_refs[0].shape[1] - EXTRA
     me = lax.axis_index("inst")
     for slot in range(slots):
         index_ref[slot] = 0
@@ -50,12 +47,16 @@
 
     loop(listed, place, 0)
     order = list(range(slots))[::-1]
-    loads, stores = {}, []
+    loads = []
     for i in order:
-        loads[i] = pltpu.make_async_copy(
-            pool_ref.at[index_ref[i]], held_ref.at[i, pl.ds(0, code_rows)], in_sems.at[i]
-        )
-        loads[i].start()
+        loads.append(
+            pltpu.make_async_copy(
+                pool_ref.at[index_ref[i]],
+                send_refs[i // CAP].at[i % CAP, pl.ds(0, code_rows)],
+                sems.at[i],
+            )
+        )
+        loads[-1].start()
     lane = lax.broadcasted_iota(jnp.int32, (1, 128), 1)
 
     def spell(m, row):
@@ -78,17 +79,9 @@
                 extra_ref[row : row + 1, :] = jnp.broadcast_to(
                     jnp.sum(one, axis=1, keepdims=True), (1, 128)
                 )
-        held_ref[i, pl.ds(code_rows, EXTRA)] = extra_ref[...].astype(jnp.bfloat16)
-    for i in order:
-        loads[i].wait()
-        stores.append(
-            pltpu.make_async_copy(
-                held_ref.at[i], send_refs[i // CAP].at[i % CAP], out_sems.at[i]
-            )
-        )
-        stores[-1].start()
-    for store in stores:
-        store.wait()
+        send_refs[i // CAP][i % CAP, pl.ds(code_rows, EXTRA)] = extra_ref[...].astype(jnp.bfloat16)
+    for load in loads:
+        load.wait()
 
 
 def split(value, size):
@@ -395,12 +388,10 @@
         functools.partial(pack_kernel, (instances, listed, heads, pool)),
         out_shape=[jax.ShapeDtypeStruct(sent_shape, bf16)] * instances,
         in_specs=[SMEM_SPEC, SMEM_SPEC, VMEM_SPEC, HBM_SPEC],
-        out_specs=[HBM_SPEC] * instances,
+        out_specs=[VMEM_SPEC] * instances,
         scratch_shapes=[
             pltpu.SMEM((slots,), jnp.int32),
             pltpu.VMEM((EXTRA, head_dim), f32),
-            pltpu.VMEM((slots,) + sent_shape[1:], bf16),
-            pltpu.SemaphoreType.DMA((slots,)),
             pltpu.SemaphoreType.DMA((slots,)),
         ],
         compiler_params=pltpu.CompilerParams(vmem_limit_bytes=56 * MIB),
@@ -414,7 +405,8 @@
     def swap(value, distance):
         return lax.ppermute(value, "inst", [(j, j ^ distance) for j in range(instances)])
 
-    arrived = [send[0]] + [swap(send[k], k) for k in range(1, instances)]
+    arrived = {k: swap(send[k], k) for k in range(instances - 1, 0, -1)}
+    arrived = [send[0]] + [arrived[k] for k in range(1, instances)]
     flat_scales = part_scales.reshape(1, -1).astype(f32)
 
     query_rows = (

time: 34.1 us -> 34.1 us (level)
  the two profiles are of different devices: /device:TPU:8 before, /device:TPU:16 now
where the time goes in v10:
time: 34.1 us; the launch traced here: 33.9 us
  Pallas kernels  18.7 us (55%)
  waiting for transfers between devices  10.3 us (30%)
  starting transfers between devices  3.55 us (10%)
  between operations  0.74 us (2%)
  local copies, waits for them, and re-layouts  0.54 us (2%)
    pallas_call x1, Pallas kernels, shards(): pl.pallas_call(functools.partial(own_kernel, (pool, heads, rows, steps, b...  12.6 us
    ppermute x3, waiting for transfers between devices, swap(): lax.ppermute(value, 'inst', [(j, j ^ distance) for j in range(instances)])  10.3 us
    ppermute x3, starting transfers between devices, swap(): lax.ppermute(value, 'inst', [(j, j ^ distance) for j in range(instances)])  3.55 us
    pallas_call x1, Pallas kernels, shards(): pl.pallas_call(functools.partial(pack_kernel, (instances, listed, heads,...  3.19 us
    pallas_call x1, Pallas kernels, shards(): pl.pallas_call(functools.partial(arrival_kernel, (pool, heads, rows, bloc...  2.91 us
  transfers between devices with their start and end apart: 3, of which 2 were waited for; matrix products, arithmetic and copies ran while one was open for 2% of the time, Pallas kernels for 37%

profile of v10, /device:TPU:16, one launch (start us, length us, event | category | flops | bytes accessed | tf_op | source)
XLA Modules:
  0.0 33.9 jit_solution(17272060691234354974)
XLA Ops:
  0.6 0.0 copy-start.4
  0.6 0.0 copy-start.3
  0.7 0.0 copy-start.5
  0.7 0.0 copy-start.2
  0.7 0.0 copy-start.1
  0.7 3.2 %pack_blocks.1 = (bf16[2,528,128]{2,1,0:T(8,128)(2,1)}, bf16[2,528,128]{2,1,0:T(8,128)(2,1)}, bf16[2,528,128]{2,1,0:T(8,128)(2,1)}, bf16[2,528,128]{2,1,0:T(8,128)(2,1)}) custom-call(s32[1,4]{1,0:T(1,128)} %dest_ref.1, s32[1,4]{1,0:T(1,128)} %block_ref.1, bf16[2,2,48]{2,1,0:T(2,128)(2,1)} %bitcast.21, bf16[48,512,128]{2,1,0:T(8,128)(2,1)} %bitcast.16), custom_call_target="tpu_custom_call" | custom-call | bytes 2162688 | tf_op jit(solution)/shard_map/pack_blocks/pallas_call | solution.py:387
  3.9 1.6 %collective-permute-start = (bf16[2,528,128]{2,1,0:T(8,128)(2,1)}, bf16[2,528,128]{2,1,0:T(8,128)(2,1)S(1)}, u32[]{:S(2)}, u32[]{:S(2)}) collective-permute-start(bf16[2,528,128]{2,1,0:T(8,128)(2,1)} %get-tuple-element.25), channel_id=1, source_target_pairs={{0,4},{4,0},{8,12},{12,8},{1,5},{5,1},{9,13},{13,9},{2,6},{6,2},{1... | collective-permute-start | bytes 811016 | tf_op jit(solution)/shard_map/ppermute | solution.py:406
  5.5 0.3 collective-permute-start.1
  5.9 1.6 %collective-permute-start.2 = (bf16[2,528,128]{2,1,0:T(8,128)(2,1)}, bf16[2,528,128]{2,1,0:T(8,128)(2,1)S(1)}, u32[]{:S(2)}, u32[]{:S(2)}) collective-permute-start(bf16[2,528,128]{2,1,0:T(8,128)(2,1)} %get-tuple-element.27), channel_id=1, source_target_pairs={{0,12},{4,8},{8,4},{12,0},{1,13},{5,9},{9,5},{13,1},{2,14},{6,10},... | collective-permute-start | bytes 811016 | tf_op jit(solution)/shard_map/ppermute | solution.py:406
  7.4 0.0 copy-done.3
  7.4 0.1 copy.14.tables_ref
  7.5 0.0 copy-done.5
  7.5 0.1 copy.15.length_ref
  7.6 0.0 copy-done.2
  7.6 0.1 copy.11
  7.7 0.0 copy-done.1
  7.7 0.0 copy-start
  7.7 0.2 copy.10
  7.9 0.0 copy-done.4
  7.9 0.1 reshape.43.scale_ref
  8.0 12.6 %own_blocks.1 = (f32[2,512,128]{2,1,0:T(8,128)S(1)}, f32[2,512,128]{2,1,0:T(8,128)S(1)}, f32[2,512,128]{2,1,0:T(8,128)S(1)}) custom-call(s32[32,16]{1,0:T(8,128)S(1)} %copy.14.tables_ref, s32[32,1]{1,0:T(8,128)S(1)} %copy.15.length_ref, f32[1,192]{1,0:T(1,128)S(1)} %reshape.43.scale_ref, bf16[2,512,128]{2,1,0:T(8,128)(2,1)S(1)} %bitcast.14, ...), custom_call_target="tpu_custom_call" | custom-call | flops 3221225472 | bytes 6291456 | tf_op jit(solution)/shard_map/own_blocks/pallas_call | solution.py:427
  20.7 0.0 collective-permute-done.refs_1_
  20.7 4.0 %collective-permute-done.1.refs_2_ = bf16[2,528,128]{2,1,0:T(8,128)(2,1)S(1)} collective-permute-done((bf16[2,528,128]{2,1,0:T(8,128)(2,1)}, bf16[2,528,128]{2,1,0:T(8,128)(2,1)S(1)}, u32[]{:S(2)}, u32[]{:S(2)}) %collective-permute-start.1) | collective-permute-done | bytes 270368 | tf_op jit(solution)/shard_map/ppermute | solution.py:406
  24.7 6.3 %collective-permute-done.2.refs_3_ = bf16[2,528,128]{2,1,0:T(8,128)(2,1)S(1)} collective-permute-done((bf16[2,528,128]{2,1,0:T(8,128)(2,1)}, bf16[2,528,128]{2,1,0:T(8,128)(2,1)S(1)}, u32[]{:S(2)}, u32[]{:S(2)}) %collective-permute-start.2) | collective-permute-done | bytes 270368 | tf_op jit(solution)/shard_map/ppermute | solution.py:406
  31.0 0.0 copy-done
  31.0 2.9 %arrived_blocks.1 = (bf16[32,2,16,128]{3,2,1,0:T(8,128)(2,1)}, s32[1,4]{1,0:T(1,128)}) custom-call(bf16[2,512,128]{2,1,0:T(8,128)(2,1)S(1)} %bitcast.15, s32[32,16]{1,0:T(8,128)S(1)} %copy.14.tables_ref, s32[32,1]{1,0:T(8,128)S(1)} %copy.15.length_ref, f32[2,512,128]{2,1,0:T(8,128)S(1)} %get-tuple-element.21.acc_ref, ...), custom_call_target="tpu_custom_call" | custom-call | flops 536870912 | bytes 1081344 | tf_op jit(solution)/shard_map/arrived_blocks/pallas_call | solution.py:453
  (1 shorter events, 0.0 us)
Async XLA Ops:
  0.6 7.3 %copy-start.4 = (bf16[48,2,2]{0,2,1:T(2,128)(2,1)S(1)}, bf16[48,2,2]{0,2,1:T(2,128)(2,1)}, u32[]{:S(2)}) copy-start(bf16[48,2,2]{0,2,1:T(2,128)(2,1)} %param.11) | copy-start | bytes 1156
  0.6 6.8 %copy-start.3 = (s32[32,16]{0,1:T(8,128)S(1)}, s32[32,16]{0,1:T(8,128)}, u32[]{:S(2)}) copy-start(s32[32,16]{0,1:T(8,128)} %param.12) | copy-start | bytes 6148
  0.7 6.9 %copy-start.5 = (s32[32]{0:T(128)S(1)}, s32[32]{0:T(128)}, u32[]{:S(2)}) copy-start(s32[32]{0:T(128)} %param.13) | copy-start | bytes 388
  0.7 6.9 %copy-start.2 = (bf16[32,2,2,2,128]{4,3,2,1,0:T(2,128)(2,1)S(1)}, bf16[32,2,2,2,128]{4,3,2,1,0:T(2,128)(2,1)}, u32[]{:S(2)}) copy-start(bf16[32,2,2,2,128]{4,3,2,1,0:T(2,128)(2,1)} %param.9) | copy-start | bytes 196612
  0.7 7.0 %copy-start.1 = (bf16[32,2,16,128]{3,2,1,0:T(8,128)(2,1)S(1)}, bf16[32,2,16,128]{3,2,1,0:T(8,128)(2,1)}, u32[]{:S(2)}) copy-start(bf16[32,2,16,128]{3,2,1,0:T(8,128)(2,1)} %param.8) | copy-start | bytes 786436
  3.9 16.8 %collective-permute-start = (bf16[2,528,128]{2,1,0:T(8,128)(2,1)}, bf16[2,528,128]{2,1,0:T(8,128)(2,1)S(1)}, u32[]{:S(2)}, u32[]{:S(2)}) collective-permute-start(bf16[2,528,128]{2,1,0:T(8,128)(2,1)} %get-tuple-element.25), channel_id=1, source_target_pairs={{0,4},{4,0},{8,12},{12,8},{1,5},{5,1},{9,13},{13,9},{2,6},{6,2},{1... | collective-permute-start | bytes 811016 | tf_op jit(solution)/shard_map/ppermute | solution.py:406
  5.5 19.2 %collective-permute-start.1 = (bf16[2,528,128]{2,1,0:T(8,128)(2,1)}, bf16[2,528,128]{2,1,0:T(8,128)(2,1)S(1)}, u32[]{:S(2)}, u32[]{:S(2)}) collective-permute-start(bf16[2,528,128]{2,1,0:T(8,128)(2,1)} %get-tuple-element.26), channel_id=1, source_target_pairs={{0,8},{4,12},{8,0},{12,4},{1,9},{5,13},{9,1},{13,5},{2,10},{6,14},... | collective-permute-start | bytes 811016 | tf_op jit(solution)/shard_map/ppermute | solution.py:406
  5.9 25.1 %collective-permute-start.2 = (bf16[2,528,128]{2,1,0:T(8,128)(2,1)}, bf16[2,528,128]{2,1,0:T(8,128)(2,1)S(1)}, u32[]{:S(2)}, u32[]{:S(2)}) collective-permute-start(bf16[2,528,128]{2,1,0:T(8,128)(2,1)} %get-tuple-element.27), channel_id=1, source_target_pairs={{0,12},{4,8},{8,4},{12,0},{1,13},{5,9},{9,5},{13,1},{2,14},{6,10},... | collective-permute-start | bytes 811016 | tf_op jit(solution)/shard_map/ppermute | solution.py:406
  7.7 23.3 %copy-start = (bf16[2,528,128]{2,1,0:T(8,128)(2,1)S(1)}, bf16[2,528,128]{2,1,0:T(8,128)(2,1)}, u32[]{:S(2)}) copy-start(bf16[2,528,128]{2,1,0:T(8,128)(2,1)} %get-tuple-element.24.refs_0_) | copy-start | bytes 811012

commit v11 on v10

--- a/solution.py
+++ b/solution.py
@@ -290,8 +290,7 @@
 
 def arrival_kernel(dims, q_ref, tables_ref, length_ref, acc_ref, top_ref, total_ref, *refs):
     pool, heads, rows, block_len, spans, listed, factor = dims
-    code_refs, (out_ref, moved_ref, log_ref, t_ref, p_ref) = refs[:-5], refs[-5:]
-    instances = len(code_refs)
+    code_refs, (out_ref, moved_ref, log_ref, t_ref, p_ref) = refs[-6::-1], refs[-5:]
     height = q_ref.shape[1]
     width = 2 * block_len
     extra = 2 * heads * block_len
@@ -394,7 +393,7 @@
             pltpu.VMEM((EXTRA, head_dim), f32),
             pltpu.SemaphoreType.DMA((slots,)),
         ],
-        compiler_params=pltpu.CompilerParams(vmem_limit_bytes=56 * MIB),
+        compiler_params=pltpu.CompilerParams(vmem_limit_bytes=547 * MIB // 10),
         cost_estimate=pl.CostEstimate(
             flops=0, bytes_accessed=2 * instances * sent_bytes, transcendentals=0
         ),
@@ -472,7 +471,7 @@
             transcendentals=heads * height * slots * block_len,
         ),
         name="arrived_blocks",
-    )(query_rows, tables, length, *own_parts, *arrived)
+    )(query_rows, tables, length, *own_parts, *arrived[::-1])
     out = (
         out.reshape(requests, q_heads, steps, head_dim)
         .transpose(0, 2, 1, 3)

time: 34.1 us -> 35.3 us (1.035)
  the two profiles are of different devices: /device:TPU:16 before, /device:TPU:0 now
where the time goes in v11:
time: 35.3 us; the launch traced here: 35.2 us
  Pallas kernels  18.8 us (53%)
  waiting for transfers between devices  9.32 us (26%)
  starting transfers between devices  5.8 us (16%)
  between operations  0.74 us (2%)
  local copies, waits for them, and re-layouts  0.54 us (2%)
    pallas_call x1, Pallas kernels, shards(): pl.pallas_call(functools.partial(own_kernel, (pool, heads, rows, steps, b...  12.6 us
    ppermute x3, waiting for transfers between devices, swap(): lax.ppermute(value, 'inst', [(j, j ^ distance) for j in range(instances)])  9.32 us
    ppermute x3, starting transfers between devices, swap(): lax.ppermute(value, 'inst', [(j, j ^ distance) for j in range(instances)])  5.8 us
    pallas_call x1, Pallas kernels, shards(): pl.pallas_call(functools.partial(pack_kernel, (instances, listed, heads,...  3.22 us
    pallas_call x1, Pallas kernels, shards(): pl.pallas_call(functools.partial(arrival_kernel, (pool, heads, rows, bloc...  2.91 us
  transfers between devices with their start and end apart: 3, of which 1 were waited for; matrix products, arithmetic and copies ran while one was open for 1% of the time, Pallas kernels for 36%

profile of v11, /device:TPU:0, one launch (start us, length us, event | category | flops | bytes accessed | tf_op | source)
XLA Modules:
  0.0 35.2 jit_solution(1866839181363909969)
XLA Ops:
  0.6 0.0 copy-start.4
  0.6 0.0 copy-start.3
  0.7 0.0 copy-start.5
  0.7 0.0 copy-start.2
  0.7 0.0 copy-start.1
  0.7 3.2 %pack_blocks.1 = (bf16[2,528,128]{2,1,0:T(8,128)(2,1)}, bf16[2,528,128]{2,1,0:T(8,128)(2,1)}, bf16[2,528,128]{2,1,0:T(8,128)(2,1)}, bf16[2,528,128]{2,1,0:T(8,128)(2,1)}) custom-call(s32[1,4]{1,0:T(1,128)} %dest_ref.1, s32[1,4]{1,0:T(1,128)} %block_ref.1, bf16[2,2,48]{2,1,0:T(2,128)(2,1)} %bitcast.21, bf16[48,512,128]{2,1,0:T(8,128)(2,1)} %bitcast.16), custom_call_target="tpu_custom_call" | custom-call | bytes 2162688 | tf_op jit(solution)/shard_map/pack_blocks/pallas_call | solution.py:386
  3.9 5.2 %collective-permute-start = (bf16[2,528,128]{2,1,0:T(8,128)(2,1)}, bf16[2,528,128]{2,1,0:T(8,128)(2,1)S(1)}, u32[]{:S(2)}, u32[]{:S(2)}) collective-permute-start(bf16[2,528,128]{2,1,0:T(8,128)(2,1)} %get-tuple-element.24), channel_id=1, source_target_pairs={{0,12},{4,8},{8,4},{12,0},{1,13},{5,9},{9,5},{13,1},{2,14},{6,10},... | collective-permute-start | bytes 811016 | tf_op jit(solution)/shard_map/ppermute | solution.py:405
  9.1 0.0 collective-permute-start.1
  9.1 0.6 %collective-permute-start.2 = (bf16[2,528,128]{2,1,0:T(8,128)(2,1)}, bf16[2,528,128]{2,1,0:T(8,128)(2,1)S(1)}, u32[]{:S(2)}, u32[]{:S(2)}) collective-permute-start(bf16[2,528,128]{2,1,0:T(8,128)(2,1)} %get-tuple-element.26), channel_id=1, source_target_pairs={{0,4},{4,0},{8,12},{12,8},{1,5},{5,1},{9,13},{13,9},{2,6},{6,2},{1... | collective-permute-start | bytes 811016 | tf_op jit(solution)/shard_map/ppermute | solution.py:405
  9.7 0.0 copy-done.3
  9.7 0.1 copy.14.tables_ref
  9.8 0.0 copy-done.5
  9.8 0.1 copy.15.length_ref
  9.9 0.0 copy-done.2
  9.9 0.1 copy.11
  9.9 0.0 copy-done.1
  9.9 0.0 copy-start
  10.0 0.2 copy.10
  10.2 0.0 copy-done.4
  10.2 0.1 reshape.43.scale_ref
  10.3 12.6 %own_blocks.1 = (f32[2,512,128]{2,1,0:T(8,128)S(1)}, f32[2,512,128]{2,1,0:T(8,128)S(1)}, f32[2,512,128]{2,1,0:T(8,128)S(1)}) custom-call(s32[32,16]{1,0:T(8,128)S(1)} %copy.14.tables_ref, s32[32,1]{1,0:T(8,128)S(1)} %copy.15.length_ref, f32[1,192]{1,0:T(1,128)S(1)} %reshape.43.scale_ref, bf16[2,512,128]{2,1,0:T(8,128)(2,1)S(1)} %bitcast.14, ...), custom_call_target="tpu_custom_call" | custom-call | flops 3221225472 | bytes 6291456 | tf_op jit(solution)/shard_map/own_blocks/pallas_call | solution.py:426
  22.9 0.0 collective-permute-done.refs_0_
  22.9 9.3 %collective-permute-done.1.refs_1_ = bf16[2,528,128]{2,1,0:T(8,128)(2,1)S(1)} collective-permute-done((bf16[2,528,128]{2,1,0:T(8,128)(2,1)}, bf16[2,528,128]{2,1,0:T(8,128)(2,1)S(1)}, u32[]{:S(2)}, u32[]{:S(2)}) %collective-permute-start.1) | collective-permute-done | bytes 270368 | tf_op jit(solution)/shard_map/ppermute | solution.py:405
  32.3 0.0 collective-permute-done.2.refs_2_
  32.3 0.0 copy-done
  32.3 2.9 %arrived_blocks.1 = (bf16[32,2,16,128]{3,2,1,0:T(8,128)(2,1)}, s32[1,4]{1,0:T(1,128)}) custom-call(bf16[2,512,128]{2,1,0:T(8,128)(2,1)S(1)} %bitcast.15, s32[32,16]{1,0:T(8,128)S(1)} %copy.14.tables_ref, s32[32,1]{1,0:T(8,128)S(1)} %copy.15.length_ref, f32[2,512,128]{2,1,0:T(8,128)S(1)} %get-tuple-element.21.acc_ref, ...), custom_call_target="tpu_custom_call" | custom-call | flops 536870912 | bytes 1081344 | tf_op jit(solution)/shard_map/arrived_blocks/pallas_call | solution.py:452
  (1 shorter events, 0.0 us)
Async XLA Ops:
  0.6 9.5 %copy-start.4 = (bf16[48,2,2]{0,2,1:T(2,128)(2,1)S(1)}, bf16[48,2,2]{0,2,1:T(2,128)(2,1)}, u32[]{:S(2)}) copy-start(bf16[48,2,2]{0,2,1:T(2,128)(2,1)} %param.11) | copy-start | bytes 1156
  0.6 9.1 %copy-start.3 = (s32[32,16]{0,1:T(8,128)S(1)}, s32[32,16]{0,1:T(8,128)}, u32[]{:S(2)}) copy-start(s32[32,16]{0,1:T(8,128)} %param.12) | copy-start | bytes 6148
  0.7 9.1 %copy-start.5 = (s32[32]{0:T(128)S(1)}, s32[32]{0:T(128)}, u32[]{:S(2)}) copy-start(s32[32]{0:T(128)} %param.13) | copy-start | bytes 388
  0.7 9.2 %copy-start.2 = (bf16[32,2,2,2,128]{4,3,2,1,0:T(2,128)(2,1)S(1)}, bf16[32,2,2,2,128]{4,3,2,1,0:T(2,128)(2,1)}, u32[]{:S(2)}) copy-start(bf16[32,2,2,2,128]{4,3,2,1,0:T(2,128)(2,1)} %param.9) | copy-start | bytes 196612
  0.7 9.3 %copy-start.1 = (bf16[32,2,16,128]{3,2,1,0:T(8,128)(2,1)S(1)}, bf16[32,2,16,128]{3,2,1,0:T(8,128)(2,1)}, u32[]{:S(2)}) copy-start(bf16[32,2,16,128]{3,2,1,0:T(8,128)(2,1)} %param.8) | copy-start | bytes 786436
  3.9 19.0 %collective-permute-start = (bf16[2,528,128]{2,1,0:T(8,128)(2,1)}, bf16[2,528,128]{2,1,0:T(8,128)(2,1)S(1)}, u32[]{:S(2)}, u32[]{:S(2)}) collective-permute-start(bf16[2,528,128]{2,1,0:T(8,128)(2,1)} %get-tuple-element.24), channel_id=1, source_target_pairs={{0,12},{4,8},{8,4},{12,0},{1,13},{5,9},{9,5},{13,1},{2,14},{6,10},... | collective-permute-start | bytes 811016 | tf_op jit(solution)/shard_map/ppermute | solution.py:405
  9.1 23.2 %collective-permute-start.1 = (bf16[2,528,128]{2,1,0:T(8,128)(2,1)}, bf16[2,528,128]{2,1,0:T(8,128)(2,1)S(1)}, u32[]{:S(2)}, u32[]{:S(2)}) collective-permute-start(bf16[2,528,128]{2,1,0:T(8,128)(2,1)} %get-tuple-element.25), channel_id=1, source_target_pairs={{0,8},{4,12},{8,0},{12,4},{1,9},{5,13},{9,1},{13,5},{2,10},{6,14},... | collective-permute-start | bytes 811016 | tf_op jit(solution)/shard_map/ppermute | solution.py:405
  9.1 23.2 %collective-permute-start.2 = (bf16[2,528,128]{2,1,0:T(8,128)(2,1)}, bf16[2,528,128]{2,1,0:T(8,128)(2,1)S(1)}, u32[]{:S(2)}, u32[]{:S(2)}) collective-permute-start(bf16[2,528,128]{2,1,0:T(8,128)(2,1)} %get-tuple-element.26), channel_id=1, source_target_pairs={{0,4},{4,0},{8,12},{12,8},{1,5},{5,1},{9,13},{13,9},{2,6},{6,2},{1... | collective-permute-start | bytes 811016 | tf_op jit(solution)/shard_map/ppermute | solution.py:405
  9.9 22.3 %copy-start = (bf16[2,528,128]{2,1,0:T(8,128)(2,1)S(1)}, bf16[2,528,128]{2,1,0:T(8,128)(2,1)}, u32[]{:S(2)}) copy-start(bf16[2,528,128]{2,1,0:T(8,128)(2,1)} %get-tuple-element.27.refs_3_) | copy-start | bytes 811012

commit v12 on v9

--- a/solution.py
+++ b/solution.py
@@ -400,48 +400,53 @@
     part_scales = jnp.transpose(pool_scales, (1, 2, 0))
     assert instances & (instances - 1) == 0 and 2 * heads < EXTRA and head_dim == 128
 
-    if general:
-        sizes = [CAP] * instances
-        copies = [(r * instances + k, [(k, r)]) for k in range(instances) for r in range(CAP)]
-    else:
-        sizes = [1, 2] + [1] * (instances - 1)
-        copies = [(CAP * instances, [(instances, 0), (1, 1)])]
-        copies += [(k, [(k, 0)]) for k in list(range(instances))[::-1]]
-    stores = sum(len(targets) for _, targets in copies)
-    send = pl.pallas_call(
-        functools.partial(pack_kernel, (instances, listed, heads, pool, copies)),
-        out_shape=[jax.ShapeDtypeStruct((size,) + sent_shape, bf16) for size in sizes],
-        in_specs=[SMEM_SPEC, SMEM_SPEC, VMEM_SPEC, HBM_SPEC],
-        out_specs=[HBM_SPEC] * len(sizes),
-        scratch_shapes=[
-            pltpu.SMEM((CAP * instances + 1,), jnp.int32),
-            pltpu.VMEM((EXTRA, head_dim), f32),
-            pltpu.VMEM((len(copies),) + sent_shape, bf16),
-            pltpu.SemaphoreType.DMA((len(copies),)),
-            pltpu.SemaphoreType.DMA((stores,)),
-        ],
-        compiler_params=pltpu.CompilerParams(vmem_limit_bytes=56 * MIB),
-        cost_estimate=pl.CostEstimate(
-            flops=0, bytes_accessed=2 * stores * sent_bytes, transcendentals=0
-        ),
-        name="pack_blocks",
-    )(mig_dest, mig_block, part_scales, pool_rows)
-    part_scales, *send = lax.optimization_barrier((part_scales, *send))
+    def pack(sizes, copies):
+        stores = sum(len(targets) for _, targets in copies)
+        return pl.pallas_call(
+            functools.partial(pack_kernel, (instances, listed, heads, pool, copies)),
+            out_shape=[jax.ShapeDtypeStruct((size,) + sent_shape, bf16) for size in sizes],
+            in_specs=[SMEM_SPEC, SMEM_SPEC, VMEM_SPEC, HBM_SPEC],
+            out_specs=[HBM_SPEC] * len(sizes),
+            scratch_shapes=[
+                pltpu.SMEM((CAP * instances + 1,), jnp.int32),
+                pltpu.VMEM((EXTRA, head_dim), f32),
+                pltpu.VMEM((len(copies),) + sent_shape, bf16),
+                pltpu.SemaphoreType.DMA((len(copies),)),
+                pltpu.SemaphoreType.DMA((stores,)),
+            ],
+            compiler_params=pltpu.CompilerParams(vmem_limit_bytes=56 * MIB),
+            cost_estimate=pl.CostEstimate(
+                flops=0, bytes_accessed=2 * stores * sent_bytes, transcendentals=0
+            ),
+            name="pack_blocks",
+        )(mig_dest, mig_block, part_scales, pool_rows)
 
     def swap(value, distance):
         return lax.ppermute(value, "inst", [(j, j ^ distance) for j in range(instances)])
 
     if general:
-        arrived = [send[0]] + [swap(send[k], k) for k in range(1, instances)]
-        places = [(k, r) for r in range(CAP) for k in range(instances)]
+        send = pack(
+            [CAP] * instances,
+            [(r * instances + k, [(k, r)]) for k in range(instances) for r in range(CAP)],
+        )
+        arrived = [swap(send[k], k) for k in range(instances - 1, 0, -1)] + [send[0]]
+        places = [(instances - 1 - k, r) for r in range(CAP) for k in range(instances)]
     else:
-        seconds = {0: send.pop()}
+        any_second = CAP * instances
+        (second,) = pack([1], [(any_second, [(0, 0)])])
+        seconds = {0: second}
         bit = instances // 2
         while bit > 1:
             for k in list(seconds):
                 seconds[k ^ bit] = swap(seconds[k], bit)
             bit //= 2
-        arrived = [send[0]] + [swap(send[k], k) for k in range(1, instances)]
+        mig_dest, second = lax.optimization_barrier((mig_dest, second))
+        send = pack(
+            [1, 2] + [1] * (instances - 2),
+            [(k, [(k, 0)]) for k in list(range(instances))[::-1]] + [(any_second, [(1, 1)])],
+        )
+        firsts = [send[0]] + [swap(send[k], k) for k in range(1, instances)]
+    part_scales, *send = lax.optimization_barrier((part_scales, *send))
     flat_scales = part_scales.reshape(1, -1).astype(f32)
 
     query_rows = (
@@ -488,10 +493,15 @@
         held, own_parts = lax.optimization_barrier((held, own_parts))
         for k in held:
             seconds[k ^ 1] = swap(held[k], 1)
-        places = [(k, 0) for k in range(instances)]
+        arrived = [held[k] for k in held] + firsts[::-1] + [seconds[0]]
+        where = {k: i for i, k in enumerate(held)}
+        where[0] = len(arrived) - 1
+        places = [(len(held) + instances - 1 - k, 0) for k in range(instances)]
         for k in range(instances):
             if k == 1:
-                places.append((1, 1))
+                places.append((places[1][0], 1))
+            elif k in where:
+                places.append((where[k], 0))
             else:
                 places.append((len(arrived), 0))
                 arrived.append(seconds[k])
@@ -522,23 +532,20 @@
         ),
         name="arrived_blocks",
     )(query_rows, tables, length, *own_parts, *arrived)
-    out = (
-        out.reshape(requests, q_heads, steps, head_dim)
-        .transpose(0, 2, 1, 3)
-        .reshape(requests, steps, q_heads * head_dim)
-    )
     return out, moved_to, more
 
 
-def shards(*args):
-    out, moved_to, more = attend(False, *args)
+def shards(queries, *args):
+    out, moved_to, more = attend(False, queries, *args)
     out = lax.cond(
         more[0] > 1,
         lambda out, *args: attend(True, *args)[0],
         lambda out, *args: out,
-        out, *args,
+        out, queries, *args,
     )
-    return out, moved_to
+    requests, steps, q_heads, head_dim = queries.shape
+    out = out.reshape(requests, q_heads, steps, head_dim).transpose(0, 2, 1, 3)
+    return out.reshape(requests, steps, q_heads * head_dim), moved_to
 
 
 def solution(mesh):

time: 35.2 us -> 35.9 us (1.020)
  waiting for transfers between devices: 5.23 us -> 2.99 us
  Pallas kernels: 17.6 us -> 19.7 us
  starting transfers between devices: 9.32 us -> 10.2 us
    ppermute x5, waiting for transfers between devices: 5.23 us -> 2.99 us  [swap(): lax.ppermute(value, 'inst', [(j, j ^ distance) for j in range(instances)])]
    pallas_call x1 -> x2, Pallas kernels: 2.75 us -> 4.88 us  [pack(): pl.pallas_call(functools.partial(pack_kernel, (instances, listed, heads,...]
    ppermute x5, starting transfers between devices: 9.32 us -> 10.2 us  [swap(): lax.ppermute(value, 'inst', [(j, j ^ distance) for j in range(instances)])]
  transfers between devices with their start and end apart: 5 -> 5, of which waited for: 2 -> 1; matrix products, arithmetic and copies ran while one was open for 1% -> 1% of each run, Pallas kernels for 35% -> 41%
where the time goes in v12:
time: 35.9 us; the launch traced here: 35.7 us
  Pallas kernels  19.7 us (55%)
  starting transfers between devices  10.2 us (28%)
  waiting for transfers between devices  2.99 us (8%)
  between operations  1.45 us (4%)
  local copies, waits for them, and re-layouts  1.36 us (4%)
    pallas_call x1, Pallas kernels, attend(): pl.pallas_call(functools.partial(own_kernel, (pool, heads, rows, steps, b...  12.3 us
    ppermute x5, starting transfers between devices, swap(): lax.ppermute(value, 'inst', [(j, j ^ distance) for j in range(instances)])  10.2 us
    pallas_call x2, Pallas kernels, pack(): pl.pallas_call(functools.partial(pack_kernel, (instances, listed, heads,...  4.88 us
    ppermute x5, waiting for transfers between devices, swap(): lax.ppermute(value, 'inst', [(j, j ^ distance) for j in range(instances)])  2.99 us
    pallas_call x1, Pallas kernels, attend(): pl.pallas_call(functools.partial(arrival_kernel, (pool, heads, rows, bloc...  2.6 us
    reshape x1, local copies, waits for them, and re-layouts, shards(): return (out.reshape(requests, steps, q_heads * head_dim), moved_to)  0.77 us
  transfers between devices with their start and end apart: 5, of which 1 were waited for; matrix products, arithmetic and copies ran while one was open for 1% of the time, Pallas kernels for 41%

profile of v12, /device:TPU:0, one launch (start us, length us, event | category | flops | bytes accessed | tf_op | source)
XLA Modules:
  0.0 35.7 jit_solution(6324313556255994785)
XLA Ops:
  0.6 0.0 copy-start.7
  0.6 0.0 copy-start.8
  0.7 0.0 copy-start.6
  0.7 0.0 copy-start.9
  0.7 0.0 copy-start.5
  0.7 0.0 copy-start.4
  0.7 0.0 copy-start.3
  0.7 2.4 %pack_blocks.4.refs_5_ = bf16[1,528,128]{2,1,0:T(8,128)(2,1)} custom-call(s32[1,4]{1,0:T(1,128)} %dest_ref.2, s32[1,4]{1,0:T(1,128)} %block_ref.3, bf16[2,2,48]{2,1,0:T(2,128)(2,1)} %bitcast.42, bf16[48,512,128]{2,1,0:T(8,128)(2,1)} %bitcast.30), custom_call_target="tpu_custom_call" | custom-call | bytes 270336 | tf_op jit(solution)/shard_map/pack_blocks/pallas_call | solution.py:405
  3.1 4.1 %collective-permute-start.3 = (bf16[1,528,128]{2,1,0:T(8,128)(2,1)}, bf16[1,528,128]{2,1,0:T(8,128)(2,1)S(1)}, u32[]{:S(2)}, u32[]{:S(2)}) collective-permute-start(bf16[1,528,128]{2,1,0:T(8,128)(2,1)} %pack_blocks.4.refs_5_), channel_id=1, source_target_pairs={{0,8},{4,12},{8,0},{12,4},{1,9},{5,13},{9,1},{13,5},{2,10},{6,14},... | collective-permute-start | bytes 405512 | tf_op jit(solution)/shard_map/ppermute | solution.py:425
  7.2 0.0 copy-done.7
  7.2 0.0 copy-done.8
  7.2 0.0 copy-done.6
  7.2 2.5 %pack_blocks.5 = (bf16[1,528,128]{2,1,0:T(8,128)(2,1)}, bf16[2,528,128]{2,1,0:T(8,128)(2,1)}, bf16[1,528,128]{2,1,0:T(8,128)(2,1)}, bf16[1,528,128]{2,1,0:T(8,128)(2,1)}) custom-call(s32[1,4]{1,0:T(1,128)S(1)} %copy-done.7, s32[1,4]{1,0:T(1,128)S(1)} %copy-done.8, bf16[2,2,48]{2,1,0:T(2,128)(2,1)S(1)} %bitcast.43, bf16[48,512,128]{2,1,0:T(8,128)(2,1)} %bitcast.31), custom_call_target="tpu_custom_call" | custom-call | bytes 1351680 | tf_op jit(solution)/shard_map/pack_blocks/pallas_call | solution.py:405
  9.7 0.1 collective-permute-start.5
  9.8 3.9 %collective-permute-start.4 = (bf16[1,528,128]{2,1,0:T(8,128)(2,1)}, bf16[1,528,128]{2,1,0:T(8,128)(2,1)S(1)}, u32[]{:S(2)}, u32[]{:S(2)}) collective-permute-start(bf16[1,528,128]{2,1,0:T(8,128)(2,1)} %get-tuple-element.59), channel_id=1, source_target_pairs={{0,12},{4,8},{8,4},{12,0},{1,13},{5,9},{9,5},{13,1},{2,14},{6,10},... | collective-permute-start | bytes 405512 | tf_op jit(solution)/shard_map/ppermute | solution.py:425
  13.7 0.0 collective-permute-start.6
  13.7 0.0 copy-done.9
  13.7 0.1 copy.18.length_ref
  13.8 0.0 copy-done.5
  13.8 0.1 copy.17.tables_ref
  13.9 0.0 copy-done.4
  13.9 0.1 copy.14
  13.9 0.0 copy-done.3
  14.0 0.0 copy-start
  14.0 0.0 copy-start.2
  14.0 0.2 copy.13
  14.2 0.1 reshape.75.scale_ref
  14.3 12.3 %own_blocks.3 = (f32[2,512,128]{2,1,0:T(8,128)S(1)}, f32[2,512,128]{2,1,0:T(8,128)S(1)}, f32[2,512,128]{2,1,0:T(8,128)S(1)}) custom-call(s32[32,16]{1,0:T(8,128)S(1)} %copy.17.tables_ref, s32[32,1]{1,0:T(8,128)S(1)} %copy.18.length_ref, f32[1,192]{1,0:T(1,128)S(1)} %reshape.75.scale_ref, bf16[2,512,128]{2,1,0:T(8,128)(2,1)S(1)} %bitcast.26, ...), custom_call_target="tpu_custom_call" | custom-call | flops 3221225472 | bytes 6291456 | tf_op jit(solution)/shard_map/own_blocks/pallas_call | solution.py:467
  26.6 0.0 collective-permute-done.3.refs_0_
  26.6 2.1 %collective-permute-start.7 = (bf16[1,528,128]{2,1,0:T(8,128)(2,1)S(1)}, bf16[1,528,128]{2,1,0:T(8,128)(2,1)S(1)}, u32[]{:S(2)}, u32[]{:S(2)}) collective-permute-start(bf16[1,528,128]{2,1,0:T(8,128)(2,1)S(1)} %collective-permute-done.3.refs_0_), channel_id=1, source_target_pairs={{0,4},{4,0},{8,12},{12,8},{1,5},{5,1},{9,13},{13,9},{2,6},{6,2},{1... | collective-permute-start | bytes 405512 | tf_op jit(solution)/shard_map/ppermute | solution.py:425
  28.7 0.0 collective-permute-done.5.refs_2_
  28.7 0.0 collective-permute-done.4.refs_1_
  28.7 0.0 collective-permute-done.6.refs_3_
  28.7 3.0 %collective-permute-done.7.refs_6_ = bf16[1,528,128]{2,1,0:T(8,128)(2,1)S(1)} collective-permute-done((bf16[1,528,128]{2,1,0:T(8,128)(2,1)S(1)}, bf16[1,528,128]{2,1,0:T(8,128)(2,1)S(1)}, u32[]{:S(2)}, u32[]{:S(2)}) %collective-permute-start.7) | collective-permute-done | bytes 135200 | tf_op jit(solution)/shard_map/ppermute | solution.py:425
  31.6 0.0 copy-done
  31.6 0.0 copy-done.2
  31.6 2.6 %arrived_blocks.3 = (bf16[32,2,16,128]{3,2,1,0:T(8,128)(2,1)S(1)}, s32[1,4]{1,0:T(1,128)}, s32[1]{0:T(128)}) custom-call(bf16[2,512,128]{2,1,0:T(8,128)(2,1)S(1)} %bitcast.27, s32[32,16]{1,0:T(8,128)S(1)} %copy.17.tables_ref, s32[32,1]{1,0:T(8,128)S(1)} %copy.18.length_ref, f32[2,512,128]{2,1,0:T(8,128)S(1)} %get-tuple-element.64.acc_ref, ...), custom_call_target="tpu_custom_call" | custom-call | flops 536870912 | bytes 1081344 | tf_op jit(solution)/shard_map/arrived_blocks/pallas_call | solution.py:511
  35.0 0.8 %reshape.73 = bf16[32,2,2048]{2,1,0:T(2,128)(2,1)} reshape(bf16[32,2,16,128]{3,2,1,0:T(8,128)(2,1)S(1)} %bitcast.37) | data formatting | bytes 524288 | tf_op jit(solution)/shard_map/reshape | solution.py:548
  (3 shorter events, 0.1 us)
Async XLA Ops:
  0.6 6.6 %copy-start.7 = (s32[1,4]{1,0:T(1,128)S(1)}, s32[1,4]{1,0:T(1,128)}, u32[]{:S(2)}) copy-start(s32[1,4]{1,0:T(1,128)} %dest_ref.2) | copy-start | bytes 52
  0.6 6.6 %copy-start.8 = (s32[1,4]{1,0:T(1,128)S(1)}, s32[1,4]{1,0:T(1,128)}, u32[]{:S(2)}) copy-start(s32[1,4]{1,0:T(1,128)} %block_ref.3) | copy-start | bytes 52
  0.7 6.6 %copy-start.6 = (bf16[48,2,2]{0,2,1:T(2,128)(2,1)S(1)}, bf16[48,2,2]{0,2,1:T(2,128)(2,1)}, u32[]{:S(2)}) copy-start(bf16[48,2,2]{0,2,1:T(2,128)(2,1)} %param.13) | copy-start | bytes 1156
  0.7 13.1 %copy-start.9 = (s32[32]{0:T(128)S(1)}, s32[32]{0:T(128)}, u32[]{:S(2)}) copy-start(s32[32]{0:T(128)} %param.15) | copy-start | bytes 388
  0.7 13.1 %copy-start.5 = (s32[32,16]{0,1:T(8,128)S(1)}, s32[32,16]{0,1:T(8,128)}, u32[]{:S(2)}) copy-start(s32[32,16]{0,1:T(8,128)} %param.14) | copy-start | bytes 6148
  0.7 13.2 %copy-start.4 = (bf16[32,2,2,2,128]{4,3,2,1,0:T(2,128)(2,1)S(1)}, bf16[32,2,2,2,128]{4,3,2,1,0:T(2,128)(2,1)}, u32[]{:S(2)}) copy-start(bf16[32,2,2,2,128]{4,3,2,1,0:T(2,128)(2,1)} %param.11) | copy-start | bytes 196612
  0.7 13.3 %copy-start.3 = (bf16[32,2,16,128]{3,2,1,0:T(8,128)(2,1)S(1)}, bf16[32,2,16,128]{3,2,1,0:T(8,128)(2,1)}, u32[]{:S(2)}) copy-start(bf16[32,2,16,128]{3,2,1,0:T(8,128)(2,1)} %param.10) | copy-start | bytes 786436
  3.1 23.4 %collective-permute-start.3 = (bf16[1,528,128]{2,1,0:T(8,128)(2,1)}, bf16[1,528,128]{2,1,0:T(8,128)(2,1)S(1)}, u32[]{:S(2)}, u32[]{:S(2)}) collective-permute-start(bf16[1,528,128]{2,1,0:T(8,128)(2,1)} %pack_blocks.4.refs_5_), channel_id=1, source_target_pairs={{0,8},{4,12},{8,0},{12,4},{1,9},{5,13},{9,1},{13,5},{2,10},{6,14},... | collective-permute-start | bytes 405512 | tf_op jit(solution)/shard_map/ppermute | solution.py:425
  9.7 18.9 %collective-permute-start.5 = (bf16[1,528,128]{2,1,0:T(8,128)(2,1)}, bf16[1,528,128]{2,1,0:T(8,128)(2,1)S(1)}, u32[]{:S(2)}, u32[]{:S(2)}) collective-permute-start(bf16[1,528,128]{2,1,0:T(8,128)(2,1)} %get-tuple-element.58), channel_id=1, source_target_pairs={{0,8},{4,12},{8,0},{12,4},{1,9},{5,13},{9,1},{13,5},{2,10},{6,14},... | collective-permute-start | bytes 405512 | tf_op jit(solution)/shard_map/ppermute | solution.py:425
  9.8 18.8 %collective-permute-start.4 = (bf16[1,528,128]{2,1,0:T(8,128)(2,1)}, bf16[1,528,128]{2,1,0:T(8,128)(2,1)S(1)}, u32[]{:S(2)}, u32[]{:S(2)}) collective-permute-start(bf16[1,528,128]{2,1,0:T(8,128)(2,1)} %get-tuple-element.59), channel_id=1, source_target_pairs={{0,12},{4,8},{8,4},{12,0},{1,13},{5,9},{9,5},{13,1},{2,14},{6,10},... | collective-permute-start | bytes 405512 | tf_op jit(solution)/shard_map/ppermute | solution.py:425
  13.7 14.9 %collective-permute-start.6 = (bf16[2,528,128]{2,1,0:T(8,128)(2,1)}, bf16[2,528,128]{2,1,0:T(8,128)(2,1)S(1)}, u32[]{:S(2)}, u32[]{:S(2)}) collective-permute-start(bf16[2,528,128]{2,1,0:T(8,128)(2,1)} %get-tuple-element.57), channel_id=1, source_target_pairs={{0,4},{4,0},{8,12},{12,8},{1,5},{5,1},{9,13},{13,9},{2,6},{6,2},{1... | collective-permute-start | bytes 811016 | tf_op jit(solution)/shard_map/ppermute | solution.py:425
  14.0 17.7 %copy-start = (bf16[1,528,128]{2,1,0:T(8,128)(2,1)S(1)}, bf16[1,528,128]{2,1,0:T(8,128)(2,1)}, u32[]{:S(2)}) copy-start(bf16[1,528,128]{2,1,0:T(8,128)(2,1)} %pack_blocks.4.refs_5_) | copy-start | bytes 405508
  14.0 17.7 %copy-start.2 = (bf16[1,528,128]{2,1,0:T(8,128)(2,1)S(1)}, bf16[1,528,128]{2,1,0:T(8,128)(2,1)}, u32[]{:S(2)}) copy-start(bf16[1,528,128]{2,1,0:T(8,128)(2,1)} %get-tuple-element.56.refs_4_) | copy-start | bytes 405508
  26.6 5.1 %collective-permute-start.7 = (bf16[1,528,128]{2,1,0:T(8,128)(2,1)S(1)}, bf16[1,528,128]{2,1,0:T(8,128)(2,1)S(1)}, u32[]{:S(2)}, u32[]{:S(2)}) collective-permute-start(bf16[1,528,128]{2,1,0:T(8,128)(2,1)S(1)} %collective-permute-done.3.refs_0_), channel_id=1, source_target_pairs={{0,4},{4,0},{8,12},{12,8},{1,5},{5,1},{9,13},{13,9},{2,6},{6,2},{1... | collective-permute-start | bytes 405512 | tf_op jit(solution)/shard_map/ppermute | solution.py:425

commit v13 on v12

--- a/solution.py
+++ b/solution.py
@@ -490,7 +490,6 @@
 
     if not general:
         held = {k: second for k, second in seconds.items() if k}
-        held, own_parts = lax.optimization_barrier((held, own_parts))
         for k in held:
             seconds[k ^ 1] = swap(held[k], 1)
         arrived = [held[k] for k in held] + firsts[::-1] + [seconds[0]]
@@ -532,20 +531,18 @@
         ),
         name="arrived_blocks",
     )(query_rows, tables, length, *own_parts, *arrived)
-    return out, moved_to, more
-
-
-def shards(queries, *args):
-    out, moved_to, more = attend(False, queries, *args)
-    out = lax.cond(
-        more[0] > 1,
-        lambda out, *args: attend(True, *args)[0],
-        lambda out, *args: out,
-        out, queries, *args,
+    out = out.reshape(requests, q_heads, steps, head_dim).transpose(0, 2, 1, 3)
+    return out.reshape(requests, steps, q_heads * head_dim), moved_to, more
+
+
+def shards(*args):
+    out, moved_to, more = attend(False, *args)
+    _, out = lax.while_loop(
+        lambda state: state[0] > 1,
+        lambda state: (jnp.int32(0), attend(True, *args)[0]),
+        (more[0], out),
     )
-    requests, steps, q_heads, head_dim = queries.shape
-    out = out.reshape(requests, q_heads, steps, head_dim).transpose(0, 2, 1, 3)
-    return out.reshape(requests, steps, q_heads * head_dim), moved_to
+    return out, moved_to
 
 
 def solution(mesh):

time: 35.9 us -> 37.2 us (1.036)
  waiting for transfers between devices: 2.99 us -> 5.62 us
  starting transfers between devices: 10.2 us -> 8.88 us
  Pallas kernels: 19.7 us -> 20.5 us
  local copies, waits for them, and re-layouts: 1.36 us -> 0.61 us
  loops' own time: 0.01 us -> 0.64 us
  between operations: 1.45 us -> 0.83 us
    ppermute x5, waiting for transfers between devices: 2.99 us -> 5.62 us  [swap(): lax.ppermute(value, 'inst', [(j, j ^ distance) for j in range(instances)])]
    ppermute x5, starting transfers between devices: 10.2 us -> 8.88 us  [swap(): lax.ppermute(value, 'inst', [(j, j ^ distance) for j in range(instances)])]
    reshape x2 -> x0, local copies, waits for them, and re-layouts: 0.8 us -> none  [the longest x1 0.77 us: shards(): return (out.reshape(requests, steps, q_heads * head_dim), moved_to)]
    another operation x1, loops' own time: 0.01 us -> 0.64 us  [shards(): lax.while_loop(lambda state: state[0] > 1, lambda state: (jnp.int32(0), a...]
    pallas_call x1, Pallas kernels: 12.3 us -> 12.7 us  [attend(): pl.pallas_call(functools.partial(own_kernel, (pool, heads, rows, steps, b...]
  transfers between devices with their start and end apart: 5 -> 5, of which waited for: 1 -> 1; matrix products, arithmetic and copies ran while one was open for 1% -> 2% of each run, Pallas kernels for 41% -> 41%
where the time goes in v13:
time: 37.2 us; the launch traced here: 37.1 us
  Pallas kernels  20.5 us (55%)
  starting transfers between devices  8.88 us (24%)
  waiting for transfers between devices  5.62 us (15%)
  between operations  0.83 us (2%)
  loops' own time  0.64 us (2%)
  local copies, waits for them, and re-layouts  0.61 us (2%)
    pallas_call x1, Pallas kernels, attend(): pl.pallas_call(functools.partial(own_kernel, (pool, heads, rows, steps, b...  12.7 us
    ppermute x5, starting transfers between devices, swap(): lax.ppermute(value, 'inst', [(j, j ^ distance) for j in range(instances)])  8.88 us
    ppermute x5, waiting for transfers between devices, swap(): lax.ppermute(value, 'inst', [(j, j ^ distance) for j in range(instances)])  5.62 us
    pallas_call x2, Pallas kernels, pack(): pl.pallas_call(functools.partial(pack_kernel, (instances, listed, heads,...  4.88 us
    pallas_call x1, Pallas kernels, attend(): pl.pallas_call(functools.partial(arrival_kernel, (pool, heads, rows, bloc...  2.92 us
  transfers between devices with their start and end apart: 5, of which 1 were waited for; matrix products, arithmetic and copies ran while one was open for 2% of the time, Pallas kernels for 41%

profile of v13, /device:TPU:0, one launch (start us, length us, event | category | flops | bytes accessed | tf_op | source)
XLA Modules:
  0.0 37.1 jit_solution(12020034699686548136)
XLA Ops:
  0.6 0.0 copy-start.6
  0.6 0.0 copy-start.7
  0.7 0.0 copy-start.5
  0.7 0.0 copy-start.9
  0.7 0.0 copy-start.8
  0.7 0.0 copy-start.4
  0.7 0.0 copy-start.3
  0.7 2.4 %pack_blocks.4.refs_5_ = bf16[1,528,128]{2,1,0:T(8,128)(2,1)} custom-call(s32[1,4]{1,0:T(1,128)} %dest_ref.2, s32[1,4]{1,0:T(1,128)} %block_ref.3, bf16[2,2,48]{2,1,0:T(2,128)(2,1)} %bitcast.44, bf16[48,512,128]{2,1,0:T(8,128)(2,1)} %bitcast.34), custom_call_target="tpu_custom_call" | custom-call | bytes 270336 | tf_op jit(solution)/shard_map/pack_blocks/pallas_call | solution.py:405
  3.1 4.1 %collective-permute-start.3 = (bf16[1,528,128]{2,1,0:T(8,128)(2,1)}, bf16[1,528,128]{2,1,0:T(8,128)(2,1)S(1)}, u32[]{:S(2)}, u32[]{:S(2)}) collective-permute-start(bf16[1,528,128]{2,1,0:T(8,128)(2,1)} %pack_blocks.4.refs_5_), channel_id=1, source_target_pairs={{0,8},{4,12},{8,0},{12,4},{1,9},{5,13},{9,1},{13,5},{2,10},{6,14},... | collective-permute-start | bytes 405512 | tf_op jit(solution)/shard_map/ppermute | solution.py:425
  7.2 0.0 copy-done.6
  7.2 0.0 copy-done.7
  7.2 0.0 copy-done.5
  7.2 2.5 %pack_blocks.5 = (bf16[1,528,128]{2,1,0:T(8,128)(2,1)}, bf16[2,528,128]{2,1,0:T(8,128)(2,1)}, bf16[1,528,128]{2,1,0:T(8,128)(2,1)}, bf16[1,528,128]{2,1,0:T(8,128)(2,1)}) custom-call(s32[1,4]{1,0:T(1,128)S(1)} %copy-done.6, s32[1,4]{1,0:T(1,128)S(1)} %copy-done.7, bf16[2,2,48]{2,1,0:T(2,128)(2,1)S(1)} %bitcast.45, bf16[48,512,128]{2,1,0:T(8,128)(2,1)} %bitcast.35), custom_call_target="tpu_custom_call" | custom-call | bytes 1351680 | tf_op jit(solution)/shard_map/pack_blocks/pallas_call | solution.py:405
  9.7 0.1 collective-permute-start.5
  9.8 3.9 %collective-permute-start.4 = (bf16[1,528,128]{2,1,0:T(8,128)(2,1)}, bf16[1,528,128]{2,1,0:T(8,128)(2,1)S(1)}, u32[]{:S(2)}, u32[]{:S(2)}) collective-permute-start(bf16[1,528,128]{2,1,0:T(8,128)(2,1)} %get-tuple-element.77), channel_id=1, source_target_pairs={{0,12},{4,8},{8,4},{12,0},{1,13},{5,9},{9,5},{13,1},{2,14},{6,10},... | collective-permute-start | bytes 405512 | tf_op jit(solution)/shard_map/ppermute | solution.py:425
  13.7 0.0 collective-permute-start.6
  13.7 0.0 copy-done.9
  13.7 0.1 copy.17.tables_ref
  13.8 0.0 copy-done.8
  13.8 0.1 copy.18.length_ref
  13.9 0.0 copy-done.4
  13.9 0.1 copy.14
  13.9 0.0 copy-done.3
  14.0 0.0 copy-start.1
  14.0 0.0 copy-start.2
  14.0 0.2 copy.13
  14.2 0.1 reshape.77.scale_ref
  14.3 5.6 %collective-permute-done.3.refs_0_ = bf16[1,528,128]{2,1,0:T(8,128)(2,1)S(1)} collective-permute-done((bf16[1,528,128]{2,1,0:T(8,128)(2,1)}, bf16[1,528,128]{2,1,0:T(8,128)(2,1)S(1)}, u32[]{:S(2)}, u32[]{:S(2)}) %collective-permute-start.3) | collective-permute-done | bytes 135200 | tf_op jit(solution)/shard_map/ppermute | solution.py:425
  19.9 0.8 %collective-permute-start.7 = (bf16[1,528,128]{2,1,0:T(8,128)(2,1)S(1)}, bf16[1,528,128]{2,1,0:T(8,128)(2,1)S(1)}, u32[]{:S(2)}, u32[]{:S(2)}) collective-permute-start(bf16[1,528,128]{2,1,0:T(8,128)(2,1)S(1)} %collective-permute-done.3.refs_0_), channel_id=1, source_target_pairs={{0,4},{4,0},{8,12},{12,8},{1,5},{5,1},{9,13},{13,9},{2,6},{6,2},{1... | collective-permute-start | bytes 405512 | tf_op jit(solution)/shard_map/ppermute | solution.py:425
  20.7 12.7 %own_blocks.3 = (f32[2,512,128]{2,1,0:T(8,128)S(1)}, f32[2,512,128]{2,1,0:T(8,128)S(1)}, f32[2,512,128]{2,1,0:T(8,128)S(1)}) custom-call(s32[32,16]{1,0:T(8,128)S(1)} %copy.17.tables_ref, s32[32,1]{1,0:T(8,128)S(1)} %copy.18.length_ref, f32[1,192]{1,0:T(1,128)S(1)} %reshape.77.scale_ref, bf16[2,512,128]{2,1,0:T(8,128)(2,1)S(1)} %bitcast.32, ...), custom_call_target="tpu_custom_call" | custom-call | flops 3221225472 | bytes 6291456 | tf_op jit(solution)/shard_map/own_blocks/pallas_call | solution.py:467
  33.4 0.1 copy.19
  33.4 0.0 collective-permute-done.5.refs_2_
  33.4 0.0 collective-permute-done.4.refs_1_
  33.4 0.0 collective-permute-done.7.refs_6_
  33.5 0.0 collective-permute-done.6.refs_3_
  33.5 0.0 copy-done.1
  33.5 0.0 copy-done.2
  33.5 2.9 %arrived_blocks.3 = (bf16[32,2,16,128]{3,2,1,0:T(8,128)(2,1)}, s32[1,4]{1,0:T(1,128)}, s32[1]{0:T(128)}) custom-call(bf16[2,512,128]{2,1,0:T(8,128)(2,1)S(1)} %bitcast.33, s32[32,16]{1,0:T(8,128)S(1)} %copy.17.tables_ref, s32[32,1]{1,0:T(8,128)S(1)} %copy.18.length_ref, f32[2,512,128]{2,1,0:T(8,128)S(1)} %get-tuple-element.79.acc_ref, ...), custom_call_target="tpu_custom_call" | custom-call | flops 536870912 | bytes 1081344 | tf_op jit(solution)/shard_map/arrived_blocks/pallas_call | solution.py:510
  36.4 0.6 %while.9 = (s32[]{:T(128)}, bf16[32,2,2048]{2,1,0:T(2,128)(2,1)}, bf16[32,2,16,128]{3,2,1,0:T(8,128)(2,1)S(1)}, s32[32]{0:T(128)S(1)}, bf16[48,2,2]{0,2,1:T(2,12...) while((s32[]{:T(128)}, bf16[32,2,2048]{2,1,0:T(2,128)(2,1)}, ...), condition=%region_1.2_spmd, body=%region_0.1_spmd | while | flops 3758096384 | bytes 14583415 | solution.py:540
  (1 shorter events, 0.0 us)
Async XLA Ops:
  0.6 6.6 %copy-start.6 = (s32[1,4]{1,0:T(1,128)S(1)}, s32[1,4]{1,0:T(1,128)}, u32[]{:S(2)}) copy-start(s32[1,4]{1,0:T(1,128)} %dest_ref.2) | copy-start | bytes 52
  0.6 6.6 %copy-start.7 = (s32[1,4]{1,0:T(1,128)S(1)}, s32[1,4]{1,0:T(1,128)}, u32[]{:S(2)}) copy-start(s32[1,4]{1,0:T(1,128)} %block_ref.3) | copy-start | bytes 52
  0.7 6.6 %copy-start.5 = (bf16[48,2,2]{0,2,1:T(2,128)(2,1)S(1)}, bf16[48,2,2]{0,2,1:T(2,128)(2,1)}, u32[]{:S(2)}) copy-start(bf16[48,2,2]{0,2,1:T(2,128)(2,1)} %param.13) | copy-start | bytes 1156
  0.7 13.1 %copy-start.9 = (s32[32,16]{0,1:T(8,128)S(1)}, s32[32,16]{0,1:T(8,128)}, u32[]{:S(2)}) copy-start(s32[32,16]{0,1:T(8,128)} %param.14) | copy-start | bytes 6148
  0.7 13.1 %copy-start.8 = (s32[32]{0:T(128)S(1)}, s32[32]{0:T(128)}, u32[]{:S(2)}) copy-start(s32[32]{0:T(128)} %param.15) | copy-start | bytes 388
  0.7 13.2 %copy-start.4 = (bf16[32,2,2,2,128]{4,3,2,1,0:T(2,128)(2,1)S(1)}, bf16[32,2,2,2,128]{4,3,2,1,0:T(2,128)(2,1)}, u32[]{:S(2)}) copy-start(bf16[32,2,2,2,128]{4,3,2,1,0:T(2,128)(2,1)} %param.11) | copy-start | bytes 196612
  0.7 13.3 %copy-start.3 = (bf16[32,2,16,128]{3,2,1,0:T(8,128)(2,1)S(1)}, bf16[32,2,16,128]{3,2,1,0:T(8,128)(2,1)}, u32[]{:S(2)}) copy-start(bf16[32,2,16,128]{3,2,1,0:T(8,128)(2,1)} %param.10) | copy-start | bytes 786436
  3.1 16.8 %collective-permute-start.3 = (bf16[1,528,128]{2,1,0:T(8,128)(2,1)}, bf16[1,528,128]{2,1,0:T(8,128)(2,1)S(1)}, u32[]{:S(2)}, u32[]{:S(2)}) collective-permute-start(bf16[1,528,128]{2,1,0:T(8,128)(2,1)} %pack_blocks.4.refs_5_), channel_id=1, source_target_pairs={{0,8},{4,12},{8,0},{12,4},{1,9},{5,13},{9,1},{13,5},{2,10},{6,14},... | collective-permute-start | bytes 405512 | tf_op jit(solution)/shard_map/ppermute | solution.py:425
  9.7 23.7 %collective-permute-start.5 = (bf16[1,528,128]{2,1,0:T(8,128)(2,1)}, bf16[1,528,128]{2,1,0:T(8,128)(2,1)S(1)}, u32[]{:S(2)}, u32[]{:S(2)}) collective-permute-start(bf16[1,528,128]{2,1,0:T(8,128)(2,1)} %get-tuple-element.76), channel_id=1, source_target_pairs={{0,8},{4,12},{8,0},{12,4},{1,9},{5,13},{9,1},{13,5},{2,10},{6,14},... | collective-permute-start | bytes 405512 | tf_op jit(solution)/shard_map/ppermute | solution.py:425
  9.8 23.6 %collective-permute-start.4 = (bf16[1,528,128]{2,1,0:T(8,128)(2,1)}, bf16[1,528,128]{2,1,0:T(8,128)(2,1)S(1)}, u32[]{:S(2)}, u32[]{:S(2)}) collective-permute-start(bf16[1,528,128]{2,1,0:T(8,128)(2,1)} %get-tuple-element.77), channel_id=1, source_target_pairs={{0,12},{4,8},{8,4},{12,0},{1,13},{5,9},{9,5},{13,1},{2,14},{6,10},... | collective-permute-start | bytes 405512 | tf_op jit(solution)/shard_map/ppermute | solution.py:425
  13.7 19.7 %collective-permute-start.6 = (bf16[2,528,128]{2,1,0:T(8,128)(2,1)}, bf16[2,528,128]{2,1,0:T(8,128)(2,1)S(1)}, u32[]{:S(2)}, u32[]{:S(2)}) collective-permute-start(bf16[2,528,128]{2,1,0:T(8,128)(2,1)} %get-tuple-element.75), channel_id=1, source_target_pairs={{0,4},{4,0},{8,12},{12,8},{1,5},{5,1},{9,13},{13,9},{2,6},{6,2},{1... | collective-permute-start | bytes 811016 | tf_op jit(solution)/shard_map/ppermute | solution.py:425
  14.0 19.5 %copy-start.1 = (bf16[1,528,128]{2,1,0:T(8,128)(2,1)S(1)}, bf16[1,528,128]{2,1,0:T(8,128)(2,1)}, u32[]{:S(2)}) copy-start(bf16[1,528,128]{2,1,0:T(8,128)(2,1)} %pack_blocks.4.refs_5_) | copy-start | bytes 405508
  14.0 19.5 %copy-start.2 = (bf16[1,528,128]{2,1,0:T(8,128)(2,1)S(1)}, bf16[1,528,128]{2,1,0:T(8,128)(2,1)}, u32[]{:S(2)}) copy-start(bf16[1,528,128]{2,1,0:T(8,128)(2,1)} %get-tuple-element.74.refs_4_) | copy-start | bytes 405508
  19.9 13.5 %collective-permute-start.7 = (bf16[1,528,128]{2,1,0:T(8,128)(2,1)S(1)}, bf16[1,528,128]{2,1,0:T(8,128)(2,1)S(1)}, u32[]{:S(2)}, u32[]{:S(2)}) collective-permute-start(bf16[1,528,128]{2,1,0:T(8,128)(2,1)S(1)} %collective-permute-done.3.refs_0_), channel_id=1, source_target_pairs={{0,4},{4,0},{8,12},{12,8},{1,5},{5,1},{9,13},{13,9},{2,6},{6,2},{1... | collective-permute-start | bytes 405512 | tf_op jit(solution)/shard_map/ppermute | solution.py:425

commit v14 on v13

--- a/solution.py
+++ b/solution.py
@@ -10,6 +10,7 @@
 
 CAP = 2
 EXTRA = 16
+NEVER = -1e30
 LOG2E = math.log2(math.e)
 MIB = 1 << 20
 SMEM_SPEC = pl.BlockSpec(memory_space=pltpu.SMEM)
@@ -108,20 +109,36 @@
         part = part + jnp.where(hit & (whole == e), 1.0, 0.0)
 
     def log2(count):
-        return jnp.where(count > 0, jnp.log(jnp.maximum(count, 1.0)) * LOG2E, -jnp.inf)
+        return jnp.where(count > 0, jnp.log(jnp.maximum(count, 1.0)) * LOG2E, NEVER)
 
     beyond, within = log2(full), log2(full + part)
     shape = (requests, block_len)
     inside = lax.broadcasted_iota(jnp.int32, shape, 1) < jnp.broadcast_to(rest, shape)
-    for b in range(width):
-        store(
-            b,
-            jnp.where(
-                inside,
-                jnp.broadcast_to(within[:, b : b + 1], shape),
-                jnp.broadcast_to(beyond[:, b : b + 1], shape),
-            ),
-        )
+    if width % 16:
+        for b in range(width):
+            store(
+                b,
+                jnp.where(
+                    inside,
+                    jnp.broadcast_to(within[:, b : b + 1], shape),
+                    jnp.broadcast_to(beyond[:, b : b + 1], shape),
+                ),
+            )
+        return
+    both = jnp.concatenate([within, beyond], axis=0)
+    high = both.astype(jnp.bfloat16)
+    low = (both - high.astype(jnp.float32)).astype(jnp.bfloat16)
+    terms = jnp.concatenate([high, low], axis=0)
+    row = lax.broadcasted_iota(jnp.int32, (width, block_len), 0)
+    for b in range(0, width, 2):
+        spots = jnp.concatenate(
+            [jnp.where(row == b + i, 1.0, 0.0).astype(jnp.bfloat16) for i in range(2)], axis=1
+        )
+        spread_out = jnp.dot(terms, spots, preferred_element_type=jnp.float32)
+        value = spread_out[: 2 * requests] + spread_out[2 * requests :]
+        for i in range(2):
+            at = slice(i * block_len, (i + 1) * block_len)
+            store(b + i, jnp.where(inside, value[:requests, at], value[requests:, at]))
 
 
 def score_tiles(query, keys, log_ref, scale_row, rows, store):
@@ -165,15 +182,16 @@
     acc_ref, top_ref, total_ref,
     log_ref, row_ref, t_ref, p_ref, codes_ref, sems,
 ):
-    pool, heads, rows, steps, block_len, spans, factor, group = dims
+    head, pool, heads, rows, steps, block_len, spans, factor, group = dims
     chunks = pool // group
     height, head_dim = q_ref.shape[1:]
     width = group * block_len
-    part_rows = heads * block_len
 
     def load(part, chunk):
         return pltpu.make_async_copy(
-            pool_ref.at[pl.ds(chunk * group, group), pl.ds(part * part_rows, part_rows)],
+            pool_ref.at[
+                pl.ds(chunk * group, group), pl.ds((part * heads + head) * block_len, block_len)
+            ],
             codes_ref.at[part, chunk],
             sems.at[part, chunk],
         )
@@ -191,78 +209,66 @@
     count_log(tables_ref[...], length_ref[...], ids, block_len, spans, store_log)
     for b in range(pool):
         lane = (b % group) * block_len
-        for row in range(2 * heads):
-            unit = factor * LOG2E if row < heads else 1.0
-            row_ref[b // group, row : row + 1, lane : lane + block_len] = jnp.full(
-                (1, block_len), scale_ref[0, row * pool + b] * unit
-            )
+        row_ref[b // group, :, lane : lane + block_len] = jnp.broadcast_to(
+            scale_ref[:, b : b + 1], (2 * heads, block_len)
+        )
     shape = (height, fresh_ref.shape[2])
     row = lax.broadcasted_iota(jnp.int32, shape, 0)
     col = lax.broadcasted_iota(jnp.int32, shape, 1)
     (request, row_step), (owner, step) = split(row, rows), split(col, steps)
     seen = (request == owner) & (split(row_step, steps)[1] >= step)
-    for h in range(heads):
-        new_score = lax.dot_general(
-            q_ref[h], fresh_ref[0, h], NT, preferred_element_type=jnp.float32
-        )
-        new_score = jnp.where(seen, new_score * (factor * LOG2E), -jnp.inf)
-        acc_ref[h] = new_score
-        top_ref[h] = lane_fold(new_score, jnp.maximum)
+    new_score = lax.dot_general(
+        q_ref[head], fresh_ref[0, head], NT, preferred_element_type=jnp.float32
+    )
+    new_score = jnp.where(seen, new_score * (factor * LOG2E), -jnp.inf)
+    acc_ref[...] = new_score
+    top_ref[...] = lane_fold(new_score, jnp.maximum)
 
     def score(chunk, carry):
         load(0, chunk).wait()
-        for h in range(heads):
-
-            def store(row, lane, value, h=h):
-                t_ref[h, chunk, row : row + rows, lane : lane + value.shape[1]] = value
-
-            score_tiles(
-                q_ref[h],
-                codes_ref[0, chunk, :, h * block_len : (h + 1) * block_len].reshape(width, head_dim),
-                log_ref.at[chunk],
-                row_ref[chunk, h : h + 1, :],
-                rows,
-                store,
-            )
-            for row in range(0, height, rows):
-                at = pl.ds(row, rows)
-                top_ref[h, at] = jnp.maximum(
-                    top_ref[h, at], lane_fold(t_ref[h, chunk, at], jnp.maximum)
-                )
+
+        def store(row, lane, value):
+            t_ref[chunk, row : row + rows, lane : lane + value.shape[1]] = value
+
+        score_tiles(
+            q_ref[head],
+            codes_ref[0, chunk].reshape(width, head_dim),
+            log_ref.at[chunk],
+            row_ref[chunk, head : head + 1, :] * (factor * LOG2E),
+            rows,
+            store,
+        )
+        for row in range(0, height, rows):
+            at = pl.ds(row, rows)
+            top_ref[at] = jnp.maximum(top_ref[at], lane_fold(t_ref[chunk, at], jnp.maximum))
         return carry
 
     lax.fori_loop(0, chunks, score, 0)
 
-    for h in range(heads):
-        top = jnp.broadcast_to(jnp.max(top_ref[h], axis=1, keepdims=True), (height, 128))
-        top_ref[h] = top
-        weight = jnp.exp2(acc_ref[h] - spread(top, acc_ref.shape[2]))
-        total_ref[h] = lane_fold(weight, jnp.add)
-        acc_ref[h] = jnp.dot(
-            weight.astype(jnp.bfloat16), fresh_ref[1, h], preferred_element_type=jnp.float32
-        )
+    top = jnp.broadcast_to(jnp.max(top_ref[...], axis=1, keepdims=True), (height, 128))
+    top_ref[...] = top
+    weight = jnp.exp2(acc_ref[...] - spread(top, acc_ref.shape[1]))
+    total_ref[...] = lane_fold(weight, jnp.add)
+    acc_ref[...] = jnp.dot(
+        weight.astype(jnp.bfloat16), fresh_ref[1, head], preferred_element_type=jnp.float32
+    )
 
     def apply(chunk, carry):
         load(1, chunk).wait()
-        for h in range(heads):
-            scale = row_ref[chunk, heads + h : heads + h + 1, :]
-            for row in range(0, height, rows):
-                at = pl.ds(row, rows)
-                weight = jnp.exp2(t_ref[h, chunk, at] - spread(top_ref[h, at], width))
-                total_ref[h, at] += lane_fold(weight, jnp.add)
-                p_ref[h, at] = (weight * scale).astype(jnp.bfloat16)
-            acc_ref[h] += jnp.dot(
-                p_ref[h],
-                codes_ref[1, chunk, :, h * block_len : (h + 1) * block_len].reshape(width, head_dim),
-                preferred_element_type=jnp.float32,
-            )
+        scale = row_ref[chunk, heads + head : heads + head + 1, :]
+        for row in range(0, height, rows):
+            at = pl.ds(row, rows)
+            weight = jnp.exp2(t_ref[chunk, at] - spread(top_ref[at], width))
+            total_ref[at] += lane_fold(weight, jnp.add)
+            p_ref[at] = (weight * scale).astype(jnp.bfloat16)
+        acc_ref[...] += jnp.dot(
+            p_ref[...],
+            codes_ref[1, chunk].reshape(width, head_dim),
+            preferred_element_type=jnp.float32,
+        )
         return carry
 
     lax.fori_loop(0, chunks, apply, 0)
-    for h in range(heads):
-        total_ref[h] = jnp.broadcast_to(
-            jnp.sum(total_ref[h], axis=1, keepdims=True), (height, 128)
-        )
 
 
 def arrival_ids(me, pool, lists, listed):
@@ -302,9 +308,10 @@
     return ids.astype(jnp.int32), moved[:, :listed].astype(jnp.int32), more
 
 
-def arrival_kernel(dims, places, q_ref, tables_ref, length_ref, acc_ref, top_ref, total_ref, *refs):
+def arrival_kernel(dims, places, q_ref, tables_ref, length_ref, *refs):
     pool, heads, rows, block_len, spans, listed, factor = dims
-    code_refs, (out_ref, moved_ref, more_ref, log_ref, t_ref, p_ref) = refs[:-6], refs[-6:]
+    own_refs, code_refs = refs[: 3 * heads], refs[3 * heads : -6]
+    out_ref, moved_ref, more_ref, log_ref, t_ref, p_ref = refs[-6:]
     height = q_ref.shape[1]
     width = 2 * block_len
     extra = 2 * heads * block_len
@@ -349,23 +356,24 @@
                 store,
             )
     for h in range(heads):
+        acc_ref, top_ref, total_ref = own_refs[3 * h : 3 * h + 3]
         scale = scale_row(heads + h)
         for row in range(0, height, rows):
             at = pl.ds(row, rows)
             score = t_ref[h, at]
-            own_top = top_ref[h, at]
+            own_top = top_ref[at]
             top = jnp.maximum(
                 own_top, jnp.max(lane_fold(score, jnp.maximum), axis=1, keepdims=True)
             )
             weight = jnp.exp2(score - spread(top, score.shape[1]))
             keep = jnp.exp2(own_top - top)
-            total = total_ref[h, at] * keep + jnp.sum(
-                lane_fold(weight, jnp.add), axis=1, keepdims=True
+            total = jnp.sum(
+                total_ref[at] * keep + lane_fold(weight, jnp.add), axis=1, keepdims=True
             )
             p_ref[h, at] = (weight * scale).astype(jnp.bfloat16)
             t_ref[h, at, 0:128] = keep
-            t_ref[h, at, 128:256] = 1.0 / total
-        mixed = acc_ref[h] * t_ref[h, :, 0:128]
+            t_ref[h, at, 128:256] = jnp.broadcast_to(1.0 / total, keep.shape)
+        mixed = acc_ref[...] * t_ref[h, :, 0:128]
         for i in range(pairs):
             mixed = mixed + jnp.dot(
                 p_ref[h, :, i * width : (i + 1) * width],
@@ -447,7 +455,7 @@
         )
         firsts = [send[0]] + [swap(send[k], k) for k in range(1, instances)]
     part_scales, *send = lax.optimization_barrier((part_scales, *send))
-    flat_scales = part_scales.reshape(1, -1).astype(f32)
+    flat_scales = part_scales.reshape(2 * heads, pool).astype(f32)
 
     query_rows = (
         queries.reshape(requests, steps, heads, per_head, head_dim)
@@ -463,30 +471,36 @@
     chunks = pool // group
     tokens = pool * block_len
 
-    stat = (heads, height, head_dim)
-    own_parts = pl.pallas_call(
-        functools.partial(
-            own_kernel, (pool, heads, rows, steps, block_len, spans, factor, group)
-        ),
-        out_shape=[jax.ShapeDtypeStruct(stat, f32)] * 3,
-        in_specs=[VMEM_SPEC, VMEM_SPEC, SMEM_SPEC, VMEM_SPEC, VMEM_SPEC, HBM_SPEC],
-        out_specs=[VMEM_SPEC] * 3,
-        scratch_shapes=[
-            pltpu.VMEM((chunks, requests, width), f32),
-            pltpu.VMEM((chunks, 2 * heads, width), f32),
-            pltpu.VMEM((heads, chunks, height, width), f32),
-            pltpu.VMEM((heads, height, width), bf16),
-            pltpu.VMEM((2, chunks, group, heads * block_len, head_dim), bf16),
-            pltpu.SemaphoreType.DMA((2, chunks)),
-        ],
-        compiler_params=pltpu.CompilerParams(vmem_limit_bytes=48 * MIB),
-        cost_estimate=pl.CostEstimate(
-            flops=4 * heads * height * tokens * head_dim,
-            bytes_accessed=pool_codes.size * 2,
-            transcendentals=heads * height * tokens,
-        ),
-        name="own_blocks",
-    )(tables, length, flat_scales, query_rows, fresh, pool_rows)
+    def own(head, query_rows):
+        return pl.pallas_call(
+            functools.partial(
+                own_kernel, (head, pool, heads, rows, steps, block_len, spans, factor, group)
+            ),
+            out_shape=[jax.ShapeDtypeStruct((height, head_dim), f32)] * 3,
+            in_specs=[VMEM_SPEC] * 5 + [HBM_SPEC],
+            out_specs=[VMEM_SPEC] * 3,
+            scratch_shapes=[
+                pltpu.VMEM((chunks, requests, width), f32),
+                pltpu.VMEM((chunks, 2 * heads, width), f32),
+                pltpu.VMEM((chunks, height, width), f32),
+                pltpu.VMEM((height, width), bf16),
+                pltpu.VMEM((2, chunks, group, block_len, head_dim), bf16),
+                pltpu.SemaphoreType.DMA((2, chunks)),
+            ],
+            compiler_params=pltpu.CompilerParams(vmem_limit_bytes=32 * MIB),
+            cost_estimate=pl.CostEstimate(
+                flops=4 * height * tokens * head_dim,
+                bytes_accessed=pool_codes.size * 2 // heads,
+                transcendentals=height * tokens,
+            ),
+            name="own_blocks",
+        )(tables, length, flat_scales, query_rows, fresh, pool_rows)
+
+    own_parts = own(0, query_rows)
+    if not general:
+        seconds, own_parts = lax.optimization_barrier((seconds, own_parts))
+    for head in range(1, heads):
+        own_parts = own_parts + own(head, query_rows)
 
     if not general:
         held = {k: second for k, second in seconds.items() if k}
@@ -516,7 +530,7 @@
             jax.ShapeDtypeStruct((1, listed), jnp.int32),
             jax.ShapeDtypeStruct((1,), jnp.int32),
         ],
-        in_specs=[VMEM_SPEC] * (6 + len(arrived)),
+        in_specs=[VMEM_SPEC] * (3 + 3 * heads + len(arrived)),
         out_specs=[VMEM_SPEC, VMEM_SPEC, SMEM_SPEC],
         scratch_shapes=[
             pltpu.VMEM((requests, slots * block_len), f32),

time: 37.2 us -> 35 us (0.941)
  waiting for transfers between devices: 5.62 us -> 0.01 us
  Pallas kernels: 20.5 us -> 22.2 us
  starting transfers between devices: 8.88 us -> 10.2 us
    ppermute x5, waiting for transfers between devices: 5.62 us -> 0.01 us  [swap(): lax.ppermute(value, 'inst', [(j, j ^ distance) for j in range(instances)])]
    pallas_call x1 -> x2, Pallas kernels: 12.7 us -> 14.6 us  [own(): pl.pallas_call(functools.partial(own_kernel, (head, pool, heads, rows, st...]
    ppermute x5, starting transfers between devices: 8.88 us -> 10.2 us  [swap(): lax.ppermute(value, 'inst', [(j, j ^ distance) for j in range(instances)])]
  transfers between devices with their start and end apart: 5 -> 5, of which waited for: 1 -> 0; matrix products, arithmetic and copies ran while one was open for 2% -> 1% of each run, Pallas kernels for 41% -> 49%
where the time goes in v14:
time: 35 us; the launch traced here: 34.8 us
  Pallas kernels  22.2 us (63%)
  starting transfers between devices  10.2 us (29%)
  between operations  1.01 us (3%)
  loops' own time  0.79 us (2%)
  local copies, waits for them, and re-layouts  0.53 us (2%)
    pallas_call x2, Pallas kernels, own(): pl.pallas_call(functools.partial(own_kernel, (head, pool, heads, rows, st...  14.6 us
    ppermute x5, starting transfers between devices, swap(): lax.ppermute(value, 'inst', [(j, j ^ distance) for j in range(instances)])  10.2 us
    pallas_call x2, Pallas kernels, pack(): pl.pallas_call(functools.partial(pack_kernel, (instances, listed, heads,...  4.87 us
    pallas_call x1, Pallas kernels, attend(): pl.pallas_call(functools.partial(arrival_kernel, (pool, heads, rows, bloc...  2.81 us
    another operation x1, loops' own time, shards(): lax.while_loop(lambda state: state[0] > 1, lambda state: (jnp.int32(0), a...  0.79 us
  transfers between devices with their start and end apart: 5, of which 0 were waited for; matrix products, arithmetic and copies ran while one was open for 1% of the time, Pallas kernels for 49%

profile of v14, /device:TPU:0, one launch (start us, length us, event | category | flops | bytes accessed | tf_op | source)
XLA Modules:
  0.0 34.8 jit_solution(7387299696398835297)
XLA Ops:
  0.6 0.0 copy-start.7
  0.6 0.0 copy-start.8
  0.7 0.0 copy-start.6
  0.7 0.0 copy-start.10
  0.7 0.0 copy-start.9
  0.7 0.0 copy-start.5
  0.7 0.0 copy-start.4
  0.7 2.4 %pack_blocks.4.refs_11_ = bf16[1,528,128]{2,1,0:T(8,128)(2,1)} custom-call(s32[1,4]{1,0:T(1,128)} %dest_ref.2, s32[1,4]{1,0:T(1,128)} %block_ref.3, bf16[2,2,48]{2,1,0:T(2,128)(2,1)} %bitcast.52, bf16[48,512,128]{2,1,0:T(8,128)(2,1)} %bitcast.40), custom_call_target="tpu_custom_call" | custom-call | bytes 270336 | tf_op jit(solution)/shard_map/pack_blocks/pallas_call | solution.py:413
  3.1 4.1 %collective-permute-start.3 = (bf16[1,528,128]{2,1,0:T(8,128)(2,1)}, bf16[1,528,128]{2,1,0:T(8,128)(2,1)S(1)}, u32[]{:S(2)}, u32[]{:S(2)}) collective-permute-start(bf16[1,528,128]{2,1,0:T(8,128)(2,1)} %pack_blocks.4.refs_11_), channel_id=1, source_target_pairs={{0,8},{4,12},{8,0},{12,4},{1,9},{5,13},{9,1},{13,5},{2,10},{6,14},... | collective-permute-start | bytes 405512 | tf_op jit(solution)/shard_map/ppermute | solution.py:433
  7.2 0.0 copy-done.7
  7.2 0.0 copy-done.8
  7.2 0.0 copy-done.6
  7.2 2.5 %pack_blocks.5 = (bf16[1,528,128]{2,1,0:T(8,128)(2,1)}, bf16[2,528,128]{2,1,0:T(8,128)(2,1)}, bf16[1,528,128]{2,1,0:T(8,128)(2,1)}, bf16[1,528,128]{2,1,0:T(8,128)(2,1)}) custom-call(s32[1,4]{1,0:T(1,128)S(1)} %copy-done.7, s32[1,4]{1,0:T(1,128)S(1)} %copy-done.8, bf16[2,2,48]{2,1,0:T(2,128)(2,1)S(1)} %bitcast.53, bf16[48,512,128]{2,1,0:T(8,128)(2,1)} %bitcast.41), custom_call_target="tpu_custom_call" | custom-call | bytes 1351680 | tf_op jit(solution)/shard_map/pack_blocks/pallas_call | solution.py:413
  9.7 0.1 collective-permute-start.5
  9.8 3.9 %collective-permute-start.4 = (bf16[1,528,128]{2,1,0:T(8,128)(2,1)}, bf16[1,528,128]{2,1,0:T(8,128)(2,1)S(1)}, u32[]{:S(2)}, u32[]{:S(2)}) collective-permute-start(bf16[1,528,128]{2,1,0:T(8,128)(2,1)} %get-tuple-element.88), channel_id=1, source_target_pairs={{0,12},{4,8},{8,4},{12,0},{1,13},{5,9},{9,5},{13,1},{2,14},{6,10},... | collective-permute-start | bytes 405512 | tf_op jit(solution)/shard_map/ppermute | solution.py:433
  13.7 0.0 collective-permute-start.6
  13.7 0.0 copy-done.10
  13.7 0.1 copy.20.tables_ref
  13.8 0.0 copy-done.9
  13.8 0.1 copy.21.length_ref
  13.9 0.0 copy-done.5
  13.9 0.1 copy.22
  13.9 0.1 copy.15
  14.0 0.0 copy-done.4
  14.0 0.2 copy.14
  14.3 0.0 copy-start.1
  14.3 0.0 copy-start.2
  14.3 7.6 %own_blocks.6 = (f32[512,128]{1,0:T(8,128)S(1)}, f32[512,128]{1,0:T(8,128)S(1)}, f32[512,128]{1,0:T(8,128)S(1)}) custom-call(s32[32,16]{1,0:T(8,128)S(1)} %copy.20.tables_ref, s32[32,1]{1,0:T(8,128)S(1)} %copy.21.length_ref, f32[4,48]{1,0:T(4,128)S(1)} %convert.3.scale_ref, bf16[2,512,128]{2,1,0:T(8,128)(2,1)S(1)} %bitcast.37, ...), custom_call_target="tpu_custom_call" | custom-call | flops 1610612736 | bytes 3145728 | tf_op jit(solution)/shard_map/own_blocks/pallas_call | solution.py:475
  21.9 0.0 collective-permute-done.3.refs_6_
  21.9 2.1 %collective-permute-start.7 = (bf16[1,528,128]{2,1,0:T(8,128)(2,1)S(1)}, bf16[1,528,128]{2,1,0:T(8,128)(2,1)S(1)}, u32[]{:S(2)}, u32[]{:S(2)}) collective-permute-start(bf16[1,528,128]{2,1,0:T(8,128)(2,1)S(1)} %collective-permute-done.3.refs_6_), channel_id=1, source_target_pairs={{0,4},{4,0},{8,12},{12,8},{1,5},{5,1},{9,13},{13,9},{2,6},{6,2},{1... | collective-permute-start | bytes 405512 | tf_op jit(solution)/shard_map/ppermute | solution.py:433
  24.0 7.0 %own_blocks.7 = (f32[512,128]{1,0:T(8,128)S(1)}, f32[512,128]{1,0:T(8,128)S(1)}, f32[512,128]{1,0:T(8,128)S(1)}) custom-call(s32[32,16]{1,0:T(8,128)S(1)} %copy.20.tables_ref, s32[32,1]{1,0:T(8,128)S(1)} %copy.21.length_ref, f32[4,48]{1,0:T(4,128)S(1)} %convert.3.scale_ref, bf16[2,512,128]{2,1,0:T(8,128)(2,1)S(1)} %bitcast.38, ...), custom_call_target="tpu_custom_call" | custom-call | flops 1610612736 | bytes 3145728 | tf_op jit(solution)/shard_map/own_blocks/pallas_call | solution.py:475
  31.0 0.0 collective-permute-done.5.refs_8_
  31.0 0.0 collective-permute-done.4.refs_7_
  31.0 0.0 collective-permute-done.6.refs_9_
  31.0 0.0 collective-permute-done.7.refs_12_
  31.0 0.0 copy-done.1
  31.0 0.0 copy-done.2
  31.0 2.8 %arrived_blocks.3 = (bf16[32,2,16,128]{3,2,1,0:T(8,128)(2,1)}, s32[1,4]{1,0:T(1,128)}, s32[1]{0:T(128)}) custom-call(bf16[2,512,128]{2,1,0:T(8,128)(2,1)S(1)} %bitcast.39, s32[32,16]{1,0:T(8,128)S(1)} %copy.20.tables_ref, s32[32,1]{1,0:T(8,128)S(1)} %copy.21.length_ref, f32[512,128]{1,0:T(8,128)S(1)} %get-tuple-element.93.refs_0_, ...), custom_call_target="tpu_custom_call" | custom-call | flops 536870912 | bytes 1081344 | tf_op jit(solution)/shard_map/arrived_blocks/pallas_call | solution.py:524
  33.8 0.8 %while.9 = (s32[]{:T(128)}, bf16[32,2,2048]{2,1,0:T(2,128)(2,1)}, bf16[32,2,16,128]{3,2,1,0:T(8,128)(2,1)S(1)}, s32[32]{0:T(128)S(1)}, bf16[48,2,2]{0,2,1:T(2,12...) while((s32[]{:T(128)}, bf16[32,2,2048]{2,1,0:T(2,128)(2,1)}, ...), condition=%region_1.2_spmd, body=%region_0.1_spmd | while | flops 3758096640 | bytes 39749268 | solution.py:554
  (2 shorter events, 0.0 us)
Async XLA Ops:
  0.6 6.6 %copy-start.7 = (s32[1,4]{1,0:T(1,128)S(1)}, s32[1,4]{1,0:T(1,128)}, u32[]{:S(2)}) copy-start(s32[1,4]{1,0:T(1,128)} %dest_ref.2) | copy-start | bytes 52
  0.6 6.6 %copy-start.8 = (s32[1,4]{1,0:T(1,128)S(1)}, s32[1,4]{1,0:T(1,128)}, u32[]{:S(2)}) copy-start(s32[1,4]{1,0:T(1,128)} %block_ref.3) | copy-start | bytes 52
  0.7 6.6 %copy-start.6 = (bf16[48,2,2]{0,2,1:T(2,128)(2,1)S(1)}, bf16[48,2,2]{0,2,1:T(2,128)(2,1)}, u32[]{:S(2)}) copy-start(bf16[48,2,2]{0,2,1:T(2,128)(2,1)} %param.13) | copy-start | bytes 1156
  0.7 13.0 %copy-start.10 = (s32[32,16]{0,1:T(8,128)S(1)}, s32[32,16]{0,1:T(8,128)}, u32[]{:S(2)}) copy-start(s32[32,16]{0,1:T(8,128)} %param.14) | copy-start | bytes 6148
  0.7 13.1 %copy-start.9 = (s32[32]{0:T(128)S(1)}, s32[32]{0:T(128)}, u32[]{:S(2)}) copy-start(s32[32]{0:T(128)} %param.15) | copy-start | bytes 388
  0.7 13.2 %copy-start.5 = (bf16[32,2,2,2,128]{4,3,2,1,0:T(2,128)(2,1)S(1)}, bf16[32,2,2,2,128]{4,3,2,1,0:T(2,128)(2,1)}, u32[]{:S(2)}) copy-start(bf16[32,2,2,2,128]{4,3,2,1,0:T(2,128)(2,1)} %param.11) | copy-start | bytes 196612
  0.7 13.3 %copy-start.4 = (bf16[32,2,16,128]{3,2,1,0:T(8,128)(2,1)S(1)}, bf16[32,2,16,128]{3,2,1,0:T(8,128)(2,1)}, u32[]{:S(2)}) copy-start(bf16[32,2,16,128]{3,2,1,0:T(8,128)(2,1)} %param.10) | copy-start | bytes 786436
  3.1 18.7 %collective-permute-start.3 = (bf16[1,528,128]{2,1,0:T(8,128)(2,1)}, bf16[1,528,128]{2,1,0:T(8,128)(2,1)S(1)}, u32[]{:S(2)}, u32[]{:S(2)}) collective-permute-start(bf16[1,528,128]{2,1,0:T(8,128)(2,1)} %pack_blocks.4.refs_11_), channel_id=1, source_target_pairs={{0,8},{4,12},{8,0},{12,4},{1,9},{5,13},{9,1},{13,5},{2,10},{6,14},... | collective-permute-start | bytes 405512 | tf_op jit(solution)/shard_map/ppermute | solution.py:433
  9.7 21.3 %collective-permute-start.5 = (bf16[1,528,128]{2,1,0:T(8,128)(2,1)}, bf16[1,528,128]{2,1,0:T(8,128)(2,1)S(1)}, u32[]{:S(2)}, u32[]{:S(2)}) collective-permute-start(bf16[1,528,128]{2,1,0:T(8,128)(2,1)} %get-tuple-element.87), channel_id=1, source_target_pairs={{0,8},{4,12},{8,0},{12,4},{1,9},{5,13},{9,1},{13,5},{2,10},{6,14},... | collective-permute-start | bytes 405512 | tf_op jit(solution)/shard_map/ppermute | solution.py:433
  9.8 21.2 %collective-permute-start.4 = (bf16[1,528,128]{2,1,0:T(8,128)(2,1)}, bf16[1,528,128]{2,1,0:T(8,128)(2,1)S(1)}, u32[]{:S(2)}, u32[]{:S(2)}) collective-permute-start(bf16[1,528,128]{2,1,0:T(8,128)(2,1)} %get-tuple-element.88), channel_id=1, source_target_pairs={{0,12},{4,8},{8,4},{12,0},{1,13},{5,9},{9,5},{13,1},{2,14},{6,10},... | collective-permute-start | bytes 405512 | tf_op jit(solution)/shard_map/ppermute | solution.py:433
  13.7 17.3 %collective-permute-start.6 = (bf16[2,528,128]{2,1,0:T(8,128)(2,1)}, bf16[2,528,128]{2,1,0:T(8,128)(2,1)S(1)}, u32[]{:S(2)}, u32[]{:S(2)}) collective-permute-start(bf16[2,528,128]{2,1,0:T(8,128)(2,1)} %get-tuple-element.86), channel_id=1, source_target_pairs={{0,4},{4,0},{8,12},{12,8},{1,5},{5,1},{9,13},{13,9},{2,6},{6,2},{1... | collective-permute-start | bytes 811016 | tf_op jit(solution)/shard_map/ppermute | solution.py:433
  14.3 16.7 %copy-start.1 = (bf16[1,528,128]{2,1,0:T(8,128)(2,1)S(1)}, bf16[1,528,128]{2,1,0:T(8,128)(2,1)}, u32[]{:S(2)}) copy-start(bf16[1,528,128]{2,1,0:T(8,128)(2,1)} %pack_blocks.4.refs_11_) | copy-start | bytes 405508
  14.3 16.7 %copy-start.2 = (bf16[1,528,128]{2,1,0:T(8,128)(2,1)S(1)}, bf16[1,528,128]{2,1,0:T(8,128)(2,1)}, u32[]{:S(2)}) copy-start(bf16[1,528,128]{2,1,0:T(8,128)(2,1)} %get-tuple-element.85.refs_10_) | copy-start | bytes 405508
  21.9 9.1 %collective-permute-start.7 = (bf16[1,528,128]{2,1,0:T(8,128)(2,1)S(1)}, bf16[1,528,128]{2,1,0:T(8,128)(2,1)S(1)}, u32[]{:S(2)}, u32[]{:S(2)}) collective-permute-start(bf16[1,528,128]{2,1,0:T(8,128)(2,1)S(1)} %collective-permute-done.3.refs_6_), channel_id=1, source_target_pairs={{0,4},{4,0},{8,12},{12,8},{1,5},{5,1},{9,13},{13,9},{2,6},{6,2},{1... | collective-permute-start | bytes 405512 | tf_op jit(solution)/shard_map/ppermute | solution.py:433

commit v15 on v13

--- a/solution.py
+++ b/solution.py
@@ -10,6 +10,7 @@
 
 CAP = 2
 EXTRA = 16
+NEVER = -1e30
 LOG2E = math.log2(math.e)
 MIB = 1 << 20
 SMEM_SPEC = pl.BlockSpec(memory_space=pltpu.SMEM)
@@ -108,20 +109,36 @@
         part = part + jnp.where(hit & (whole == e), 1.0, 0.0)
 
     def log2(count):
-        return jnp.where(count > 0, jnp.log(jnp.maximum(count, 1.0)) * LOG2E, -jnp.inf)
+        return jnp.where(count > 0, jnp.log(jnp.maximum(count, 1.0)) * LOG2E, NEVER)
 
     beyond, within = log2(full), log2(full + part)
     shape = (requests, block_len)
     inside = lax.broadcasted_iota(jnp.int32, shape, 1) < jnp.broadcast_to(rest, shape)
-    for b in range(width):
-        store(
-            b,
-            jnp.where(
-                inside,
-                jnp.broadcast_to(within[:, b : b + 1], shape),
-                jnp.broadcast_to(beyond[:, b : b + 1], shape),
-            ),
-        )
+    if width % 16:
+        for b in range(width):
+            store(
+                b,
+                jnp.where(
+                    inside,
+                    jnp.broadcast_to(within[:, b : b + 1], shape),
+                    jnp.broadcast_to(beyond[:, b : b + 1], shape),
+                ),
+            )
+        return
+    both = jnp.concatenate([within, beyond], axis=0)
+    high = both.astype(jnp.bfloat16)
+    low = (both - high.astype(jnp.float32)).astype(jnp.bfloat16)
+    terms = jnp.concatenate([high, low], axis=0)
+    row = lax.broadcasted_iota(jnp.int32, (width, block_len), 0)
+    for b in range(0, width, 2):
+        spots = jnp.concatenate(
+            [jnp.where(row == b + i, 1.0, 0.0).astype(jnp.bfloat16) for i in range(2)], axis=1
+        )
+        spread_out = jnp.dot(terms, spots, preferred_element_type=jnp.float32)
+        value = spread_out[: 2 * requests] + spread_out[2 * requests :]
+        for i in range(2):
+            at = slice(i * block_len, (i + 1) * block_len)
+            store(b + i, jnp.where(inside, value[:requests, at], value[requests:, at]))
 
 
 def score_tiles(query, keys, log_ref, scale_row, rows, store):
@@ -178,6 +195,10 @@
             sems.at[part, chunk],
         )
 
+    def codes(part, chunk, h):
+        at = pl.ds(h * block_len, block_len)
+        return codes_ref[part, chunk, :, at].reshape(width, head_dim)
+
     for part in range(2):
         for chunk in range(chunks):
             load(part, chunk).start()
@@ -191,11 +212,9 @@
     count_log(tables_ref[...], length_ref[...], ids, block_len, spans, store_log)
     for b in range(pool):
         lane = (b % group) * block_len
-        for row in range(2 * heads):
-            unit = factor * LOG2E if row < heads else 1.0
-            row_ref[b // group, row : row + 1, lane : lane + block_len] = jnp.full(
-                (1, block_len), scale_ref[0, row * pool + b] * unit
-            )
+        row_ref[b // group, :, lane : lane + block_len] = jnp.broadcast_to(
+            scale_ref[:, b : b + 1], (2 * heads, block_len)
+        )
     shape = (height, fresh_ref.shape[2])
     row = lax.broadcasted_iota(jnp.int32, shape, 0)
     col = lax.broadcasted_iota(jnp.int32, shape, 1)
@@ -218,9 +237,9 @@
 
             score_tiles(
                 q_ref[h],
-                codes_ref[0, chunk, :, h * block_len : (h + 1) * block_len].reshape(width, head_dim),
+                codes(0, chunk, h),
                 log_ref.at[chunk],
-                row_ref[chunk, h : h + 1, :],
+                row_ref[chunk, h : h + 1, :] * (factor * LOG2E),
                 rows,
                 store,
             )
@@ -252,17 +271,11 @@
                 total_ref[h, at] += lane_fold(weight, jnp.add)
                 p_ref[h, at] = (weight * scale).astype(jnp.bfloat16)
             acc_ref[h] += jnp.dot(
-                p_ref[h],
-                codes_ref[1, chunk, :, h * block_len : (h + 1) * block_len].reshape(width, head_dim),
-                preferred_element_type=jnp.float32,
+                p_ref[h], codes(1, chunk, h), preferred_element_type=jnp.float32
             )
         return carry
 
     lax.fori_loop(0, chunks, apply, 0)
-    for h in range(heads):
-        total_ref[h] = jnp.broadcast_to(
-            jnp.sum(total_ref[h], axis=1, keepdims=True), (height, 128)
-        )
 
 
 def arrival_ids(me, pool, lists, listed):
@@ -302,9 +315,11 @@
     return ids.astype(jnp.int32), moved[:, :listed].astype(jnp.int32), more
 
 
-def arrival_kernel(dims, places, q_ref, tables_ref, length_ref, acc_ref, top_ref, total_ref, *refs):
+def arrival_kernel(dims, places, q_ref, tables_ref, length_ref, *refs):
     pool, heads, rows, block_len, spans, listed, factor = dims
-    code_refs, (out_ref, moved_ref, more_ref, log_ref, t_ref, p_ref) = refs[:-6], refs[-6:]
+    acc_ref, top_ref, total_ref = refs[:3]
+    code_refs = refs[3:-6]
+    out_ref, moved_ref, more_ref, log_ref, t_ref, p_ref = refs[-6:]
     height = q_ref.shape[1]
     width = 2 * block_len
     extra = 2 * heads * block_len
@@ -359,12 +374,12 @@
             )
             weight = jnp.exp2(score - spread(top, score.shape[1]))
             keep = jnp.exp2(own_top - top)
-            total = total_ref[h, at] * keep + jnp.sum(
-                lane_fold(weight, jnp.add), axis=1, keepdims=True
+            total = jnp.sum(
+                total_ref[h, at] * keep + lane_fold(weight, jnp.add), axis=1, keepdims=True
             )
             p_ref[h, at] = (weight * scale).astype(jnp.bfloat16)
             t_ref[h, at, 0:128] = keep
-            t_ref[h, at, 128:256] = 1.0 / total
+            t_ref[h, at, 128:256] = jnp.broadcast_to(1.0 / total, keep.shape)
         mixed = acc_ref[h] * t_ref[h, :, 0:128]
         for i in range(pairs):
             mixed = mixed + jnp.dot(
@@ -391,7 +406,7 @@
     rows = per_head * steps
     height = requests * rows
     slots = instances * CAP
-    group = 8
+    group = 16
     f32, bf16 = jnp.float32, jnp.bfloat16
     code_rows = 2 * heads * block_len
     pool_rows = pool_codes.reshape(pool, code_rows, head_dim)
@@ -424,30 +439,20 @@
     def swap(value, distance):
         return lax.ppermute(value, "inst", [(j, j ^ distance) for j in range(instances)])
 
+    straight = [k for k in range(1, instances) if k & (k - 1) == 0]
+    any_second = CAP * instances
     if general:
-        send = pack(
-            [CAP] * instances,
-            [(r * instances + k, [(k, r)]) for k in range(instances) for r in range(CAP)],
-        )
-        arrived = [swap(send[k], k) for k in range(instances - 1, 0, -1)] + [send[0]]
-        places = [(instances - 1 - k, r) for r in range(CAP) for k in range(instances)]
+        sizes = [CAP] * instances
+        copies = [(r * instances + k, [(k, r)]) for k in range(instances) for r in range(CAP)]
     else:
-        any_second = CAP * instances
-        (second,) = pack([1], [(any_second, [(0, 0)])])
-        seconds = {0: second}
-        bit = instances // 2
-        while bit > 1:
-            for k in list(seconds):
-                seconds[k ^ bit] = swap(seconds[k], bit)
-            bit //= 2
-        mig_dest, second = lax.optimization_barrier((mig_dest, second))
-        send = pack(
-            [1, 2] + [1] * (instances - 2),
-            [(k, [(k, 0)]) for k in list(range(instances))[::-1]] + [(any_second, [(1, 1)])],
-        )
-        firsts = [send[0]] + [swap(send[k], k) for k in range(1, instances)]
+        sizes = [CAP if k in straight or k == 0 else 1 for k in range(instances)]
+        copies = [(any_second, [(k, 1) for k in straight[::-1] + [0]])]
+        copies += [(k, [(k, 0)]) for k in list(range(instances))[::-1]]
+    send = pack(sizes, copies)
     part_scales, *send = lax.optimization_barrier((part_scales, *send))
-    flat_scales = part_scales.reshape(1, -1).astype(f32)
+    arrived = {k: swap(send[k], k) for k in range(instances - 1, 0, -1)}
+    arrived[0] = send[0]
+    flat_scales = part_scales.reshape(2 * heads, pool).astype(f32)
 
     query_rows = (
         queries.reshape(requests, steps, heads, per_head, head_dim)
@@ -469,7 +474,7 @@
             own_kernel, (pool, heads, rows, steps, block_len, spans, factor, group)
         ),
         out_shape=[jax.ShapeDtypeStruct(stat, f32)] * 3,
-        in_specs=[VMEM_SPEC, VMEM_SPEC, SMEM_SPEC, VMEM_SPEC, VMEM_SPEC, HBM_SPEC],
+        in_specs=[VMEM_SPEC] * 5 + [HBM_SPEC],
         out_specs=[VMEM_SPEC] * 3,
         scratch_shapes=[
             pltpu.VMEM((chunks, requests, width), f32),
@@ -488,22 +493,25 @@
         name="own_blocks",
     )(tables, length, flat_scales, query_rows, fresh, pool_rows)
 
-    if not general:
-        held = {k: second for k, second in seconds.items() if k}
-        for k in held:
-            seconds[k ^ 1] = swap(held[k], 1)
-        arrived = [held[k] for k in held] + firsts[::-1] + [seconds[0]]
-        where = {k: i for i, k in enumerate(held)}
-        where[0] = len(arrived) - 1
-        places = [(len(held) + instances - 1 - k, 0) for k in range(instances)]
+    order = straight[::-1] + [k for k in range(instances) if k not in straight]
+    arrays = [arrived[k] for k in order]
+    places = [(order.index(k), 0) for k in range(instances)]
+    if general:
+        places += [(order.index(k), 1) for k in range(instances)]
+    else:
+        relayed = {k: arrived[k] for k in straight if k > 1}
+        relayed, own_parts = lax.optimization_barrier((relayed, own_parts))
+        seconds = {k: relayed[k][1:] for k in relayed}
+        for bit in straight[::-1]:
+            for k in list(seconds):
+                if k > bit and k & (bit - 1) == 0 and k ^ bit not in seconds:
+                    seconds[k ^ bit] = swap(seconds[k], bit)
         for k in range(instances):
-            if k == 1:
-                places.append((places[1][0], 1))
-            elif k in where:
-                places.append((where[k], 0))
+            if k in straight or k == 0:
+                places.append((order.index(k), 1))
             else:
-                places.append((len(arrived), 0))
-                arrived.append(seconds[k])
+                places.append((len(arrays), 0))
+                arrays.append(seconds[k])
 
     arrival_bytes = 6 * heads * height * slots * block_len + 2 * 12 * height * head_dim * heads
     arrival_bytes += 2 * slots * sent_bytes + 4 * requests * slots * block_len
@@ -516,7 +524,7 @@
             jax.ShapeDtypeStruct((1, listed), jnp.int32),
             jax.ShapeDtypeStruct((1,), jnp.int32),
         ],
-        in_specs=[VMEM_SPEC] * (6 + len(arrived)),
+        in_specs=[VMEM_SPEC] * (6 + len(arrays)),
         out_specs=[VMEM_SPEC, VMEM_SPEC, SMEM_SPEC],
         scratch_shapes=[
             pltpu.VMEM((requests, slots * block_len), f32),
@@ -530,7 +538,7 @@
             transcendentals=heads * height * slots * block_len,
         ),
         name="arrived_blocks",
-    )(query_rows, tables, length, *own_parts, *arrived)
+    )(query_rows, tables, length, *own_parts, *arrays)
     out = out.reshape(requests, q_heads, steps, head_dim).transpose(0, 2, 1, 3)
     return out.reshape(requests, steps, q_heads * head_dim), moved_to, more
 

time: 37.2 us -> 35.2 us (0.946)
  waiting for transfers between devices: 5.62 us -> 10.6 us
  Pallas kernels: 20.5 us -> 16.2 us
  starting transfers between devices: 8.88 us -> 5.83 us
    ppermute x5 -> x4, waiting for transfers between devices: 5.62 us -> 10.6 us  [swap(): lax.ppermute(value, 'inst', [(j, j ^ distance) for j in range(instances)])]
    ppermute x5 -> x4, starting transfers between devices: 8.88 us -> 5.83 us  [swap(): lax.ppermute(value, 'inst', [(j, j ^ distance) for j in range(instances)])]
    pallas_call x1, Pallas kernels: 12.7 us -> 10.5 us  [attend(): pl.pallas_call(functools.partial(own_kernel, (pool, heads, rows, steps, b...]
    pallas_call x2 -> x1, Pallas kernels: 4.88 us -> 2.76 us  [pack(): pl.pallas_call(functools.partial(pack_kernel, (instances, listed, heads,...]
  transfers between devices with their start and end apart: 5 -> 4, of which waited for: 1 -> 2; matrix products, arithmetic and copies ran while one was open for 2% -> 1% of each run, Pallas kernels for 41% -> 30%
where the time goes in v15:
time: 35.2 us; the launch traced here: 35 us
  Pallas kernels  16.2 us (46%)
  waiting for transfers between devices  10.6 us (30%)
  starting transfers between devices  5.83 us (17%)
  between operations  0.98 us (3%)
  loops' own time  0.81 us (2%)
  local copies, waits for them, and re-layouts  0.53 us (2%)
    ppermute x4, waiting for transfers between devices, swap(): lax.ppermute(value, 'inst', [(j, j ^ distance) for j in range(instances)])  10.6 us
    pallas_call x1, Pallas kernels, attend(): pl.pallas_call(functools.partial(own_kernel, (pool, heads, rows, steps, b...  10.5 us
    ppermute x4, starting transfers between devices, swap(): lax.ppermute(value, 'inst', [(j, j ^ distance) for j in range(instances)])  5.83 us
    pallas_call x1, Pallas kernels, attend(): pl.pallas_call(functools.partial(arrival_kernel, (pool, heads, rows, bloc...  2.9 us
    pallas_call x1, Pallas kernels, pack(): pl.pallas_call(functools.partial(pack_kernel, (instances, listed, heads,...  2.76 us
    another operation x1, loops' own time, shards(): lax.while_loop(lambda state: state[0] > 1, lambda state: (jnp.int32(0), a...  0.81 us
  transfers between devices with their start and end apart: 4, of which 2 were waited for; matrix products, arithmetic and copies ran while one was open for 1% of the time, Pallas kernels for 30%

profile of v15, /device:TPU:0, one launch (start us, length us, event | category | flops | bytes accessed | tf_op | source)
XLA Modules:
  0.0 35.0 jit_solution(11566511321595149535)
XLA Ops:
  0.6 0.0 copy-start.4
  0.6 0.0 copy-start.8
  0.7 0.0 copy-start.7
  0.7 0.0 copy-start.3
  0.7 0.0 copy-start.2
  0.7 2.8 %pack_blocks.3 = (bf16[2,528,128]{2,1,0:T(8,128)(2,1)}, bf16[2,528,128]{2,1,0:T(8,128)(2,1)}, bf16[2,528,128]{2,1,0:T(8,128)(2,1)}, bf16[1,528,128]{2,1,0:T(8,128)(2,1)}) custom-call(s32[1,4]{1,0:T(1,128)} %dest_ref.1, s32[1,4]{1,0:T(1,128)} %block_ref.1, bf16[2,2,48]{2,1,0:T(2,128)(2,1)} %bitcast.47, bf16[48,512,128]{2,1,0:T(8,128)(2,1)} %bitcast.38), custom_call_target="tpu_custom_call" | custom-call | bytes 1892352 | tf_op jit(solution)/shard_map/pack_blocks/pallas_call | solution.py:420
  3.5 5.1 %collective-permute-start.5 = (bf16[1,528,128]{2,1,0:T(8,128)(2,1)}, bf16[1,528,128]{2,1,0:T(8,128)(2,1)S(1)}, u32[]{:S(2)}, u32[]{:S(2)}) collective-permute-start(bf16[1,528,128]{2,1,0:T(8,128)(2,1)} %get-tuple-element.98), channel_id=1, source_target_pairs={{0,12},{4,8},{8,4},{12,0},{1,13},{5,9},{9,5},{13,1},{2,14},{6,10},... | collective-permute-start | bytes 405512 | tf_op jit(solution)/shard_map/ppermute | solution.py:440
  8.6 0.0 collective-permute-start.3
  8.6 0.6 %collective-permute-start.4 = (bf16[2,528,128]{2,1,0:T(8,128)(2,1)}, bf16[2,528,128]{2,1,0:T(8,128)(2,1)S(1)}, u32[]{:S(2)}, u32[]{:S(2)}) collective-permute-start(bf16[2,528,128]{2,1,0:T(8,128)(2,1)} %get-tuple-element.96), channel_id=1, source_target_pairs={{0,4},{4,0},{8,12},{12,8},{1,5},{5,1},{9,13},{13,9},{2,6},{6,2},{1... | collective-permute-start | bytes 811016 | tf_op jit(solution)/shard_map/ppermute | solution.py:440
  9.2 0.0 copy-done.8
  9.2 0.1 copy.17.tables_ref
  9.3 0.0 copy-done.7
  9.3 0.1 copy.18.length_ref
  9.4 0.0 copy-done.3
  9.4 0.1 copy.14
  9.4 0.0 copy-done.2
  9.4 0.2 copy.13
  9.7 0.0 copy-start.1
  9.7 0.0 copy-done.4
  9.7 0.0 copy-start.5
  9.7 0.0 copy-start.6
  9.7 10.5 %own_blocks.3 = (f32[2,512,128]{2,1,0:T(8,128)S(1)}, f32[2,512,128]{2,1,0:T(8,128)S(1)}, f32[2,512,128]{2,1,0:T(8,128)S(1)}) custom-call(s32[32,16]{1,0:T(8,128)S(1)} %copy.17.tables_ref, s32[32,1]{1,0:T(8,128)S(1)} %copy.18.length_ref, f32[4,48]{1,0:T(4,128)S(1)} %convert.3.scale_ref, bf16[2,512,128]{2,1,0:T(8,128)(2,1)S(1)} %bitcast.36, ...), custom_call_target="tpu_custom_call" | custom-call | flops 3221225472 | bytes 6291456 | tf_op jit(solution)/shard_map/own_blocks/pallas_call | solution.py:472
  20.3 5.7 %collective-permute-done.3.refs_3_ = bf16[2,528,128]{2,1,0:T(8,128)(2,1)S(1)} collective-permute-done((bf16[2,528,128]{2,1,0:T(8,128)(2,1)}, bf16[2,528,128]{2,1,0:T(8,128)(2,1)S(1)}, u32[]{:S(2)}, u32[]{:S(2)}) %collective-permute-start.3) | collective-permute-done | bytes 270368 | tf_op jit(solution)/shard_map/ppermute | solution.py:440
  26.0 0.1 collective-permute-start.6
  26.1 0.1 copy.19
  26.1 0.0 collective-permute-done.5.refs_6_
  26.2 0.0 collective-permute-done.4.refs_4_
  26.2 4.9 %collective-permute-done.6.refs_7_ = bf16[1,528,128]{2,1,0:T(8,128)(2,1)S(1)} collective-permute-done((bf16[1,528,128]{2,1,0:T(8,128)(2,1)S(1)}, bf16[1,528,128]{2,1,0:T(8,128)(2,1)S(1)}, u32[]{:S(2)}, u32[]{:S(2)}) %collective-permute-start.6) | collective-permute-done | bytes 135200 | tf_op jit(solution)/shard_map/ppermute | solution.py:440
  31.1 0.0 copy-done.1
  31.1 2.9 %arrived_blocks.3 = (bf16[32,2,16,128]{3,2,1,0:T(8,128)(2,1)}, s32[1,4]{1,0:T(1,128)}, s32[1]{0:T(128)}) custom-call(bf16[2,512,128]{2,1,0:T(8,128)(2,1)S(1)} %bitcast.37, s32[32,16]{1,0:T(8,128)S(1)} %copy.17.tables_ref, s32[32,1]{1,0:T(8,128)S(1)} %copy.18.length_ref, f32[2,512,128]{2,1,0:T(8,128)S(1)} %get-tuple-element.93.refs_0_, ...), custom_call_target="tpu_custom_call" | custom-call | flops 536870912 | bytes 1081344 | tf_op jit(solution)/shard_map/arrived_blocks/pallas_call | solution.py:518
  34.0 0.0 copy-done.5
  34.0 0.0 copy-done.6
  34.0 0.8 %while.9 = (s32[]{:T(128)}, bf16[32,2,2048]{2,1,0:T(2,128)(2,1)}, bf16[32,2,16,128]{3,2,1,0:T(8,128)(2,1)S(1)}, s32[32]{0:T(128)S(1)}, bf16[48,2,2]{0,2,1:T(2,12...) while((s32[]{:T(128)}, bf16[32,2,2048]{2,1,0:T(2,128)(2,1)}, ...), condition=%region_1.2_spmd, body=%region_0.1_spmd | while | flops 3758096640 | bytes 14583415 | solution.py:548
  (3 shorter events, 0.0 us)
Async XLA Ops:
  0.6 9.0 %copy-start.4 = (bf16[48,2,2]{0,2,1:T(2,128)(2,1)S(1)}, bf16[48,2,2]{0,2,1:T(2,128)(2,1)}, u32[]{:S(2)}) copy-start(bf16[48,2,2]{0,2,1:T(2,128)(2,1)} %param.13) | copy-start | bytes 1156
  0.6 8.6 %copy-start.8 = (s32[32,16]{0,1:T(8,128)S(1)}, s32[32,16]{0,1:T(8,128)}, u32[]{:S(2)}) copy-start(s32[32,16]{0,1:T(8,128)} %param.14) | copy-start | bytes 6148
  0.7 8.6 %copy-start.7 = (s32[32]{0:T(128)S(1)}, s32[32]{0:T(128)}, u32[]{:S(2)}) copy-start(s32[32]{0:T(128)} %param.15) | copy-start | bytes 388
  0.7 8.7 %copy-start.3 = (bf16[32,2,2,2,128]{4,3,2,1,0:T(2,128)(2,1)S(1)}, bf16[32,2,2,2,128]{4,3,2,1,0:T(2,128)(2,1)}, u32[]{:S(2)}) copy-start(bf16[32,2,2,2,128]{4,3,2,1,0:T(2,128)(2,1)} %param.11) | copy-start | bytes 196612
  0.7 8.8 %copy-start.2 = (bf16[32,2,16,128]{3,2,1,0:T(8,128)(2,1)S(1)}, bf16[32,2,16,128]{3,2,1,0:T(8,128)(2,1)}, u32[]{:S(2)}) copy-start(bf16[32,2,16,128]{3,2,1,0:T(8,128)(2,1)} %param.10) | copy-start | bytes 786436
  3.5 22.7 %collective-permute-start.5 = (bf16[1,528,128]{2,1,0:T(8,128)(2,1)}, bf16[1,528,128]{2,1,0:T(8,128)(2,1)S(1)}, u32[]{:S(2)}, u32[]{:S(2)}) collective-permute-start(bf16[1,528,128]{2,1,0:T(8,128)(2,1)} %get-tuple-element.98), channel_id=1, source_target_pairs={{0,12},{4,8},{8,4},{12,0},{1,13},{5,9},{9,5},{13,1},{2,14},{6,10},... | collective-permute-start | bytes 405512 | tf_op jit(solution)/shard_map/ppermute | solution.py:440
  8.6 17.4 %collective-permute-start.3 = (bf16[2,528,128]{2,1,0:T(8,128)(2,1)}, bf16[2,528,128]{2,1,0:T(8,128)(2,1)S(1)}, u32[]{:S(2)}, u32[]{:S(2)}) collective-permute-start(bf16[2,528,128]{2,1,0:T(8,128)(2,1)} %get-tuple-element.88), channel_id=1, source_target_pairs={{0,8},{4,12},{8,0},{12,4},{1,9},{5,13},{9,1},{13,5},{2,10},{6,14},... | collective-permute-start | bytes 811016 | tf_op jit(solution)/shard_map/ppermute | solution.py:440
  8.6 17.6 %collective-permute-start.4 = (bf16[2,528,128]{2,1,0:T(8,128)(2,1)}, bf16[2,528,128]{2,1,0:T(8,128)(2,1)S(1)}, u32[]{:S(2)}, u32[]{:S(2)}) collective-permute-start(bf16[2,528,128]{2,1,0:T(8,128)(2,1)} %get-tuple-element.96), channel_id=1, source_target_pairs={{0,4},{4,0},{8,12},{12,8},{1,5},{5,1},{9,13},{13,9},{2,6},{6,2},{1... | collective-permute-start | bytes 811016 | tf_op jit(solution)/shard_map/ppermute | solution.py:440
  9.7 21.4 %copy-start.1 = (bf16[2,528,128]{2,1,0:T(8,128)(2,1)S(1)}, bf16[2,528,128]{2,1,0:T(8,128)(2,1)}, u32[]{:S(2)}) copy-start(bf16[2,528,128]{2,1,0:T(8,128)(2,1)} %get-tuple-element.97.refs_5_) | copy-start | bytes 811012
  9.7 24.3 %copy-start.5 = (s32[1,4]{1,0:T(1,128)S(1)}, s32[1,4]{1,0:T(1,128)}, u32[]{:S(2)}) copy-start(s32[1,4]{1,0:T(1,128)} %dest_ref.1) | copy-start | bytes 52
  9.7 24.3 %copy-start.6 = (s32[1,4]{1,0:T(1,128)S(1)}, s32[1,4]{1,0:T(1,128)}, u32[]{:S(2)}) copy-start(s32[1,4]{1,0:T(1,128)} %block_ref.1) | copy-start | bytes 52
  26.0 5.1 %collective-permute-start.6 = (bf16[1,528,128]{2,1,0:T(8,128)(2,1)S(1)}, bf16[1,528,128]{2,1,0:T(8,128)(2,1)S(1)}, u32[]{:S(2)}, u32[]{:S(2)}) collective-permute-start(bf16[1,528,128]{2,1,0:T(8,128)(2,1)S(1)} %slice.3), channel_id=1, source_target_pairs={{0,4},{4,0},{8,12},{12,8},{1,5},{5,1},{9,13},{13,9},{2,6},{6,2},{1... | collective-permute-start | bytes 405512 | tf_op jit(solution)/shard_map/ppermute | solution.py:440

commit v16 on v14

--- a/solution.py
+++ b/solution.py
@@ -177,11 +177,13 @@
 
 
 def own_kernel(
-    dims,
-    tables_ref, length_ref, scale_ref, q_ref, fresh_ref, pool_ref,
-    acc_ref, top_ref, total_ref,
-    log_ref, row_ref, t_ref, p_ref, codes_ref, sems,
+    dims, q_ref, fresh_ref, pool_ref, *refs
 ):
+    if dims[0] == 0:
+        tables_ref, length_ref, scale_ref, acc_ref, top_ref, total_ref, log_ref, row_ref = refs[:8]
+    else:
+        log_ref, row_ref, acc_ref, top_ref, total_ref = refs[:5]
+    t_ref, p_ref, codes_ref, sems = refs[-4:]
     head, pool, heads, rows, steps, block_len, spans, factor, group = dims
     chunks = pool // group
     height, head_dim = q_ref.shape[1:]
@@ -200,18 +202,19 @@
         for chunk in range(chunks):
             load(part, chunk).start()
 
-    ids = lax.broadcasted_iota(jnp.int32, (1, pool), 1)
-
-    def store_log(b, value):
-        lane = (b % group) * block_len
-        log_ref[b // group, :, lane : lane + block_len] = value
-
-    count_log(tables_ref[...], length_ref[...], ids, block_len, spans, store_log)
-    for b in range(pool):
-        lane = (b % group) * block_len
-        row_ref[b // group, :, lane : lane + block_len] = jnp.broadcast_to(
-            scale_ref[:, b : b + 1], (2 * heads, block_len)
-        )
+    if head == 0:
+        ids = lax.broadcasted_iota(jnp.int32, (1, pool), 1)
+
+        def store_log(b, value):
+            lane = (b % group) * block_len
+            log_ref[b // group, :, lane : lane + block_len] = value
+
+        count_log(tables_ref[...], length_ref[...], ids, block_len, spans, store_log)
+        for b in range(pool):
+            lane = (b % group) * block_len
+            row_ref[b // group, :, lane : lane + block_len] = jnp.broadcast_to(
+                scale_ref[:, b : b + 1], (2 * heads, block_len)
+            )
     shape = (height, fresh_ref.shape[2])
     row = lax.broadcasted_iota(jnp.int32, shape, 0)
     col = lax.broadcasted_iota(jnp.int32, shape, 1)
@@ -399,7 +402,7 @@
     rows = per_head * steps
     height = requests * rows
     slots = instances * CAP
-    group = 8
+    group = 16
     f32, bf16 = jnp.float32, jnp.bfloat16
     code_rows = 2 * heads * block_len
     pool_rows = pool_codes.reshape(pool, code_rows, head_dim)
@@ -471,17 +474,18 @@
     chunks = pool // group
     tokens = pool * block_len
 
-    def own(head, query_rows):
+    mask_shapes = [(chunks, requests, width), (chunks, 2 * heads, width)]
+
+    def own(head, *masks):
+        shapes = [(height, head_dim)] * 3 + ([] if head else mask_shapes)
         return pl.pallas_call(
             functools.partial(
                 own_kernel, (head, pool, heads, rows, steps, block_len, spans, factor, group)
             ),
-            out_shape=[jax.ShapeDtypeStruct((height, head_dim), f32)] * 3,
-            in_specs=[VMEM_SPEC] * 5 + [HBM_SPEC],
-            out_specs=[VMEM_SPEC] * 3,
+            out_shape=[jax.ShapeDtypeStruct(shape, f32) for shape in shapes],
+            in_specs=[VMEM_SPEC, VMEM_SPEC, HBM_SPEC] + [VMEM_SPEC] * len(masks),
+            out_specs=[VMEM_SPEC] * len(shapes),
             scratch_shapes=[
-                pltpu.VMEM((chunks, requests, width), f32),
-                pltpu.VMEM((chunks, 2 * heads, width), f32),
                 pltpu.VMEM((chunks, height, width), f32),
                 pltpu.VMEM((height, width), bf16),
                 pltpu.VMEM((2, chunks, group, block_len, head_dim), bf16),
@@ -494,13 +498,13 @@
                 transcendentals=height * tokens,
             ),
             name="own_blocks",
-        )(tables, length, flat_scales, query_rows, fresh, pool_rows)
-
-    own_parts = own(0, query_rows)
+        )(query_rows, fresh, pool_rows, *masks)
+
+    *own_parts, log_rows, scale_rows = own(0, tables, length, flat_scales)
     if not general:
-        seconds, own_parts = lax.optimization_barrier((seconds, own_parts))
+        seconds, own_parts, log_rows = lax.optimization_barrier((seconds, own_parts, log_rows))
     for head in range(1, heads):
-        own_parts = own_parts + own(head, query_rows)
+        own_parts = own_parts + list(own(head, log_rows, scale_rows))
 
     if not general:
         held = {k: second for k, second in seconds.items() if k}

time: 35 us -> 33 us (0.943)
  Pallas kernels: 22.2 us -> 20.3 us
    pallas_call x2, Pallas kernels: 14.6 us -> 12.6 us  [own(): pl.pallas_call(functools.partial(own_kernel, (head, pool, heads, rows, st...]
  transfers between devices with their start and end apart: 5 -> 5, of which waited for: 0 -> 0; matrix products, arithmetic and copies ran while one was open for 1% -> 1% of each run, Pallas kernels for 49% -> 46%
where the time goes in v16:
time: 33 us; the launch traced here: 32.8 us
  Pallas kernels  20.3 us (62%)
  starting transfers between devices  10.2 us (31%)
  between operations  1 us (3%)
  loops' own time  0.79 us (2%)
  local copies, waits for them, and re-layouts  0.53 us (2%)
    pallas_call x2, Pallas kernels, own(): pl.pallas_call(functools.partial(own_kernel, (head, pool, heads, rows, st...  12.6 us
    ppermute x5, starting transfers between devices, swap(): lax.ppermute(value, 'inst', [(j, j ^ distance) for j in range(instances)])  10.2 us
    pallas_call x2, Pallas kernels, pack(): pl.pallas_call(functools.partial(pack_kernel, (instances, listed, heads,...  4.87 us
    pallas_call x1, Pallas kernels, attend(): pl.pallas_call(functools.partial(arrival_kernel, (pool, heads, rows, bloc...  2.86 us
    another operation x1, loops' own time, shards(): lax.while_loop(lambda state: state[0] > 1, lambda state: (jnp.int32(0), a...  0.79 us
  transfers between devices with their start and end apart: 5, of which 0 were waited for; matrix products, arithmetic and copies ran while one was open for 1% of the time, Pallas kernels for 46%

profile of v16, /device:TPU:0, one launch (start us, length us, event | category | flops | bytes accessed | tf_op | source)
XLA Modules:
  0.0 32.8 jit_solution(6644452982307003440)
XLA Ops:
  0.6 0.0 copy-start.6
  0.6 0.0 copy-start.8
  0.7 0.0 copy-start.7
  0.7 0.0 copy-start.4
  0.7 0.0 copy-start.10
  0.7 0.0 copy-start.5
  0.7 0.0 copy-start.9
  0.7 2.4 %pack_blocks.4.refs_11_ = bf16[1,528,128]{2,1,0:T(8,128)(2,1)} custom-call(s32[1,4]{1,0:T(1,128)} %dest_ref.2, s32[1,4]{1,0:T(1,128)} %block_ref.3, bf16[2,2,48]{2,1,0:T(2,128)(2,1)} %bitcast.52, bf16[48,512,128]{2,1,0:T(8,128)(2,1)} %bitcast.40), custom_call_target="tpu_custom_call" | custom-call | bytes 270336 | tf_op jit(solution)/shard_map/pack_blocks/pallas_call | solution.py:416
  3.1 4.1 %collective-permute-start.3 = (bf16[1,528,128]{2,1,0:T(8,128)(2,1)}, bf16[1,528,128]{2,1,0:T(8,128)(2,1)S(1)}, u32[]{:S(2)}, u32[]{:S(2)}) collective-permute-start(bf16[1,528,128]{2,1,0:T(8,128)(2,1)} %pack_blocks.4.refs_11_), channel_id=1, source_target_pairs={{0,8},{4,12},{8,0},{12,4},{1,9},{5,13},{9,1},{13,5},{2,10},{6,14},... | collective-permute-start | bytes 405512 | tf_op jit(solution)/shard_map/ppermute | solution.py:436
  7.2 0.0 copy-done.6
  7.2 0.0 copy-done.8
  7.2 0.0 copy-done.7
  7.2 2.5 %pack_blocks.5 = (bf16[1,528,128]{2,1,0:T(8,128)(2,1)}, bf16[2,528,128]{2,1,0:T(8,128)(2,1)}, bf16[1,528,128]{2,1,0:T(8,128)(2,1)}, bf16[1,528,128]{2,1,0:T(8,128)(2,1)}) custom-call(s32[1,4]{1,0:T(1,128)S(1)} %copy-done.7, s32[1,4]{1,0:T(1,128)S(1)} %copy-done.8, bf16[2,2,48]{2,1,0:T(2,128)(2,1)S(1)} %bitcast.53, bf16[48,512,128]{2,1,0:T(8,128)(2,1)} %bitcast.41), custom_call_target="tpu_custom_call" | custom-call | bytes 1351680 | tf_op jit(solution)/shard_map/pack_blocks/pallas_call | solution.py:416
  9.7 1.6 %collective-permute-start.6 = (bf16[2,528,128]{2,1,0:T(8,128)(2,1)}, bf16[2,528,128]{2,1,0:T(8,128)(2,1)S(1)}, u32[]{:S(2)}, u32[]{:S(2)}) collective-permute-start(bf16[2,528,128]{2,1,0:T(8,128)(2,1)} %get-tuple-element.91), channel_id=1, source_target_pairs={{0,4},{4,0},{8,12},{12,8},{1,5},{5,1},{9,13},{13,9},{2,6},{6,2},{1... | collective-permute-start | bytes 811016 | tf_op jit(solution)/shard_map/ppermute | solution.py:436
  11.3 0.0 collective-permute-start.4
  11.3 1.9 %collective-permute-start.5 = (bf16[1,528,128]{2,1,0:T(8,128)(2,1)}, bf16[1,528,128]{2,1,0:T(8,128)(2,1)S(1)}, u32[]{:S(2)}, u32[]{:S(2)}) collective-permute-start(bf16[1,528,128]{2,1,0:T(8,128)(2,1)} %get-tuple-element.92), channel_id=1, source_target_pairs={{0,8},{4,12},{8,0},{12,4},{1,9},{5,13},{9,1},{13,5},{2,10},{6,14},... | collective-permute-start | bytes 405512 | tf_op jit(solution)/shard_map/ppermute | solution.py:436
  13.3 0.0 copy-done.4
  13.3 0.2 copy.13
  13.5 0.0 copy-done.10
  13.5 0.1 copy.17.refs_0_.tables_ref
  13.6 0.0 copy-done.5
  13.6 0.1 copy.19
  13.6 0.1 copy.14
  13.7 0.0 copy-done.9
  13.7 0.1 copy.18.refs_1_.length_ref
  13.8 0.0 copy-start.1
  13.8 0.0 copy-start.2
  13.8 6.2 %own_blocks.6 = (f32[512,128]{1,0:T(8,128)S(1)}, f32[512,128]{1,0:T(8,128)S(1)}, f32[512,128]{1,0:T(8,128)S(1)}, f32[3,32,2048]{2,1,0:T(8,128)S(1)}, f32[3,4,2048]{2,1,0:T(4,128)S(1)}) custom-call(bf16[2,512,128]{2,1,0:T(8,128)(2,1)S(1)} %bitcast.37, bf16[2,2,128,128]{3,2,1,0:T(8,128)(2,1)S(1)} %pad.8.fresh_ref, bf16[48,512,128]{2,1,0:T(8,128)(2,1)} %bitcast.42, ...), custom_call_target="tpu_custom_call" | custom-call | flops 1610612736 | bytes 3145728 | tf_op jit(solution)/shard_map/own_blocks/pallas_call | solution.py:481
  20.1 0.0 collective-permute-done.3.refs_6_
  20.1 2.5 %collective-permute-start.7 = (bf16[1,528,128]{2,1,0:T(8,128)(2,1)S(1)}, bf16[1,528,128]{2,1,0:T(8,128)(2,1)S(1)}, u32[]{:S(2)}, u32[]{:S(2)}) collective-permute-start(bf16[1,528,128]{2,1,0:T(8,128)(2,1)S(1)} %collective-permute-done.3.refs_6_), channel_id=1, source_target_pairs={{0,4},{4,0},{8,12},{12,8},{1,5},{5,1},{9,13},{13,9},{2,6},{6,2},{1... | collective-permute-start | bytes 405512 | tf_op jit(solution)/shard_map/ppermute | solution.py:436
  22.6 6.3 %own_blocks.7 = (f32[512,128]{1,0:T(8,128)S(1)}, f32[512,128]{1,0:T(8,128)S(1)}, f32[512,128]{1,0:T(8,128)S(1)}) custom-call(bf16[2,512,128]{2,1,0:T(8,128)(2,1)S(1)} %bitcast.38, bf16[2,2,128,128]{3,2,1,0:T(8,128)(2,1)S(1)} %pad.8.fresh_ref, bf16[48,512,128]{2,1,0:T(8,128)(2,1)} %bitcast.43, f32[3,32,2048]{2,1,0:T(8,128)S(1)} %get-tuple-element.102.refs_0_, ...), custom_call_target="tpu_custom_call" | custom-call | flops 1610612736 | bytes 3145728 | tf_op jit(solution)/shard_map/own_blocks/pallas_call | solution.py:481
  28.9 0.0 collective-permute-done.4.refs_7_
  29.0 0.0 collective-permute-done.5.refs_8_
  29.0 0.0 collective-permute-done.7.refs_12_
  29.0 0.0 collective-permute-done.6.refs_9_
  29.0 0.0 copy-done.1
  29.0 0.0 copy-done.2
  29.0 2.9 %arrived_blocks.3 = (bf16[32,2,16,128]{3,2,1,0:T(8,128)(2,1)}, s32[1,4]{1,0:T(1,128)}, s32[1]{0:T(128)}) custom-call(bf16[2,512,128]{2,1,0:T(8,128)(2,1)S(1)} %bitcast.39, s32[32,16]{1,0:T(8,128)S(1)} %copy.17.refs_0_.tables_ref, s32[32,1]{1,0:T(8,128)S(1)} %copy.18.refs_1_.length_ref, f32[512,128]{1,0:T(8,128)S(1)} %get-tuple-element.99.refs_0_, ...), custom_call_target="tpu_custom_call" | custom-call | flops 536870912 | bytes 1081344 | tf_op jit(solution)/shard_map/arrived_blocks/pallas_call | solution.py:528
  31.9 0.8 %while.9 = (s32[]{:T(128)}, bf16[32,2,2048]{2,1,0:T(2,128)(2,1)}, bf16[32,2,16,128]{3,2,1,0:T(8,128)(2,1)S(1)}, s32[32]{0:T(128)S(1)}, bf16[32,2,2,2,128]{4,1,0,...) while((s32[]{:T(128)}, bf16[32,2,2048]{2,1,0:T(2,128)(2,1)}, ...), condition=%region_1.2_spmd, body=%region_0.1_spmd | while | flops 3758096640 | bytes 39749268 | solution.py:558
  (2 shorter events, 0.0 us)
Async XLA Ops:
  0.6 6.6 %copy-start.6 = (bf16[48,2,2]{0,2,1:T(2,128)(2,1)S(1)}, bf16[48,2,2]{0,2,1:T(2,128)(2,1)}, u32[]{:S(2)}) copy-start(bf16[48,2,2]{0,2,1:T(2,128)(2,1)} %param.13) | copy-start | bytes 1156
  0.6 6.6 %copy-start.8 = (s32[1,4]{1,0:T(1,128)S(1)}, s32[1,4]{1,0:T(1,128)}, u32[]{:S(2)}) copy-start(s32[1,4]{1,0:T(1,128)} %block_ref.3) | copy-start | bytes 52
  0.7 6.6 %copy-start.7 = (s32[1,4]{1,0:T(1,128)S(1)}, s32[1,4]{1,0:T(1,128)}, u32[]{:S(2)}) copy-start(s32[1,4]{1,0:T(1,128)} %dest_ref.2) | copy-start | bytes 52
  0.7 12.6 %copy-start.4 = (bf16[32,2,16,128]{3,2,1,0:T(8,128)(2,1)S(1)}, bf16[32,2,16,128]{3,2,1,0:T(8,128)(2,1)}, u32[]{:S(2)}) copy-start(bf16[32,2,16,128]{3,2,1,0:T(8,128)(2,1)} %param.10) | copy-start | bytes 786436
  0.7 12.8 %copy-start.10 = (s32[32,16]{0,1:T(8,128)S(1)}, s32[32,16]{0,1:T(8,128)}, u32[]{:S(2)}) copy-start(s32[32,16]{0,1:T(8,128)} %param.14) | copy-start | bytes 6148
  0.7 12.9 %copy-start.5 = (bf16[32,2,2,2,128]{4,3,2,1,0:T(2,128)(2,1)S(1)}, bf16[32,2,2,2,128]{4,3,2,1,0:T(2,128)(2,1)}, u32[]{:S(2)}) copy-start(bf16[32,2,2,2,128]{4,3,2,1,0:T(2,128)(2,1)} %param.11) | copy-start | bytes 196612
  0.7 13.0 %copy-start.9 = (s32[32]{0:T(128)S(1)}, s32[32]{0:T(128)}, u32[]{:S(2)}) copy-start(s32[32]{0:T(128)} %param.15) | copy-start | bytes 388
  3.1 16.9 %collective-permute-start.3 = (bf16[1,528,128]{2,1,0:T(8,128)(2,1)}, bf16[1,528,128]{2,1,0:T(8,128)(2,1)S(1)}, u32[]{:S(2)}, u32[]{:S(2)}) collective-permute-start(bf16[1,528,128]{2,1,0:T(8,128)(2,1)} %pack_blocks.4.refs_11_), channel_id=1, source_target_pairs={{0,8},{4,12},{8,0},{12,4},{1,9},{5,13},{9,1},{13,5},{2,10},{6,14},... | collective-permute-start | bytes 405512 | tf_op jit(solution)/shard_map/ppermute | solution.py:436
  9.7 19.3 %collective-permute-start.6 = (bf16[2,528,128]{2,1,0:T(8,128)(2,1)}, bf16[2,528,128]{2,1,0:T(8,128)(2,1)S(1)}, u32[]{:S(2)}, u32[]{:S(2)}) collective-permute-start(bf16[2,528,128]{2,1,0:T(8,128)(2,1)} %get-tuple-element.91), channel_id=1, source_target_pairs={{0,4},{4,0},{8,12},{12,8},{1,5},{5,1},{9,13},{13,9},{2,6},{6,2},{1... | collective-permute-start | bytes 811016 | tf_op jit(solution)/shard_map/ppermute | solution.py:436
  11.3 17.6 %collective-permute-start.4 = (bf16[1,528,128]{2,1,0:T(8,128)(2,1)}, bf16[1,528,128]{2,1,0:T(8,128)(2,1)S(1)}, u32[]{:S(2)}, u32[]{:S(2)}) collective-permute-start(bf16[1,528,128]{2,1,0:T(8,128)(2,1)} %get-tuple-element.93), channel_id=1, source_target_pairs={{0,12},{4,8},{8,4},{12,0},{1,13},{5,9},{9,5},{13,1},{2,14},{6,10},... | collective-permute-start | bytes 405512 | tf_op jit(solution)/shard_map/ppermute | solution.py:436
  11.3 17.6 %collective-permute-start.5 = (bf16[1,528,128]{2,1,0:T(8,128)(2,1)}, bf16[1,528,128]{2,1,0:T(8,128)(2,1)S(1)}, u32[]{:S(2)}, u32[]{:S(2)}) collective-permute-start(bf16[1,528,128]{2,1,0:T(8,128)(2,1)} %get-tuple-element.92), channel_id=1, source_target_pairs={{0,8},{4,12},{8,0},{12,4},{1,9},{5,13},{9,1},{13,5},{2,10},{6,14},... | collective-permute-start | bytes 405512 | tf_op jit(solution)/shard_map/ppermute | solution.py:436
  13.8 15.2 %copy-start.1 = (bf16[1,528,128]{2,1,0:T(8,128)(2,1)S(1)}, bf16[1,528,128]{2,1,0:T(8,128)(2,1)}, u32[]{:S(2)}) copy-start(bf16[1,528,128]{2,1,0:T(8,128)(2,1)} %pack_blocks.4.refs_11_) | copy-start | bytes 405508
  13.8 15.2 %copy-start.2 = (bf16[1,528,128]{2,1,0:T(8,128)(2,1)S(1)}, bf16[1,528,128]{2,1,0:T(8,128)(2,1)}, u32[]{:S(2)}) copy-start(bf16[1,528,128]{2,1,0:T(8,128)(2,1)} %get-tuple-element.90.refs_10_) | copy-start | bytes 405508
  20.1 8.9 %collective-permute-start.7 = (bf16[1,528,128]{2,1,0:T(8,128)(2,1)S(1)}, bf16[1,528,128]{2,1,0:T(8,128)(2,1)S(1)}, u32[]{:S(2)}, u32[]{:S(2)}) collective-permute-start(bf16[1,528,128]{2,1,0:T(8,128)(2,1)S(1)} %collective-permute-done.3.refs_6_), channel_id=1, source_target_pairs={{0,4},{4,0},{8,12},{12,8},{1,5},{5,1},{9,13},{13,9},{2,6},{6,2},{1... | collective-permute-start | bytes 405512 | tf_op jit(solution)/shard_map/ppermute | solution.py:436

commit v17 on v16

--- a/solution.py
+++ b/solution.py
@@ -183,24 +183,16 @@
         tables_ref, length_ref, scale_ref, acc_ref, top_ref, total_ref, log_ref, row_ref = refs[:8]
     else:
         log_ref, row_ref, acc_ref, top_ref, total_ref = refs[:5]
-    t_ref, p_ref, codes_ref, sems = refs[-4:]
+    t_ref, p_ref = refs[-2:]
     head, pool, heads, rows, steps, block_len, spans, factor, group = dims
     chunks = pool // group
     height, head_dim = q_ref.shape[1:]
     width = group * block_len
 
-    def load(part, chunk):
-        return pltpu.make_async_copy(
-            pool_ref.at[
-                pl.ds(chunk * group, group), pl.ds((part * heads + head) * block_len, block_len)
-            ],
-            codes_ref.at[part, chunk],
-            sems.at[part, chunk],
-        )
-
-    for part in range(2):
-        for chunk in range(chunks):
-            load(part, chunk).start()
+    def codes(part, chunk):
+        blocks = pl.ds(chunk * group, group)
+        at = pl.ds((part * heads + head) * block_len, block_len)
+        return pool_ref[blocks, at].reshape(width, head_dim)
 
     if head == 0:
         ids = lax.broadcasted_iota(jnp.int32, (1, pool), 1)
@@ -228,14 +220,13 @@
     top_ref[...] = lane_fold(new_score, jnp.maximum)
 
     def score(chunk, carry):
-        load(0, chunk).wait()
 
         def store(row, lane, value):
             t_ref[chunk, row : row + rows, lane : lane + value.shape[1]] = value
 
         score_tiles(
             q_ref[head],
-            codes_ref[0, chunk].reshape(width, head_dim),
+            codes(0, chunk),
             log_ref.at[chunk],
             row_ref[chunk, head : head + 1, :] * (factor * LOG2E),
             rows,
@@ -257,7 +248,6 @@
     )
 
     def apply(chunk, carry):
-        load(1, chunk).wait()
         scale = row_ref[chunk, heads + head : heads + head + 1, :]
         for row in range(0, height, rows):
             at = pl.ds(row, rows)
@@ -266,7 +256,7 @@
             p_ref[at] = (weight * scale).astype(jnp.bfloat16)
         acc_ref[...] += jnp.dot(
             p_ref[...],
-            codes_ref[1, chunk].reshape(width, head_dim),
+            codes(1, chunk),
             preferred_element_type=jnp.float32,
         )
         return carry
@@ -483,13 +473,11 @@
                 own_kernel, (head, pool, heads, rows, steps, block_len, spans, factor, group)
             ),
             out_shape=[jax.ShapeDtypeStruct(shape, f32) for shape in shapes],
-            in_specs=[VMEM_SPEC, VMEM_SPEC, HBM_SPEC] + [VMEM_SPEC] * len(masks),
+            in_specs=[VMEM_SPEC] * (3 + len(masks)),
             out_specs=[VMEM_SPEC] * len(shapes),
             scratch_shapes=[
                 pltpu.VMEM((chunks, height, width), f32),
                 pltpu.VMEM((height, width), bf16),
-                pltpu.VMEM((2, chunks, group, block_len, head_dim), bf16),
-                pltpu.SemaphoreType.DMA((2, chunks)),
             ],
             compiler_params=pltpu.CompilerParams(vmem_limit_bytes=32 * MIB),
             cost_estimate=pl.CostEstimate(

time: 33 us -> 37.3 us (1.13)
  Pallas kernels: 20.3 us -> 24.5 us
    pallas_call x2, Pallas kernels: 12.6 us -> 16.8 us  [own(): pl.pallas_call(functools.partial(own_kernel, (head, pool, heads, rows, st...]
  transfers between devices with their start and end apart: 5 -> 5, of which waited for: 0 -> 0; matrix products, arithmetic and copies ran while one was open for 1% -> 1% of each run, Pallas kernels for 46% -> 52%
where the time goes in v17:
time: 37.3 us; the launch traced here: 37.1 us
  Pallas kernels  24.5 us (66%)
  starting transfers between devices  10.2 us (27%)
  between operations  1 us (3%)
  loops' own time  0.79 us (2%)
  local copies, waits for them, and re-layouts  0.53 us (1%)
    pallas_call x2, Pallas kernels, own(): pl.pallas_call(functools.partial(own_kernel, (head, pool, heads, rows, st...  16.8 us
    ppermute x5, starting transfers between devices, swap(): lax.ppermute(value, 'inst', [(j, j ^ distance) for j in range(instances)])  10.2 us
    pallas_call x2, Pallas kernels, pack(): pl.pallas_call(functools.partial(pack_kernel, (instances, listed, heads,...  4.87 us
    pallas_call x1, Pallas kernels, attend(): pl.pallas_call(functools.partial(arrival_kernel, (pool, heads, rows, bloc...  2.86 us
    another operation x1, loops' own time, shards(): lax.while_loop(lambda state: state[0] > 1, lambda state: (jnp.int32(0), a...  0.79 us
  transfers between devices with their start and end apart: 5, of which 0 were waited for; matrix products, arithmetic and copies ran while one was open for 1% of the time, Pallas kernels for 52%

profile of v17, /device:TPU:0, one launch (start us, length us, event | category | flops | bytes accessed | tf_op | source)
XLA Modules:
  0.0 37.1 jit_solution(12207331487233066894)
XLA Ops:
  0.6 0.0 copy-start.6
  0.6 0.0 copy-start.8
  0.7 0.0 copy-start.7
  0.7 0.0 copy-start.4
  0.7 0.0 copy-start.10
  0.7 0.0 copy-start.5
  0.7 0.0 copy-start.9
  0.7 2.4 %pack_blocks.4.refs_11_ = bf16[1,528,128]{2,1,0:T(8,128)(2,1)} custom-call(s32[1,4]{1,0:T(1,128)} %dest_ref.2, s32[1,4]{1,0:T(1,128)} %block_ref.3, bf16[2,2,48]{2,1,0:T(2,128)(2,1)} %bitcast.52, bf16[48,512,128]{2,1,0:T(8,128)(2,1)} %bitcast.40), custom_call_target="tpu_custom_call" | custom-call | bytes 270336 | tf_op jit(solution)/shard_map/pack_blocks/pallas_call | solution.py:406
  3.1 4.1 %collective-permute-start.3 = (bf16[1,528,128]{2,1,0:T(8,128)(2,1)}, bf16[1,528,128]{2,1,0:T(8,128)(2,1)S(1)}, u32[]{:S(2)}, u32[]{:S(2)}) collective-permute-start(bf16[1,528,128]{2,1,0:T(8,128)(2,1)} %pack_blocks.4.refs_11_), channel_id=1, source_target_pairs={{0,8},{4,12},{8,0},{12,4},{1,9},{5,13},{9,1},{13,5},{2,10},{6,14},... | collective-permute-start | bytes 405512 | tf_op jit(solution)/shard_map/ppermute | solution.py:426
  7.2 0.0 copy-done.6
  7.2 0.0 copy-done.8
  7.2 0.0 copy-done.7
  7.2 2.5 %pack_blocks.5 = (bf16[1,528,128]{2,1,0:T(8,128)(2,1)}, bf16[2,528,128]{2,1,0:T(8,128)(2,1)}, bf16[1,528,128]{2,1,0:T(8,128)(2,1)}, bf16[1,528,128]{2,1,0:T(8,128)(2,1)}) custom-call(s32[1,4]{1,0:T(1,128)S(1)} %copy-done.7, s32[1,4]{1,0:T(1,128)S(1)} %copy-done.8, bf16[2,2,48]{2,1,0:T(2,128)(2,1)S(1)} %bitcast.53, bf16[48,512,128]{2,1,0:T(8,128)(2,1)} %bitcast.41), custom_call_target="tpu_custom_call" | custom-call | bytes 1351680 | tf_op jit(solution)/shard_map/pack_blocks/pallas_call | solution.py:406
  9.7 1.6 %collective-permute-start.6 = (bf16[2,528,128]{2,1,0:T(8,128)(2,1)}, bf16[2,528,128]{2,1,0:T(8,128)(2,1)S(1)}, u32[]{:S(2)}, u32[]{:S(2)}) collective-permute-start(bf16[2,528,128]{2,1,0:T(8,128)(2,1)} %get-tuple-element.91), channel_id=1, source_target_pairs={{0,4},{4,0},{8,12},{12,8},{1,5},{5,1},{9,13},{13,9},{2,6},{6,2},{1... | collective-permute-start | bytes 811016 | tf_op jit(solution)/shard_map/ppermute | solution.py:426
  11.3 0.0 collective-permute-start.4
  11.3 1.9 %collective-permute-start.5 = (bf16[1,528,128]{2,1,0:T(8,128)(2,1)}, bf16[1,528,128]{2,1,0:T(8,128)(2,1)S(1)}, u32[]{:S(2)}, u32[]{:S(2)}) collective-permute-start(bf16[1,528,128]{2,1,0:T(8,128)(2,1)} %get-tuple-element.92), channel_id=1, source_target_pairs={{0,8},{4,12},{8,0},{12,4},{1,9},{5,13},{9,1},{13,5},{2,10},{6,14},... | collective-permute-start | bytes 405512 | tf_op jit(solution)/shard_map/ppermute | solution.py:426
  13.3 0.0 copy-done.4
  13.3 0.2 copy.13
  13.5 0.0 copy-done.10
  13.5 0.1 copy.17.refs_0_.tables_ref
  13.6 0.0 copy-done.5
  13.6 0.1 copy.19
  13.6 0.1 copy.14
  13.7 0.0 copy-done.9
  13.7 0.1 copy.18.refs_1_.length_ref
  13.8 0.0 copy-start.1
  13.8 0.0 copy-start.2
  13.8 8.6 %own_blocks.6 = (f32[512,128]{1,0:T(8,128)S(1)}, f32[512,128]{1,0:T(8,128)S(1)}, f32[512,128]{1,0:T(8,128)S(1)}, f32[3,32,2048]{2,1,0:T(8,128)S(1)}, f32[3,4,2048]{2,1,0:T(4,128)S(1)}) custom-call(bf16[2,512,128]{2,1,0:T(8,128)(2,1)S(1)} %bitcast.37, bf16[2,2,128,128]{3,2,1,0:T(8,128)(2,1)S(1)} %pad.8.fresh_ref, bf16[48,512,128]{2,1,0:T(8,128)(2,1)} %bitcast.42, ...), custom_call_target="tpu_custom_call" | custom-call | flops 1610612736 | bytes 3145728 | tf_op jit(solution)/shard_map/own_blocks/pallas_call | solution.py:471
  22.4 0.0 collective-permute-done.3.refs_6_
  22.5 2.5 %collective-permute-start.7 = (bf16[1,528,128]{2,1,0:T(8,128)(2,1)S(1)}, bf16[1,528,128]{2,1,0:T(8,128)(2,1)S(1)}, u32[]{:S(2)}, u32[]{:S(2)}) collective-permute-start(bf16[1,528,128]{2,1,0:T(8,128)(2,1)S(1)} %collective-permute-done.3.refs_6_), channel_id=1, source_target_pairs={{0,4},{4,0},{8,12},{12,8},{1,5},{5,1},{9,13},{13,9},{2,6},{6,2},{1... | collective-permute-start | bytes 405512 | tf_op jit(solution)/shard_map/ppermute | solution.py:426
  25.0 8.2 %own_blocks.7 = (f32[512,128]{1,0:T(8,128)S(1)}, f32[512,128]{1,0:T(8,128)S(1)}, f32[512,128]{1,0:T(8,128)S(1)}) custom-call(bf16[2,512,128]{2,1,0:T(8,128)(2,1)S(1)} %bitcast.38, bf16[2,2,128,128]{3,2,1,0:T(8,128)(2,1)S(1)} %pad.8.fresh_ref, bf16[48,512,128]{2,1,0:T(8,128)(2,1)} %bitcast.43, f32[3,32,2048]{2,1,0:T(8,128)S(1)} %get-tuple-element.102.refs_0_, ...), custom_call_target="tpu_custom_call" | custom-call | flops 1610612736 | bytes 3145728 | tf_op jit(solution)/shard_map/own_blocks/pallas_call | solution.py:471
  33.2 0.0 collective-permute-done.4.refs_7_
  33.2 0.0 collective-permute-done.5.refs_8_
  33.2 0.0 collective-permute-done.7.refs_12_
  33.2 0.0 collective-permute-done.6.refs_9_
  33.2 0.0 copy-done.1
  33.2 0.0 copy-done.2
  33.2 2.9 %arrived_blocks.3 = (bf16[32,2,16,128]{3,2,1,0:T(8,128)(2,1)}, s32[1,4]{1,0:T(1,128)}, s32[1]{0:T(128)}) custom-call(bf16[2,512,128]{2,1,0:T(8,128)(2,1)S(1)} %bitcast.39, s32[32,16]{1,0:T(8,128)S(1)} %copy.17.refs_0_.tables_ref, s32[32,1]{1,0:T(8,128)S(1)} %copy.18.refs_1_.length_ref, f32[512,128]{1,0:T(8,128)S(1)} %get-tuple-element.99.refs_0_, ...), custom_call_target="tpu_custom_call" | custom-call | flops 536870912 | bytes 1081344 | tf_op jit(solution)/shard_map/arrived_blocks/pallas_call | solution.py:516
  36.1 0.8 %while.9 = (s32[]{:T(128)}, bf16[32,2,2048]{2,1,0:T(2,128)(2,1)}, bf16[32,2,16,128]{3,2,1,0:T(8,128)(2,1)S(1)}, s32[32]{0:T(128)S(1)}, bf16[32,2,2,2,128]{4,1,0,...) while((s32[]{:T(128)}, bf16[32,2,2048]{2,1,0:T(2,128)(2,1)}, ...), condition=%region_1.2_spmd, body=%region_0.1_spmd | while | flops 3758096640 | bytes 39749268 | solution.py:546
  (2 shorter events, 0.0 us)
Async XLA Ops:
  0.6 6.6 %copy-start.6 = (bf16[48,2,2]{0,2,1:T(2,128)(2,1)S(1)}, bf16[48,2,2]{0,2,1:T(2,128)(2,1)}, u32[]{:S(2)}) copy-start(bf16[48,2,2]{0,2,1:T(2,128)(2,1)} %param.13) | copy-start | bytes 1156
  0.6 6.6 %copy-start.8 = (s32[1,4]{1,0:T(1,128)S(1)}, s32[1,4]{1,0:T(1,128)}, u32[]{:S(2)}) copy-start(s32[1,4]{1,0:T(1,128)} %block_ref.3) | copy-start | bytes 52
  0.7 6.6 %copy-start.7 = (s32[1,4]{1,0:T(1,128)S(1)}, s32[1,4]{1,0:T(1,128)}, u32[]{:S(2)}) copy-start(s32[1,4]{1,0:T(1,128)} %dest_ref.2) | copy-start | bytes 52
  0.7 12.6 %copy-start.4 = (bf16[32,2,16,128]{3,2,1,0:T(8,128)(2,1)S(1)}, bf16[32,2,16,128]{3,2,1,0:T(8,128)(2,1)}, u32[]{:S(2)}) copy-start(bf16[32,2,16,128]{3,2,1,0:T(8,128)(2,1)} %param.10) | copy-start | bytes 786436
  0.7 12.8 %copy-start.10 = (s32[32,16]{0,1:T(8,128)S(1)}, s32[32,16]{0,1:T(8,128)}, u32[]{:S(2)}) copy-start(s32[32,16]{0,1:T(8,128)} %param.14) | copy-start | bytes 6148
  0.7 12.9 %copy-start.5 = (bf16[32,2,2,2,128]{4,3,2,1,0:T(2,128)(2,1)S(1)}, bf16[32,2,2,2,128]{4,3,2,1,0:T(2,128)(2,1)}, u32[]{:S(2)}) copy-start(bf16[32,2,2,2,128]{4,3,2,1,0:T(2,128)(2,1)} %param.11) | copy-start | bytes 196612
  0.7 13.0 %copy-start.9 = (s32[32]{0:T(128)S(1)}, s32[32]{0:T(128)}, u32[]{:S(2)}) copy-start(s32[32]{0:T(128)} %param.15) | copy-start | bytes 388
  3.1 19.3 %collective-permute-start.3 = (bf16[1,528,128]{2,1,0:T(8,128)(2,1)}, bf16[1,528,128]{2,1,0:T(8,128)(2,1)S(1)}, u32[]{:S(2)}, u32[]{:S(2)}) collective-permute-start(bf16[1,528,128]{2,1,0:T(8,128)(2,1)} %pack_blocks.4.refs_11_), channel_id=1, source_target_pairs={{0,8},{4,12},{8,0},{12,4},{1,9},{5,13},{9,1},{13,5},{2,10},{6,14},... | collective-permute-start | bytes 405512 | tf_op jit(solution)/shard_map/ppermute | solution.py:426
  9.7 23.5 %collective-permute-start.6 = (bf16[2,528,128]{2,1,0:T(8,128)(2,1)}, bf16[2,528,128]{2,1,0:T(8,128)(2,1)S(1)}, u32[]{:S(2)}, u32[]{:S(2)}) collective-permute-start(bf16[2,528,128]{2,1,0:T(8,128)(2,1)} %get-tuple-element.91), channel_id=1, source_target_pairs={{0,4},{4,0},{8,12},{12,8},{1,5},{5,1},{9,13},{13,9},{2,6},{6,2},{1... | collective-permute-start | bytes 811016 | tf_op jit(solution)/shard_map/ppermute | solution.py:426
  11.3 21.8 %collective-permute-start.4 = (bf16[1,528,128]{2,1,0:T(8,128)(2,1)}, bf16[1,528,128]{2,1,0:T(8,128)(2,1)S(1)}, u32[]{:S(2)}, u32[]{:S(2)}) collective-permute-start(bf16[1,528,128]{2,1,0:T(8,128)(2,1)} %get-tuple-element.93), channel_id=1, source_target_pairs={{0,12},{4,8},{8,4},{12,0},{1,13},{5,9},{9,5},{13,1},{2,14},{6,10},... | collective-permute-start | bytes 405512 | tf_op jit(solution)/shard_map/ppermute | solution.py:426
  11.3 21.8 %collective-permute-start.5 = (bf16[1,528,128]{2,1,0:T(8,128)(2,1)}, bf16[1,528,128]{2,1,0:T(8,128)(2,1)S(1)}, u32[]{:S(2)}, u32[]{:S(2)}) collective-permute-start(bf16[1,528,128]{2,1,0:T(8,128)(2,1)} %get-tuple-element.92), channel_id=1, source_target_pairs={{0,8},{4,12},{8,0},{12,4},{1,9},{5,13},{9,1},{13,5},{2,10},{6,14},... | collective-permute-start | bytes 405512 | tf_op jit(solution)/shard_map/ppermute | solution.py:426
  13.8 19.4 %copy-start.1 = (bf16[1,528,128]{2,1,0:T(8,128)(2,1)S(1)}, bf16[1,528,128]{2,1,0:T(8,128)(2,1)}, u32[]{:S(2)}) copy-start(bf16[1,528,128]{2,1,0:T(8,128)(2,1)} %pack_blocks.4.refs_11_) | copy-start | bytes 405508
  13.8 19.4 %copy-start.2 = (bf16[1,528,128]{2,1,0:T(8,128)(2,1)S(1)}, bf16[1,528,128]{2,1,0:T(8,128)(2,1)}, u32[]{:S(2)}) copy-start(bf16[1,528,128]{2,1,0:T(8,128)(2,1)} %get-tuple-element.90.refs_10_) | copy-start | bytes 405508
  22.5 10.7 %collective-permute-start.7 = (bf16[1,528,128]{2,1,0:T(8,128)(2,1)S(1)}, bf16[1,528,128]{2,1,0:T(8,128)(2,1)S(1)}, u32[]{:S(2)}, u32[]{:S(2)}) collective-permute-start(bf16[1,528,128]{2,1,0:T(8,128)(2,1)S(1)} %collective-permute-done.3.refs_6_), channel_id=1, source_target_pairs={{0,4},{4,0},{8,12},{12,8},{1,5},{5,1},{9,13},{13,9},{2,6},{6,2},{1... | collective-permute-start | bytes 405512 | tf_op jit(solution)/shard_map/ppermute | solution.py:426

commit v18 on v16

--- a/solution.py
+++ b/solution.py
@@ -231,7 +231,9 @@
         load(0, chunk).wait()
 
         def store(row, lane, value):
-            t_ref[chunk, row : row + rows, lane : lane + value.shape[1]] = value
+            at = pl.ds(row, rows)
+            t_ref[chunk, at, lane : lane + value.shape[1]] = value
+            top_ref[at] = jnp.maximum(top_ref[at], lane_fold(value, jnp.maximum))
 
         score_tiles(
             q_ref[head],
@@ -241,9 +243,6 @@
             rows,
             store,
         )
-        for row in range(0, height, rows):
-            at = pl.ds(row, rows)
-            top_ref[at] = jnp.maximum(top_ref[at], lane_fold(t_ref[chunk, at], jnp.maximum))
         return carry
 
     lax.fori_loop(0, chunks, score, 0)
@@ -259,16 +258,18 @@
     def apply(chunk, carry):
         load(1, chunk).wait()
         scale = row_ref[chunk, heads + head : heads + head + 1, :]
-        for row in range(0, height, rows):
-            at = pl.ds(row, rows)
-            weight = jnp.exp2(t_ref[chunk, at] - spread(top_ref[at], width))
-            total_ref[at] += lane_fold(weight, jnp.add)
-            p_ref[at] = (weight * scale).astype(jnp.bfloat16)
-        acc_ref[...] += jnp.dot(
-            p_ref[...],
-            codes_ref[1, chunk].reshape(width, head_dim),
-            preferred_element_type=jnp.float32,
-        )
+        tile = min(256, height)
+        for start in range(0, height, tile):
+            for row in range(start, start + tile, rows):
+                at = pl.ds(row, rows)
+                weight = jnp.exp2(t_ref[chunk, at] - spread(top_ref[at], width))
+                total_ref[at] += lane_fold(weight, jnp.add)
+                p_ref[at] = (weight * scale).astype(jnp.bfloat16)
+            at = pl.ds(start, tile)
+            acc_ref[at] += jnp.dot(
+                p_ref[at], codes_ref[1, chunk].reshape(width, head_dim),
+                preferred_element_type=jnp.float32,
+            )
         return carry
 
     lax.fori_loop(0, chunks, apply, 0)

time: 33 us -> 33.2 us (level)
  no operation moved by 1% of the time
where the time goes in v18:
time: 33.2 us; the launch traced here: 33 us
  Pallas kernels  20.5 us (62%)
  starting transfers between devices  10.2 us (31%)
  between operations  1 us (3%)
  loops' own time  0.79 us (2%)
  local copies, waits for them, and re-layouts  0.53 us (2%)
    pallas_call x2, Pallas kernels, own(): pl.pallas_call(functools.partial(own_kernel, (head, pool, heads, rows, st...  12.8 us
    ppermute x5, starting transfers between devices, swap(): lax.ppermute(value, 'inst', [(j, j ^ distance) for j in range(instances)])  10.2 us
    pallas_call x2, Pallas kernels, pack(): pl.pallas_call(functools.partial(pack_kernel, (instances, listed, heads,...  4.87 us
    pallas_call x1, Pallas kernels, attend(): pl.pallas_call(functools.partial(arrival_kernel, (pool, heads, rows, bloc...  2.86 us
    another operation x1, loops' own time, shards(): lax.while_loop(lambda state: state[0] > 1, lambda state: (jnp.int32(0), a...  0.79 us
  transfers between devices with their start and end apart: 5, of which 0 were waited for; matrix products, arithmetic and copies ran while one was open for 1% of the time, Pallas kernels for 46%

profile of v18, /device:TPU:0, one launch (start us, length us, event | category | flops | bytes accessed | tf_op | source)
XLA Modules:
  0.0 33.0 jit_solution(801590744144722017)
XLA Ops:
  0.6 0.0 copy-start.6
  0.6 0.0 copy-start.8
  0.7 0.0 copy-start.7
  0.7 0.0 copy-start.4
  0.7 0.0 copy-start.10
  0.7 0.0 copy-start.5
  0.7 0.0 copy-start.9
  0.7 2.4 %pack_blocks.4.refs_11_ = bf16[1,528,128]{2,1,0:T(8,128)(2,1)} custom-call(s32[1,4]{1,0:T(1,128)} %dest_ref.2, s32[1,4]{1,0:T(1,128)} %block_ref.3, bf16[2,2,48]{2,1,0:T(2,128)(2,1)} %bitcast.52, bf16[48,512,128]{2,1,0:T(8,128)(2,1)} %bitcast.40), custom_call_target="tpu_custom_call" | custom-call | bytes 270336 | tf_op jit(solution)/shard_map/pack_blocks/pallas_call | solution.py:417
  3.1 4.1 %collective-permute-start.3 = (bf16[1,528,128]{2,1,0:T(8,128)(2,1)}, bf16[1,528,128]{2,1,0:T(8,128)(2,1)S(1)}, u32[]{:S(2)}, u32[]{:S(2)}) collective-permute-start(bf16[1,528,128]{2,1,0:T(8,128)(2,1)} %pack_blocks.4.refs_11_), channel_id=1, source_target_pairs={{0,8},{4,12},{8,0},{12,4},{1,9},{5,13},{9,1},{13,5},{2,10},{6,14},... | collective-permute-start | bytes 405512 | tf_op jit(solution)/shard_map/ppermute | solution.py:437
  7.2 0.0 copy-done.6
  7.2 0.0 copy-done.8
  7.2 0.0 copy-done.7
  7.2 2.5 %pack_blocks.5 = (bf16[1,528,128]{2,1,0:T(8,128)(2,1)}, bf16[2,528,128]{2,1,0:T(8,128)(2,1)}, bf16[1,528,128]{2,1,0:T(8,128)(2,1)}, bf16[1,528,128]{2,1,0:T(8,128)(2,1)}) custom-call(s32[1,4]{1,0:T(1,128)S(1)} %copy-done.7, s32[1,4]{1,0:T(1,128)S(1)} %copy-done.8, bf16[2,2,48]{2,1,0:T(2,128)(2,1)S(1)} %bitcast.53, bf16[48,512,128]{2,1,0:T(8,128)(2,1)} %bitcast.41), custom_call_target="tpu_custom_call" | custom-call | bytes 1351680 | tf_op jit(solution)/shard_map/pack_blocks/pallas_call | solution.py:417
  9.7 1.6 %collective-permute-start.6 = (bf16[2,528,128]{2,1,0:T(8,128)(2,1)}, bf16[2,528,128]{2,1,0:T(8,128)(2,1)S(1)}, u32[]{:S(2)}, u32[]{:S(2)}) collective-permute-start(bf16[2,528,128]{2,1,0:T(8,128)(2,1)} %get-tuple-element.91), channel_id=1, source_target_pairs={{0,4},{4,0},{8,12},{12,8},{1,5},{5,1},{9,13},{13,9},{2,6},{6,2},{1... | collective-permute-start | bytes 811016 | tf_op jit(solution)/shard_map/ppermute | solution.py:437
  11.3 0.0 collective-permute-start.4
  11.3 1.9 %collective-permute-start.5 = (bf16[1,528,128]{2,1,0:T(8,128)(2,1)}, bf16[1,528,128]{2,1,0:T(8,128)(2,1)S(1)}, u32[]{:S(2)}, u32[]{:S(2)}) collective-permute-start(bf16[1,528,128]{2,1,0:T(8,128)(2,1)} %get-tuple-element.92), channel_id=1, source_target_pairs={{0,8},{4,12},{8,0},{12,4},{1,9},{5,13},{9,1},{13,5},{2,10},{6,14},... | collective-permute-start | bytes 405512 | tf_op jit(solution)/shard_map/ppermute | solution.py:437
  13.3 0.0 copy-done.4
  13.3 0.2 copy.13
  13.5 0.0 copy-done.10
  13.5 0.1 copy.17.refs_0_.tables_ref
  13.6 0.0 copy-done.5
  13.6 0.1 copy.19
  13.6 0.1 copy.14
  13.7 0.0 copy-done.9
  13.7 0.1 copy.18.refs_1_.length_ref
  13.8 0.0 copy-start.1
  13.8 0.0 copy-start.2
  13.8 6.3 %own_blocks.6 = (f32[512,128]{1,0:T(8,128)S(1)}, f32[512,128]{1,0:T(8,128)S(1)}, f32[512,128]{1,0:T(8,128)S(1)}, f32[3,32,2048]{2,1,0:T(8,128)S(1)}, f32[3,4,2048]{2,1,0:T(4,128)S(1)}) custom-call(bf16[2,512,128]{2,1,0:T(8,128)(2,1)S(1)} %bitcast.37, bf16[2,2,128,128]{3,2,1,0:T(8,128)(2,1)S(1)} %pad.8.fresh_ref, bf16[48,512,128]{2,1,0:T(8,128)(2,1)} %bitcast.42, ...), custom_call_target="tpu_custom_call" | custom-call | flops 1610612736 | bytes 3145728 | tf_op jit(solution)/shard_map/own_blocks/pallas_call | solution.py:482
  20.2 0.0 collective-permute-done.3.refs_6_
  20.2 2.5 %collective-permute-start.7 = (bf16[1,528,128]{2,1,0:T(8,128)(2,1)S(1)}, bf16[1,528,128]{2,1,0:T(8,128)(2,1)S(1)}, u32[]{:S(2)}, u32[]{:S(2)}) collective-permute-start(bf16[1,528,128]{2,1,0:T(8,128)(2,1)S(1)} %collective-permute-done.3.refs_6_), channel_id=1, source_target_pairs={{0,4},{4,0},{8,12},{12,8},{1,5},{5,1},{9,13},{13,9},{2,6},{6,2},{1... | collective-permute-start | bytes 405512 | tf_op jit(solution)/shard_map/ppermute | solution.py:437
  22.7 6.4 %own_blocks.7 = (f32[512,128]{1,0:T(8,128)S(1)}, f32[512,128]{1,0:T(8,128)S(1)}, f32[512,128]{1,0:T(8,128)S(1)}) custom-call(bf16[2,512,128]{2,1,0:T(8,128)(2,1)S(1)} %bitcast.38, bf16[2,2,128,128]{3,2,1,0:T(8,128)(2,1)S(1)} %pad.8.fresh_ref, bf16[48,512,128]{2,1,0:T(8,128)(2,1)} %bitcast.43, f32[3,32,2048]{2,1,0:T(8,128)S(1)} %get-tuple-element.102.refs_0_, ...), custom_call_target="tpu_custom_call" | custom-call | flops 1610612736 | bytes 3145728 | tf_op jit(solution)/shard_map/own_blocks/pallas_call | solution.py:482
  29.1 0.0 collective-permute-done.4.refs_7_
  29.2 0.0 collective-permute-done.5.refs_8_
  29.2 0.0 collective-permute-done.7.refs_12_
  29.2 0.0 collective-permute-done.6.refs_9_
  29.2 0.0 copy-done.1
  29.2 0.0 copy-done.2
  29.2 2.9 %arrived_blocks.3 = (bf16[32,2,16,128]{3,2,1,0:T(8,128)(2,1)}, s32[1,4]{1,0:T(1,128)}, s32[1]{0:T(128)}) custom-call(bf16[2,512,128]{2,1,0:T(8,128)(2,1)S(1)} %bitcast.39, s32[32,16]{1,0:T(8,128)S(1)} %copy.17.refs_0_.tables_ref, s32[32,1]{1,0:T(8,128)S(1)} %copy.18.refs_1_.length_ref, f32[512,128]{1,0:T(8,128)S(1)} %get-tuple-element.99.refs_0_, ...), custom_call_target="tpu_custom_call" | custom-call | flops 536870912 | bytes 1081344 | tf_op jit(solution)/shard_map/arrived_blocks/pallas_call | solution.py:529
  32.1 0.8 %while.9 = (s32[]{:T(128)}, bf16[32,2,2048]{2,1,0:T(2,128)(2,1)}, bf16[32,2,16,128]{3,2,1,0:T(8,128)(2,1)S(1)}, s32[32]{0:T(128)S(1)}, bf16[32,2,2,2,128]{4,1,0,...) while((s32[]{:T(128)}, bf16[32,2,2048]{2,1,0:T(2,128)(2,1)}, ...), condition=%region_1.2_spmd, body=%region_0.1_spmd | while | flops 3758096640 | bytes 39749268 | solution.py:559
  (2 shorter events, 0.0 us)
Async XLA Ops:
  0.6 6.6 %copy-start.6 = (bf16[48,2,2]{0,2,1:T(2,128)(2,1)S(1)}, bf16[48,2,2]{0,2,1:T(2,128)(2,1)}, u32[]{:S(2)}) copy-start(bf16[48,2,2]{0,2,1:T(2,128)(2,1)} %param.13) | copy-start | bytes 1156
  0.6 6.6 %copy-start.8 = (s32[1,4]{1,0:T(1,128)S(1)}, s32[1,4]{1,0:T(1,128)}, u32[]{:S(2)}) copy-start(s32[1,4]{1,0:T(1,128)} %block_ref.3) | copy-start | bytes 52
  0.7 6.6 %copy-start.7 = (s32[1,4]{1,0:T(1,128)S(1)}, s32[1,4]{1,0:T(1,128)}, u32[]{:S(2)}) copy-start(s32[1,4]{1,0:T(1,128)} %dest_ref.2) | copy-start | bytes 52
  0.7 12.6 %copy-start.4 = (bf16[32,2,16,128]{3,2,1,0:T(8,128)(2,1)S(1)}, bf16[32,2,16,128]{3,2,1,0:T(8,128)(2,1)}, u32[]{:S(2)}) copy-start(bf16[32,2,16,128]{3,2,1,0:T(8,128)(2,1)} %param.10) | copy-start | bytes 786436
  0.7 12.8 %copy-start.10 = (s32[32,16]{0,1:T(8,128)S(1)}, s32[32,16]{0,1:T(8,128)}, u32[]{:S(2)}) copy-start(s32[32,16]{0,1:T(8,128)} %param.14) | copy-start | bytes 6148
  0.7 12.9 %copy-start.5 = (bf16[32,2,2,2,128]{4,3,2,1,0:T(2,128)(2,1)S(1)}, bf16[32,2,2,2,128]{4,3,2,1,0:T(2,128)(2,1)}, u32[]{:S(2)}) copy-start(bf16[32,2,2,2,128]{4,3,2,1,0:T(2,128)(2,1)} %param.11) | copy-start | bytes 196612
  0.7 13.0 %copy-start.9 = (s32[32]{0:T(128)S(1)}, s32[32]{0:T(128)}, u32[]{:S(2)}) copy-start(s32[32]{0:T(128)} %param.15) | copy-start | bytes 388
  3.1 17.0 %collective-permute-start.3 = (bf16[1,528,128]{2,1,0:T(8,128)(2,1)}, bf16[1,528,128]{2,1,0:T(8,128)(2,1)S(1)}, u32[]{:S(2)}, u32[]{:S(2)}) collective-permute-start(bf16[1,528,128]{2,1,0:T(8,128)(2,1)} %pack_blocks.4.refs_11_), channel_id=1, source_target_pairs={{0,8},{4,12},{8,0},{12,4},{1,9},{5,13},{9,1},{13,5},{2,10},{6,14},... | collective-permute-start | bytes 405512 | tf_op jit(solution)/shard_map/ppermute | solution.py:437
  9.7 19.5 %collective-permute-start.6 = (bf16[2,528,128]{2,1,0:T(8,128)(2,1)}, bf16[2,528,128]{2,1,0:T(8,128)(2,1)S(1)}, u32[]{:S(2)}, u32[]{:S(2)}) collective-permute-start(bf16[2,528,128]{2,1,0:T(8,128)(2,1)} %get-tuple-element.91), channel_id=1, source_target_pairs={{0,4},{4,0},{8,12},{12,8},{1,5},{5,1},{9,13},{13,9},{2,6},{6,2},{1... | collective-permute-start | bytes 811016 | tf_op jit(solution)/shard_map/ppermute | solution.py:437
  11.3 17.8 %collective-permute-start.4 = (bf16[1,528,128]{2,1,0:T(8,128)(2,1)}, bf16[1,528,128]{2,1,0:T(8,128)(2,1)S(1)}, u32[]{:S(2)}, u32[]{:S(2)}) collective-permute-start(bf16[1,528,128]{2,1,0:T(8,128)(2,1)} %get-tuple-element.93), channel_id=1, source_target_pairs={{0,12},{4,8},{8,4},{12,0},{1,13},{5,9},{9,5},{13,1},{2,14},{6,10},... | collective-permute-start | bytes 405512 | tf_op jit(solution)/shard_map/ppermute | solution.py:437
  11.3 17.8 %collective-permute-start.5 = (bf16[1,528,128]{2,1,0:T(8,128)(2,1)}, bf16[1,528,128]{2,1,0:T(8,128)(2,1)S(1)}, u32[]{:S(2)}, u32[]{:S(2)}) collective-permute-start(bf16[1,528,128]{2,1,0:T(8,128)(2,1)} %get-tuple-element.92), channel_id=1, source_target_pairs={{0,8},{4,12},{8,0},{12,4},{1,9},{5,13},{9,1},{13,5},{2,10},{6,14},... | collective-permute-start | bytes 405512 | tf_op jit(solution)/shard_map/ppermute | solution.py:437
  13.8 15.4 %copy-start.1 = (bf16[1,528,128]{2,1,0:T(8,128)(2,1)S(1)}, bf16[1,528,128]{2,1,0:T(8,128)(2,1)}, u32[]{:S(2)}) copy-start(bf16[1,528,128]{2,1,0:T(8,128)(2,1)} %pack_blocks.4.refs_11_) | copy-start | bytes 405508
  13.8 15.4 %copy-start.2 = (bf16[1,528,128]{2,1,0:T(8,128)(2,1)S(1)}, bf16[1,528,128]{2,1,0:T(8,128)(2,1)}, u32[]{:S(2)}) copy-start(bf16[1,528,128]{2,1,0:T(8,128)(2,1)} %get-tuple-element.90.refs_10_) | copy-start | bytes 405508
  20.2 9.0 %collective-permute-start.7 = (bf16[1,528,128]{2,1,0:T(8,128)(2,1)S(1)}, bf16[1,528,128]{2,1,0:T(8,128)(2,1)S(1)}, u32[]{:S(2)}, u32[]{:S(2)}) collective-permute-start(bf16[1,528,128]{2,1,0:T(8,128)(2,1)S(1)} %collective-permute-done.3.refs_6_), channel_id=1, source_target_pairs={{0,4},{4,0},{8,12},{12,8},{1,5},{5,1},{9,13},{13,9},{2,6},{6,2},{1... | collective-permute-start | bytes 405512 | tf_op jit(solution)/shard_map/ppermute | solution.py:437

commit v19 on v16

--- a/solution.py
+++ b/solution.py
@@ -189,7 +189,7 @@
     height, head_dim = q_ref.shape[1:]
     width = group * block_len
 
-    def load(part, chunk):
+    def arrival(part, chunk):
         return pltpu.make_async_copy(
             pool_ref.at[
                 pl.ds(chunk * group, group), pl.ds((part * heads + head) * block_len, block_len)
@@ -198,9 +198,16 @@
             sems.at[part, chunk],
         )
 
-    for part in range(2):
-        for chunk in range(chunks):
-            load(part, chunk).start()
+    def start_copies(part):
+        for b in range(pool):
+            pltpu.make_async_copy(
+                pool_ref.at[b, pl.ds((part * heads + head) * block_len, block_len)],
+                codes_ref.at[part, b // group, b % group],
+                sems.at[part, b // group],
+            ).start()
+
+    start_copies(0)
+    start_copies(1)
 
     if head == 0:
         ids = lax.broadcasted_iota(jnp.int32, (1, pool), 1)
@@ -228,7 +235,7 @@
     top_ref[...] = lane_fold(new_score, jnp.maximum)
 
     def score(chunk, carry):
-        load(0, chunk).wait()
+        arrival(0, chunk).wait()
 
         def store(row, lane, value):
             t_ref[chunk, row : row + rows, lane : lane + value.shape[1]] = value
@@ -257,7 +264,7 @@
     )
 
     def apply(chunk, carry):
-        load(1, chunk).wait()
+        arrival(1, chunk).wait()
         scale = row_ref[chunk, heads + head : heads + head + 1, :]
         for row in range(0, height, rows):
             at = pl.ds(row, rows)

time: 33 us -> 33.5 us (1.015)
  Pallas kernels: 20.3 us -> 20.7 us
    pallas_call x2, Pallas kernels: 12.6 us -> 13 us  [own(): pl.pallas_call(functools.partial(own_kernel, (head, pool, heads, rows, st...]
where the time goes in v19:
time: 33.5 us; the launch traced here: 33.2 us
  Pallas kernels  20.7 us (62%)
  starting transfers between devices  10.2 us (30%)
  between operations  1 us (3%)
  loops' own time  0.79 us (2%)
  local copies, waits for them, and re-layouts  0.53 us (2%)
    pallas_call x2, Pallas kernels, own(): pl.pallas_call(functools.partial(own_kernel, (head, pool, heads, rows, st...  13 us
    ppermute x5, starting transfers between devices, swap(): lax.ppermute(value, 'inst', [(j, j ^ distance) for j in range(instances)])  10.2 us
    pallas_call x2, Pallas kernels, pack(): pl.pallas_call(functools.partial(pack_kernel, (instances, listed, heads,...  4.87 us
    pallas_call x1, Pallas kernels, attend(): pl.pallas_call(functools.partial(arrival_kernel, (pool, heads, rows, bloc...  2.86 us
    another operation x1, loops' own time, shards(): lax.while_loop(lambda state: state[0] > 1, lambda state: (jnp.int32(0), a...  0.79 us
  transfers between devices with their start and end apart: 5, of which 0 were waited for; matrix products, arithmetic and copies ran while one was open for 1% of the time, Pallas kernels for 46%

profile of v19, /device:TPU:0, one launch (start us, length us, event | category | flops | bytes accessed | tf_op | source)
XLA Modules:
  0.0 33.2 jit_solution(4776617837511993843)
XLA Ops:
  0.6 0.0 copy-start.6
  0.6 0.0 copy-start.8
  0.7 0.0 copy-start.7
  0.7 0.0 copy-start.4
  0.7 0.0 copy-start.10
  0.7 0.0 copy-start.5
  0.7 0.0 copy-start.9
  0.7 2.4 %pack_blocks.4.refs_11_ = bf16[1,528,128]{2,1,0:T(8,128)(2,1)} custom-call(s32[1,4]{1,0:T(1,128)} %dest_ref.2, s32[1,4]{1,0:T(1,128)} %block_ref.3, bf16[2,2,48]{2,1,0:T(2,128)(2,1)} %bitcast.52, bf16[48,512,128]{2,1,0:T(8,128)(2,1)} %bitcast.40), custom_call_target="tpu_custom_call" | custom-call | bytes 270336 | tf_op jit(solution)/shard_map/pack_blocks/pallas_call | solution.py:423
  3.1 4.1 %collective-permute-start.3 = (bf16[1,528,128]{2,1,0:T(8,128)(2,1)}, bf16[1,528,128]{2,1,0:T(8,128)(2,1)S(1)}, u32[]{:S(2)}, u32[]{:S(2)}) collective-permute-start(bf16[1,528,128]{2,1,0:T(8,128)(2,1)} %pack_blocks.4.refs_11_), channel_id=1, source_target_pairs={{0,8},{4,12},{8,0},{12,4},{1,9},{5,13},{9,1},{13,5},{2,10},{6,14},... | collective-permute-start | bytes 405512 | tf_op jit(solution)/shard_map/ppermute | solution.py:443
  7.2 0.0 copy-done.6
  7.2 0.0 copy-done.8
  7.2 0.0 copy-done.7
  7.2 2.5 %pack_blocks.5 = (bf16[1,528,128]{2,1,0:T(8,128)(2,1)}, bf16[2,528,128]{2,1,0:T(8,128)(2,1)}, bf16[1,528,128]{2,1,0:T(8,128)(2,1)}, bf16[1,528,128]{2,1,0:T(8,128)(2,1)}) custom-call(s32[1,4]{1,0:T(1,128)S(1)} %copy-done.7, s32[1,4]{1,0:T(1,128)S(1)} %copy-done.8, bf16[2,2,48]{2,1,0:T(2,128)(2,1)S(1)} %bitcast.53, bf16[48,512,128]{2,1,0:T(8,128)(2,1)} %bitcast.41), custom_call_target="tpu_custom_call" | custom-call | bytes 1351680 | tf_op jit(solution)/shard_map/pack_blocks/pallas_call | solution.py:423
  9.7 1.6 %collective-permute-start.6 = (bf16[2,528,128]{2,1,0:T(8,128)(2,1)}, bf16[2,528,128]{2,1,0:T(8,128)(2,1)S(1)}, u32[]{:S(2)}, u32[]{:S(2)}) collective-permute-start(bf16[2,528,128]{2,1,0:T(8,128)(2,1)} %get-tuple-element.91), channel_id=1, source_target_pairs={{0,4},{4,0},{8,12},{12,8},{1,5},{5,1},{9,13},{13,9},{2,6},{6,2},{1... | collective-permute-start | bytes 811016 | tf_op jit(solution)/shard_map/ppermute | solution.py:443
  11.3 0.0 collective-permute-start.4
  11.3 1.9 %collective-permute-start.5 = (bf16[1,528,128]{2,1,0:T(8,128)(2,1)}, bf16[1,528,128]{2,1,0:T(8,128)(2,1)S(1)}, u32[]{:S(2)}, u32[]{:S(2)}) collective-permute-start(bf16[1,528,128]{2,1,0:T(8,128)(2,1)} %get-tuple-element.92), channel_id=1, source_target_pairs={{0,8},{4,12},{8,0},{12,4},{1,9},{5,13},{9,1},{13,5},{2,10},{6,14},... | collective-permute-start | bytes 405512 | tf_op jit(solution)/shard_map/ppermute | solution.py:443
  13.3 0.0 copy-done.4
  13.3 0.2 copy.13
  13.5 0.0 copy-done.10
  13.5 0.1 copy.17.refs_0_.tables_ref
  13.6 0.0 copy-done.5
  13.6 0.1 copy.19
  13.6 0.1 copy.14
  13.7 0.0 copy-done.9
  13.7 0.1 copy.18.refs_1_.length_ref
  13.8 0.0 copy-start.1
  13.8 0.0 copy-start.2
  13.8 6.7 %own_blocks.6 = (f32[512,128]{1,0:T(8,128)S(1)}, f32[512,128]{1,0:T(8,128)S(1)}, f32[512,128]{1,0:T(8,128)S(1)}, f32[3,32,2048]{2,1,0:T(8,128)S(1)}, f32[3,4,2048]{2,1,0:T(4,128)S(1)}) custom-call(bf16[2,512,128]{2,1,0:T(8,128)(2,1)S(1)} %bitcast.37, bf16[2,2,128,128]{3,2,1,0:T(8,128)(2,1)S(1)} %pad.8.fresh_ref, bf16[48,512,128]{2,1,0:T(8,128)(2,1)} %bitcast.42, ...), custom_call_target="tpu_custom_call" | custom-call | flops 1610612736 | bytes 3145728 | tf_op jit(solution)/shard_map/own_blocks/pallas_call | solution.py:488
  20.5 0.0 collective-permute-done.3.refs_6_
  20.5 2.5 %collective-permute-start.7 = (bf16[1,528,128]{2,1,0:T(8,128)(2,1)S(1)}, bf16[1,528,128]{2,1,0:T(8,128)(2,1)S(1)}, u32[]{:S(2)}, u32[]{:S(2)}) collective-permute-start(bf16[1,528,128]{2,1,0:T(8,128)(2,1)S(1)} %collective-permute-done.3.refs_6_), channel_id=1, source_target_pairs={{0,4},{4,0},{8,12},{12,8},{1,5},{5,1},{9,13},{13,9},{2,6},{6,2},{1... | collective-permute-start | bytes 405512 | tf_op jit(solution)/shard_map/ppermute | solution.py:443
  23.0 6.3 %own_blocks.7 = (f32[512,128]{1,0:T(8,128)S(1)}, f32[512,128]{1,0:T(8,128)S(1)}, f32[512,128]{1,0:T(8,128)S(1)}) custom-call(bf16[2,512,128]{2,1,0:T(8,128)(2,1)S(1)} %bitcast.38, bf16[2,2,128,128]{3,2,1,0:T(8,128)(2,1)S(1)} %pad.8.fresh_ref, bf16[48,512,128]{2,1,0:T(8,128)(2,1)} %bitcast.43, f32[3,32,2048]{2,1,0:T(8,128)S(1)} %get-tuple-element.102.refs_0_, ...), custom_call_target="tpu_custom_call" | custom-call | flops 1610612736 | bytes 3145728 | tf_op jit(solution)/shard_map/own_blocks/pallas_call | solution.py:488
  29.3 0.0 collective-permute-done.4.refs_7_
  29.3 0.0 collective-permute-done.5.refs_8_
  29.4 0.0 collective-permute-done.7.refs_12_
  29.4 0.0 collective-permute-done.6.refs_9_
  29.4 0.0 copy-done.1
  29.4 0.0 copy-done.2
  29.4 2.9 %arrived_blocks.3 = (bf16[32,2,16,128]{3,2,1,0:T(8,128)(2,1)}, s32[1,4]{1,0:T(1,128)}, s32[1]{0:T(128)}) custom-call(bf16[2,512,128]{2,1,0:T(8,128)(2,1)S(1)} %bitcast.39, s32[32,16]{1,0:T(8,128)S(1)} %copy.17.refs_0_.tables_ref, s32[32,1]{1,0:T(8,128)S(1)} %copy.18.refs_1_.length_ref, f32[512,128]{1,0:T(8,128)S(1)} %get-tuple-element.99.refs_0_, ...), custom_call_target="tpu_custom_call" | custom-call | flops 536870912 | bytes 1081344 | tf_op jit(solution)/shard_map/arrived_blocks/pallas_call | solution.py:535
  32.3 0.8 %while.9 = (s32[]{:T(128)}, bf16[32,2,2048]{2,1,0:T(2,128)(2,1)}, bf16[32,2,16,128]{3,2,1,0:T(8,128)(2,1)S(1)}, s32[32]{0:T(128)S(1)}, bf16[32,2,2,2,128]{4,1,0,...) while((s32[]{:T(128)}, bf16[32,2,2048]{2,1,0:T(2,128)(2,1)}, ...), condition=%region_1.2_spmd, body=%region_0.1_spmd | while | flops 3758096640 | bytes 39749268 | solution.py:565
  (2 shorter events, 0.0 us)
Async XLA Ops:
  0.6 6.6 %copy-start.6 = (bf16[48,2,2]{0,2,1:T(2,128)(2,1)S(1)}, bf16[48,2,2]{0,2,1:T(2,128)(2,1)}, u32[]{:S(2)}) copy-start(bf16[48,2,2]{0,2,1:T(2,128)(2,1)} %param.13) | copy-start | bytes 1156
  0.6 6.6 %copy-start.8 = (s32[1,4]{1,0:T(1,128)S(1)}, s32[1,4]{1,0:T(1,128)}, u32[]{:S(2)}) copy-start(s32[1,4]{1,0:T(1,128)} %block_ref.3) | copy-start | bytes 52
  0.7 6.6 %copy-start.7 = (s32[1,4]{1,0:T(1,128)S(1)}, s32[1,4]{1,0:T(1,128)}, u32[]{:S(2)}) copy-start(s32[1,4]{1,0:T(1,128)} %dest_ref.2) | copy-start | bytes 52
  0.7 12.6 %copy-start.4 = (bf16[32,2,16,128]{3,2,1,0:T(8,128)(2,1)S(1)}, bf16[32,2,16,128]{3,2,1,0:T(8,128)(2,1)}, u32[]{:S(2)}) copy-start(bf16[32,2,16,128]{3,2,1,0:T(8,128)(2,1)} %param.10) | copy-start | bytes 786436
  0.7 12.8 %copy-start.10 = (s32[32,16]{0,1:T(8,128)S(1)}, s32[32,16]{0,1:T(8,128)}, u32[]{:S(2)}) copy-start(s32[32,16]{0,1:T(8,128)} %param.14) | copy-start | bytes 6148
  0.7 12.9 %copy-start.5 = (bf16[32,2,2,2,128]{4,3,2,1,0:T(2,128)(2,1)S(1)}, bf16[32,2,2,2,128]{4,3,2,1,0:T(2,128)(2,1)}, u32[]{:S(2)}) copy-start(bf16[32,2,2,2,128]{4,3,2,1,0:T(2,128)(2,1)} %param.11) | copy-start | bytes 196612
  0.7 13.0 %copy-start.9 = (s32[32]{0:T(128)S(1)}, s32[32]{0:T(128)}, u32[]{:S(2)}) copy-start(s32[32]{0:T(128)} %param.15) | copy-start | bytes 388
  3.1 17.4 %collective-permute-start.3 = (bf16[1,528,128]{2,1,0:T(8,128)(2,1)}, bf16[1,528,128]{2,1,0:T(8,128)(2,1)S(1)}, u32[]{:S(2)}, u32[]{:S(2)}) collective-permute-start(bf16[1,528,128]{2,1,0:T(8,128)(2,1)} %pack_blocks.4.refs_11_), channel_id=1, source_target_pairs={{0,8},{4,12},{8,0},{12,4},{1,9},{5,13},{9,1},{13,5},{2,10},{6,14},... | collective-permute-start | bytes 405512 | tf_op jit(solution)/shard_map/ppermute | solution.py:443
  9.7 19.7 %collective-permute-start.6 = (bf16[2,528,128]{2,1,0:T(8,128)(2,1)}, bf16[2,528,128]{2,1,0:T(8,128)(2,1)S(1)}, u32[]{:S(2)}, u32[]{:S(2)}) collective-permute-start(bf16[2,528,128]{2,1,0:T(8,128)(2,1)} %get-tuple-element.91), channel_id=1, source_target_pairs={{0,4},{4,0},{8,12},{12,8},{1,5},{5,1},{9,13},{13,9},{2,6},{6,2},{1... | collective-permute-start | bytes 811016 | tf_op jit(solution)/shard_map/ppermute | solution.py:443
  11.3 18.0 %collective-permute-start.4 = (bf16[1,528,128]{2,1,0:T(8,128)(2,1)}, bf16[1,528,128]{2,1,0:T(8,128)(2,1)S(1)}, u32[]{:S(2)}, u32[]{:S(2)}) collective-permute-start(bf16[1,528,128]{2,1,0:T(8,128)(2,1)} %get-tuple-element.93), channel_id=1, source_target_pairs={{0,12},{4,8},{8,4},{12,0},{1,13},{5,9},{9,5},{13,1},{2,14},{6,10},... | collective-permute-start | bytes 405512 | tf_op jit(solution)/shard_map/ppermute | solution.py:443
  11.3 18.0 %collective-permute-start.5 = (bf16[1,528,128]{2,1,0:T(8,128)(2,1)}, bf16[1,528,128]{2,1,0:T(8,128)(2,1)S(1)}, u32[]{:S(2)}, u32[]{:S(2)}) collective-permute-start(bf16[1,528,128]{2,1,0:T(8,128)(2,1)} %get-tuple-element.92), channel_id=1, source_target_pairs={{0,8},{4,12},{8,0},{12,4},{1,9},{5,13},{9,1},{13,5},{2,10},{6,14},... | collective-permute-start | bytes 405512 | tf_op jit(solution)/shard_map/ppermute | solution.py:443
  13.8 15.6 %copy-start.1 = (bf16[1,528,128]{2,1,0:T(8,128)(2,1)S(1)}, bf16[1,528,128]{2,1,0:T(8,128)(2,1)}, u32[]{:S(2)}) copy-start(bf16[1,528,128]{2,1,0:T(8,128)(2,1)} %pack_blocks.4.refs_11_) | copy-start | bytes 405508
  13.8 15.6 %copy-start.2 = (bf16[1,528,128]{2,1,0:T(8,128)(2,1)S(1)}, bf16[1,528,128]{2,1,0:T(8,128)(2,1)}, u32[]{:S(2)}) copy-start(bf16[1,528,128]{2,1,0:T(8,128)(2,1)} %get-tuple-element.90.refs_10_) | copy-start | bytes 405508
  20.5 8.9 %collective-permute-start.7 = (bf16[1,528,128]{2,1,0:T(8,128)(2,1)S(1)}, bf16[1,528,128]{2,1,0:T(8,128)(2,1)S(1)}, u32[]{:S(2)}, u32[]{:S(2)}) collective-permute-start(bf16[1,528,128]{2,1,0:T(8,128)(2,1)S(1)} %collective-permute-done.3.refs_6_), channel_id=1, source_target_pairs={{0,4},{4,0},{8,12},{12,8},{1,5},{5,1},{9,13},{13,9},{2,6},{6,2},{1... | collective-permute-start | bytes 405512 | tf_op jit(solution)/shard_map/ppermute | solution.py:443

commit v20 on v16

--- a/solution.py
+++ b/solution.py
@@ -142,7 +142,7 @@
 
 
 def score_tiles(query, keys, log_ref, scale_row, rows, store):
-    height, wide = min(256, query.shape[0]), min(256, keys.shape[0])
+    height, wide = min(512, query.shape[0]), min(256, keys.shape[0])
     for top in range(0, query.shape[0], height):
         for left in range(0, keys.shape[0], wide):
             part = lax.dot_general(

time: 33 us -> 32.9 us (level)
  no operation moved by 1% of the time
where the time goes in v20:
time: 32.9 us; the launch traced here: 32.7 us
  Pallas kernels  20.2 us (61%)
  starting transfers between devices  10.2 us (31%)
  between operations  1 us (3%)
  loops' own time  0.79 us (2%)
  local copies, waits for them, and re-layouts  0.53 us (2%)
    pallas_call x2, Pallas kernels, own(): pl.pallas_call(functools.partial(own_kernel, (head, pool, heads, rows, st...  12.5 us
    ppermute x5, starting transfers between devices, swap(): lax.ppermute(value, 'inst', [(j, j ^ distance) for j in range(instances)])  10.2 us
    pallas_call x2, Pallas kernels, pack(): pl.pallas_call(functools.partial(pack_kernel, (instances, listed, heads,...  4.87 us
    pallas_call x1, Pallas kernels, attend(): pl.pallas_call(functools.partial(arrival_kernel, (pool, heads, rows, bloc...  2.79 us
    another operation x1, loops' own time, shards(): lax.while_loop(lambda state: state[0] > 1, lambda state: (jnp.int32(0), a...  0.79 us
  transfers between devices with their start and end apart: 5, of which 0 were waited for; matrix products, arithmetic and copies ran while one was open for 1% of the time, Pallas kernels for 46%

profile of v20, /device:TPU:0, one launch (start us, length us, event | category | flops | bytes accessed | tf_op | source)
XLA Modules:
  0.0 32.7 jit_solution(100938341307104465)
XLA Ops:
  0.6 0.0 copy-start.6
  0.6 0.0 copy-start.8
  0.7 0.0 copy-start.7
  0.7 0.0 copy-start.4
  0.7 0.0 copy-start.10
  0.7 0.0 copy-start.5
  0.7 0.0 copy-start.9
  0.7 2.4 %pack_blocks.4.refs_11_ = bf16[1,528,128]{2,1,0:T(8,128)(2,1)} custom-call(s32[1,4]{1,0:T(1,128)} %dest_ref.2, s32[1,4]{1,0:T(1,128)} %block_ref.3, bf16[2,2,48]{2,1,0:T(2,128)(2,1)} %bitcast.52, bf16[48,512,128]{2,1,0:T(8,128)(2,1)} %bitcast.40), custom_call_target="tpu_custom_call" | custom-call | bytes 270336 | tf_op jit(solution)/shard_map/pack_blocks/pallas_call | solution.py:416
  3.1 4.1 %collective-permute-start.3 = (bf16[1,528,128]{2,1,0:T(8,128)(2,1)}, bf16[1,528,128]{2,1,0:T(8,128)(2,1)S(1)}, u32[]{:S(2)}, u32[]{:S(2)}) collective-permute-start(bf16[1,528,128]{2,1,0:T(8,128)(2,1)} %pack_blocks.4.refs_11_), channel_id=1, source_target_pairs={{0,8},{4,12},{8,0},{12,4},{1,9},{5,13},{9,1},{13,5},{2,10},{6,14},... | collective-permute-start | bytes 405512 | tf_op jit(solution)/shard_map/ppermute | solution.py:436
  7.2 0.0 copy-done.6
  7.2 0.0 copy-done.8
  7.2 0.0 copy-done.7
  7.2 2.5 %pack_blocks.5 = (bf16[1,528,128]{2,1,0:T(8,128)(2,1)}, bf16[2,528,128]{2,1,0:T(8,128)(2,1)}, bf16[1,528,128]{2,1,0:T(8,128)(2,1)}, bf16[1,528,128]{2,1,0:T(8,128)(2,1)}) custom-call(s32[1,4]{1,0:T(1,128)S(1)} %copy-done.7, s32[1,4]{1,0:T(1,128)S(1)} %copy-done.8, bf16[2,2,48]{2,1,0:T(2,128)(2,1)S(1)} %bitcast.53, bf16[48,512,128]{2,1,0:T(8,128)(2,1)} %bitcast.41), custom_call_target="tpu_custom_call" | custom-call | bytes 1351680 | tf_op jit(solution)/shard_map/pack_blocks/pallas_call | solution.py:416
  9.7 1.6 %collective-permute-start.6 = (bf16[2,528,128]{2,1,0:T(8,128)(2,1)}, bf16[2,528,128]{2,1,0:T(8,128)(2,1)S(1)}, u32[]{:S(2)}, u32[]{:S(2)}) collective-permute-start(bf16[2,528,128]{2,1,0:T(8,128)(2,1)} %get-tuple-element.91), channel_id=1, source_target_pairs={{0,4},{4,0},{8,12},{12,8},{1,5},{5,1},{9,13},{13,9},{2,6},{6,2},{1... | collective-permute-start | bytes 811016 | tf_op jit(solution)/shard_map/ppermute | solution.py:436
  11.3 0.0 collective-permute-start.4
  11.3 1.9 %collective-permute-start.5 = (bf16[1,528,128]{2,1,0:T(8,128)(2,1)}, bf16[1,528,128]{2,1,0:T(8,128)(2,1)S(1)}, u32[]{:S(2)}, u32[]{:S(2)}) collective-permute-start(bf16[1,528,128]{2,1,0:T(8,128)(2,1)} %get-tuple-element.92), channel_id=1, source_target_pairs={{0,8},{4,12},{8,0},{12,4},{1,9},{5,13},{9,1},{13,5},{2,10},{6,14},... | collective-permute-start | bytes 405512 | tf_op jit(solution)/shard_map/ppermute | solution.py:436
  13.3 0.0 copy-done.4
  13.3 0.2 copy.13
  13.5 0.0 copy-done.10
  13.5 0.1 copy.17.refs_0_.tables_ref
  13.6 0.0 copy-done.5
  13.6 0.1 copy.19
  13.6 0.1 copy.14
  13.7 0.0 copy-done.9
  13.7 0.1 copy.18.refs_1_.length_ref
  13.8 0.0 copy-start.1
  13.8 0.0 copy-start.2
  13.8 6.2 %own_blocks.6 = (f32[512,128]{1,0:T(8,128)S(1)}, f32[512,128]{1,0:T(8,128)S(1)}, f32[512,128]{1,0:T(8,128)S(1)}, f32[3,32,2048]{2,1,0:T(8,128)S(1)}, f32[3,4,2048]{2,1,0:T(4,128)S(1)}) custom-call(bf16[2,512,128]{2,1,0:T(8,128)(2,1)S(1)} %bitcast.37, bf16[2,2,128,128]{3,2,1,0:T(8,128)(2,1)S(1)} %pad.8.fresh_ref, bf16[48,512,128]{2,1,0:T(8,128)(2,1)} %bitcast.42, ...), custom_call_target="tpu_custom_call" | custom-call | flops 1610612736 | bytes 3145728 | tf_op jit(solution)/shard_map/own_blocks/pallas_call | solution.py:481
  20.0 0.0 collective-permute-done.3.refs_6_
  20.0 2.5 %collective-permute-start.7 = (bf16[1,528,128]{2,1,0:T(8,128)(2,1)S(1)}, bf16[1,528,128]{2,1,0:T(8,128)(2,1)S(1)}, u32[]{:S(2)}, u32[]{:S(2)}) collective-permute-start(bf16[1,528,128]{2,1,0:T(8,128)(2,1)S(1)} %collective-permute-done.3.refs_6_), channel_id=1, source_target_pairs={{0,4},{4,0},{8,12},{12,8},{1,5},{5,1},{9,13},{13,9},{2,6},{6,2},{1... | collective-permute-start | bytes 405512 | tf_op jit(solution)/shard_map/ppermute | solution.py:436
  22.5 6.3 %own_blocks.7 = (f32[512,128]{1,0:T(8,128)S(1)}, f32[512,128]{1,0:T(8,128)S(1)}, f32[512,128]{1,0:T(8,128)S(1)}) custom-call(bf16[2,512,128]{2,1,0:T(8,128)(2,1)S(1)} %bitcast.38, bf16[2,2,128,128]{3,2,1,0:T(8,128)(2,1)S(1)} %pad.8.fresh_ref, bf16[48,512,128]{2,1,0:T(8,128)(2,1)} %bitcast.43, f32[3,32,2048]{2,1,0:T(8,128)S(1)} %get-tuple-element.102.refs_0_, ...), custom_call_target="tpu_custom_call" | custom-call | flops 1610612736 | bytes 3145728 | tf_op jit(solution)/shard_map/own_blocks/pallas_call | solution.py:481
  28.9 0.0 collective-permute-done.4.refs_7_
  28.9 0.0 collective-permute-done.5.refs_8_
  28.9 0.0 collective-permute-done.7.refs_12_
  28.9 0.0 collective-permute-done.6.refs_9_
  28.9 0.0 copy-done.1
  28.9 0.0 copy-done.2
  28.9 2.8 %arrived_blocks.3 = (bf16[32,2,16,128]{3,2,1,0:T(8,128)(2,1)}, s32[1,4]{1,0:T(1,128)}, s32[1]{0:T(128)}) custom-call(bf16[2,512,128]{2,1,0:T(8,128)(2,1)S(1)} %bitcast.39, s32[32,16]{1,0:T(8,128)S(1)} %copy.17.refs_0_.tables_ref, s32[32,1]{1,0:T(8,128)S(1)} %copy.18.refs_1_.length_ref, f32[512,128]{1,0:T(8,128)S(1)} %get-tuple-element.99.refs_0_, ...), custom_call_target="tpu_custom_call" | custom-call | flops 536870912 | bytes 1081344 | tf_op jit(solution)/shard_map/arrived_blocks/pallas_call | solution.py:528
  31.7 0.8 %while.9 = (s32[]{:T(128)}, bf16[32,2,2048]{2,1,0:T(2,128)(2,1)}, bf16[32,2,16,128]{3,2,1,0:T(8,128)(2,1)S(1)}, s32[32]{0:T(128)S(1)}, bf16[32,2,2,2,128]{4,1,0,...) while((s32[]{:T(128)}, bf16[32,2,2048]{2,1,0:T(2,128)(2,1)}, ...), condition=%region_1.2_spmd, body=%region_0.1_spmd | while | flops 3758096640 | bytes 39749268 | solution.py:558
  (2 shorter events, 0.0 us)
Async XLA Ops:
  0.6 6.6 %copy-start.6 = (bf16[48,2,2]{0,2,1:T(2,128)(2,1)S(1)}, bf16[48,2,2]{0,2,1:T(2,128)(2,1)}, u32[]{:S(2)}) copy-start(bf16[48,2,2]{0,2,1:T(2,128)(2,1)} %param.13) | copy-start | bytes 1156
  0.6 6.6 %copy-start.8 = (s32[1,4]{1,0:T(1,128)S(1)}, s32[1,4]{1,0:T(1,128)}, u32[]{:S(2)}) copy-start(s32[1,4]{1,0:T(1,128)} %block_ref.3) | copy-start | bytes 52
  0.7 6.6 %copy-start.7 = (s32[1,4]{1,0:T(1,128)S(1)}, s32[1,4]{1,0:T(1,128)}, u32[]{:S(2)}) copy-start(s32[1,4]{1,0:T(1,128)} %dest_ref.2) | copy-start | bytes 52
  0.7 12.6 %copy-start.4 = (bf16[32,2,16,128]{3,2,1,0:T(8,128)(2,1)S(1)}, bf16[32,2,16,128]{3,2,1,0:T(8,128)(2,1)}, u32[]{:S(2)}) copy-start(bf16[32,2,16,128]{3,2,1,0:T(8,128)(2,1)} %param.10) | copy-start | bytes 786436
  0.7 12.8 %copy-start.10 = (s32[32,16]{0,1:T(8,128)S(1)}, s32[32,16]{0,1:T(8,128)}, u32[]{:S(2)}) copy-start(s32[32,16]{0,1:T(8,128)} %param.14) | copy-start | bytes 6148
  0.7 12.9 %copy-start.5 = (bf16[32,2,2,2,128]{4,3,2,1,0:T(2,128)(2,1)S(1)}, bf16[32,2,2,2,128]{4,3,2,1,0:T(2,128)(2,1)}, u32[]{:S(2)}) copy-start(bf16[32,2,2,2,128]{4,3,2,1,0:T(2,128)(2,1)} %param.11) | copy-start | bytes 196612
  0.7 13.0 %copy-start.9 = (s32[32]{0:T(128)S(1)}, s32[32]{0:T(128)}, u32[]{:S(2)}) copy-start(s32[32]{0:T(128)} %param.15) | copy-start | bytes 388
  3.1 16.9 %collective-permute-start.3 = (bf16[1,528,128]{2,1,0:T(8,128)(2,1)}, bf16[1,528,128]{2,1,0:T(8,128)(2,1)S(1)}, u32[]{:S(2)}, u32[]{:S(2)}) collective-permute-start(bf16[1,528,128]{2,1,0:T(8,128)(2,1)} %pack_blocks.4.refs_11_), channel_id=1, source_target_pairs={{0,8},{4,12},{8,0},{12,4},{1,9},{5,13},{9,1},{13,5},{2,10},{6,14},... | collective-permute-start | bytes 405512 | tf_op jit(solution)/shard_map/ppermute | solution.py:436
  9.7 19.2 %collective-permute-start.6 = (bf16[2,528,128]{2,1,0:T(8,128)(2,1)}, bf16[2,528,128]{2,1,0:T(8,128)(2,1)S(1)}, u32[]{:S(2)}, u32[]{:S(2)}) collective-permute-start(bf16[2,528,128]{2,1,0:T(8,128)(2,1)} %get-tuple-element.91), channel_id=1, source_target_pairs={{0,4},{4,0},{8,12},{12,8},{1,5},{5,1},{9,13},{13,9},{2,6},{6,2},{1... | collective-permute-start | bytes 811016 | tf_op jit(solution)/shard_map/ppermute | solution.py:436
  11.3 17.5 %collective-permute-start.4 = (bf16[1,528,128]{2,1,0:T(8,128)(2,1)}, bf16[1,528,128]{2,1,0:T(8,128)(2,1)S(1)}, u32[]{:S(2)}, u32[]{:S(2)}) collective-permute-start(bf16[1,528,128]{2,1,0:T(8,128)(2,1)} %get-tuple-element.93), channel_id=1, source_target_pairs={{0,12},{4,8},{8,4},{12,0},{1,13},{5,9},{9,5},{13,1},{2,14},{6,10},... | collective-permute-start | bytes 405512 | tf_op jit(solution)/shard_map/ppermute | solution.py:436
  11.3 17.5 %collective-permute-start.5 = (bf16[1,528,128]{2,1,0:T(8,128)(2,1)}, bf16[1,528,128]{2,1,0:T(8,128)(2,1)S(1)}, u32[]{:S(2)}, u32[]{:S(2)}) collective-permute-start(bf16[1,528,128]{2,1,0:T(8,128)(2,1)} %get-tuple-element.92), channel_id=1, source_target_pairs={{0,8},{4,12},{8,0},{12,4},{1,9},{5,13},{9,1},{13,5},{2,10},{6,14},... | collective-permute-start | bytes 405512 | tf_op jit(solution)/shard_map/ppermute | solution.py:436
  13.8 15.1 %copy-start.1 = (bf16[1,528,128]{2,1,0:T(8,128)(2,1)S(1)}, bf16[1,528,128]{2,1,0:T(8,128)(2,1)}, u32[]{:S(2)}) copy-start(bf16[1,528,128]{2,1,0:T(8,128)(2,1)} %pack_blocks.4.refs_11_) | copy-start | bytes 405508
  13.8 15.1 %copy-start.2 = (bf16[1,528,128]{2,1,0:T(8,128)(2,1)S(1)}, bf16[1,528,128]{2,1,0:T(8,128)(2,1)}, u32[]{:S(2)}) copy-start(bf16[1,528,128]{2,1,0:T(8,128)(2,1)} %get-tuple-element.90.refs_10_) | copy-start | bytes 405508
  20.0 8.9 %collective-permute-start.7 = (bf16[1,528,128]{2,1,0:T(8,128)(2,1)S(1)}, bf16[1,528,128]{2,1,0:T(8,128)(2,1)S(1)}, u32[]{:S(2)}, u32[]{:S(2)}) collective-permute-start(bf16[1,528,128]{2,1,0:T(8,128)(2,1)S(1)} %collective-permute-done.3.refs_6_), channel_id=1, source_target_pairs={{0,4},{4,0},{8,12},{12,8},{1,5},{5,1},{9,13},{13,9},{2,6},{6,2},{1... | collective-permute-start | bytes 405512 | tf_op jit(solution)/shard_map/ppermute | solution.py:436

commit v21 on v20

--- a/solution.py
+++ b/solution.py
@@ -402,7 +402,7 @@
     rows = per_head * steps
     height = requests * rows
     slots = instances * CAP
-    group = 16
+    group = 24
     f32, bf16 = jnp.float32, jnp.bfloat16
     code_rows = 2 * heads * block_len
     pool_rows = pool_codes.reshape(pool, code_rows, head_dim)

time: 32.9 us -> 32.5 us (0.988)
  Pallas kernels: 20.2 us -> 19.7 us
    pallas_call x2, Pallas kernels: 12.5 us -> 12.1 us  [own(): pl.pallas_call(functools.partial(own_kernel, (head, pool, heads, rows, st...]
  transfers between devices with their start and end apart: 5 -> 5, of which waited for: 0 -> 0; matrix products, arithmetic and copies ran while one was open for 1% -> 2% of each run, Pallas kernels for 46% -> 45%
where the time goes in v21:
time: 32.5 us; the launch traced here: 32.3 us
  Pallas kernels  19.7 us (61%)
  starting transfers between devices  10.2 us (31%)
  between operations  1 us (3%)
  loops' own time  0.79 us (2%)
  local copies, waits for them, and re-layouts  0.53 us (2%)
    pallas_call x2, Pallas kernels, own(): pl.pallas_call(functools.partial(own_kernel, (head, pool, heads, rows, st...  12.1 us
    ppermute x5, starting transfers between devices, swap(): lax.ppermute(value, 'inst', [(j, j ^ distance) for j in range(instances)])  10.2 us
    pallas_call x2, Pallas kernels, pack(): pl.pallas_call(functools.partial(pack_kernel, (instances, listed, heads,...  4.87 us
    pallas_call x1, Pallas kernels, attend(): pl.pallas_call(functools.partial(arrival_kernel, (pool, heads, rows, bloc...  2.8 us
    another operation x1, loops' own time, shards(): lax.while_loop(lambda state: state[0] > 1, lambda state: (jnp.int32(0), a...  0.79 us
  transfers between devices with their start and end apart: 5, of which 0 were waited for; matrix products, arithmetic and copies ran while one was open for 2% of the time, Pallas kernels for 45%

profile of v21, /device:TPU:0, one launch (start us, length us, event | category | flops | bytes accessed | tf_op | source)
XLA Modules:
  0.0 32.3 jit_solution(2897586695267163452)
XLA Ops:
  0.6 0.0 copy-start.6
  0.6 0.0 copy-start.8
  0.7 0.0 copy-start.7
  0.7 0.0 copy-start.4
  0.7 0.0 copy-start.10
  0.7 0.0 copy-start.5
  0.7 0.0 copy-start.9
  0.7 2.4 %pack_blocks.4.refs_11_ = bf16[1,528,128]{2,1,0:T(8,128)(2,1)} custom-call(s32[1,4]{1,0:T(1,128)} %dest_ref.2, s32[1,4]{1,0:T(1,128)} %block_ref.3, bf16[2,2,48]{2,1,0:T(2,128)(2,1)} %bitcast.52, bf16[48,512,128]{2,1,0:T(8,128)(2,1)} %bitcast.40), custom_call_target="tpu_custom_call" | custom-call | bytes 270336 | tf_op jit(solution)/shard_map/pack_blocks/pallas_call | solution.py:416
  3.1 4.1 %collective-permute-start.3 = (bf16[1,528,128]{2,1,0:T(8,128)(2,1)}, bf16[1,528,128]{2,1,0:T(8,128)(2,1)S(1)}, u32[]{:S(2)}, u32[]{:S(2)}) collective-permute-start(bf16[1,528,128]{2,1,0:T(8,128)(2,1)} %pack_blocks.4.refs_11_), channel_id=1, source_target_pairs={{0,8},{4,12},{8,0},{12,4},{1,9},{5,13},{9,1},{13,5},{2,10},{6,14},... | collective-permute-start | bytes 405512 | tf_op jit(solution)/shard_map/ppermute | solution.py:436
  7.2 0.0 copy-done.6
  7.2 0.0 copy-done.8
  7.2 0.0 copy-done.7
  7.2 2.5 %pack_blocks.5 = (bf16[1,528,128]{2,1,0:T(8,128)(2,1)}, bf16[2,528,128]{2,1,0:T(8,128)(2,1)}, bf16[1,528,128]{2,1,0:T(8,128)(2,1)}, bf16[1,528,128]{2,1,0:T(8,128)(2,1)}) custom-call(s32[1,4]{1,0:T(1,128)S(1)} %copy-done.7, s32[1,4]{1,0:T(1,128)S(1)} %copy-done.8, bf16[2,2,48]{2,1,0:T(2,128)(2,1)S(1)} %bitcast.53, bf16[48,512,128]{2,1,0:T(8,128)(2,1)} %bitcast.41), custom_call_target="tpu_custom_call" | custom-call | bytes 1351680 | tf_op jit(solution)/shard_map/pack_blocks/pallas_call | solution.py:416
  9.7 1.6 %collective-permute-start.6 = (bf16[2,528,128]{2,1,0:T(8,128)(2,1)}, bf16[2,528,128]{2,1,0:T(8,128)(2,1)S(1)}, u32[]{:S(2)}, u32[]{:S(2)}) collective-permute-start(bf16[2,528,128]{2,1,0:T(8,128)(2,1)} %get-tuple-element.91), channel_id=1, source_target_pairs={{0,4},{4,0},{8,12},{12,8},{1,5},{5,1},{9,13},{13,9},{2,6},{6,2},{1... | collective-permute-start | bytes 811016 | tf_op jit(solution)/shard_map/ppermute | solution.py:436
  11.3 0.0 collective-permute-start.4
  11.3 1.9 %collective-permute-start.5 = (bf16[1,528,128]{2,1,0:T(8,128)(2,1)}, bf16[1,528,128]{2,1,0:T(8,128)(2,1)S(1)}, u32[]{:S(2)}, u32[]{:S(2)}) collective-permute-start(bf16[1,528,128]{2,1,0:T(8,128)(2,1)} %get-tuple-element.92), channel_id=1, source_target_pairs={{0,8},{4,12},{8,0},{12,4},{1,9},{5,13},{9,1},{13,5},{2,10},{6,14},... | collective-permute-start | bytes 405512 | tf_op jit(solution)/shard_map/ppermute | solution.py:436
  13.3 0.0 copy-done.4
  13.3 0.2 copy.13
  13.5 0.0 copy-done.10
  13.5 0.1 copy.17.refs_0_.tables_ref
  13.6 0.0 copy-done.5
  13.6 0.1 copy.19
  13.6 0.1 copy.14
  13.7 0.0 copy-done.9
  13.7 0.1 copy.18.refs_1_.length_ref
  13.8 0.0 copy-start.1
  13.8 0.0 copy-start.2
  13.8 6.1 %own_blocks.6 = (f32[512,128]{1,0:T(8,128)S(1)}, f32[512,128]{1,0:T(8,128)S(1)}, f32[512,128]{1,0:T(8,128)S(1)}, f32[2,32,3072]{2,1,0:T(8,128)S(1)}, f32[2,4,3072]{2,1,0:T(4,128)S(1)}) custom-call(bf16[2,512,128]{2,1,0:T(8,128)(2,1)S(1)} %bitcast.37, bf16[2,2,128,128]{3,2,1,0:T(8,128)(2,1)S(1)} %pad.8.fresh_ref, bf16[48,512,128]{2,1,0:T(8,128)(2,1)} %bitcast.42, ...), custom_call_target="tpu_custom_call" | custom-call | flops 1610612736 | bytes 3145728 | tf_op jit(solution)/shard_map/own_blocks/pallas_call | solution.py:481
  19.9 0.0 collective-permute-done.3.refs_6_
  19.9 2.5 %collective-permute-start.7 = (bf16[1,528,128]{2,1,0:T(8,128)(2,1)S(1)}, bf16[1,528,128]{2,1,0:T(8,128)(2,1)S(1)}, u32[]{:S(2)}, u32[]{:S(2)}) collective-permute-start(bf16[1,528,128]{2,1,0:T(8,128)(2,1)S(1)} %collective-permute-done.3.refs_6_), channel_id=1, source_target_pairs={{0,4},{4,0},{8,12},{12,8},{1,5},{5,1},{9,13},{13,9},{2,6},{6,2},{1... | collective-permute-start | bytes 405512 | tf_op jit(solution)/shard_map/ppermute | solution.py:436
  22.4 6.0 %own_blocks.7 = (f32[512,128]{1,0:T(8,128)S(1)}, f32[512,128]{1,0:T(8,128)S(1)}, f32[512,128]{1,0:T(8,128)S(1)}) custom-call(bf16[2,512,128]{2,1,0:T(8,128)(2,1)S(1)} %bitcast.38, bf16[2,2,128,128]{3,2,1,0:T(8,128)(2,1)S(1)} %pad.8.fresh_ref, bf16[48,512,128]{2,1,0:T(8,128)(2,1)} %bitcast.43, f32[2,32,3072]{2,1,0:T(8,128)S(1)} %get-tuple-element.102.refs_0_, ...), custom_call_target="tpu_custom_call" | custom-call | flops 1610612736 | bytes 3145728 | tf_op jit(solution)/shard_map/own_blocks/pallas_call | solution.py:481
  28.5 0.0 collective-permute-done.4.refs_7_
  28.5 0.0 collective-permute-done.5.refs_8_
  28.5 0.0 collective-permute-done.7.refs_12_
  28.5 0.0 collective-permute-done.6.refs_9_
  28.5 0.0 copy-done.1
  28.5 0.0 copy-done.2
  28.5 2.8 %arrived_blocks.3 = (bf16[32,2,16,128]{3,2,1,0:T(8,128)(2,1)}, s32[1,4]{1,0:T(1,128)}, s32[1]{0:T(128)}) custom-call(bf16[2,512,128]{2,1,0:T(8,128)(2,1)S(1)} %bitcast.39, s32[32,16]{1,0:T(8,128)S(1)} %copy.17.refs_0_.tables_ref, s32[32,1]{1,0:T(8,128)S(1)} %copy.18.refs_1_.length_ref, f32[512,128]{1,0:T(8,128)S(1)} %get-tuple-element.99.refs_0_, ...), custom_call_target="tpu_custom_call" | custom-call | flops 536870912 | bytes 1081344 | tf_op jit(solution)/shard_map/arrived_blocks/pallas_call | solution.py:528
  31.3 0.8 %while.9 = (s32[]{:T(128)}, bf16[32,2,2048]{2,1,0:T(2,128)(2,1)}, bf16[32,2,16,128]{3,2,1,0:T(8,128)(2,1)S(1)}, s32[32]{0:T(128)S(1)}, bf16[32,2,2,2,128]{4,1,0,...) while((s32[]{:T(128)}, bf16[32,2,2048]{2,1,0:T(2,128)(2,1)}, ...), condition=%region_1.2_spmd, body=%region_0.1_spmd | while | flops 3758096640 | bytes 39749268 | solution.py:558
  (2 shorter events, 0.0 us)
Async XLA Ops:
  0.6 6.6 %copy-start.6 = (bf16[48,2,2]{0,2,1:T(2,128)(2,1)S(1)}, bf16[48,2,2]{0,2,1:T(2,128)(2,1)}, u32[]{:S(2)}) copy-start(bf16[48,2,2]{0,2,1:T(2,128)(2,1)} %param.13) | copy-start | bytes 1156
  0.6 6.6 %copy-start.8 = (s32[1,4]{1,0:T(1,128)S(1)}, s32[1,4]{1,0:T(1,128)}, u32[]{:S(2)}) copy-start(s32[1,4]{1,0:T(1,128)} %block_ref.3) | copy-start | bytes 52
  0.7 6.6 %copy-start.7 = (s32[1,4]{1,0:T(1,128)S(1)}, s32[1,4]{1,0:T(1,128)}, u32[]{:S(2)}) copy-start(s32[1,4]{1,0:T(1,128)} %dest_ref.2) | copy-start | bytes 52
  0.7 12.6 %copy-start.4 = (bf16[32,2,16,128]{3,2,1,0:T(8,128)(2,1)S(1)}, bf16[32,2,16,128]{3,2,1,0:T(8,128)(2,1)}, u32[]{:S(2)}) copy-start(bf16[32,2,16,128]{3,2,1,0:T(8,128)(2,1)} %param.10) | copy-start | bytes 786436
  0.7 12.8 %copy-start.10 = (s32[32,16]{0,1:T(8,128)S(1)}, s32[32,16]{0,1:T(8,128)}, u32[]{:S(2)}) copy-start(s32[32,16]{0,1:T(8,128)} %param.14) | copy-start | bytes 6148
  0.7 12.9 %copy-start.5 = (bf16[32,2,2,2,128]{4,3,2,1,0:T(2,128)(2,1)S(1)}, bf16[32,2,2,2,128]{4,3,2,1,0:T(2,128)(2,1)}, u32[]{:S(2)}) copy-start(bf16[32,2,2,2,128]{4,3,2,1,0:T(2,128)(2,1)} %param.11) | copy-start | bytes 196612
  0.7 13.0 %copy-start.9 = (s32[32]{0:T(128)S(1)}, s32[32]{0:T(128)}, u32[]{:S(2)}) copy-start(s32[32]{0:T(128)} %param.15) | copy-start | bytes 388
  3.1 16.8 %collective-permute-start.3 = (bf16[1,528,128]{2,1,0:T(8,128)(2,1)}, bf16[1,528,128]{2,1,0:T(8,128)(2,1)S(1)}, u32[]{:S(2)}, u32[]{:S(2)}) collective-permute-start(bf16[1,528,128]{2,1,0:T(8,128)(2,1)} %pack_blocks.4.refs_11_), channel_id=1, source_target_pairs={{0,8},{4,12},{8,0},{12,4},{1,9},{5,13},{9,1},{13,5},{2,10},{6,14},... | collective-permute-start | bytes 405512 | tf_op jit(solution)/shard_map/ppermute | solution.py:436
  9.7 18.8 %collective-permute-start.6 = (bf16[2,528,128]{2,1,0:T(8,128)(2,1)}, bf16[2,528,128]{2,1,0:T(8,128)(2,1)S(1)}, u32[]{:S(2)}, u32[]{:S(2)}) collective-permute-start(bf16[2,528,128]{2,1,0:T(8,128)(2,1)} %get-tuple-element.91), channel_id=1, source_target_pairs={{0,4},{4,0},{8,12},{12,8},{1,5},{5,1},{9,13},{13,9},{2,6},{6,2},{1... | collective-permute-start | bytes 811016 | tf_op jit(solution)/shard_map/ppermute | solution.py:436
  11.3 17.1 %collective-permute-start.4 = (bf16[1,528,128]{2,1,0:T(8,128)(2,1)}, bf16[1,528,128]{2,1,0:T(8,128)(2,1)S(1)}, u32[]{:S(2)}, u32[]{:S(2)}) collective-permute-start(bf16[1,528,128]{2,1,0:T(8,128)(2,1)} %get-tuple-element.93), channel_id=1, source_target_pairs={{0,12},{4,8},{8,4},{12,0},{1,13},{5,9},{9,5},{13,1},{2,14},{6,10},... | collective-permute-start | bytes 405512 | tf_op jit(solution)/shard_map/ppermute | solution.py:436
  11.3 17.1 %collective-permute-start.5 = (bf16[1,528,128]{2,1,0:T(8,128)(2,1)}, bf16[1,528,128]{2,1,0:T(8,128)(2,1)S(1)}, u32[]{:S(2)}, u32[]{:S(2)}) collective-permute-start(bf16[1,528,128]{2,1,0:T(8,128)(2,1)} %get-tuple-element.92), channel_id=1, source_target_pairs={{0,8},{4,12},{8,0},{12,4},{1,9},{5,13},{9,1},{13,5},{2,10},{6,14},... | collective-permute-start | bytes 405512 | tf_op jit(solution)/shard_map/ppermute | solution.py:436
  13.8 14.7 %copy-start.1 = (bf16[1,528,128]{2,1,0:T(8,128)(2,1)S(1)}, bf16[1,528,128]{2,1,0:T(8,128)(2,1)}, u32[]{:S(2)}) copy-start(bf16[1,528,128]{2,1,0:T(8,128)(2,1)} %pack_blocks.4.refs_11_) | copy-start | bytes 405508
  13.8 14.7 %copy-start.2 = (bf16[1,528,128]{2,1,0:T(8,128)(2,1)S(1)}, bf16[1,528,128]{2,1,0:T(8,128)(2,1)}, u32[]{:S(2)}) copy-start(bf16[1,528,128]{2,1,0:T(8,128)(2,1)} %get-tuple-element.90.refs_10_) | copy-start | bytes 405508
  19.9 8.6 %collective-permute-start.7 = (bf16[1,528,128]{2,1,0:T(8,128)(2,1)S(1)}, bf16[1,528,128]{2,1,0:T(8,128)(2,1)S(1)}, u32[]{:S(2)}, u32[]{:S(2)}) collective-permute-start(bf16[1,528,128]{2,1,0:T(8,128)(2,1)S(1)} %collective-permute-done.3.refs_6_), channel_id=1, source_target_pairs={{0,4},{4,0},{8,12},{12,8},{1,5},{5,1},{9,13},{13,9},{2,6},{6,2},{1... | collective-permute-start | bytes 405512 | tf_op jit(solution)/shard_map/ppermute | solution.py:436

commit v22 on v21

--- a/solution.py
+++ b/solution.py
@@ -261,9 +261,11 @@
         scale = row_ref[chunk, heads + head : heads + head + 1, :]
         for row in range(0, height, rows):
             at = pl.ds(row, rows)
-            weight = jnp.exp2(t_ref[chunk, at] - spread(top_ref[at], width))
-            total_ref[at] += lane_fold(weight, jnp.add)
-            p_ref[at] = (weight * scale).astype(jnp.bfloat16)
+            for lane in range(0, width, 1024):
+                part = slice(lane, lane + 1024)
+                weight = jnp.exp2(t_ref[chunk, at, part] - spread(top_ref[at], 1024))
+                total_ref[at] += lane_fold(weight, jnp.add)
+                p_ref[at, part] = (weight * scale[:, part]).astype(jnp.bfloat16)
         acc_ref[...] += jnp.dot(
             p_ref[...],
             codes_ref[1, chunk].reshape(width, head_dim),

time: 32.5 us -> 32.5 us (level)
  no operation moved by 1% of the time
where the time goes in v22:
time: 32.5 us; the launch traced here: 32.3 us
  Pallas kernels  19.8 us (61%)
  starting transfers between devices  10.2 us (31%)
  between operations  1 us (3%)
  loops' own time  0.79 us (2%)
  local copies, waits for them, and re-layouts  0.53 us (2%)
    pallas_call x2, Pallas kernels, own(): pl.pallas_call(functools.partial(own_kernel, (head, pool, heads, rows, st...  12.1 us
    ppermute x5, starting transfers between devices, swap(): lax.ppermute(value, 'inst', [(j, j ^ distance) for j in range(instances)])  10.2 us
    pallas_call x2, Pallas kernels, pack(): pl.pallas_call(functools.partial(pack_kernel, (instances, listed, heads,...  4.87 us
    pallas_call x1, Pallas kernels, attend(): pl.pallas_call(functools.partial(arrival_kernel, (pool, heads, rows, bloc...  2.8 us
    another operation x1, loops' own time, shards(): lax.while_loop(lambda state: state[0] > 1, lambda state: (jnp.int32(0), a...  0.79 us
  transfers between devices with their start and end apart: 5, of which 0 were waited for; matrix products, arithmetic and copies ran while one was open for 2% of the time, Pallas kernels for 45%

profile of v22, /device:TPU:0, one launch (start us, length us, event | category | flops | bytes accessed | tf_op | source)
XLA Modules:
  0.0 32.3 jit_solution(13740192086856160312)
XLA Ops:
  0.6 0.0 copy-start.6
  0.6 0.0 copy-start.8
  0.7 0.0 copy-start.7
  0.7 0.0 copy-start.4
  0.7 0.0 copy-start.10
  0.7 0.0 copy-start.5
  0.7 0.0 copy-start.9
  0.7 2.4 %pack_blocks.4.refs_11_ = bf16[1,528,128]{2,1,0:T(8,128)(2,1)} custom-call(s32[1,4]{1,0:T(1,128)} %dest_ref.2, s32[1,4]{1,0:T(1,128)} %block_ref.3, bf16[2,2,48]{2,1,0:T(2,128)(2,1)} %bitcast.52, bf16[48,512,128]{2,1,0:T(8,128)(2,1)} %bitcast.40), custom_call_target="tpu_custom_call" | custom-call | bytes 270336 | tf_op jit(solution)/shard_map/pack_blocks/pallas_call | solution.py:418
  3.1 4.1 %collective-permute-start.3 = (bf16[1,528,128]{2,1,0:T(8,128)(2,1)}, bf16[1,528,128]{2,1,0:T(8,128)(2,1)S(1)}, u32[]{:S(2)}, u32[]{:S(2)}) collective-permute-start(bf16[1,528,128]{2,1,0:T(8,128)(2,1)} %pack_blocks.4.refs_11_), channel_id=1, source_target_pairs={{0,8},{4,12},{8,0},{12,4},{1,9},{5,13},{9,1},{13,5},{2,10},{6,14},... | collective-permute-start | bytes 405512 | tf_op jit(solution)/shard_map/ppermute | solution.py:438
  7.2 0.0 copy-done.6
  7.2 0.0 copy-done.8
  7.2 0.0 copy-done.7
  7.2 2.5 %pack_blocks.5 = (bf16[1,528,128]{2,1,0:T(8,128)(2,1)}, bf16[2,528,128]{2,1,0:T(8,128)(2,1)}, bf16[1,528,128]{2,1,0:T(8,128)(2,1)}, bf16[1,528,128]{2,1,0:T(8,128)(2,1)}) custom-call(s32[1,4]{1,0:T(1,128)S(1)} %copy-done.7, s32[1,4]{1,0:T(1,128)S(1)} %copy-done.8, bf16[2,2,48]{2,1,0:T(2,128)(2,1)S(1)} %bitcast.53, bf16[48,512,128]{2,1,0:T(8,128)(2,1)} %bitcast.41), custom_call_target="tpu_custom_call" | custom-call | bytes 1351680 | tf_op jit(solution)/shard_map/pack_blocks/pallas_call | solution.py:418
  9.7 1.6 %collective-permute-start.6 = (bf16[2,528,128]{2,1,0:T(8,128)(2,1)}, bf16[2,528,128]{2,1,0:T(8,128)(2,1)S(1)}, u32[]{:S(2)}, u32[]{:S(2)}) collective-permute-start(bf16[2,528,128]{2,1,0:T(8,128)(2,1)} %get-tuple-element.91), channel_id=1, source_target_pairs={{0,4},{4,0},{8,12},{12,8},{1,5},{5,1},{9,13},{13,9},{2,6},{6,2},{1... | collective-permute-start | bytes 811016 | tf_op jit(solution)/shard_map/ppermute | solution.py:438
  11.3 0.0 collective-permute-start.4
  11.3 1.9 %collective-permute-start.5 = (bf16[1,528,128]{2,1,0:T(8,128)(2,1)}, bf16[1,528,128]{2,1,0:T(8,128)(2,1)S(1)}, u32[]{:S(2)}, u32[]{:S(2)}) collective-permute-start(bf16[1,528,128]{2,1,0:T(8,128)(2,1)} %get-tuple-element.92), channel_id=1, source_target_pairs={{0,8},{4,12},{8,0},{12,4},{1,9},{5,13},{9,1},{13,5},{2,10},{6,14},... | collective-permute-start | bytes 405512 | tf_op jit(solution)/shard_map/ppermute | solution.py:438
  13.3 0.0 copy-done.4
  13.3 0.2 copy.13
  13.5 0.0 copy-done.10
  13.5 0.1 copy.17.refs_0_.tables_ref
  13.6 0.0 copy-done.5
  13.6 0.1 copy.19
  13.6 0.1 copy.14
  13.7 0.0 copy-done.9
  13.7 0.1 copy.18.refs_1_.length_ref
  13.8 0.0 copy-start.1
  13.8 0.0 copy-start.2
  13.8 6.1 %own_blocks.6 = (f32[512,128]{1,0:T(8,128)S(1)}, f32[512,128]{1,0:T(8,128)S(1)}, f32[512,128]{1,0:T(8,128)S(1)}, f32[2,32,3072]{2,1,0:T(8,128)S(1)}, f32[2,4,3072]{2,1,0:T(4,128)S(1)}) custom-call(bf16[2,512,128]{2,1,0:T(8,128)(2,1)S(1)} %bitcast.37, bf16[2,2,128,128]{3,2,1,0:T(8,128)(2,1)S(1)} %pad.8.fresh_ref, bf16[48,512,128]{2,1,0:T(8,128)(2,1)} %bitcast.42, ...), custom_call_target="tpu_custom_call" | custom-call | flops 1610612736 | bytes 3145728 | tf_op jit(solution)/shard_map/own_blocks/pallas_call | solution.py:483
  19.9 0.0 collective-permute-done.3.refs_6_
  19.9 2.5 %collective-permute-start.7 = (bf16[1,528,128]{2,1,0:T(8,128)(2,1)S(1)}, bf16[1,528,128]{2,1,0:T(8,128)(2,1)S(1)}, u32[]{:S(2)}, u32[]{:S(2)}) collective-permute-start(bf16[1,528,128]{2,1,0:T(8,128)(2,1)S(1)} %collective-permute-done.3.refs_6_), channel_id=1, source_target_pairs={{0,4},{4,0},{8,12},{12,8},{1,5},{5,1},{9,13},{13,9},{2,6},{6,2},{1... | collective-permute-start | bytes 405512 | tf_op jit(solution)/shard_map/ppermute | solution.py:438
  22.4 6.0 %own_blocks.7 = (f32[512,128]{1,0:T(8,128)S(1)}, f32[512,128]{1,0:T(8,128)S(1)}, f32[512,128]{1,0:T(8,128)S(1)}) custom-call(bf16[2,512,128]{2,1,0:T(8,128)(2,1)S(1)} %bitcast.38, bf16[2,2,128,128]{3,2,1,0:T(8,128)(2,1)S(1)} %pad.8.fresh_ref, bf16[48,512,128]{2,1,0:T(8,128)(2,1)} %bitcast.43, f32[2,32,3072]{2,1,0:T(8,128)S(1)} %get-tuple-element.102.refs_0_, ...), custom_call_target="tpu_custom_call" | custom-call | flops 1610612736 | bytes 3145728 | tf_op jit(solution)/shard_map/own_blocks/pallas_call | solution.py:483
  28.5 0.0 collective-permute-done.4.refs_7_
  28.5 0.0 collective-permute-done.5.refs_8_
  28.5 0.0 collective-permute-done.7.refs_12_
  28.5 0.0 collective-permute-done.6.refs_9_
  28.5 0.0 copy-done.1
  28.5 0.0 copy-done.2
  28.6 2.8 %arrived_blocks.3 = (bf16[32,2,16,128]{3,2,1,0:T(8,128)(2,1)}, s32[1,4]{1,0:T(1,128)}, s32[1]{0:T(128)}) custom-call(bf16[2,512,128]{2,1,0:T(8,128)(2,1)S(1)} %bitcast.39, s32[32,16]{1,0:T(8,128)S(1)} %copy.17.refs_0_.tables_ref, s32[32,1]{1,0:T(8,128)S(1)} %copy.18.refs_1_.length_ref, f32[512,128]{1,0:T(8,128)S(1)} %get-tuple-element.99.refs_0_, ...), custom_call_target="tpu_custom_call" | custom-call | flops 536870912 | bytes 1081344 | tf_op jit(solution)/shard_map/arrived_blocks/pallas_call | solution.py:530
  31.4 0.8 %while.9 = (s32[]{:T(128)}, bf16[32,2,2048]{2,1,0:T(2,128)(2,1)}, bf16[32,2,16,128]{3,2,1,0:T(8,128)(2,1)S(1)}, s32[32]{0:T(128)S(1)}, bf16[32,2,2,2,128]{4,1,0,...) while((s32[]{:T(128)}, bf16[32,2,2048]{2,1,0:T(2,128)(2,1)}, ...), condition=%region_1.2_spmd, body=%region_0.1_spmd | while | flops 3758096640 | bytes 39749268 | solution.py:560
  (2 shorter events, 0.0 us)
Async XLA Ops:
  0.6 6.6 %copy-start.6 = (bf16[48,2,2]{0,2,1:T(2,128)(2,1)S(1)}, bf16[48,2,2]{0,2,1:T(2,128)(2,1)}, u32[]{:S(2)}) copy-start(bf16[48,2,2]{0,2,1:T(2,128)(2,1)} %param.13) | copy-start | bytes 1156
  0.6 6.6 %copy-start.8 = (s32[1,4]{1,0:T(1,128)S(1)}, s32[1,4]{1,0:T(1,128)}, u32[]{:S(2)}) copy-start(s32[1,4]{1,0:T(1,128)} %block_ref.3) | copy-start | bytes 52
  0.7 6.6 %copy-start.7 = (s32[1,4]{1,0:T(1,128)S(1)}, s32[1,4]{1,0:T(1,128)}, u32[]{:S(2)}) copy-start(s32[1,4]{1,0:T(1,128)} %dest_ref.2) | copy-start | bytes 52
  0.7 12.6 %copy-start.4 = (bf16[32,2,16,128]{3,2,1,0:T(8,128)(2,1)S(1)}, bf16[32,2,16,128]{3,2,1,0:T(8,128)(2,1)}, u32[]{:S(2)}) copy-start(bf16[32,2,16,128]{3,2,1,0:T(8,128)(2,1)} %param.10) | copy-start | bytes 786436
  0.7 12.8 %copy-start.10 = (s32[32,16]{0,1:T(8,128)S(1)}, s32[32,16]{0,1:T(8,128)}, u32[]{:S(2)}) copy-start(s32[32,16]{0,1:T(8,128)} %param.14) | copy-start | bytes 6148
  0.7 12.9 %copy-start.5 = (bf16[32,2,2,2,128]{4,3,2,1,0:T(2,128)(2,1)S(1)}, bf16[32,2,2,2,128]{4,3,2,1,0:T(2,128)(2,1)}, u32[]{:S(2)}) copy-start(bf16[32,2,2,2,128]{4,3,2,1,0:T(2,128)(2,1)} %param.11) | copy-start | bytes 196612
  0.7 13.0 %copy-start.9 = (s32[32]{0:T(128)S(1)}, s32[32]{0:T(128)}, u32[]{:S(2)}) copy-start(s32[32]{0:T(128)} %param.15) | copy-start | bytes 388
  3.1 16.8 %collective-permute-start.3 = (bf16[1,528,128]{2,1,0:T(8,128)(2,1)}, bf16[1,528,128]{2,1,0:T(8,128)(2,1)S(1)}, u32[]{:S(2)}, u32[]{:S(2)}) collective-permute-start(bf16[1,528,128]{2,1,0:T(8,128)(2,1)} %pack_blocks.4.refs_11_), channel_id=1, source_target_pairs={{0,8},{4,12},{8,0},{12,4},{1,9},{5,13},{9,1},{13,5},{2,10},{6,14},... | collective-permute-start | bytes 405512 | tf_op jit(solution)/shard_map/ppermute | solution.py:438
  9.7 18.8 %collective-permute-start.6 = (bf16[2,528,128]{2,1,0:T(8,128)(2,1)}, bf16[2,528,128]{2,1,0:T(8,128)(2,1)S(1)}, u32[]{:S(2)}, u32[]{:S(2)}) collective-permute-start(bf16[2,528,128]{2,1,0:T(8,128)(2,1)} %get-tuple-element.91), channel_id=1, source_target_pairs={{0,4},{4,0},{8,12},{12,8},{1,5},{5,1},{9,13},{13,9},{2,6},{6,2},{1... | collective-permute-start | bytes 811016 | tf_op jit(solution)/shard_map/ppermute | solution.py:438
  11.3 17.2 %collective-permute-start.4 = (bf16[1,528,128]{2,1,0:T(8,128)(2,1)}, bf16[1,528,128]{2,1,0:T(8,128)(2,1)S(1)}, u32[]{:S(2)}, u32[]{:S(2)}) collective-permute-start(bf16[1,528,128]{2,1,0:T(8,128)(2,1)} %get-tuple-element.93), channel_id=1, source_target_pairs={{0,12},{4,8},{8,4},{12,0},{1,13},{5,9},{9,5},{13,1},{2,14},{6,10},... | collective-permute-start | bytes 405512 | tf_op jit(solution)/shard_map/ppermute | solution.py:438
  11.3 17.2 %collective-permute-start.5 = (bf16[1,528,128]{2,1,0:T(8,128)(2,1)}, bf16[1,528,128]{2,1,0:T(8,128)(2,1)S(1)}, u32[]{:S(2)}, u32[]{:S(2)}) collective-permute-start(bf16[1,528,128]{2,1,0:T(8,128)(2,1)} %get-tuple-element.92), channel_id=1, source_target_pairs={{0,8},{4,12},{8,0},{12,4},{1,9},{5,13},{9,1},{13,5},{2,10},{6,14},... | collective-permute-start | bytes 405512 | tf_op jit(solution)/shard_map/ppermute | solution.py:438
  13.8 14.7 %copy-start.1 = (bf16[1,528,128]{2,1,0:T(8,128)(2,1)S(1)}, bf16[1,528,128]{2,1,0:T(8,128)(2,1)}, u32[]{:S(2)}) copy-start(bf16[1,528,128]{2,1,0:T(8,128)(2,1)} %pack_blocks.4.refs_11_) | copy-start | bytes 405508
  13.8 14.7 %copy-start.2 = (bf16[1,528,128]{2,1,0:T(8,128)(2,1)S(1)}, bf16[1,528,128]{2,1,0:T(8,128)(2,1)}, u32[]{:S(2)}) copy-start(bf16[1,528,128]{2,1,0:T(8,128)(2,1)} %get-tuple-element.90.refs_10_) | copy-start | bytes 405508
  19.9 8.6 %collective-permute-start.7 = (bf16[1,528,128]{2,1,0:T(8,128)(2,1)S(1)}, bf16[1,528,128]{2,1,0:T(8,128)(2,1)S(1)}, u32[]{:S(2)}, u32[]{:S(2)}) collective-permute-start(bf16[1,528,128]{2,1,0:T(8,128)(2,1)S(1)} %collective-permute-done.3.refs_6_), channel_id=1, source_target_pairs={{0,4},{4,0},{8,12},{12,8},{1,5},{5,1},{9,13},{13,9},{2,6},{6,2},{1... | collective-permute-start | bytes 405512 | tf_op jit(solution)/shard_map/ppermute | solution.py:438
